TPU v7x, 128 devices: a whole 4x4x4 slice. The times are simulated.
128 devices in a mesh: ex: 4 (over x), tp: 4 (over z), ps: 8 (over y, core).
Axes of the slice: x: 4, y: 4, z: 4, core: 2. Of those that a mesh axis runs over, the one named last changes fastest.
Arguments:
- tokens: bfloat16 [4096, 8192], P(('ex', 'ps'), 'tp'), may hold values from -6 to 6
- output_gradient: bfloat16 [4096, 29568], P(('ex', 'ps'), 'tp'), may hold values from -6 to 6
- adapter_down_factor: bfloat16 [8192, 128], P('tp'), may hold values from -0.0625 to 0.0625
- adapter_up_factor: bfloat16 [29568, 128], P('tp'), may hold values from -0.03125 to 0.03125
- first_moment_down: float32 [4, 2048, 128], P('tp', ('ex', 'ps')), may hold values from -0.012 to 0.012
- second_moment_down: float32 [4, 2048, 128], P('tp', ('ex', 'ps')), may hold values from 2e-07 to 2e-06
- first_moment_up: float32 [4, 7392, 128], P('tp', ('ex', 'ps')), may hold values from -0.012 to 0.012
- second_moment_up: float32 [4, 7392, 128], P('tp', ('ex', 'ps')), may hold values from 2e-07 to 2e-06
- down_row_seeds: int32 [4, 2048], P('tp', ('ex', 'ps')), may hold values from 0 to 15
- up_row_seeds: int32 [4, 7392], P('tp', ('ex', 'ps')), may hold values from 0 to 15
- segments: int32 [4096], replicated, may hold values from 0 to 3, never falling along the last dimension, each value on 1 to 2048 neighbouring positions
- bank: bfloat16 [16, 128, 8192], P(None, None, ('ex', 'tp', 'ps')), may hold values from -6 to 6
Outputs:
- sketch: float32 [4, 8192], P(None, ('ex', 'tp', 'ps'))
Inputs may be any that keep to these rules, and one draw needn't show every extreme that they name: `segments`: never falls along the rows; every example has 1 to 2048 rows and one has exactly 2048.
All inputs are finite; a program needn't handle non-finite values.
Results may differ from a plain program's by a relative error of at most 0.0033.
Values may be sent and summed in bfloat16 or wider, within the bound.
No kernel may reach another device: no remote copies, remote signals or barrier semaphores. Data moves between devices by JAX's collectives and lax.ppermute only.
A program may use at most 64 MiB of HBM per device.

v0:
```python
import math

import jax
import jax.numpy as jnp
from jax import lax
from jax.sharding import PartitionSpec as P

MODEL_WIDTH = 8192
HIDDEN_WIDTH = 29568
ADAPTER_RANK = 128
BANK = 16
EXAMPLES = 4


def spread_rows(values, labels):
    count = values.shape[0]
    picks = (labels[:, None] == jnp.arange(EXAMPLES, dtype=jnp.int32)[None, :]).astype(values.dtype)
    return (values[:, None, :] * picks[:, :, None]).reshape(count, EXAMPLES * values.shape[1])


def contract_rows(left, right):
    return lax.dot_general(
        left, right, (((0,), (0,)), ((), ())), preferred_element_type=jnp.float32
    )


def adam_feature(grad, first, second, lengths):
    rows = grad.shape[0]
    scaled_grad = grad.reshape(rows, EXAMPLES, ADAPTER_RANK) / lengths[None, :, None]
    moved = 0.9 * first[0][:, None, :] + 0.1 * scaled_grad
    scaled = 0.999 * second[0][:, None, :] + 0.001 * scaled_grad * scaled_grad
    return moved / (jnp.sqrt(scaled) + 1e-08)


def block_sums(feature, seeds):
    select = (seeds[0][:, None] == jnp.arange(BANK, dtype=jnp.int32)[None, :]).astype(jnp.float32)
    return jnp.einsum("nj,ner->ejr", select, feature, precision=lax.Precision.HIGHEST)


def on_device(
    tokens,
    output_gradient,
    adapter_down_factor,
    adapter_up_factor,
    first_moment_down,
    second_moment_down,
    first_moment_up,
    second_moment_up,
    down_row_seeds,
    up_row_seeds,
    segments,
    bank,
):
    hidden_portion = jnp.dot(tokens, adapter_down_factor, preferred_element_type=jnp.float32)
    input_portion = jnp.dot(output_gradient, adapter_up_factor, preferred_element_type=jnp.float32)
    summed_h, summed_u = lax.psum((hidden_portion, input_portion), "tp")
    hidden_inner_product = summed_h.astype(jnp.bfloat16)
    input_inner_product = summed_u.astype(jnp.bfloat16)
    labels = jnp.arange(EXAMPLES, dtype=jnp.int32)
    lengths = jnp.sum((segments[None, :] == labels[:, None]).astype(jnp.int32), axis=1).astype(
        jnp.float32
    )
    cols_x, cols_g = (
        lax.all_to_all(tokens, ("ex", "ps"), split_axis=1, concat_axis=0, tiled=True),
        lax.all_to_all(output_gradient, ("ex", "ps"), split_axis=1, concat_axis=0, tiled=True),
    )
    piece_h = lax.all_gather(hidden_inner_product, ("ex", "ps"), axis=0, tiled=True)
    piece_u = lax.all_gather(input_inner_product, ("ex", "ps"), axis=0, tiled=True)
    new_a = contract_rows(cols_x, spread_rows(piece_u, segments))
    new_b = contract_rows(cols_g, spread_rows(piece_h, segments))
    feature_a = adam_feature(new_a, first_moment_down, second_moment_down, lengths)
    feature_b = adam_feature(new_b, first_moment_up, second_moment_up, lengths)
    partial_value = block_sums(feature_a, down_row_seeds) + block_sums(feature_b, up_row_seeds)
    summed = lax.psum(partial_value, ("ex", "tp", "ps"))
    inverse = 1.0 / math.sqrt((MODEL_WIDTH + HIDDEN_WIDTH) * ADAPTER_RANK)
    sketch = jnp.einsum(
        "ejr,jrk->ek", summed, bank.astype(jnp.float32), precision=lax.Precision.HIGHEST
    )
    return sketch * inverse


def solution(mesh):
    return jax.shard_map(
        on_device,
        mesh=mesh,
        in_specs=(
            P(("ex", "ps"), "tp"),
            P(("ex", "ps"), "tp"),
            P("tp", None),
            P("tp", None),
            P("tp", ("ex", "ps"), None),
            P("tp", ("ex", "ps"), None),
            P("tp", ("ex", "ps"), None),
            P("tp", ("ex", "ps"), None),
            P("tp", ("ex", "ps")),
            P("tp", ("ex", "ps")),
            P(),
            P(None, None, ("ex", "tp", "ps")),
        ),
        out_specs=P(None, ("ex", "tp", "ps")),
        check_vma=False,
    )
```

profile of v0, /device:TPU:0, one launch (start us, length us, event | category | flops | bytes accessed | tf_op | source)
XLA Modules:
  0.0 235.5 jit_solution(12190122180769735772)
XLA Ops:
  6.5 1.5 copy-done
  8.1 2.2 fusion.53
  10.3 0.3 fusion.54
  10.6 20.3 %all-reduce.2 = (bf16[128,128]{1,0:T(8,128)(2,1)}, bf16[128,128]{1,0:T(8,128)(2,1)}) all-reduce(f32[128,128]{1,0:T(8,128)S(1)} %fusion.54, f32[128,128]{1,0:T(8,128)S(1)} %fusion.53), channel_id=1, replica_groups=mesh['ex'=4,'tp'=4,'ps'=8] {'tp'}, use_global_device_ids=true, to_apply=%region_2.0 | all-reduce | flops 32768 | bytes 196608 | tf_op jit(solution)/shard_map/psum | solution.py:56
  31.0 0.7 all-gather.5.cloned.1.call-update
  31.7 2.7 %all_to_all.32 = bf16[128,32,231]{0,2,1:T(8,128)(2,1)} reshape(bf16[128,7392]{0,1:T(8,128)(2,1)} %param.13) | data formatting | bytes 3784704 | tf_op jit(solution)/shard_map/all_to_all | solution.py:65
  34.4 7.6 %all-to-all-start.1 = ((bf16[128,32,231]{0,2,1:T(8,128)(2,1)}), bf16[128,32,231]{0,2,1:T(8,128)(2,1)}, u32[]{:S(2)}, u32[]{:S(2)}) async-start(bf16[128,32,231]{0,2,1:T(8,128)(2,1)} %all_to_all.32), calls=%async_computation.1 | async-start | bytes 3801088 | tf_op jit(solution)/shard_map/all_to_all | solution.py:65
  42.0 1.0 copy.17
  43.1 0.5 copy.16
  44.1 0.8 copy_bitcast_fusion.1
  44.8 24.2 %all-to-all-done.1 = bf16[128,32,231]{0,2,1:T(8,128)(2,1)} async-done(((bf16[128,32,231]{0,2,1:T(8,128)(2,1)}), bf16[128,32,231]{0,2,1:T(8,128)(2,1)}, u32[]{:S(2)}, u32[]{:S(2)}) %all-to-all-start.1) | async-done | bytes 1892384 | tf_op jit(solution)/shard_map/all_to_all | solution.py:65
  69.1 3.9 %all-to-all-start = ((bf16[128,32,64]{0,2,1:T(8,128)(2,1)}), bf16[128,32,64]{0,2,1:T(8,128)(2,1)S(1)}, u32[]{:S(2)}, u32[]{:S(2)}) async-start(bf16[128,32,64]{0,2,1:T(8,128)(2,1)} %bitcast.1), calls=%async_computation | async-start | bytes 1048576 | tf_op jit(solution)/shard_map/all_to_all | solution.py:64
  72.9 1.8 copy.59
  74.8 0.3 pad
  75.1 2.1 copy.29
  77.2 9.9 %all-gather.3.cloned.1.call-done = bf16[4096,128]{1,0:T(8,128)(2,1)} async-done(((bf16[128,128]{1,0:T(8,128)(2,1)}), bf16[4096,128]{1,0:T(8,128)(2,1)}) %all-gather.3.cloned.1.call-update) | async-done | bytes 1048592 | tf_op jit(solution)/shard_map/all_gather | solution.py:68
  87.2 45.1 %all-gather.5.cloned.1.call-done = bf16[4096,128]{1,0:T(8,128)(2,1)} async-done(((bf16[128,128]{1,0:T(8,128)(2,1)}), bf16[4096,128]{1,0:T(8,128)(2,1)}) %all-gather.5.cloned.1.call-update) | async-done | bytes 1048592 | tf_op jit(solution)/shard_map/all_gather | solution.py:67
  132.3 24.3 %broadcast_multiply_fusion.1 = (bf16[4096,4,128]{2,1,0:T(4,128)(2,1)}, bf16[4096,4,128]{2,1,0:T(4,128)(2,1)S(1)}) fusion(bf16[4096,4]{1,0:T(8,128)(2,1)S(1)} %copy.16, bf16[4096,128]{1,0:T(8,128)(2,1)} %all-gather.3.cloned.1.call-done, bf16[4096,128]{1,0:T(8,128)(2,1)} %all-gather.5.cloned.1.call-done), kind=kLoop, calls=%fused_computation.7 | loop fusion | flops 4194304 | bytes 10518528 | tf_op jit(solution)/shard_map/mul | solution.py:18
  156.5 1.1 fusion.6
  157.9 1.6 fusion.20
  159.5 3.1 %fusion.9 = f32[8,4,8,128]{3,2,1,0:T(8,128)S(1)} fusion(bf16[512,8,4,128]{3,2,1,0:T(4,128)(2,1)} %bitcast.71, bf16[128,32,64]{0,2,1:T(8,128)(2,1)S(1)} %all-to-all-done), kind=kOutput, calls=%fused_computation.10 | convolution fusion | flops 268435456 | bytes 4849664 | tf_op jit(solution)/shard_map/dot_general | solution.py:22
  162.6 0.3 fusion.12
  162.9 64.8 %psum.23 = f32[4,16,128]{2,1,0:T(8,128)S(1)} all-reduce(f32[4,16,128]{2,1,0:T(8,128)S(1)} %fusion.12), channel_id=1, replica_groups=mesh['ex'=4,'tp'=4,'ps'=8] {'ex','tp','ps'}, use_global_device_ids=true, to_apply=%region_3.0 | all-reduce | flops 8192 | bytes 65536 | tf_op jit(solution)/shard_map/psum | solution.py:74
  227.8 0.9 fusion.13
  (34 shorter events, 0.7 us)
Async XLA Ops:
  6.5 1.5 copy-start
  6.5 3.7 %copy-start.1 = (bf16[128,2048]{1,0:T(8,128)(2,1)S(1)}, bf16[128,2048]{1,0:T(8,128)(2,1)}, u32[]{:S(2)}) copy-start(bf16[128,2048]{1,0:T(8,128)(2,1)} %param.12) | copy-start | bytes 1572868
  6.5 3.7 %copy-start.3 = (bf16[2048,128]{1,0:T(8,128)(2,1)S(1)}, bf16[2048,128]{1,0:T(8,128)(2,1)}, u32[]{:S(2)}) copy-start(bf16[2048,128]{1,0:T(8,128)(2,1)} %param.14) | copy-start | bytes 1572868
  6.5 80.6 %all-gather.3.cloned.1.call-start = ((), (), s32[]{:S(2)}) async-start(), calls=%async_computation.2 | async-start | bytes 1081344 | tf_op jit(solution)/shard_map/all_gather | solution.py:68
  30.9 101.3 %all-gather.5.cloned.1.call-start = ((), (), s32[]{:S(2)}) async-start(), calls=%async_computation.3 | async-start | bytes 1081344 | tf_op jit(solution)/shard_map/all_gather | solution.py:67
  34.4 8.7 %copy-start.7 = (s32[4096]{0:T(1024)S(1)}, s32[4096]{0:T(1024)}, u32[]{:S(2)}) copy-start(s32[4096]{0:T(1024)} %param.22) | copy-start | bytes 49156
  34.4 34.7 %all-to-all-start.1 = ((bf16[128,32,231]{0,2,1:T(8,128)(2,1)}), bf16[128,32,231]{0,2,1:T(8,128)(2,1)}, u32[]{:S(2)}, u32[]{:S(2)}) async-start(bf16[128,32,231]{0,2,1:T(8,128)(2,1)} %all_to_all.32), calls=%async_computation.1 | async-start | bytes 3801088 | tf_op jit(solution)/shard_map/all_to_all | solution.py:65
  42.0 1.8 copy-start.8
  42.0 1.8 copy-start.9
  42.0 1.8 copy-start.5
  42.0 1.9 copy-start.6
  69.1 90.4 %all-to-all-start = ((bf16[128,32,64]{0,2,1:T(8,128)(2,1)}), bf16[128,32,64]{0,2,1:T(8,128)(2,1)S(1)}, u32[]{:S(2)}, u32[]{:S(2)}) async-start(bf16[128,32,64]{0,2,1:T(8,128)(2,1)} %bitcast.1), calls=%async_computation | async-start | bytes 1048576 | tf_op jit(solution)/shard_map/all_to_all | solution.py:64
  132.3 24.3 %copy-start.2 = (bf16[29,8,32,128]{3,1,2,0:T(8,128)(2,1)S(1)}, bf16[29,8,32,128]{3,1,2,0:T(8,128)(2,1)}, u32[]{:S(2)}) copy-start(bf16[29,8,32,128]{3,1,2,0:T(8,128)(2,1)} %copy.29) | copy-start | bytes 5701636
  156.5 1.3 copy-start.10
  159.5 3.1 %copy-start.11 = (s32[1,64]{1,0:T(1,128)S(1)}, s32[1,64]{1,0:T(1,128)}, u32[]{:S(2)}) copy-start(s32[1,64]{1,0:T(1,128)} %param.20) | copy-start | bytes 772
  159.5 68.3 %copy-start.4 = (bf16[16,128,64]{1,2,0:T(8,128)(2,1)S(1)}, bf16[16,128,64]{1,2,0:T(8,128)(2,1)}, u32[]{:S(2)}) copy-start(bf16[16,128,64]{1,2,0:T(8,128)(2,1)} %param.23) | copy-start | bytes 786436
Sparse Core Ops, SparseCore 0:
  31.0 56.1 all-gather.2
  89.4 42.7 all-gather.4
where the time goes:
time: 237 us; the launch traced here: 236 us
  blocking collectives  85.1 us (36%)
  waiting for transfers between devices  80 us (34%)
  other arithmetic  24.7 us (10%)
  between operations  13.7 us (6%)
  starting transfers between devices  11.5 us (5%)
  local copies, waits for them, and re-layouts  11 us (5%)
  matrix products  9.53 us (4%)
    psum x1, blocking collectives, on_device(): summed = lax.psum(partial_value, ('ex', 'tp', 'ps'))  64.8 us
    all_gather x1, waiting for transfers between devices, on_device(): lax.all_gather(hidden_inner_product, ('ex', 'ps'), axis=0, tiled=True)  45.1 us
    mul x1, other arithmetic, spread_rows(): values[:, None, :] * picks[:, :, None]  24.3 us
    all_to_all x1, waiting for transfers between devices, on_device(): lax.all_to_all(output_gradient, ('ex', 'ps'), split_axis=1, concat_axis=0...  24.2 us
    psum x1, blocking collectives, on_device(): summed_h, summed_u = lax.psum((hidden_portion, input_portion), 'tp')  20.3 us
    all_gather x1, waiting for transfers between devices, on_device(): lax.all_gather(input_inner_product, ('ex', 'ps'), axis=0, tiled=True)  9.94 us
    all_to_all x1, starting transfers between devices, on_device(): lax.all_to_all(output_gradient, ('ex', 'ps'), split_axis=1, concat_axis=0...  7.56 us
    unnamed x28, local copies, waits for them, and re-layouts  5.83 us
  transfers between devices with their start and end apart: 4, of which 3 were waited for; matrix products, arithmetic and copies ran while one was open for 15% of the time, Pallas kernels for 0%

commit v1 on v0

v1 whole, which is shorter than its diff:
```python
import functools
import math

import jax
import jax.numpy as jnp
from jax import lax
from jax.experimental import pallas as pl
from jax.experimental.pallas import tpu as pltpu
from jax.sharding import Mesh, PartitionSpec as P

MODEL_WIDTH = 8192
HIDDEN_WIDTH = 29568
RANK = 128
BANK = 16
EXAMPLES = 4
UP_ROWS = 231
DOWN_ROWS = 64
WINDOW = 256
ROWS = WINDOW + DOWN_ROWS
LOCAL_UP = 7392
PAIR = 2 * RANK
WIDE = EXAMPLES * RANK
BF = jnp.bfloat16
F32 = jnp.float32
VMEM = pl.BlockSpec(memory_space=pltpu.VMEM)
SMEM = pl.BlockSpec(memory_space=pltpu.SMEM)
PLANE = ("ex", "py", "co")


def window_start(owner):
    return jnp.minimum((owner * UP_ROWS) // 16 * 16, LOCAL_UP - WINDOW)


def along(position, shift):
    x, y, c = position
    return (x, (y + shift) % 4, 0) if c == 0 else ((x + shift) % 4, y, 1)


def across(position, shift):
    x, y, c = position
    return ((x + shift) % 4, y, 0) if c == 0 else (x, (y + shift) % 4, 1)


def flat(position):
    return position[0] * 8 + position[1] * 2 + position[2]


def pairs(move):
    everyone = [(x, y, c) for x in range(4) for y in range(4) for c in range(2)]
    return [(flat(p), flat(move(p))) for p in everyone]


def send_same(value, shift):
    return lax.ppermute(value, PLANE, pairs(lambda p: along(p, shift)))


def send_other(value, shift):
    return lax.ppermute(value, PLANE, pairs(lambda p: along((p[0], p[1], 1 - p[2]), shift)))


def send_across(value, shift):
    return lax.ppermute(value, PLANE, pairs(lambda p: across(p, shift)))


def pack_kernel(owner_ref, start_ref, grad_ref, tokens_ref, *rest):
    outs, turned = rest[:8], rest[8]
    turned[...] = tokens_ref[...].T
    for slot in range(8):
        for i in range(4):
            start = pl.multiple_of(start_ref[slot * 4 + i], 16)
            column = pl.multiple_of(owner_ref[slot * 4 + i] * DOWN_ROWS, DOWN_ROWS)
            outs[slot][i, :WINDOW, :] = grad_ref[pl.ds(start, WINDOW), :]
            outs[slot][i, WINDOW:, :] = turned[pl.ds(column, DOWN_ROWS), :]


def partial_kernel(order_ref, *rest):
    same, other, inner, mask_ref = rest[0:4], rest[4:8], rest[8:12], rest[12]
    own_ref, sends = rest[13], rest[14:17]
    right_h, right_u = rest[17], rest[18]
    for k in range(4):
        for e in range(EXAMPLES):
            picked = mask_ref[k, :, e * RANK:(e + 1) * RANK]
            right_h[k, :, e * RANK:(e + 1) * RANK] = inner[k][:, :RANK] * picked
            right_u[k, :, e * RANK:(e + 1) * RANK] = inner[k][:, RANK:] * picked
    for j in range(4):
        i = order_ref[j]
        up = jnp.zeros((WINDOW, WIDE), F32)
        down = jnp.zeros((DOWN_ROWS, WIDE), F32)
        for k in range(4):
            left = jnp.concatenate([same[k][i], other[k][i]], axis=1)
            up += jnp.dot(left[:WINDOW], right_h[k], preferred_element_type=F32)
            down += jnp.dot(left[WINDOW:], right_u[k], preferred_element_type=F32)
        out = own_ref if j == 0 else sends[j - 1]
        out[:WINDOW, :] = up.astype(out.dtype)
        out[WINDOW:, :] = down.astype(out.dtype)


def feature_kernel(own_ref, a_ref, b_ref, c_ref, length_ref, first_ref, second_ref, select_ref, out_ref):
    first = 0.9 * first_ref[...]
    second = 0.999 * second_ref[...]
    select = select_ref[...]
    for e in range(EXAMPLES):
        at = pl.ds(e * RANK, RANK)
        total = own_ref[:, at] + a_ref[:, at].astype(F32) + b_ref[:, at].astype(F32) + c_ref[:, at].astype(F32)
        grad = total / length_ref[e]
        feature = (first + 0.1 * grad) / (jnp.sqrt(second + 0.001 * grad * grad) + 1e-08)
        high = feature.astype(BF)
        low = (feature - high.astype(F32)).astype(BF)
        out_ref[:, at] = jnp.dot(select, high, preferred_element_type=F32) + jnp.dot(
            select, low, preferred_element_type=F32
        )


def spread_sum(value, axes, count):
    copies = jnp.broadcast_to(value[None], (count,) + value.shape)
    return jnp.sum(lax.all_to_all(copies, axes, split_axis=0, concat_axis=0, tiled=True), axis=0)


def on_device(
    tokens,
    output_gradient,
    adapter_down_factor,
    adapter_up_factor,
    first_moment_down,
    second_moment_down,
    first_moment_up,
    second_moment_up,
    down_row_seeds,
    up_row_seeds,
    segments,
    bank,
):
    x, y, c = lax.axis_index("ex"), lax.axis_index("py"), lax.axis_index("co")
    me = x * 8 + y * 2 + c

    portion = jnp.concatenate(
        [
            jnp.dot(tokens, adapter_down_factor, preferred_element_type=F32),
            jnp.dot(output_gradient, adapter_up_factor, preferred_element_type=F32),
        ],
        axis=1,
    )
    whole = portion
    for shift in (1, 2, 3):
        whole = whole + lax.ppermute(portion, ("t1", "t0"), [(i, (i + shift) % 4) for i in range(4)])
    whole = whole.astype(BF)
    sibling = lax.ppermute(whole, "co", [(0, 1), (1, 0)])
    chip_inner = jnp.concatenate([whole, sibling], axis=0)
    inner = [chip_inner] + [send_same(chip_inner, k) for k in (1, 2, 3)]

    steps = jnp.arange(4, dtype=jnp.int32)
    owners_y = 8 * steps[None, :] + 2 * ((y + steps) % 4)[:, None]
    owners_x = 8 * ((x + steps) % 4)[:, None] + 2 * steps[None, :] + 1
    same_owners = jnp.where(c == 0, owners_y, owners_x)
    other_owners = jnp.where(c == 0, owners_x, owners_y)
    owners = jnp.concatenate([same_owners, other_owners], axis=0).reshape(32)
    packed = pl.pallas_call(
        pack_kernel,
        out_shape=[jax.ShapeDtypeStruct((4, ROWS, 128), BF)] * 8,
        in_specs=[SMEM, SMEM, VMEM, VMEM],
        out_specs=[VMEM] * 8,
        scratch_shapes=[pltpu.VMEM((2048, 128), BF)],
        compiler_params=pltpu.CompilerParams(vmem_limit_bytes=32 << 20),
        cost_estimate=pl.CostEstimate(flops=0, bytes_accessed=5 << 20, transcendentals=0),
    )(owners, window_start(owners), output_gradient.T, tokens)
    same = [packed[0]] + [send_same(packed[k], k) for k in (1, 2, 3)]
    other = [send_other(packed[4 + k], k) for k in range(4)]

    chip_x = jnp.where(c == 0, x, (x - steps) % 4)
    chip_y = jnp.where(c == 0, (y - steps) % 4, y)
    chips = segments.reshape(16, 2, 128)[chip_x * 4 + chip_y]
    labels = jnp.concatenate([jnp.where(c == 0, chips[:, 0], chips[:, 1]), jnp.where(c == 0, chips[:, 1], chips[:, 0])], axis=1)
    mask = (labels[:, :, None] == (jnp.arange(WIDE, dtype=jnp.int32) // RANK)).astype(BF)

    order = (jnp.where(c == 0, x, y) + steps) % 4
    sums = pl.pallas_call(
        partial_kernel,
        out_shape=[jax.ShapeDtypeStruct((ROWS, WIDE), F32)] + [jax.ShapeDtypeStruct((ROWS, WIDE), BF)] * 3,
        in_specs=[SMEM] + [VMEM] * 13,
        out_specs=[VMEM] * 4,
        scratch_shapes=[pltpu.VMEM((4, PAIR, WIDE), BF), pltpu.VMEM((4, PAIR, WIDE), BF)],
        compiler_params=pltpu.CompilerParams(vmem_limit_bytes=32 << 20),
        cost_estimate=pl.CostEstimate(flops=2 * 4 * ROWS * 1024 * WIDE, bytes_accessed=6 << 20, transcendentals=0),
    )(order, *same, *other, *inner, mask)
    arrived = [send_across(sums[k], k) for k in (1, 2, 3)]

    lengths = jnp.sum(
        (segments[None, :] == jnp.arange(EXAMPLES, dtype=jnp.int32)[:, None]).astype(jnp.int32), axis=1
    ).astype(F32)
    offset = me * UP_ROWS - window_start(me)

    def placed(up, down, fill):
        space = jnp.full((WINDOW,) + up.shape[1:], fill, up.dtype)
        return jnp.concatenate([lax.dynamic_update_slice_in_dim(space, up, offset, 0), down], axis=0)

    first = placed(first_moment_up[0], first_moment_down[0], 0)
    second = placed(second_moment_up[0], second_moment_down[0], 0)
    seeds = placed(up_row_seeds[0], down_row_seeds[0], -1)
    select = (jnp.arange(BANK, dtype=jnp.int32)[:, None] == seeds[None, :]).astype(BF)
    blocks = pl.pallas_call(
        feature_kernel,
        out_shape=jax.ShapeDtypeStruct((BANK, WIDE), F32),
        in_specs=[VMEM] * 4 + [SMEM] + [VMEM] * 3,
        out_specs=VMEM,
        compiler_params=pltpu.CompilerParams(vmem_limit_bytes=32 << 20),
        cost_estimate=pl.CostEstimate(flops=0, bytes_accessed=3 << 20, transcendentals=0),
    )(sums[0], *arrived, lengths, first, second, select)

    half = BANK // 2
    kept = lax.dynamic_slice_in_dim(blocks, c * half, half, 0)
    given = lax.dynamic_slice_in_dim(blocks, (1 - c) * half, half, 0)
    total = kept + lax.ppermute(given, "co", [(0, 1), (1, 0)])
    total = spread_sum(total, ("ex", "t1"), 8)
    total = spread_sum(total, ("t0", "py"), 8)
    theirs = lax.ppermute(total, "co", [(0, 1), (1, 0)])
    summed = jnp.concatenate([jnp.where(c == 0, total, theirs), jnp.where(c == 0, theirs, total)], axis=0)
    inverse = 1.0 / math.sqrt((MODEL_WIDTH + HIDDEN_WIDTH) * RANK)
    sketch = jnp.einsum(
        "jer,jrk->ek", summed.reshape(BANK, EXAMPLES, RANK), bank.astype(F32), precision=lax.Precision.HIGHEST
    )
    return sketch * inverse


def solution(mesh):
    rows = ("ex", "py", "co")
    tp = ("t1", "t0")
    split = Mesh(mesh.devices.reshape(4, 2, 2, 4, 2), ("ex", "t1", "t0", "py", "co"))
    return jax.shard_map(
        on_device,
        mesh=split,
        in_specs=(
            P(rows, tp),
            P(rows, tp),
            P(tp, None),
            P(tp, None),
            P(tp, rows, None),
            P(tp, rows, None),
            P(tp, rows, None),
            P(tp, rows, None),
            P(tp, rows),
            P(tp, rows),
            P(),
            P(None, None, ("ex", "t1", "t0", "py", "co")),
        ),
        out_specs=P(None, ("ex", "t1", "t0", "py", "co")),
        check_vma=False,
    )
```

time: 237 us -> 96.4 us (0.41)
  waiting for transfers between devices: 80 us -> 12.1 us
  blocking collectives: 85.1 us -> 22.2 us
  other arithmetic: 24.7 us -> 3.88 us
  starting transfers between devices: 11.5 us -> 27.2 us
  between operations: 13.7 us -> 0.28 us
  local copies, waits for them, and re-layouts: 11 us -> 17.7 us
  Pallas kernels: 0 us -> 6.54 us
  matrix products: 9.53 us -> 4.8 us
    psum x2 -> x0, blocking collectives: 85.1 us -> none  [the longest x1 64.8 us: on_device(): summed = lax.psum(partial_value, ('ex', 'tp', 'ps'))]
    all_gather x2 -> x0, waiting for transfers between devices: 55 us -> none  [the longest x1 45.1 us: on_device(): lax.all_gather(hidden_inner_product, ('ex', 'ps'), axis=0, tiled=True)]
    ppermute x0 -> x19, starting transfers between devices: none -> 27.2 us  [the longest x6 7.19 us: send_same(): return lax.ppermute(value, PLANE, pairs(lambda p: along(p, shift)))]
    mul x4 -> x2, other arithmetic: 24.5 us -> 0.01 us  [the longest x1 0.01 us: on_device(): owners_y = 8 * steps[None, :] + 2 * ((y + steps) % 4)[:, None]]
    all_to_all x2 -> x0, waiting for transfers between devices: 24.2 us -> none  [the longest x1 24.2 us: on_device(): lax.all_to_all(output_gradient, ('ex', 'ps'), split_axis=1, concat_axis=0...]
    all_to_all x0 -> x2, blocking collectives: none -> 22.2 us  [spread_sum(): lax.all_to_all(copies, axes, split_axis=0, concat_axis=0, tiled=True)]
    ppermute x0 -> x19, waiting for transfers between devices: none -> 12.1 us  [the longest x3 6.95 us: send_across(): return lax.ppermute(value, PLANE, pairs(lambda p: across(p, shift)))]
    all_to_all x2 -> x0, starting transfers between devices: 11.5 us -> none  [the longest x1 7.56 us: on_device(): lax.all_to_all(output_gradient, ('ex', 'ps'), split_axis=1, concat_axis=0...]
  transfers between devices with their start and end apart: 4 -> 19, of which waited for: 3 -> 6; matrix products, arithmetic and copies ran while one was open for 15% -> 12% of each run, Pallas kernels for 0% -> 2%
where the time goes in v1:
time: 96.4 us; the launch traced here: 94.7 us
  starting transfers between devices  27.2 us (28%)
  blocking collectives  22.2 us (23%)
  local copies, waits for them, and re-layouts  17.7 us (18%)
  waiting for transfers between devices  12.1 us (13%)
  Pallas kernels  6.54 us (7%)
  matrix products  4.8 us (5%)
  other arithmetic  3.88 us (4%)
    all_to_all x2, blocking collectives, spread_sum(): lax.all_to_all(copies, axes, split_axis=0, concat_axis=0, tiled=True)  22.2 us
    unnamed x40, local copies, waits for them, and re-layouts  12.1 us
    ppermute x6, starting transfers between devices, send_same(): return lax.ppermute(value, PLANE, pairs(lambda p: along(p, shift)))  7.19 us
    ppermute x3, waiting for transfers between devices, send_across(): return lax.ppermute(value, PLANE, pairs(lambda p: across(p, shift)))  6.95 us
    ppermute x4, starting transfers between devices, send_other(): lax.ppermute(value, PLANE, pairs(lambda p: along((p[0], p[1], 1 - p[2]),...  6.61 us
    ppermute x3, starting transfers between devices, on_device(): lax.ppermute(portion, ('t1', 't0'), [(i, (i + shift) % 4) for i in range(...  6.59 us
    ppermute x3, starting transfers between devices, send_across(): return lax.ppermute(value, PLANE, pairs(lambda p: across(p, shift)))  6.13 us
    pallas_call x1, Pallas kernels, on_device(): pl.pallas_call(partial_kernel, out_shape=[jax.ShapeDtypeStruct((ROWS, WID...  3.59 us
  transfers between devices with their start and end apart: 19, of which 6 were waited for; matrix products, arithmetic and copies ran while one was open for 12% of the time, Pallas kernels for 2%

profile of v1, /device:TPU:0, one launch (start us, length us, event | category | flops | bytes accessed | tf_op | source)
XLA Modules:
  0.0 94.7 jit_solution(754036058307386943)
XLA Ops:
  0.0 1.6 %fusion.15 = f32[128,128]{1,0:T(8,128)S(1)} fusion(bf16[128,2048]{1,0:T(8,128)(2,1)} %tokens_ref.1, bf16[2048,128]{1,0:T(8,128)(2,1)} %param.14), kind=kOutput, calls=%fused_computation.71 | convolution fusion | flops 67108864 | bytes 1114112 | tf_op jit(solution)/shard_map/dot_general | solution.py:138
  1.8 2.3 %fusion.16 = f32[128,128]{1,0:T(8,128)S(1)} fusion(bf16[128,7392]{0,1:T(8,128)(2,1)} %param.13, bf16[7392,128]{1,0:T(8,128)(2,1)S(1)} %copy-done), kind=kOutput, calls=%fused_computation.72 | convolution fusion | flops 242221056 | bytes 3850240 | tf_op jit(solution)/shard_map/dot_general | solution.py:139
  4.8 2.0 %collective-permute-start.7 = (f32[128,256]{1,0:T(8,128)}, f32[128,256]{1,0:T(8,128)}, u32[]{:S(2)}, u32[]{:S(2)}) collective-permute-start(f32[128,256]{1,0:T(8,128)} %pad_maximum_fusion.2), channel_id=1, source_target_pairs={{0,8},{8,16},{16,24},{24,0},{1,9},{9,17},{17,25},{25,1},{2,10},{10... | collective-permute-start | bytes 393224 | tf_op jit(solution)/shard_map/ppermute | solution.py:145
  6.8 3.6 %collective-permute-start.8 = (f32[128,256]{1,0:T(8,128)}, f32[128,256]{1,0:T(8,128)}, u32[]{:S(2)}, u32[]{:S(2)}) collective-permute-start(f32[128,256]{1,0:T(8,128)} %pad_maximum_fusion.2), channel_id=1, source_target_pairs={{0,16},{8,24},{16,0},{24,8},{1,17},{9,25},{17,1},{25,9},{2,18},{10... | collective-permute-start | bytes 393224 | tf_op jit(solution)/shard_map/ppermute | solution.py:145
  11.6 1.5 %copy-done.1 = bf16[128,7392]{0,1:T(8,128)(2,1)S(1)} copy-done((bf16[128,7392]{0,1:T(8,128)(2,1)S(1)}, bf16[128,7392]{0,1:T(8,128)(2,1)}, u32[]{:S(2)}) %copy-start.1) | copy-done | bytes 1892376
  13.1 1.7 %shard_map.118 = (bf16[4,320,128]{2,1,0:T(8,128)(2,1)S(1)}, bf16[4,320,128]{2,1,0:T(8,128)(2,1)}, bf16[4,320,128]{2,1,0:T(8,128)(2,1)}, bf16[4,320,128]{2,1,0:T(...) custom-call(s32[32]{0:T(128)S(1)} %reshape.175.owner_ref, ...), custom_call_target="tpu_custom_call" | custom-call | bytes 5242880 | tf_op jit(solution)/shard_map/pallas_call | solution.py:157
  17.0 1.6 %collective-permute-start = (bf16[4,320,128]{2,1,0:T(8,128)(2,1)}, bf16[4,320,128]{2,1,0:T(8,128)(2,1)}, u32[]{:S(2)}, u32[]{:S(2)}) collective-permute-start(bf16[4,320,128]{2,1,0:T(8,128)(2,1)} %get-tuple-element.18), channel_id=1, source_target_pairs={{0,2},{1,33},{2,4},{3,35},{4,6},{5,37},{6,0},{7,39},{32,34},{33,65... | collective-permute-start | bytes 983048 | tf_op jit(solution)/shard_map/ppermute | solution.py:54
  18.6 2.9 %collective-permute-start.1 = (bf16[4,320,128]{2,1,0:T(8,128)(2,1)}, bf16[4,320,128]{2,1,0:T(8,128)(2,1)}, u32[]{:S(2)}, u32[]{:S(2)}) collective-permute-start(bf16[4,320,128]{2,1,0:T(8,128)(2,1)} %get-tuple-element.19), channel_id=1, source_target_pairs={{0,4},{1,65},{2,6},{3,67},{4,0},{5,69},{6,2},{7,71},{32,36},{33,97... | collective-permute-start | bytes 983048 | tf_op jit(solution)/shard_map/ppermute | solution.py:54
  26.7 1.4 %collective-permute-start.4 = (bf16[4,320,128]{2,1,0:T(8,128)(2,1)}, bf16[4,320,128]{2,1,0:T(8,128)(2,1)S(1)}, u32[]{:S(2)}, u32[]{:S(2)}) collective-permute-start(bf16[4,320,128]{2,1,0:T(8,128)(2,1)} %copy-done.11), channel_id=1, source_target_pairs={{0,33},{1,2},{2,35},{3,4},{4,37},{5,6},{6,39},{7,0},{32,65},{33,34... | collective-permute-start | bytes 983048 | tf_op jit(solution)/shard_map/ppermute | solution.py:58
  28.4 2.0 %collective-permute-start.5 = (bf16[4,320,128]{2,1,0:T(8,128)(2,1)}, bf16[4,320,128]{2,1,0:T(8,128)(2,1)}, u32[]{:S(2)}, u32[]{:S(2)}) collective-permute-start(bf16[4,320,128]{2,1,0:T(8,128)(2,1)} %copy-done.4), channel_id=1, source_target_pairs={{0,65},{1,4},{2,67},{3,6},{4,69},{5,0},{6,71},{7,2},{32,97},{33,36... | collective-permute-start | bytes 983048 | tf_op jit(solution)/shard_map/ppermute | solution.py:58
  30.5 3.1 %collective-permute-start.6 = (bf16[4,320,128]{2,1,0:T(8,128)(2,1)}, bf16[4,320,128]{2,1,0:T(8,128)(2,1)}, u32[]{:S(2)}, u32[]{:S(2)}) collective-permute-start(bf16[4,320,128]{2,1,0:T(8,128)(2,1)} %copy-done.3), channel_id=1, source_target_pairs={{0,97},{1,6},{2,99},{3,0},{4,101},{5,2},{6,103},{7,4},{32,1},{33,3... | collective-permute-start | bytes 983048 | tf_op jit(solution)/shard_map/ppermute | solution.py:58
  36.3 1.9 %collective-permute-done.4.rest_5_ = bf16[4,320,128]{2,1,0:T(8,128)(2,1)S(1)} collective-permute-done((bf16[4,320,128]{2,1,0:T(8,128)(2,1)}, bf16[4,320,128]{2,1,0:T(8,128)(2,1)S(1)}, u32[]{:S(2)}, u32[]{:S(2)}) %collective-permute-start.4) | collective-permute-done | bytes 327712 | tf_op jit(solution)/shard_map/ppermute | solution.py:58
  39.1 1.5 %copy.35 = f32[1,231,128]{2,1,0:T(8,128)} copy(f32[1,231,128]{2,0,1:T(1,128)} %param.19) | data formatting | bytes 236544
  40.6 1.5 %copy.36 = f32[1,231,128]{2,1,0:T(8,128)} copy(f32[1,231,128]{2,0,1:T(1,128)} %param.18) | data formatting | bytes 236544
  42.8 1.7 %dynamic_update_slice.10 = f32[256,128]{1,0:T(8,128)} dynamic-update-slice(f32[256,128]{1,0:T(8,128)} %broadcast.294.clone.1, f32[231,128]{1,0:T(8,128)} %bitcast.33, s32[]{:T(128)S(6)} %select_n.179, s32[]{:T(128)} %constant.97.clone.1) | dynamic-update-slice | bytes 236548 | tf_op jit(solution)/shard_map/dynamic_update_slice | solution.py:194
  45.1 1.6 %dynamic_update_slice.9 = f32[256,128]{1,0:T(8,128)} dynamic-update-slice(f32[256,128]{1,0:T(8,128)} %broadcast.294.clone, f32[231,128]{1,0:T(8,128)} %bitcast.32, s32[]{:T(128)S(6)} %select_n.179, s32[]{:T(128)} %constant.97.clone.1) | dynamic-update-slice | bytes 236548 | tf_op jit(solution)/shard_map/dynamic_update_slice | solution.py:194
  51.0 3.6 %shard_map.119 = (f32[320,512]{1,0:T(8,128)S(1)}, bf16[320,512]{1,0:T(8,128)(2,1)S(1)}, bf16[320,512]{1,0:T(8,128)(2,1)S(1)}, bf16[320,512]{1,0:T(8,128)(2,1)S(1)}) custom-call(s32[4]{0:T(128)S(1)} %and_select_fusion.5.order_ref, bf16[4,320,128]{2,1,0:T(8,128)(2,1)S(1)} %get-tuple-element.17.rest_0_, bf16[4,320,128]{2,1,0:T(8,128)(2,1)} %collective-permute-done.rest_1_, ...), custom_call_target="tpu_custom_call" | custom-call | flops 1342177280 | bytes 6291456 | tf_op jit(solution)/shard_map/pallas_call | solution.py:176
  54.6 2.0 %collective-permute-start.14 = (bf16[320,512]{1,0:T(8,128)(2,1)S(1)}, bf16[320,512]{1,0:T(8,128)(2,1)S(1)}, u32[]{:S(2)}, u32[]{:S(2)}) collective-permute-start(bf16[320,512]{1,0:T(8,128)(2,1)S(1)} %get-tuple-element.26), channel_id=1, source_target_pairs={{0,32},{1,3},{2,34},{3,5},{4,36},{5,7},{6,38},{7,1},{32,64},{33,35... | collective-permute-start | bytes 983048 | tf_op jit(solution)/shard_map/ppermute | solution.py:62
  56.6 2.6 %collective-permute-start.15 = (bf16[320,512]{1,0:T(8,128)(2,1)S(1)}, bf16[320,512]{1,0:T(8,128)(2,1)S(1)}, u32[]{:S(2)}, u32[]{:S(2)}) collective-permute-start(bf16[320,512]{1,0:T(8,128)(2,1)S(1)} %get-tuple-element.27), channel_id=1, source_target_pairs={{0,64},{1,5},{2,66},{3,7},{4,68},{5,1},{6,70},{7,3},{32,96},{33,37... | collective-permute-start | bytes 983048 | tf_op jit(solution)/shard_map/ppermute | solution.py:62
  59.2 1.6 %collective-permute-start.16 = (bf16[320,512]{1,0:T(8,128)(2,1)S(1)}, bf16[320,512]{1,0:T(8,128)(2,1)S(1)}, u32[]{:S(2)}, u32[]{:S(2)}) collective-permute-start(bf16[320,512]{1,0:T(8,128)(2,1)S(1)} %get-tuple-element.28), channel_id=1, source_target_pairs={{0,96},{1,7},{2,98},{3,1},{4,100},{5,3},{6,102},{7,5},{32,0},{33,3... | collective-permute-start | bytes 983048 | tf_op jit(solution)/shard_map/ppermute | solution.py:62
  60.8 2.2 %collective-permute-done.14.a_ref = bf16[320,512]{1,0:T(8,128)(2,1)S(1)} collective-permute-done((bf16[320,512]{1,0:T(8,128)(2,1)S(1)}, bf16[320,512]{1,0:T(8,128)(2,1)S(1)}, u32[]{:S(2)}, u32[]{:S(2)}) %collective-permute-start.14) | collective-permute-done | bytes 327712 | tf_op jit(solution)/shard_map/ppermute | solution.py:62
  63.0 4.7 %collective-permute-done.15.b_ref = bf16[320,512]{1,0:T(8,128)(2,1)S(1)} collective-permute-done((bf16[320,512]{1,0:T(8,128)(2,1)S(1)}, bf16[320,512]{1,0:T(8,128)(2,1)S(1)}, u32[]{:S(2)}, u32[]{:S(2)}) %collective-permute-start.15) | collective-permute-done | bytes 327712 | tf_op jit(solution)/shard_map/ppermute | solution.py:62
  70.3 12.1 %all_to_all.10 = f32[8,8,512]{2,1,0:T(8,128)S(1)} all-to-all(f32[8,8,512]{2,1,0:T(8,128)S(1)} %broadcast_in_dim.11), channel_id=1, replica_groups=mesh['ex'=4,'t1'=2,'t0'=2,'py'=4,'co'=2] {'ex','t1'}, dimensions={0} | all-to-all | bytes 262144 | tf_op jit(solution)/shard_map/all_to_all | solution.py:116
  82.4 10.1 %all_to_all.11 = f32[8,8,512]{2,1,0:T(8,128)S(1)} all-to-all(f32[8,8,512]{2,1,0:T(8,128)S(1)} %broadcast_in_dim.12), channel_id=1, replica_groups=mesh['ex'=4,'t1'=2,'t0'=2,'py'=4,'co'=2] {'t0','py'}, dimensions={0} | all-to-all | bytes 262144 | tf_op jit(solution)/shard_map/all_to_all | solution.py:116
  (100 shorter events, 23.6 us)
Async XLA Ops:
  4.1 17.4 %copy-start.15 = (s32[4096]{0:T(1024)S(1)}, s32[4096]{0:T(1024)}, u32[]{:S(2)}) copy-start(s32[4096]{0:T(1024)} %param.22) | copy-start | bytes 49156
  4.8 18.0 %collective-permute-start.7 = (f32[128,256]{1,0:T(8,128)}, f32[128,256]{1,0:T(8,128)}, u32[]{:S(2)}, u32[]{:S(2)}) collective-permute-start(f32[128,256]{1,0:T(8,128)} %pad_maximum_fusion.2), channel_id=1, source_target_pairs={{0,8},{8,16},{16,24},{24,0},{1,9},{9,17},{17,25},{25,1},{2,10},{10... | collective-permute-start | bytes 393224 | tf_op jit(solution)/shard_map/ppermute | solution.py:145
  6.8 17.4 %collective-permute-start.8 = (f32[128,256]{1,0:T(8,128)}, f32[128,256]{1,0:T(8,128)}, u32[]{:S(2)}, u32[]{:S(2)}) collective-permute-start(f32[128,256]{1,0:T(8,128)} %pad_maximum_fusion.2), channel_id=1, source_target_pairs={{0,16},{8,24},{16,0},{24,8},{1,17},{9,25},{17,1},{25,9},{2,18},{10... | collective-permute-start | bytes 393224 | tf_op jit(solution)/shard_map/ppermute | solution.py:145
  10.4 13.8 %collective-permute-start.9 = (f32[128,256]{1,0:T(8,128)}, f32[128,256]{1,0:T(8,128)}, u32[]{:S(2)}, u32[]{:S(2)}) collective-permute-start(f32[128,256]{1,0:T(8,128)} %pad_maximum_fusion.2), channel_id=1, source_target_pairs={{0,24},{8,0},{16,8},{24,16},{1,25},{9,1},{17,9},{25,17},{2,26},{10... | collective-permute-start | bytes 393224 | tf_op jit(solution)/shard_map/ppermute | solution.py:145
  17.0 29.8 %copy-start.16 = (s32[1,231]{1,0:T(1,128)S(1)}, s32[1,231]{1,0:T(1,128)}, u32[]{:S(2)}) copy-start(s32[1,231]{1,0:T(1,128)} %param.21) | copy-start | bytes 2776
  17.0 11.4 %collective-permute-start = (bf16[4,320,128]{2,1,0:T(8,128)(2,1)}, bf16[4,320,128]{2,1,0:T(8,128)(2,1)}, u32[]{:S(2)}, u32[]{:S(2)}) collective-permute-start(bf16[4,320,128]{2,1,0:T(8,128)(2,1)} %get-tuple-element.18), channel_id=1, source_target_pairs={{0,2},{1,33},{2,4},{3,35},{4,6},{5,37},{6,0},{7,39},{32,34},{33,65... | collective-permute-start | bytes 983048 | tf_op jit(solution)/shard_map/ppermute | solution.py:54
  18.6 11.9 %collective-permute-start.1 = (bf16[4,320,128]{2,1,0:T(8,128)(2,1)}, bf16[4,320,128]{2,1,0:T(8,128)(2,1)}, u32[]{:S(2)}, u32[]{:S(2)}) collective-permute-start(bf16[4,320,128]{2,1,0:T(8,128)(2,1)} %get-tuple-element.19), channel_id=1, source_target_pairs={{0,4},{1,65},{2,6},{3,67},{4,0},{5,69},{6,2},{7,71},{32,36},{33,97... | collective-permute-start | bytes 983048 | tf_op jit(solution)/shard_map/ppermute | solution.py:54
  22.8 19.4 %copy-start.18 = (s32[4]{0:T(128)S(1)}, s32[4]{0:T(128)}, u32[]{:S(2)}) copy-start(s32[4]{0:T(128)} %convert_reduce_fusion) | copy-start | bytes 52
  22.8 10.8 %collective-permute-start.2 = (bf16[4,320,128]{2,1,0:T(8,128)(2,1)}, bf16[4,320,128]{2,1,0:T(8,128)(2,1)S(1)}, u32[]{:S(2)}, u32[]{:S(2)}) collective-permute-start(bf16[4,320,128]{2,1,0:T(8,128)(2,1)} %copy-done.13), channel_id=1, source_target_pairs={{0,6},{1,97},{2,0},{3,99},{4,2},{5,101},{6,4},{7,103},{32,38},{33,... | collective-permute-start | bytes 983048 | tf_op jit(solution)/shard_map/ppermute | solution.py:54
  24.1 10.2 %collective-permute-start.3 = (bf16[4,320,128]{2,1,0:T(8,128)(2,1)}, bf16[4,320,128]{2,1,0:T(8,128)(2,1)S(1)}, u32[]{:S(2)}, u32[]{:S(2)}) collective-permute-start(bf16[4,320,128]{2,1,0:T(8,128)(2,1)} %copy-done.12), channel_id=1, source_target_pairs={{0,1},{1,0},{2,3},{3,2},{4,5},{5,4},{6,7},{7,6},{32,33},{33,32},{3... | collective-permute-start | bytes 983048 | tf_op jit(solution)/shard_map/ppermute | solution.py:58
  25.2 1.5 %collective-permute-start.10 = (bf16[128,256]{1,0:T(8,128)(2,1)S(1)}, bf16[128,256]{1,0:T(8,128)(2,1)S(1)}, u32[]{:S(2)}, u32[]{:S(2)}) collective-permute-start(bf16[128,256]{1,0:T(8,128)(2,1)S(1)} %add_convert_fusion), channel_id=1, source_target_pairs={{0,1},{1,0},{2,3},{3,2},{4,5},{5,4},{6,7},{7,6},{8,9},{9,8},{10,11... | collective-permute-start | bytes 196616 | tf_op jit(solution)/shard_map/ppermute | solution.py:147
  26.7 11.4 %collective-permute-start.4 = (bf16[4,320,128]{2,1,0:T(8,128)(2,1)}, bf16[4,320,128]{2,1,0:T(8,128)(2,1)S(1)}, u32[]{:S(2)}, u32[]{:S(2)}) collective-permute-start(bf16[4,320,128]{2,1,0:T(8,128)(2,1)} %copy-done.11), channel_id=1, source_target_pairs={{0,33},{1,2},{2,35},{3,4},{4,37},{5,6},{6,39},{7,0},{32,65},{33,34... | collective-permute-start | bytes 983048 | tf_op jit(solution)/shard_map/ppermute | solution.py:58
  28.4 19.6 %collective-permute-start.5 = (bf16[4,320,128]{2,1,0:T(8,128)(2,1)}, bf16[4,320,128]{2,1,0:T(8,128)(2,1)}, u32[]{:S(2)}, u32[]{:S(2)}) collective-permute-start(bf16[4,320,128]{2,1,0:T(8,128)(2,1)} %copy-done.4), channel_id=1, source_target_pairs={{0,65},{1,4},{2,67},{3,6},{4,69},{5,0},{6,71},{7,2},{32,97},{33,36... | collective-permute-start | bytes 983048 | tf_op jit(solution)/shard_map/ppermute | solution.py:58
  30.5 17.6 %collective-permute-start.6 = (bf16[4,320,128]{2,1,0:T(8,128)(2,1)}, bf16[4,320,128]{2,1,0:T(8,128)(2,1)}, u32[]{:S(2)}, u32[]{:S(2)}) collective-permute-start(bf16[4,320,128]{2,1,0:T(8,128)(2,1)} %copy-done.3), channel_id=1, source_target_pairs={{0,97},{1,6},{2,99},{3,0},{4,101},{5,2},{6,103},{7,4},{32,1},{33,3... | collective-permute-start | bytes 983048 | tf_op jit(solution)/shard_map/ppermute | solution.py:58
  34.3 13.7 %collective-permute-start.11 = (bf16[256,256]{1,0:T(8,128)(2,1)S(1)}, bf16[256,256]{1,0:T(8,128)(2,1)S(1)}, u32[]{:S(2)}, u32[]{:S(2)}) collective-permute-start(bf16[256,256]{1,0:T(8,128)(2,1)S(1)} %pad_maximum_fusion.3.rest_8_), channel_id=1, source_target_pairs={{0,2},{1,33},{2,4},{3,35},{4,6},{5,37},{6,0},{7,39},{32,34},{33,65... | collective-permute-start | bytes 393224 | tf_op jit(solution)/shard_map/ppermute | solution.py:54
  35.1 13.0 %collective-permute-start.12 = (bf16[256,256]{1,0:T(8,128)(2,1)S(1)}, bf16[256,256]{1,0:T(8,128)(2,1)}, u32[]{:S(2)}, u32[]{:S(2)}) collective-permute-start(bf16[256,256]{1,0:T(8,128)(2,1)S(1)} %pad_maximum_fusion.3.rest_8_), channel_id=1, source_target_pairs={{0,4},{1,65},{2,6},{3,67},{4,0},{5,69},{6,2},{7,71},{32,36},{33,97... | collective-permute-start | bytes 393224 | tf_op jit(solution)/shard_map/ppermute | solution.py:54
  38.9 9.2 %collective-permute-start.13 = (bf16[256,256]{1,0:T(8,128)(2,1)S(1)}, bf16[256,256]{1,0:T(8,128)(2,1)}, u32[]{:S(2)}, u32[]{:S(2)}) collective-permute-start(bf16[256,256]{1,0:T(8,128)(2,1)S(1)} %pad_maximum_fusion.3.rest_8_), channel_id=1, source_target_pairs={{0,6},{1,97},{2,0},{3,99},{4,2},{5,101},{6,4},{7,103},{32,38},{33,... | collective-permute-start | bytes 393224 | tf_op jit(solution)/shard_map/ppermute | solution.py:54
  51.0 9.8 %copy-start.17 = (s32[1,64]{1,0:T(1,128)S(1)}, s32[1,64]{1,0:T(1,128)}, u32[]{:S(2)}) copy-start(s32[1,64]{1,0:T(1,128)} %param.20) | copy-start | bytes 772
  54.6 39.2 %copy-start.14 = (bf16[16,128,64]{1,2,0:T(8,128)(2,1)S(1)}, bf16[16,128,64]{1,2,0:T(8,128)(2,1)}, u32[]{:S(2)}) copy-start(bf16[16,128,64]{1,2,0:T(8,128)(2,1)} %param.23) | copy-start | bytes 786436
  54.6 8.4 %collective-permute-start.14 = (bf16[320,512]{1,0:T(8,128)(2,1)S(1)}, bf16[320,512]{1,0:T(8,128)(2,1)S(1)}, u32[]{:S(2)}, u32[]{:S(2)}) collective-permute-start(bf16[320,512]{1,0:T(8,128)(2,1)S(1)} %get-tuple-element.26), channel_id=1, source_target_pairs={{0,32},{1,3},{2,34},{3,5},{4,36},{5,7},{6,38},{7,1},{32,64},{33,35... | collective-permute-start | bytes 983048 | tf_op jit(solution)/shard_map/ppermute | solution.py:62
  56.6 11.1 %collective-permute-start.15 = (bf16[320,512]{1,0:T(8,128)(2,1)S(1)}, bf16[320,512]{1,0:T(8,128)(2,1)S(1)}, u32[]{:S(2)}, u32[]{:S(2)}) collective-permute-start(bf16[320,512]{1,0:T(8,128)(2,1)S(1)} %get-tuple-element.27), channel_id=1, source_target_pairs={{0,64},{1,5},{2,66},{3,7},{4,68},{5,1},{6,70},{7,3},{32,96},{33,37... | collective-permute-start | bytes 983048 | tf_op jit(solution)/shard_map/ppermute | solution.py:62
  59.2 8.6 %collective-permute-start.16 = (bf16[320,512]{1,0:T(8,128)(2,1)S(1)}, bf16[320,512]{1,0:T(8,128)(2,1)S(1)}, u32[]{:S(2)}, u32[]{:S(2)}) collective-permute-start(bf16[320,512]{1,0:T(8,128)(2,1)S(1)} %get-tuple-element.28), channel_id=1, source_target_pairs={{0,96},{1,7},{2,98},{3,1},{4,100},{5,3},{6,102},{7,5},{32,0},{33,3... | collective-permute-start | bytes 983048 | tf_op jit(solution)/shard_map/ppermute | solution.py:62
  69.0 1.2 %collective-permute-start.17 = (f32[8,512]{1,0:T(8,128)S(1)}, f32[8,512]{1,0:T(8,128)S(1)}, u32[]{:S(2)}, u32[]{:S(2)}) collective-permute-start(f32[8,512]{1,0:T(8,128)S(1)} %constant_dynamic-slice_fusion), channel_id=1, source_target_pairs={{0,1},{1,0},{2,3},{3,2},{4,5},{5,4},{6,7},{7,6},{8,9},{9,8},{10,11... | collective-permute-start | bytes 49160 | tf_op jit(solution)/shard_map/ppermute | solution.py:212
  92.5 1.3 %collective-permute-start.18 = (f32[8,512]{1,0:T(8,128)S(1)}, f32[8,512]{1,0:T(8,128)S(1)}, u32[]{:S(2)}, u32[]{:S(2)}) collective-permute-start(f32[8,512]{1,0:T(8,128)S(1)} %reduce_sum.29), channel_id=1, source_target_pairs={{0,1},{1,0},{2,3},{3,2},{4,5},{5,4},{6,7},{7,6},{8,9},{9,8},{10,11... | collective-permute-start | bytes 49160 | tf_op jit(solution)/shard_map/ppermute | solution.py:215
  (14 other events, 39.8 us)

commit v2 on v1

v2 whole, which is shorter than its diff:
```python
import functools
import math

import jax
import jax.numpy as jnp
from jax import lax
from jax.experimental import pallas as pl
from jax.experimental.pallas import tpu as pltpu
from jax.sharding import Mesh, PartitionSpec as P

MODEL_WIDTH = 8192
HIDDEN_WIDTH = 29568
RANK = 128
BANK = 16
EXAMPLES = 4
UP_ROWS = 231
DOWN_ROWS = 64
WINDOW = 256
ROWS = WINDOW + DOWN_ROWS
LOCAL_UP = 7392
PAIR = 2 * RANK
WIDE = EXAMPLES * RANK
BF = jnp.bfloat16
F32 = jnp.float32
VMEM = pl.BlockSpec(memory_space=pltpu.VMEM)
ANY = pl.BlockSpec(memory_space=pl.ANY)
SMEM = pl.BlockSpec(memory_space=pltpu.SMEM)
PLANE = ("ex", "py", "co")


def window_start(owner):
    return jnp.minimum((owner * UP_ROWS) // 16 * 16, LOCAL_UP - WINDOW)


def along(position, shift):
    x, y, c = position
    return (x, (y + shift) % 4, 0) if c == 0 else ((x + shift) % 4, y, 1)


def across(position, shift):
    x, y, c = position
    return ((x + shift) % 4, y, 0) if c == 0 else (x, (y + shift) % 4, 1)


def flat(position):
    return position[0] * 8 + position[1] * 2 + position[2]


def pairs(move):
    everyone = [(x, y, c) for x in range(4) for y in range(4) for c in range(2)]
    return [(flat(p), flat(move(p))) for p in everyone]


def send_same(value, shift):
    return lax.ppermute(value, PLANE, pairs(lambda p: along(p, shift)))


def send_other(value, shift):
    return lax.ppermute(value, PLANE, pairs(lambda p: along((p[0], p[1], 1 - p[2]), shift)))


def send_across(value, shift):
    return lax.ppermute(value, PLANE, pairs(lambda p: across(p, shift)))


def pack_kernel(where_ref, grad_hbm, tokens_ref, down_ref, up_ref, *rest):
    outs, portion_ref = rest[:8], rest[8]
    grad, turned, load, sent = rest[9:]
    load_grad = pltpu.make_async_copy(grad_hbm, grad, load)
    load_grad.start()
    x, y, c = where_ref[0], where_ref[1], where_ref[2]
    turned[...] = tokens_ref[...].T
    copies = []
    for slot in range(8):
        target = c if slot < 4 else 1 - c
        k = slot % 4
        for i in range(4):
            to_x = lax.rem(x + jnp.where(target == 0, i, k), 4)
            to_y = lax.rem(y + jnp.where(target == 0, k, i), 4)
            owner = to_x * 8 + to_y * 2 + target
            start = pl.multiple_of(window_start(owner), 16)
            column = pl.multiple_of(owner * DOWN_ROWS, DOWN_ROWS)
            copies.append(
                pltpu.make_async_copy(
                    grad.at[pl.ds(start, WINDOW)], outs[slot].at[pl.ds(i * WINDOW, WINDOW)], sent
                )
            )
            copies.append(
                pltpu.make_async_copy(
                    turned.at[pl.ds(column, DOWN_ROWS)], outs[slot].at[pl.ds(4 * WINDOW + i * DOWN_ROWS, DOWN_ROWS)], sent
                )
            )
    portion_ref[:, :RANK] = jnp.dot(tokens_ref[...], down_ref[...], preferred_element_type=F32)
    load_grad.wait()
    for copy in copies:
        copy.start()
    product = jnp.zeros((128, RANK), F32)
    for begin in range(0, LOCAL_UP, 1024):
        end = min(begin + 1024, LOCAL_UP)
        product += lax.dot_general(
            grad[begin:end, :], up_ref[begin:end, :], (((0,), (0,)), ((), ())), preferred_element_type=F32
        )
    portion_ref[:, RANK:] = product
    for copy in copies:
        copy.wait()


def partial_kernel(where_ref, bounds_ref, *rest):
    columns, inner = rest[0:8], rest[8:12]
    own_ref, sends = rest[12], rest[13:16]
    left, right_h, right_u, arrive = rest[16:]
    copies = [
        pltpu.make_async_copy(columns[s], left.at[:, pl.ds((2 * (s % 4) + s // 4) * 128, 128)], arrive) for s in range(8)
    ]
    for copy in copies:
        copy.start()
    x, y, c = where_ref[0], where_ref[1], where_ref[2]
    row = lax.broadcasted_iota(jnp.int32, (128, RANK), 0)
    for k in range(4):
        chip = jnp.where(c == 0, x * 4 + lax.rem(y - k + 4, 4), lax.rem(x - k + 4, 4) * 4 + y)
        for part in range(2):
            token = row + (chip * PAIR + jnp.where(part == 0, c, 1 - c) * 128)
            rows = pl.ds(k * PAIR + part * 128, 128)
            h = inner[k][part * 128:(part + 1) * 128, :RANK]
            u = inner[k][part * 128:(part + 1) * 128, RANK:]
            for e in range(EXAMPLES):
                inside = (token >= bounds_ref[e]) & (token < bounds_ref[e + 1])
                picked = jnp.where(inside, 1.0, 0.0).astype(BF)
                right_h[rows, e * RANK:(e + 1) * RANK] = h * picked
                right_u[rows, e * RANK:(e + 1) * RANK] = u * picked
    for copy in copies:
        copy.wait()
    for j in range(4):
        up = jnp.dot(left[j * WINDOW:(j + 1) * WINDOW, :], right_h[...], preferred_element_type=F32)
        out = own_ref if j == 0 else sends[j - 1]
        out[:WINDOW, :] = up.astype(out.dtype)
    down = jnp.dot(left[4 * WINDOW:, :], right_u[...], preferred_element_type=F32)
    for j in range(4):
        out = own_ref if j == 0 else sends[j - 1]
        out[WINDOW:, :] = down[j * DOWN_ROWS:(j + 1) * DOWN_ROWS].astype(out.dtype)


def feature_kernel(
    own_ref, a_ref, b_ref, c_ref, bounds_ref, offset_ref, select_ref,
    first_up, first_down, second_up, second_down, out_ref, first_ref, second_ref,
):
    for up, down, space in ((first_up, first_down, first_ref), (second_up, second_down, second_ref)):
        space[:WINDOW, :] = jnp.zeros((WINDOW, RANK), F32)
        space[:UP_ROWS, :] = up[...]
        space[:WINDOW, :] = pltpu.roll(space[:WINDOW, :], offset_ref[0], 0)
        space[WINDOW:, :] = down[...]
    first = 0.9 * first_ref[...]
    second = 0.999 * second_ref[...]
    select = select_ref[...]
    for e in range(EXAMPLES):
        at = pl.ds(e * RANK, RANK)
        length = (bounds_ref[e + 1] - bounds_ref[e]).astype(F32)
        total = own_ref[:, at] + a_ref[:, at].astype(F32) + b_ref[:, at].astype(F32) + c_ref[:, at].astype(F32)
        grad = total / length
        feature = (first + 0.1 * grad) / (jnp.sqrt(second + 0.001 * grad * grad) + 1e-08)
        high = feature.astype(BF)
        low = (feature - high.astype(F32)).astype(BF)
        out_ref[:, at] = jnp.dot(select, high, preferred_element_type=F32) + jnp.dot(
            select, low, preferred_element_type=F32
        )


def spread_sum(value, axes, count):
    copies = jnp.broadcast_to(value[None], (count,) + value.shape)
    return jnp.sum(lax.all_to_all(copies, axes, split_axis=0, concat_axis=0, tiled=True), axis=0)


def on_device(
    tokens,
    output_gradient,
    adapter_down_factor,
    adapter_up_factor,
    first_moment_down,
    second_moment_down,
    first_moment_up,
    second_moment_up,
    down_row_seeds,
    up_row_seeds,
    segments,
    bank,
):
    x, y, c = lax.axis_index("ex"), lax.axis_index("py"), lax.axis_index("co")
    me = x * 8 + y * 2 + c
    where = jnp.stack([x, y, c]).astype(jnp.int32)
    bounds = jnp.sum(
        (segments[None, :] < jnp.arange(EXAMPLES + 1, dtype=jnp.int32)[:, None]).astype(jnp.int32), axis=1
    )

    packed = pl.pallas_call(
        pack_kernel,
        out_shape=[jax.ShapeDtypeStruct((4 * ROWS, 128), BF)] * 8 + [jax.ShapeDtypeStruct((128, PAIR), F32)],
        in_specs=[SMEM, ANY, VMEM, VMEM, VMEM],
        out_specs=[ANY] * 8 + [VMEM],
        scratch_shapes=[
            pltpu.VMEM((LOCAL_UP, 128), BF),
            pltpu.VMEM((2048, 128), BF),
            pltpu.SemaphoreType.DMA,
            pltpu.SemaphoreType.DMA,
        ],
        compiler_params=pltpu.CompilerParams(vmem_limit_bytes=24 << 20),
        cost_estimate=pl.CostEstimate(flops=2 * 128 * 9440 * 128, bytes_accessed=8 << 20, transcendentals=0),
    )(where, output_gradient.T, tokens, adapter_down_factor, adapter_up_factor)
    portion = packed[8]
    whole = portion
    for shift in (1, 2, 3):
        whole = whole + lax.ppermute(portion, ("t1", "t0"), [(i, (i + shift) % 4) for i in range(4)])
    whole = whole.astype(BF)
    sibling = lax.ppermute(whole, "co", [(0, 1), (1, 0)])
    chip_inner = jnp.concatenate([whole, sibling], axis=0)
    inner = [chip_inner] + [send_same(chip_inner, k) for k in (1, 2, 3)]
    same = [packed[0]] + [send_same(packed[k], k) for k in (1, 2, 3)]
    other = [send_other(packed[4 + k], k) for k in range(4)]

    sums = pl.pallas_call(
        partial_kernel,
        out_shape=[jax.ShapeDtypeStruct((ROWS, WIDE), F32)] + [jax.ShapeDtypeStruct((ROWS, WIDE), BF)] * 3,
        in_specs=[SMEM, SMEM] + [ANY] * 8 + [VMEM] * 4,
        out_specs=[VMEM] * 4,
        scratch_shapes=[
            pltpu.VMEM((4 * ROWS, 1024), BF),
            pltpu.VMEM((1024, WIDE), BF),
            pltpu.VMEM((1024, WIDE), BF),
            pltpu.SemaphoreType.DMA,
        ],
        compiler_params=pltpu.CompilerParams(vmem_limit_bytes=24 << 20),
        cost_estimate=pl.CostEstimate(flops=2 * 4 * ROWS * 1024 * WIDE, bytes_accessed=6 << 20, transcendentals=0),
    )(where, bounds, *same, *other, *inner)
    arrived = [send_across(sums[k], k) for k in (1, 2, 3)]

    kept = (first_moment_up, second_moment_up, up_row_seeds, down_row_seeds)
    own, kept = lax.optimization_barrier((sums[0], kept))
    first_moment_up, second_moment_up, up_row_seeds, down_row_seeds = kept
    offset = me * UP_ROWS - window_start(me)
    seeds = jnp.concatenate(
        [
            lax.dynamic_update_slice_in_dim(jnp.full((WINDOW,), -1, jnp.int32), up_row_seeds[0], offset, 0),
            down_row_seeds[0],
        ]
    )
    select = (jnp.arange(BANK, dtype=jnp.int32)[:, None] == seeds[None, :]).astype(BF)
    blocks = pl.pallas_call(
        feature_kernel,
        out_shape=jax.ShapeDtypeStruct((BANK, WIDE), F32),
        in_specs=[VMEM] * 4 + [SMEM] * 2 + [VMEM] * 5,
        out_specs=VMEM,
        scratch_shapes=[pltpu.VMEM((ROWS, RANK), F32), pltpu.VMEM((ROWS, RANK), F32)],
        compiler_params=pltpu.CompilerParams(vmem_limit_bytes=24 << 20),
        cost_estimate=pl.CostEstimate(flops=0, bytes_accessed=3 << 20, transcendentals=0),
    )(
        own, *arrived, bounds, offset.astype(jnp.int32)[None], select,
        first_moment_up[0], first_moment_down[0], second_moment_up[0], second_moment_down[0],
    )

    half = BANK // 2
    kept = lax.dynamic_slice_in_dim(blocks, c * half, half, 0)
    given = lax.dynamic_slice_in_dim(blocks, (1 - c) * half, half, 0)
    total = kept + lax.ppermute(given, "co", [(0, 1), (1, 0)])
    total = spread_sum(total, ("ex", "t1"), 8)
    total = spread_sum(total, ("t0", "py"), 8)
    theirs = lax.ppermute(total, "co", [(0, 1), (1, 0)])
    summed = jnp.concatenate([jnp.where(c == 0, total, theirs), jnp.where(c == 0, theirs, total)], axis=0)
    inverse = 1.0 / math.sqrt((MODEL_WIDTH + HIDDEN_WIDTH) * RANK)
    sketch = jnp.einsum(
        "jer,jrk->ek", summed.reshape(BANK, EXAMPLES, RANK), bank.astype(F32), precision=lax.Precision.HIGHEST
    )
    return sketch * inverse


def solution(mesh):
    rows = ("ex", "py", "co")
    tp = ("t1", "t0")
    split = Mesh(mesh.devices.reshape(4, 2, 2, 4, 2), ("ex", "t1", "t0", "py", "co"))
    return jax.shard_map(
        on_device,
        mesh=split,
        in_specs=(
            P(rows, tp),
            P(rows, tp),
            P(tp, None),
            P(tp, None),
            P(tp, rows, None),
            P(tp, rows, None),
            P(tp, rows, None),
            P(tp, rows, None),
            P(tp, rows),
            P(tp, rows),
            P(),
            P(None, None, ("ex", "t1", "t0", "py", "co")),
        ),
        out_specs=P(None, ("ex", "t1", "t0", "py", "co")),
        check_vma=False,
    )
```

time: 96.4 us -> 95.1 us (0.987)
  local copies, waits for them, and re-layouts: 17.7 us -> 7.93 us
  waiting for transfers between devices: 12.1 us -> 20.5 us
  Pallas kernels: 6.54 us -> 11.9 us
  matrix products: 4.8 us -> 0.91 us
  other arithmetic: 3.88 us -> 0.32 us
  blocking collectives: 22.2 us -> 23.6 us
  starting transfers between devices: 27.2 us -> 28.3 us
    ppermute x4, waiting for transfers between devices: 1.88 us -> 6.61 us  [send_other(): lax.ppermute(value, PLANE, pairs(lambda p: along((p[0], p[1], 1 - p[2]),...]
    unnamed x40 -> x25, local copies, waits for them, and re-layouts: 12.1 us -> 7.69 us
    pallas_call x1, Pallas kernels: 1.69 us -> 6.13 us  [on_device(): pl.pallas_call(pack_kernel, out_shape=[jax.ShapeDtypeStruct((4 * ROWS, 12...]
    dot_general x2 -> x0, matrix products: 3.89 us -> none  [the longest x1 2.27 us: on_device(): jnp.dot(output_gradient, adapter_up_factor, preferred_element_type=F32)]
    ppermute x6, starting transfers between devices: 7.19 us -> 11 us  [send_same(): return lax.ppermute(value, PLANE, pairs(lambda p: along(p, shift)))]
    ppermute x6, waiting for transfers between devices: 0.02 us -> 3.65 us  [send_same(): return lax.ppermute(value, PLANE, pairs(lambda p: along(p, shift)))]
    dynamic_update_slice x3 -> x1, local copies, waits for them, and re-layouts: 3.54 us -> 0.18 us  [on_device(): lax.dynamic_update_slice_in_dim(jnp.full((WINDOW,), -1, jnp.int32), up_ro...]
    ppermute x4, starting transfers between devices: 6.61 us -> 4.72 us  [send_other(): lax.ppermute(value, PLANE, pairs(lambda p: along((p[0], p[1], 1 - p[2]),...]
  transfers between devices with their start and end apart: 19 -> 19, of which waited for: 6 -> 11; matrix products, arithmetic and copies ran while one was open for 12% -> 1% of each run, Pallas kernels for 2% -> 0%
where the time goes in v2:
time: 95.1 us; the launch traced here: 93.6 us
  starting transfers between devices  28.3 us (30%)
  blocking collectives  23.6 us (25%)
  waiting for transfers between devices  20.5 us (22%)
  Pallas kernels  11.9 us (13%)
  local copies, waits for them, and re-layouts  7.93 us (8%)
    all_to_all x2, blocking collectives, spread_sum(): lax.all_to_all(copies, axes, split_axis=0, concat_axis=0, tiled=True)  23.6 us
    ppermute x6, starting transfers between devices, send_same(): return lax.ppermute(value, PLANE, pairs(lambda p: along(p, shift)))  11 us
    unnamed x25, local copies, waits for them, and re-layouts  7.69 us
    ppermute x3, starting transfers between devices, on_device(): lax.ppermute(portion, ('t1', 't0'), [(i, (i + shift) % 4) for i in range(...  6.67 us
    ppermute x4, waiting for transfers between devices, send_other(): lax.ppermute(value, PLANE, pairs(lambda p: along((p[0], p[1], 1 - p[2]),...  6.61 us
    ppermute x3, waiting for transfers between devices, send_across(): return lax.ppermute(value, PLANE, pairs(lambda p: across(p, shift)))  6.15 us
    pallas_call x1, Pallas kernels, on_device(): pl.pallas_call(pack_kernel, out_shape=[jax.ShapeDtypeStruct((4 * ROWS, 12...  6.13 us
    ppermute x3, starting transfers between devices, send_across(): return lax.ppermute(value, PLANE, pairs(lambda p: across(p, shift)))  5.72 us
  transfers between devices with their start and end apart: 19, of which 11 were waited for; matrix products, arithmetic and copies ran while one was open for 1% of the time, Pallas kernels for 0%

profile of v2, /device:TPU:0, one launch (start us, length us, event | category | flops | bytes accessed | tf_op | source)
XLA Modules:
  0.0 93.6 jit_solution(246876349283885715)
XLA Ops:
  0.1 1.5 %copy-done.1 = bf16[128,7392]{0,1:T(8,128)(2,1)S(1)} copy-done((bf16[128,7392]{0,1:T(8,128)(2,1)S(1)}, bf16[128,7392]{0,1:T(8,128)(2,1)}, u32[]{:S(2)}) %copy-start.1) | copy-done | bytes 1892376
  1.6 1.5 %copy-done.2 = bf16[7392,128]{1,0:T(8,128)(2,1)S(1)} copy-done((bf16[7392,128]{1,0:T(8,128)(2,1)S(1)}, bf16[7392,128]{1,0:T(8,128)(2,1)}, u32[]{:S(2)}) %copy-start.2) | copy-done | bytes 1892376
  5.2 6.1 %shard_map.118 = (bf16[1280,128]{1,0:T(8,128)(2,1)S(1)}, bf16[1280,128]{1,0:T(8,128)(2,1)S(1)}, bf16[1280,128]{1,0:T(8,128)(2,1)S(1)}, bf16[1280,128]{1,0:T(8,12...) custom-call(s32[3]{0:T(128)S(1)} %pad_add_fusion.1.where_ref, ...), custom_call_target="tpu_custom_call" | custom-call | flops 309329920 | bytes 8388608 | tf_op jit(solution)/shard_map/pallas_call | solution.py:194
  11.3 2.1 %collective-permute-start.7 = (f32[128,256]{1,0:T(8,128)S(1)}, f32[128,256]{1,0:T(8,128)S(1)}, u32[]{:S(2)}, u32[]{:S(2)}) collective-permute-start(f32[128,256]{1,0:T(8,128)S(1)} %get-tuple-element.31), channel_id=1, source_target_pairs={{0,8},{8,16},{16,24},{24,0},{1,9},{9,17},{17,25},{25,1},{2,10},{10... | collective-permute-start | bytes 393224 | tf_op jit(solution)/shard_map/ppermute | solution.py:211
  13.4 3.6 %collective-permute-start.8 = (f32[128,256]{1,0:T(8,128)S(1)}, f32[128,256]{1,0:T(8,128)S(1)}, u32[]{:S(2)}, u32[]{:S(2)}) collective-permute-start(f32[128,256]{1,0:T(8,128)S(1)} %get-tuple-element.31), channel_id=1, source_target_pairs={{0,16},{8,24},{16,0},{24,8},{1,17},{9,25},{17,1},{25,9},{2,18},{10... | collective-permute-start | bytes 393224 | tf_op jit(solution)/shard_map/ppermute | solution.py:211
  18.0 1.6 %collective-permute-start = (bf16[1280,128]{1,0:T(8,128)(2,1)S(1)}, bf16[1280,128]{1,0:T(8,128)(2,1)S(1)}, u32[]{:S(2)}, u32[]{:S(2)}) collective-permute-start(bf16[1280,128]{1,0:T(8,128)(2,1)S(1)} %get-tuple-element.24), channel_id=1, source_target_pairs={{0,2},{1,33},{2,4},{3,35},{4,6},{5,37},{6,0},{7,39},{32,34},{33,65... | collective-permute-start | bytes 983048 | tf_op jit(solution)/shard_map/ppermute | solution.py:55
  19.6 2.9 %collective-permute-start.1 = (bf16[1280,128]{1,0:T(8,128)(2,1)S(1)}, bf16[1280,128]{1,0:T(8,128)(2,1)S(1)}, u32[]{:S(2)}, u32[]{:S(2)}) collective-permute-start(bf16[1280,128]{1,0:T(8,128)(2,1)S(1)} %get-tuple-element.25), channel_id=1, source_target_pairs={{0,4},{1,65},{2,6},{3,67},{4,0},{5,69},{6,2},{7,71},{32,36},{33,97... | collective-permute-start | bytes 983048 | tf_op jit(solution)/shard_map/ppermute | solution.py:55
  24.4 1.6 %collective-permute-start.11 = (bf16[256,256]{1,0:T(8,128)(2,1)S(1)}, bf16[256,256]{1,0:T(8,128)(2,1)S(1)}, u32[]{:S(2)}, u32[]{:S(2)}) collective-permute-start(bf16[256,256]{1,0:T(8,128)(2,1)S(1)} %pad_maximum_fusion.rest_8_), channel_id=1, source_target_pairs={{0,2},{1,33},{2,4},{3,35},{4,6},{5,37},{6,0},{7,39},{32,34},{33,65... | collective-permute-start | bytes 393224 | tf_op jit(solution)/shard_map/ppermute | solution.py:55
  26.1 2.9 %collective-permute-start.12 = (bf16[256,256]{1,0:T(8,128)(2,1)S(1)}, bf16[256,256]{1,0:T(8,128)(2,1)S(1)}, u32[]{:S(2)}, u32[]{:S(2)}) collective-permute-start(bf16[256,256]{1,0:T(8,128)(2,1)S(1)} %pad_maximum_fusion.rest_8_), channel_id=1, source_target_pairs={{0,4},{1,65},{2,6},{3,67},{4,0},{5,69},{6,2},{7,71},{32,36},{33,97... | collective-permute-start | bytes 393224 | tf_op jit(solution)/shard_map/ppermute | solution.py:55
  29.0 1.3 %collective-permute-start.13 = (bf16[256,256]{1,0:T(8,128)(2,1)S(1)}, bf16[256,256]{1,0:T(8,128)(2,1)S(1)}, u32[]{:S(2)}, u32[]{:S(2)}) collective-permute-start(bf16[256,256]{1,0:T(8,128)(2,1)S(1)} %pad_maximum_fusion.rest_8_), channel_id=1, source_target_pairs={{0,6},{1,97},{2,0},{3,99},{4,2},{5,101},{6,4},{7,103},{32,38},{33,... | collective-permute-start | bytes 393224 | tf_op jit(solution)/shard_map/ppermute | solution.py:55
  30.3 2.1 %collective-permute-done.11.rest_9_ = bf16[256,256]{1,0:T(8,128)(2,1)S(1)} collective-permute-done((bf16[256,256]{1,0:T(8,128)(2,1)S(1)}, bf16[256,256]{1,0:T(8,128)(2,1)S(1)}, u32[]{:S(2)}, u32[]{:S(2)}) %collective-permute-start.11) | collective-permute-done | bytes 131104 | tf_op jit(solution)/shard_map/ppermute | solution.py:55
  34.6 1.6 %collective-permute-start.4 = (bf16[1280,128]{1,0:T(8,128)(2,1)S(1)}, bf16[1280,128]{1,0:T(8,128)(2,1)}, u32[]{:S(2)}, u32[]{:S(2)}) collective-permute-start(bf16[1280,128]{1,0:T(8,128)(2,1)S(1)} %get-tuple-element.28), channel_id=1, source_target_pairs={{0,33},{1,2},{2,35},{3,4},{4,37},{5,6},{6,39},{7,0},{32,65},{33,34... | collective-permute-start | bytes 983048 | tf_op jit(solution)/shard_map/ppermute | solution.py:59
  36.2 2.2 %collective-permute-start.5 = (bf16[1280,128]{1,0:T(8,128)(2,1)S(1)}, bf16[1280,128]{1,0:T(8,128)(2,1)}, u32[]{:S(2)}, u32[]{:S(2)}) collective-permute-start(bf16[1280,128]{1,0:T(8,128)(2,1)S(1)} %get-tuple-element.29), channel_id=1, source_target_pairs={{0,65},{1,4},{2,67},{3,6},{4,69},{5,0},{6,71},{7,2},{32,97},{33,36... | collective-permute-start | bytes 983048 | tf_op jit(solution)/shard_map/ppermute | solution.py:59
  40.1 2.3 %collective-permute-done.4.rest_5_ = bf16[1280,128]{1,0:T(8,128)(2,1)} collective-permute-done((bf16[1280,128]{1,0:T(8,128)(2,1)S(1)}, bf16[1280,128]{1,0:T(8,128)(2,1)}, u32[]{:S(2)}, u32[]{:S(2)}) %collective-permute-start.4) | collective-permute-done | bytes 327712 | tf_op jit(solution)/shard_map/ppermute | solution.py:59
  42.4 4.3 %collective-permute-done.5.rest_6_ = bf16[1280,128]{1,0:T(8,128)(2,1)} collective-permute-done((bf16[1280,128]{1,0:T(8,128)(2,1)S(1)}, bf16[1280,128]{1,0:T(8,128)(2,1)}, u32[]{:S(2)}, u32[]{:S(2)}) %collective-permute-start.5) | collective-permute-done | bytes 327712 | tf_op jit(solution)/shard_map/ppermute | solution.py:59
  47.6 4.5 %shard_map.119 = (f32[320,512]{1,0:T(8,128)S(1)}, bf16[320,512]{1,0:T(8,128)(2,1)}, bf16[320,512]{1,0:T(8,128)(2,1)S(1)}, bf16[320,512]{1,0:T(8,128)(2,1)S(1)}) custom-call(s32[3]{0:T(128)S(1)} %pad_add_fusion.1.where_ref, s32[5]{0:T(128)S(1)} %convert_reduce_fusion.bounds_ref, bf16[1280,128]{1,0:T(8,128)(2,1)S(1)} %get-tuple-element.23.rest_0_, ...), custom_call_target="tpu_custom_call" | custom-call | flops 1342177280 | bytes 6291456 | tf_op jit(solution)/shard_map/pallas_call | solution.py:219
  52.1 1.6 %collective-permute-start.14 = (bf16[320,512]{1,0:T(8,128)(2,1)}, bf16[320,512]{1,0:T(8,128)(2,1)S(1)}, u32[]{:S(2)}, u32[]{:S(2)}) collective-permute-start(bf16[320,512]{1,0:T(8,128)(2,1)} %get-tuple-element.34), channel_id=1, source_target_pairs={{0,32},{1,3},{2,34},{3,5},{4,36},{5,7},{6,38},{7,1},{32,64},{33,35... | collective-permute-start | bytes 983048 | tf_op jit(solution)/shard_map/ppermute | solution.py:63
  53.7 2.7 %collective-permute-start.15 = (bf16[320,512]{1,0:T(8,128)(2,1)S(1)}, bf16[320,512]{1,0:T(8,128)(2,1)S(1)}, u32[]{:S(2)}, u32[]{:S(2)}) collective-permute-start(bf16[320,512]{1,0:T(8,128)(2,1)S(1)} %get-tuple-element.35), channel_id=1, source_target_pairs={{0,64},{1,5},{2,66},{3,7},{4,68},{5,1},{6,70},{7,3},{32,96},{33,37... | collective-permute-start | bytes 983048 | tf_op jit(solution)/shard_map/ppermute | solution.py:63
  56.4 1.4 %collective-permute-start.16 = (bf16[320,512]{1,0:T(8,128)(2,1)S(1)}, bf16[320,512]{1,0:T(8,128)(2,1)S(1)}, u32[]{:S(2)}, u32[]{:S(2)}) collective-permute-start(bf16[320,512]{1,0:T(8,128)(2,1)S(1)} %get-tuple-element.36), channel_id=1, source_target_pairs={{0,96},{1,7},{2,98},{3,1},{4,100},{5,3},{6,102},{7,5},{32,0},{33,3... | collective-permute-start | bytes 983048 | tf_op jit(solution)/shard_map/ppermute | solution.py:63
  59.0 1.7 %collective-permute-done.14.a_ref = bf16[320,512]{1,0:T(8,128)(2,1)S(1)} collective-permute-done((bf16[320,512]{1,0:T(8,128)(2,1)}, bf16[320,512]{1,0:T(8,128)(2,1)S(1)}, u32[]{:S(2)}, u32[]{:S(2)}) %collective-permute-start.14) | collective-permute-done | bytes 327712 | tf_op jit(solution)/shard_map/ppermute | solution.py:63
  60.7 4.5 %collective-permute-done.15.b_ref = bf16[320,512]{1,0:T(8,128)(2,1)S(1)} collective-permute-done((bf16[320,512]{1,0:T(8,128)(2,1)S(1)}, bf16[320,512]{1,0:T(8,128)(2,1)S(1)}, u32[]{:S(2)}, u32[]{:S(2)}) %collective-permute-start.15) | collective-permute-done | bytes 327712 | tf_op jit(solution)/shard_map/ppermute | solution.py:63
  65.2 1.3 %shard_map.120 = f32[16,512]{1,0:T(8,128)S(1)} custom-call(f32[320,512]{1,0:T(8,128)S(1)} %get-tuple-element.33.own_ref, bf16[320,512]{1,0:T(8,128)(2,1)S(1)} %collective-permute-done.14.a_ref, bf16[320,512]{1,0:T(8,128)(2,1)S(1)} %collective-permute-done.15.b_ref, bf16[320,512]{1,0:T(8,128)(2,1)S(1)} %collective-permute-done.16.c_ref, ...), custom_call_target="tpu_custom_call" | custom-call | bytes 3145728 | tf_op jit(solution)/shard_map/pallas_call | solution.py:246
  67.8 13.4 %all_to_all.10 = f32[8,8,512]{2,1,0:T(8,128)S(1)} all-to-all(f32[8,8,512]{2,1,0:T(8,128)S(1)} %broadcast_in_dim.10), channel_id=1, replica_groups=mesh['ex'=4,'t1'=2,'t0'=2,'py'=4,'co'=2] {'ex','t1'}, dimensions={0} | all-to-all | bytes 262144 | tf_op jit(solution)/shard_map/all_to_all | solution.py:170
  81.2 10.2 %all_to_all.11 = f32[8,8,512]{2,1,0:T(8,128)S(1)} all-to-all(f32[8,8,512]{2,1,0:T(8,128)S(1)} %broadcast_in_dim.11), channel_id=1, replica_groups=mesh['ex'=4,'t1'=2,'t0'=2,'py'=4,'co'=2] {'t0','py'}, dimensions={0} | all-to-all | bytes 262144 | tf_op jit(solution)/shard_map/all_to_all | solution.py:170
  (62 shorter events, 14.5 us)
Async XLA Ops:
  0.0 92.7 %copy-start = (bf16[16,128,64]{1,2,0:T(8,128)(2,1)S(1)}, bf16[16,128,64]{1,2,0:T(8,128)(2,1)}, u32[]{:S(2)}) copy-start(bf16[16,128,64]{1,2,0:T(8,128)(2,1)} %param.23) | copy-start | bytes 786436
  5.2 34.1 %copy-start.9 = (s32[4096]{0:T(1024)S(1)}, s32[4096]{0:T(1024)}, u32[]{:S(2)}) copy-start(s32[4096]{0:T(1024)} %param.22) | copy-start | bytes 49156
  11.3 11.1 %collective-permute-start.7 = (f32[128,256]{1,0:T(8,128)S(1)}, f32[128,256]{1,0:T(8,128)S(1)}, u32[]{:S(2)}, u32[]{:S(2)}) collective-permute-start(f32[128,256]{1,0:T(8,128)S(1)} %get-tuple-element.31), channel_id=1, source_target_pairs={{0,8},{8,16},{16,24},{24,0},{1,9},{9,17},{17,25},{25,1},{2,10},{10... | collective-permute-start | bytes 393224 | tf_op jit(solution)/shard_map/ppermute | solution.py:211
  13.4 9.6 %collective-permute-start.8 = (f32[128,256]{1,0:T(8,128)S(1)}, f32[128,256]{1,0:T(8,128)S(1)}, u32[]{:S(2)}, u32[]{:S(2)}) collective-permute-start(f32[128,256]{1,0:T(8,128)S(1)} %get-tuple-element.31), channel_id=1, source_target_pairs={{0,16},{8,24},{16,0},{24,8},{1,17},{9,25},{17,1},{25,9},{2,18},{10... | collective-permute-start | bytes 393224 | tf_op jit(solution)/shard_map/ppermute | solution.py:211
  17.0 6.0 %collective-permute-start.9 = (f32[128,256]{1,0:T(8,128)S(1)}, f32[128,256]{1,0:T(8,128)S(1)}, u32[]{:S(2)}, u32[]{:S(2)}) collective-permute-start(f32[128,256]{1,0:T(8,128)S(1)} %get-tuple-element.31), channel_id=1, source_target_pairs={{0,24},{8,0},{16,8},{24,16},{1,25},{9,1},{17,9},{25,17},{2,26},{10... | collective-permute-start | bytes 393224 | tf_op jit(solution)/shard_map/ppermute | solution.py:211
  18.0 18.2 %collective-permute-start = (bf16[1280,128]{1,0:T(8,128)(2,1)S(1)}, bf16[1280,128]{1,0:T(8,128)(2,1)S(1)}, u32[]{:S(2)}, u32[]{:S(2)}) collective-permute-start(bf16[1280,128]{1,0:T(8,128)(2,1)S(1)} %get-tuple-element.24), channel_id=1, source_target_pairs={{0,2},{1,33},{2,4},{3,35},{4,6},{5,37},{6,0},{7,39},{32,34},{33,65... | collective-permute-start | bytes 983048 | tf_op jit(solution)/shard_map/ppermute | solution.py:55
  19.6 18.8 %collective-permute-start.1 = (bf16[1280,128]{1,0:T(8,128)(2,1)S(1)}, bf16[1280,128]{1,0:T(8,128)(2,1)S(1)}, u32[]{:S(2)}, u32[]{:S(2)}) collective-permute-start(bf16[1280,128]{1,0:T(8,128)(2,1)S(1)} %get-tuple-element.25), channel_id=1, source_target_pairs={{0,4},{1,65},{2,6},{3,67},{4,0},{5,69},{6,2},{7,71},{32,36},{33,97... | collective-permute-start | bytes 983048 | tf_op jit(solution)/shard_map/ppermute | solution.py:55
  23.1 1.3 %collective-permute-start.10 = (bf16[128,256]{1,0:T(8,128)(2,1)S(1)}, bf16[128,256]{1,0:T(8,128)(2,1)S(1)}, u32[]{:S(2)}, u32[]{:S(2)}) collective-permute-start(bf16[128,256]{1,0:T(8,128)(2,1)S(1)} %add_convert_fusion), channel_id=1, source_target_pairs={{0,1},{1,0},{2,3},{3,2},{4,5},{5,4},{6,7},{7,6},{8,9},{9,8},{10,11... | collective-permute-start | bytes 196616 | tf_op jit(solution)/shard_map/ppermute | solution.py:213
  24.4 8.0 %collective-permute-start.11 = (bf16[256,256]{1,0:T(8,128)(2,1)S(1)}, bf16[256,256]{1,0:T(8,128)(2,1)S(1)}, u32[]{:S(2)}, u32[]{:S(2)}) collective-permute-start(bf16[256,256]{1,0:T(8,128)(2,1)S(1)} %pad_maximum_fusion.rest_8_), channel_id=1, source_target_pairs={{0,2},{1,33},{2,4},{3,35},{4,6},{5,37},{6,0},{7,39},{32,34},{33,65... | collective-permute-start | bytes 393224 | tf_op jit(solution)/shard_map/ppermute | solution.py:55
  26.1 7.8 %collective-permute-start.12 = (bf16[256,256]{1,0:T(8,128)(2,1)S(1)}, bf16[256,256]{1,0:T(8,128)(2,1)S(1)}, u32[]{:S(2)}, u32[]{:S(2)}) collective-permute-start(bf16[256,256]{1,0:T(8,128)(2,1)S(1)} %pad_maximum_fusion.rest_8_), channel_id=1, source_target_pairs={{0,4},{1,65},{2,6},{3,67},{4,0},{5,69},{6,2},{7,71},{32,36},{33,97... | collective-permute-start | bytes 393224 | tf_op jit(solution)/shard_map/ppermute | solution.py:55
  29.0 5.0 %collective-permute-start.13 = (bf16[256,256]{1,0:T(8,128)(2,1)S(1)}, bf16[256,256]{1,0:T(8,128)(2,1)S(1)}, u32[]{:S(2)}, u32[]{:S(2)}) collective-permute-start(bf16[256,256]{1,0:T(8,128)(2,1)S(1)} %pad_maximum_fusion.rest_8_), channel_id=1, source_target_pairs={{0,6},{1,97},{2,0},{3,99},{4,2},{5,101},{6,4},{7,103},{32,38},{33,... | collective-permute-start | bytes 393224 | tf_op jit(solution)/shard_map/ppermute | solution.py:55
  32.5 7.7 %collective-permute-start.2 = (bf16[1280,128]{1,0:T(8,128)(2,1)S(1)}, bf16[1280,128]{1,0:T(8,128)(2,1)}, u32[]{:S(2)}, u32[]{:S(2)}) collective-permute-start(bf16[1280,128]{1,0:T(8,128)(2,1)S(1)} %get-tuple-element.26), channel_id=1, source_target_pairs={{0,6},{1,97},{2,0},{3,99},{4,2},{5,101},{6,4},{7,103},{32,38},{33,... | collective-permute-start | bytes 983048 | tf_op jit(solution)/shard_map/ppermute | solution.py:55
  33.9 6.2 %collective-permute-start.3 = (bf16[1280,128]{1,0:T(8,128)(2,1)S(1)}, bf16[1280,128]{1,0:T(8,128)(2,1)}, u32[]{:S(2)}, u32[]{:S(2)}) collective-permute-start(bf16[1280,128]{1,0:T(8,128)(2,1)S(1)} %get-tuple-element.27), channel_id=1, source_target_pairs={{0,1},{1,0},{2,3},{3,2},{4,5},{5,4},{6,7},{7,6},{32,33},{33,32},{3... | collective-permute-start | bytes 983048 | tf_op jit(solution)/shard_map/ppermute | solution.py:59
  34.6 7.8 %collective-permute-start.4 = (bf16[1280,128]{1,0:T(8,128)(2,1)S(1)}, bf16[1280,128]{1,0:T(8,128)(2,1)}, u32[]{:S(2)}, u32[]{:S(2)}) collective-permute-start(bf16[1280,128]{1,0:T(8,128)(2,1)S(1)} %get-tuple-element.28), channel_id=1, source_target_pairs={{0,33},{1,2},{2,35},{3,4},{4,37},{5,6},{6,39},{7,0},{32,65},{33,34... | collective-permute-start | bytes 983048 | tf_op jit(solution)/shard_map/ppermute | solution.py:59
  36.2 10.5 %collective-permute-start.5 = (bf16[1280,128]{1,0:T(8,128)(2,1)S(1)}, bf16[1280,128]{1,0:T(8,128)(2,1)}, u32[]{:S(2)}, u32[]{:S(2)}) collective-permute-start(bf16[1280,128]{1,0:T(8,128)(2,1)S(1)} %get-tuple-element.29), channel_id=1, source_target_pairs={{0,65},{1,4},{2,67},{3,6},{4,69},{5,0},{6,71},{7,2},{32,97},{33,36... | collective-permute-start | bytes 983048 | tf_op jit(solution)/shard_map/ppermute | solution.py:59
  38.4 8.3 %collective-permute-start.6 = (bf16[1280,128]{1,0:T(8,128)(2,1)S(1)}, bf16[1280,128]{1,0:T(8,128)(2,1)}, u32[]{:S(2)}, u32[]{:S(2)}) collective-permute-start(bf16[1280,128]{1,0:T(8,128)(2,1)S(1)} %get-tuple-element.30), channel_id=1, source_target_pairs={{0,97},{1,6},{2,99},{3,0},{4,101},{5,2},{6,103},{7,4},{32,1},{33,3... | collective-permute-start | bytes 983048 | tf_op jit(solution)/shard_map/ppermute | solution.py:59
  47.6 10.4 %copy-start.11 = (s32[1,64]{1,0:T(1,128)S(1)}, s32[1,64]{1,0:T(1,128)}, u32[]{:S(2)}) copy-start(s32[1,64]{1,0:T(1,128)} %param.20) | copy-start | bytes 772
  47.6 17.5 %copy-start.5 = (f32[1,64,128]{2,1,0:T(8,128)S(1)}, f32[1,64,128]{2,1,0:T(8,128)}, u32[]{:S(2)}) copy-start(f32[1,64,128]{2,1,0:T(8,128)} %param.16) | copy-start | bytes 98308
  47.6 17.5 %copy-start.6 = (f32[1,64,128]{2,1,0:T(8,128)S(1)}, f32[1,64,128]{2,1,0:T(8,128)}, u32[]{:S(2)}) copy-start(f32[1,64,128]{2,1,0:T(8,128)} %param.17) | copy-start | bytes 98308
  52.1 8.6 %collective-permute-start.14 = (bf16[320,512]{1,0:T(8,128)(2,1)}, bf16[320,512]{1,0:T(8,128)(2,1)S(1)}, u32[]{:S(2)}, u32[]{:S(2)}) collective-permute-start(bf16[320,512]{1,0:T(8,128)(2,1)} %get-tuple-element.34), channel_id=1, source_target_pairs={{0,32},{1,3},{2,34},{3,5},{4,36},{5,7},{6,38},{7,1},{32,64},{33,35... | collective-permute-start | bytes 983048 | tf_op jit(solution)/shard_map/ppermute | solution.py:63
  53.7 11.5 %collective-permute-start.15 = (bf16[320,512]{1,0:T(8,128)(2,1)S(1)}, bf16[320,512]{1,0:T(8,128)(2,1)S(1)}, u32[]{:S(2)}, u32[]{:S(2)}) collective-permute-start(bf16[320,512]{1,0:T(8,128)(2,1)S(1)} %get-tuple-element.35), channel_id=1, source_target_pairs={{0,64},{1,5},{2,66},{3,7},{4,68},{5,1},{6,70},{7,3},{32,96},{33,37... | collective-permute-start | bytes 983048 | tf_op jit(solution)/shard_map/ppermute | solution.py:63
  56.4 8.8 %collective-permute-start.16 = (bf16[320,512]{1,0:T(8,128)(2,1)S(1)}, bf16[320,512]{1,0:T(8,128)(2,1)S(1)}, u32[]{:S(2)}, u32[]{:S(2)}) collective-permute-start(bf16[320,512]{1,0:T(8,128)(2,1)S(1)} %get-tuple-element.36), channel_id=1, source_target_pairs={{0,96},{1,7},{2,98},{3,1},{4,100},{5,3},{6,102},{7,5},{32,0},{33,3... | collective-permute-start | bytes 983048 | tf_op jit(solution)/shard_map/ppermute | solution.py:63
  66.5 1.2 %collective-permute-start.17 = (f32[8,512]{1,0:T(8,128)S(1)}, f32[8,512]{1,0:T(8,128)S(1)}, u32[]{:S(2)}, u32[]{:S(2)}) collective-permute-start(f32[8,512]{1,0:T(8,128)S(1)} %constant_dynamic-slice_fusion), channel_id=1, source_target_pairs={{0,1},{1,0},{2,3},{3,2},{4,5},{5,4},{6,7},{7,6},{8,9},{9,8},{10,11... | collective-permute-start | bytes 49160 | tf_op jit(solution)/shard_map/ppermute | solution.py:262
  91.4 1.3 %collective-permute-start.18 = (f32[8,512]{1,0:T(8,128)S(1)}, f32[8,512]{1,0:T(8,128)S(1)}, u32[]{:S(2)}, u32[]{:S(2)}) collective-permute-start(f32[8,512]{1,0:T(8,128)S(1)} %reduce_sum.29), channel_id=1, source_target_pairs={{0,1},{1,0},{2,3},{3,2},{4,5},{5,4},{6,7},{7,6},{8,9},{9,8},{10,11... | collective-permute-start | bytes 49160 | tf_op jit(solution)/shard_map/ppermute | solution.py:265
  (7 other events, 16.9 us)

commit v3 on v2

--- a/solution.py
+++ b/solution.py
@@ -63,14 +63,17 @@
     return lax.ppermute(value, PLANE, pairs(lambda p: across(p, shift)))
 
 
-def pack_kernel(where_ref, grad_hbm, tokens_ref, down_ref, up_ref, *rest):
+def pack_kernel(where_ref, grad_hbm, tokens_hbm, down_hbm, up_hbm, *rest):
     outs, portion_ref = rest[:8], rest[8]
-    grad, turned, load, sent = rest[9:]
-    load_grad = pltpu.make_async_copy(grad_hbm, grad, load)
-    load_grad.start()
+    grad, tokens, down, up, turned, loads, sent = rest[9:]
+    arrivals = [
+        pltpu.make_async_copy(source, target, loads.at[i])
+        for i, (source, target) in enumerate(((tokens_hbm, tokens), (grad_hbm, grad), (down_hbm, down), (up_hbm, up)))
+    ]
+    for arrival in arrivals:
+        arrival.start()
     x, y, c = where_ref[0], where_ref[1], where_ref[2]
-    turned[...] = tokens_ref[...].T
-    copies = []
+    turned_copies, grad_copies = [], []
     for slot in range(8):
         target = c if slot < 4 else 1 - c
         k = slot % 4
@@ -80,64 +83,77 @@
             owner = to_x * 8 + to_y * 2 + target
             start = pl.multiple_of(window_start(owner), 16)
             column = pl.multiple_of(owner * DOWN_ROWS, DOWN_ROWS)
-            copies.append(
+            grad_copies.append(
                 pltpu.make_async_copy(
                     grad.at[pl.ds(start, WINDOW)], outs[slot].at[pl.ds(i * WINDOW, WINDOW)], sent
                 )
             )
-            copies.append(
+            turned_copies.append(
                 pltpu.make_async_copy(
                     turned.at[pl.ds(column, DOWN_ROWS)], outs[slot].at[pl.ds(4 * WINDOW + i * DOWN_ROWS, DOWN_ROWS)], sent
                 )
             )
-    portion_ref[:, :RANK] = jnp.dot(tokens_ref[...], down_ref[...], preferred_element_type=F32)
-    load_grad.wait()
-    for copy in copies:
+    arrivals[0].wait()
+    turned[...] = tokens[...].T
+    for copy in turned_copies:
         copy.start()
+    arrivals[1].wait()
+    for copy in grad_copies:
+        copy.start()
+    arrivals[2].wait()
+    portion_ref[:, :RANK] = jnp.dot(tokens[...], down[...], preferred_element_type=F32)
+    arrivals[3].wait()
     product = jnp.zeros((128, RANK), F32)
     for begin in range(0, LOCAL_UP, 1024):
         end = min(begin + 1024, LOCAL_UP)
         product += lax.dot_general(
-            grad[begin:end, :], up_ref[begin:end, :], (((0,), (0,)), ((), ())), preferred_element_type=F32
+            grad[begin:end, :], up[begin:end, :], (((0,), (0,)), ((), ())), preferred_element_type=F32
         )
     portion_ref[:, RANK:] = product
-    for copy in copies:
+    for copy in turned_copies + grad_copies:
         copy.wait()
 
 
 def partial_kernel(where_ref, bounds_ref, *rest):
-    columns, inner = rest[0:8], rest[8:12]
-    own_ref, sends = rest[12], rest[13:16]
-    left, right_h, right_u, arrive = rest[16:]
-    copies = [
-        pltpu.make_async_copy(columns[s], left.at[:, pl.ds((2 * (s % 4) + s // 4) * 128, 128)], arrive) for s in range(8)
-    ]
-    for copy in copies:
+    columns, inner, outs = rest[0:8], rest[8:12], rest[12:16]
+    left, side, right_h, right_u, own, sends, inner_sem, columns_sem, sent = rest[16:]
+    inner_copies = [pltpu.make_async_copy(inner[k], side.at[k], inner_sem) for k in range(4)]
+    column_copies = [pltpu.make_async_copy(columns[s], left.at[2 * (s % 4) + s // 4], columns_sem) for s in range(8)]
+    for copy in inner_copies + column_copies:
         copy.start()
     x, y, c = where_ref[0], where_ref[1], where_ref[2]
     row = lax.broadcasted_iota(jnp.int32, (128, RANK), 0)
+    for copy in inner_copies:
+        copy.wait()
     for k in range(4):
         chip = jnp.where(c == 0, x * 4 + lax.rem(y - k + 4, 4), lax.rem(x - k + 4, 4) * 4 + y)
         for part in range(2):
             token = row + (chip * PAIR + jnp.where(part == 0, c, 1 - c) * 128)
             rows = pl.ds(k * PAIR + part * 128, 128)
-            h = inner[k][part * 128:(part + 1) * 128, :RANK]
-            u = inner[k][part * 128:(part + 1) * 128, RANK:]
+            h = side[k, part * 128:(part + 1) * 128, :RANK]
+            u = side[k, part * 128:(part + 1) * 128, RANK:]
             for e in range(EXAMPLES):
                 inside = (token >= bounds_ref[e]) & (token < bounds_ref[e + 1])
                 picked = jnp.where(inside, 1.0, 0.0).astype(BF)
                 right_h[rows, e * RANK:(e + 1) * RANK] = h * picked
                 right_u[rows, e * RANK:(e + 1) * RANK] = u * picked
-    for copy in copies:
+    for copy in column_copies:
         copy.wait()
-    for j in range(4):
-        up = jnp.dot(left[j * WINDOW:(j + 1) * WINDOW, :], right_h[...], preferred_element_type=F32)
-        out = own_ref if j == 0 else sends[j - 1]
+
+    def joined(begin, count):
+        return jnp.concatenate([left[s, begin:begin + count, :] for s in range(8)], axis=1)
+
+    down = jnp.dot(joined(4 * WINDOW, 4 * DOWN_ROWS), right_u[...], preferred_element_type=F32)
+    out_copies = []
+    for j in (1, 2, 3, 0):
+        up = jnp.dot(joined(j * WINDOW, WINDOW), right_h[...], preferred_element_type=F32)
+        out = own if j == 0 else sends.at[j - 1]
         out[:WINDOW, :] = up.astype(out.dtype)
-    down = jnp.dot(left[4 * WINDOW:, :], right_u[...], preferred_element_type=F32)
-    for j in range(4):
-        out = own_ref if j == 0 else sends[j - 1]
         out[WINDOW:, :] = down[j * DOWN_ROWS:(j + 1) * DOWN_ROWS].astype(out.dtype)
+        out_copies.append(pltpu.make_async_copy(out, outs[j], sent))
+        out_copies[-1].start()
+    for copy in out_copies:
+        copy.wait()
 
 
 def feature_kernel(
@@ -165,9 +181,31 @@
         )
 
 
-def spread_sum(value, axes, count):
-    copies = jnp.broadcast_to(value[None], (count,) + value.shape)
-    return jnp.sum(lax.all_to_all(copies, axes, split_axis=0, concat_axis=0, tiled=True), axis=0)
+EVERY = ("ex", "t1", "t0", "py", "co")
+
+
+def groups(along_x):
+    found = []
+    for fixed in range(4):
+        for c in range(2):
+            for zs in ((0, 1), (2, 3)) if along_x else ((0, 3), (1, 2)):
+                found.append(
+                    [
+                        (((x * 4 + z) * 4) + y) * 2 + c
+                        for w in range(4)
+                        for z in zs
+                        for x, y in [(w, fixed) if along_x else (fixed, w)]
+                    ]
+                )
+    return found
+
+
+def spread_sum(value, along_x):
+    copies = jnp.broadcast_to(value[None], (8,) + value.shape)
+    arrived = lax.all_to_all(
+        copies, EVERY, split_axis=0, concat_axis=0, tiled=True, axis_index_groups=groups(along_x)
+    )
+    return jnp.sum(arrived, axis=0)
 
 
 def on_device(
@@ -194,15 +232,18 @@
     packed = pl.pallas_call(
         pack_kernel,
         out_shape=[jax.ShapeDtypeStruct((4 * ROWS, 128), BF)] * 8 + [jax.ShapeDtypeStruct((128, PAIR), F32)],
-        in_specs=[SMEM, ANY, VMEM, VMEM, VMEM],
+        in_specs=[SMEM, ANY, ANY, ANY, ANY],
         out_specs=[ANY] * 8 + [VMEM],
         scratch_shapes=[
             pltpu.VMEM((LOCAL_UP, 128), BF),
+            pltpu.VMEM((128, 2048), BF),
             pltpu.VMEM((2048, 128), BF),
-            pltpu.SemaphoreType.DMA,
+            pltpu.VMEM((LOCAL_UP, 128), BF),
+            pltpu.VMEM((2048, 128), BF),
+            pltpu.SemaphoreType.DMA((4,)),
             pltpu.SemaphoreType.DMA,
         ],
-        compiler_params=pltpu.CompilerParams(vmem_limit_bytes=24 << 20),
+        compiler_params=pltpu.CompilerParams(vmem_limit_bytes=60 << 20),
         cost_estimate=pl.CostEstimate(flops=2 * 128 * 9440 * 128, bytes_accessed=8 << 20, transcendentals=0),
     )(where, output_gradient.T, tokens, adapter_down_factor, adapter_up_factor)
     portion = packed[8]
@@ -212,22 +253,28 @@
     whole = whole.astype(BF)
     sibling = lax.ppermute(whole, "co", [(0, 1), (1, 0)])
     chip_inner = jnp.concatenate([whole, sibling], axis=0)
-    inner = [chip_inner] + [send_same(chip_inner, k) for k in (1, 2, 3)]
     same = [packed[0]] + [send_same(packed[k], k) for k in (1, 2, 3)]
     other = [send_other(packed[4 + k], k) for k in range(4)]
+    chip_inner, same[1] = lax.optimization_barrier((chip_inner, same[1]))
+    inner = [chip_inner] + [send_same(chip_inner, k) for k in (1, 2, 3)]
 
     sums = pl.pallas_call(
         partial_kernel,
         out_shape=[jax.ShapeDtypeStruct((ROWS, WIDE), F32)] + [jax.ShapeDtypeStruct((ROWS, WIDE), BF)] * 3,
-        in_specs=[SMEM, SMEM] + [ANY] * 8 + [VMEM] * 4,
-        out_specs=[VMEM] * 4,
+        in_specs=[SMEM, SMEM] + [ANY] * 12,
+        out_specs=[ANY] * 4,
         scratch_shapes=[
-            pltpu.VMEM((4 * ROWS, 1024), BF),
+            pltpu.VMEM((8, 4 * ROWS, 128), BF),
+            pltpu.VMEM((4, PAIR, PAIR), BF),
             pltpu.VMEM((1024, WIDE), BF),
             pltpu.VMEM((1024, WIDE), BF),
+            pltpu.VMEM((ROWS, WIDE), F32),
+            pltpu.VMEM((3, ROWS, WIDE), BF),
+            pltpu.SemaphoreType.DMA,
+            pltpu.SemaphoreType.DMA,
             pltpu.SemaphoreType.DMA,
         ],
-        compiler_params=pltpu.CompilerParams(vmem_limit_bytes=24 << 20),
+        compiler_params=pltpu.CompilerParams(vmem_limit_bytes=60 << 20),
         cost_estimate=pl.CostEstimate(flops=2 * 4 * ROWS * 1024 * WIDE, bytes_accessed=6 << 20, transcendentals=0),
     )(where, bounds, *same, *other, *inner)
     arrived = [send_across(sums[k], k) for k in (1, 2, 3)]
@@ -260,8 +307,8 @@
     kept = lax.dynamic_slice_in_dim(blocks, c * half, half, 0)
     given = lax.dynamic_slice_in_dim(blocks, (1 - c) * half, half, 0)
     total = kept + lax.ppermute(given, "co", [(0, 1), (1, 0)])
-    total = spread_sum(total, ("ex", "t1"), 8)
-    total = spread_sum(total, ("t0", "py"), 8)
+    total = spread_sum(total, True)
+    total = spread_sum(total, False)
     theirs = lax.ppermute(total, "co", [(0, 1), (1, 0)])
     summed = jnp.concatenate([jnp.where(c == 0, total, theirs), jnp.where(c == 0, theirs, total)], axis=0)
     inverse = 1.0 / math.sqrt((MODEL_WIDTH + HIDDEN_WIDTH) * RANK)

time: 95.1 us -> 92.8 us (0.976)
  local copies, waits for them, and re-layouts: 7.93 us -> 1.98 us
  waiting for transfers between devices: 20.5 us -> 23.5 us
  other arithmetic: 0.32 us -> 2.26 us
  starting transfers between devices: 28.3 us -> 26.9 us
    ppermute x6, waiting for transfers between devices: 3.65 us -> 10.7 us  [send_same(): return lax.ppermute(value, PLANE, pairs(lambda p: along(p, shift)))]
    ppermute x4, waiting for transfers between devices: 6.61 us -> 0.01 us  [send_other(): lax.ppermute(value, PLANE, pairs(lambda p: along((p[0], p[1], 1 - p[2]),...]
    unnamed x25 -> x43, local copies, waits for them, and re-layouts: 7.69 us -> 1.75 us
    ppermute x3, waiting for transfers between devices: 0.53 us -> 3.64 us  [on_device(): lax.ppermute(portion, ('t1', 't0'), [(i, (i + shift) % 4) for i in range(...]
    pallas_call x1, Pallas kernels: 6.13 us -> 4.79 us  [on_device(): pl.pallas_call(pack_kernel, out_shape=[jax.ShapeDtypeStruct((4 * ROWS, 12...]
    ppermute x1, waiting for transfers between devices: 1.24 us -> 0.01 us  [on_device(): sibling = lax.ppermute(whole, 'co', [(0, 1), (1, 0)])]
    ppermute x6, starting transfers between devices: 11 us -> 9.85 us  [send_same(): return lax.ppermute(value, PLANE, pairs(lambda p: along(p, shift)))]
    pallas_call x1, Pallas kernels: 4.46 us -> 5.48 us  [on_device(): pl.pallas_call(partial_kernel, out_shape=[jax.ShapeDtypeStruct((ROWS, WID...]
  transfers between devices with their start and end apart: 19 -> 19, of which waited for: 11 -> 9; matrix products, arithmetic and copies ran while one was open for 1% -> 2% of each run, Pallas kernels for 0% -> 0%
where the time goes in v3:
time: 92.8 us; the launch traced here: 91.5 us
  starting transfers between devices  26.9 us (29%)
  blocking collectives  24 us (26%)
  waiting for transfers between devices  23.5 us (25%)
  Pallas kernels  11.6 us (12%)
  other arithmetic  2.26 us (2%)
  local copies, waits for them, and re-layouts  1.98 us (2%)
    all_to_all x2, blocking collectives, spread_sum(): lax.all_to_all(copies, EVERY, split_axis=0, concat_axis=0, tiled=True, ax...  24 us
    ppermute x6, waiting for transfers between devices, send_same(): return lax.ppermute(value, PLANE, pairs(lambda p: along(p, shift)))  10.7 us
    ppermute x6, starting transfers between devices, send_same(): return lax.ppermute(value, PLANE, pairs(lambda p: along(p, shift)))  9.85 us
    ppermute x3, waiting for transfers between devices, send_across(): return lax.ppermute(value, PLANE, pairs(lambda p: across(p, shift)))  6.83 us
    ppermute x3, starting transfers between devices, on_device(): lax.ppermute(portion, ('t1', 't0'), [(i, (i + shift) % 4) for i in range(...  6.66 us
    ppermute x3, starting transfers between devices, send_across(): return lax.ppermute(value, PLANE, pairs(lambda p: across(p, shift)))  6.37 us
    pallas_call x1, Pallas kernels, on_device(): pl.pallas_call(partial_kernel, out_shape=[jax.ShapeDtypeStruct((ROWS, WID...  5.48 us
    pallas_call x1, Pallas kernels, on_device(): pl.pallas_call(pack_kernel, out_shape=[jax.ShapeDtypeStruct((4 * ROWS, 12...  4.79 us
  transfers between devices with their start and end apart: 19, of which 9 were waited for; matrix products, arithmetic and copies ran while one was open for 2% of the time, Pallas kernels for 0%

profile of v3, /device:TPU:0, one launch (start us, length us, event | category | flops | bytes accessed | tf_op | source)
XLA Modules:
  0.0 91.5 jit_solution(15457720289938131618)
XLA Ops:
  0.6 4.8 %shard_map.118 = (bf16[1280,128]{1,0:T(8,128)(2,1)}, bf16[1280,128]{1,0:T(8,128)(2,1)}, bf16[1280,128]{1,0:T(8,128)(2,1)}, bf16[1280,128]{1,0:T(8,128)(2,1)}, bf...) custom-call(s32[3]{0:T(128)} %pad_add_fusion.1.where_ref, ...), custom_call_target="tpu_custom_call" | custom-call | flops 309329920 | bytes 8388608 | tf_op jit(solution)/shard_map/pallas_call | solution.py:232
  5.4 2.1 %collective-permute-start = (f32[128,256]{1,0:T(8,128)}, f32[128,256]{1,0:T(8,128)S(1)}, u32[]{:S(2)}, u32[]{:S(2)}) collective-permute-start(f32[128,256]{1,0:T(8,128)} %get-tuple-element.26), channel_id=1, source_target_pairs={{0,8},{8,16},{16,24},{24,0},{1,9},{9,17},{17,25},{25,1},{2,10},{10... | collective-permute-start | bytes 393224 | tf_op jit(solution)/shard_map/ppermute | solution.py:252
  7.5 3.6 %collective-permute-start.1 = (f32[128,256]{1,0:T(8,128)}, f32[128,256]{1,0:T(8,128)S(1)}, u32[]{:S(2)}, u32[]{:S(2)}) collective-permute-start(f32[128,256]{1,0:T(8,128)} %get-tuple-element.26), channel_id=1, source_target_pairs={{0,16},{8,24},{16,0},{24,8},{1,17},{9,25},{17,1},{25,9},{2,18},{10... | collective-permute-start | bytes 393224 | tf_op jit(solution)/shard_map/ppermute | solution.py:252
  12.1 1.6 %collective-permute-start.4 = (bf16[1280,128]{1,0:T(8,128)(2,1)}, bf16[1280,128]{1,0:T(8,128)(2,1)S(1)}, u32[]{:S(2)}, u32[]{:S(2)}) collective-permute-start(bf16[1280,128]{1,0:T(8,128)(2,1)} %get-tuple-element.27), channel_id=1, source_target_pairs={{0,2},{1,33},{2,4},{3,35},{4,6},{5,37},{6,0},{7,39},{32,34},{33,65... | collective-permute-start | bytes 983048 | tf_op jit(solution)/shard_map/ppermute | solution.py:55
  13.6 3.6 %collective-permute-done.1 = f32[128,256]{1,0:T(8,128)S(1)} collective-permute-done((f32[128,256]{1,0:T(8,128)}, f32[128,256]{1,0:T(8,128)S(1)}, u32[]{:S(2)}, u32[]{:S(2)}) %collective-permute-start.1) | collective-permute-done | bytes 131104 | tf_op jit(solution)/shard_map/ppermute | solution.py:252
  18.3 3.3 %collective-permute-start.5 = (bf16[1280,128]{1,0:T(8,128)(2,1)}, bf16[1280,128]{1,0:T(8,128)(2,1)S(1)}, u32[]{:S(2)}, u32[]{:S(2)}) collective-permute-start(bf16[1280,128]{1,0:T(8,128)(2,1)} %get-tuple-element.29), channel_id=1, source_target_pairs={{0,4},{1,65},{2,6},{3,67},{4,0},{5,69},{6,2},{7,71},{32,36},{33,97... | collective-permute-start | bytes 983048 | tf_op jit(solution)/shard_map/ppermute | solution.py:55
  22.7 1.6 %collective-permute-start.8 = (bf16[1280,128]{1,0:T(8,128)(2,1)}, bf16[1280,128]{1,0:T(8,128)(2,1)S(1)}, u32[]{:S(2)}, u32[]{:S(2)}) collective-permute-start(bf16[1280,128]{1,0:T(8,128)(2,1)} %get-tuple-element.32), channel_id=1, source_target_pairs={{0,33},{1,2},{2,35},{3,4},{4,37},{5,6},{6,39},{7,0},{32,65},{33,34... | collective-permute-start | bytes 983048 | tf_op jit(solution)/shard_map/ppermute | solution.py:59
  24.3 2.2 %collective-permute-start.9 = (bf16[1280,128]{1,0:T(8,128)(2,1)}, bf16[1280,128]{1,0:T(8,128)(2,1)S(1)}, u32[]{:S(2)}, u32[]{:S(2)}) collective-permute-start(bf16[1280,128]{1,0:T(8,128)(2,1)} %get-tuple-element.33), channel_id=1, source_target_pairs={{0,65},{1,4},{2,67},{3,6},{4,69},{5,0},{6,71},{7,2},{32,97},{33,36... | collective-permute-start | bytes 983048 | tf_op jit(solution)/shard_map/ppermute | solution.py:59
  26.5 1.6 %collective-permute-done.5.rest_2_ = bf16[1280,128]{1,0:T(8,128)(2,1)S(1)} collective-permute-done((bf16[1280,128]{1,0:T(8,128)(2,1)}, bf16[1280,128]{1,0:T(8,128)(2,1)S(1)}, u32[]{:S(2)}, u32[]{:S(2)}) %collective-permute-start.5) | collective-permute-done | bytes 327712 | tf_op jit(solution)/shard_map/ppermute | solution.py:55
  28.9 5.2 %collective-permute-done.6.rest_3_ = bf16[1280,128]{1,0:T(8,128)(2,1)S(1)} collective-permute-done((bf16[1280,128]{1,0:T(8,128)(2,1)}, bf16[1280,128]{1,0:T(8,128)(2,1)S(1)}, u32[]{:S(2)}, u32[]{:S(2)}) %collective-permute-start.6) | collective-permute-done | bytes 327712 | tf_op jit(solution)/shard_map/ppermute | solution.py:55
  34.0 1.2 %collective-permute-start.12 = (bf16[256,256]{1,0:T(8,128)(2,1)S(1)}, bf16[256,256]{1,0:T(8,128)(2,1)S(1)}, u32[]{:S(2)}, u32[]{:S(2)}) collective-permute-start(bf16[256,256]{1,0:T(8,128)(2,1)S(1)} %pad_maximum_fusion.rest_8_), channel_id=1, source_target_pairs={{0,4},{1,65},{2,6},{3,67},{4,0},{5,69},{6,2},{7,71},{32,36},{33,97... | collective-permute-start | bytes 393224 | tf_op jit(solution)/shard_map/ppermute | solution.py:55
  35.2 2.0 %collective-permute-start.13 = (bf16[256,256]{1,0:T(8,128)(2,1)S(1)}, bf16[256,256]{1,0:T(8,128)(2,1)S(1)}, u32[]{:S(2)}, u32[]{:S(2)}) collective-permute-start(bf16[256,256]{1,0:T(8,128)(2,1)S(1)} %pad_maximum_fusion.rest_8_), channel_id=1, source_target_pairs={{0,6},{1,97},{2,0},{3,99},{4,2},{5,101},{6,4},{7,103},{32,38},{33,... | collective-permute-start | bytes 393224 | tf_op jit(solution)/shard_map/ppermute | solution.py:55
  37.9 2.6 %collective-permute-done.12.rest_10_ = bf16[256,256]{1,0:T(8,128)(2,1)S(1)} collective-permute-done((bf16[256,256]{1,0:T(8,128)(2,1)S(1)}, bf16[256,256]{1,0:T(8,128)(2,1)S(1)}, u32[]{:S(2)}, u32[]{:S(2)}) %collective-permute-start.12) | collective-permute-done | bytes 131104 | tf_op jit(solution)/shard_map/ppermute | solution.py:55
  40.5 1.3 %collective-permute-done.13.rest_11_ = bf16[256,256]{1,0:T(8,128)(2,1)S(1)} collective-permute-done((bf16[256,256]{1,0:T(8,128)(2,1)S(1)}, bf16[256,256]{1,0:T(8,128)(2,1)S(1)}, u32[]{:S(2)}, u32[]{:S(2)}) %collective-permute-start.13) | collective-permute-done | bytes 131104 | tf_op jit(solution)/shard_map/ppermute | solution.py:55
  42.5 5.5 %shard_map.119 = (f32[320,512]{1,0:T(8,128)}, bf16[320,512]{1,0:T(8,128)(2,1)}, bf16[320,512]{1,0:T(8,128)(2,1)}, bf16[320,512]{1,0:T(8,128)(2,1)}) custom-call(s32[3]{0:T(128)} %pad_add_fusion.1.where_ref, s32[5]{0:T(128)} %convert_reduce_fusion.bounds_ref, bf16[1280,128]{1,0:T(8,128)(2,1)} %get-tuple-element.25.rest_0_, bf16[1280,128]{1,0:T(8,128)(2,1)} %copy-done.11, ...), custom_call_target="tpu_custom_call" | custom-call | flops 1342177280 | bytes 6291456 | tf_op jit(solution)/shard_map/pallas_call | solution.py:261
  48.0 2.2 %collective-permute-start.14 = (bf16[320,512]{1,0:T(8,128)(2,1)}, bf16[320,512]{1,0:T(8,128)(2,1)S(1)}, u32[]{:S(2)}, u32[]{:S(2)}) collective-permute-start(bf16[320,512]{1,0:T(8,128)(2,1)} %get-tuple-element.38), channel_id=1, source_target_pairs={{0,32},{1,3},{2,34},{3,5},{4,36},{5,7},{6,38},{7,1},{32,64},{33,35... | collective-permute-start | bytes 983048 | tf_op jit(solution)/shard_map/ppermute | solution.py:63
  50.2 2.5 %collective-permute-start.15 = (bf16[320,512]{1,0:T(8,128)(2,1)}, bf16[320,512]{1,0:T(8,128)(2,1)S(1)}, u32[]{:S(2)}, u32[]{:S(2)}) collective-permute-start(bf16[320,512]{1,0:T(8,128)(2,1)} %get-tuple-element.39), channel_id=1, source_target_pairs={{0,64},{1,5},{2,66},{3,7},{4,68},{5,1},{6,70},{7,3},{32,96},{33,37... | collective-permute-start | bytes 983048 | tf_op jit(solution)/shard_map/ppermute | solution.py:63
  52.7 1.7 %collective-permute-start.16 = (bf16[320,512]{1,0:T(8,128)(2,1)}, bf16[320,512]{1,0:T(8,128)(2,1)S(1)}, u32[]{:S(2)}, u32[]{:S(2)}) collective-permute-start(bf16[320,512]{1,0:T(8,128)(2,1)} %get-tuple-element.40), channel_id=1, source_target_pairs={{0,96},{1,7},{2,98},{3,1},{4,100},{5,3},{6,102},{7,5},{32,0},{33,3... | collective-permute-start | bytes 983048 | tf_op jit(solution)/shard_map/ppermute | solution.py:63
  54.6 1.9 %collective-permute-done.14.a_ref = bf16[320,512]{1,0:T(8,128)(2,1)S(1)} collective-permute-done((bf16[320,512]{1,0:T(8,128)(2,1)}, bf16[320,512]{1,0:T(8,128)(2,1)S(1)}, u32[]{:S(2)}, u32[]{:S(2)}) %collective-permute-start.14) | collective-permute-done | bytes 327712 | tf_op jit(solution)/shard_map/ppermute | solution.py:63
  56.6 4.9 %collective-permute-done.15.b_ref = bf16[320,512]{1,0:T(8,128)(2,1)S(1)} collective-permute-done((bf16[320,512]{1,0:T(8,128)(2,1)}, bf16[320,512]{1,0:T(8,128)(2,1)S(1)}, u32[]{:S(2)}, u32[]{:S(2)}) %collective-permute-start.15) | collective-permute-done | bytes 327712 | tf_op jit(solution)/shard_map/ppermute | solution.py:63
  62.6 1.3 %shard_map.120 = f32[16,512]{1,0:T(8,128)S(1)} custom-call(f32[320,512]{1,0:T(8,128)S(1)} %copy-done.1, bf16[320,512]{1,0:T(8,128)(2,1)S(1)} %collective-permute-done.14.a_ref, bf16[320,512]{1,0:T(8,128)(2,1)S(1)} %collective-permute-done.15.b_ref, bf16[320,512]{1,0:T(8,128)(2,1)S(1)} %collective-permute-done.16.c_ref, s32[5]{0:T(128)S(1)} %copy-done.4, ...), custom_call_target="tpu_custom_call" | custom-call | bytes 3145728 | tf_op jit(solution)/shard_map/pallas_call | solution.py:293
  64.0 1.2 %collective-permute-done.17 = f32[8,512]{1,0:T(8,128)S(1)} collective-permute-done((f32[8,512]{1,0:T(8,128)S(1)}, f32[8,512]{1,0:T(8,128)S(1)}, u32[]{:S(2)}, u32[]{:S(2)}) %collective-permute-start.17) | collective-permute-done | bytes 16416 | tf_op jit(solution)/shard_map/ppermute | solution.py:309
  65.2 11.3 %all_to_all.10 = f32[8,8,512]{2,1,0:T(8,128)S(1)} all-to-all(f32[8,8,512]{2,1,0:T(8,128)S(1)} %broadcast_in_dim.10), channel_id=1, replica_groups={{0,8,32,40,64,72,96,104},{16,24,48,56,80,88,112,120},{1,9,33,41,65,73,9..., dimensions={0} | all-to-all | bytes 262144 | tf_op jit(solution)/shard_map/all_to_all | solution.py:205
  76.5 12.7 %all_to_all.11 = f32[8,8,512]{2,1,0:T(8,128)S(1)} all-to-all(f32[8,8,512]{2,1,0:T(8,128)S(1)} %broadcast_in_dim.11), channel_id=1, replica_groups={{0,24,2,26,4,28,6,30},{8,16,10,18,12,20,14,22},{1,25,3,27,5,29,7,31},{9..., dimensions={0} | all-to-all | bytes 262144 | tf_op jit(solution)/shard_map/all_to_all | solution.py:205
  (80 shorter events, 9.4 us)
Async XLA Ops:
  0.0 90.5 %copy-start = (bf16[16,128,64]{1,2,0:T(8,128)(2,1)S(1)}, bf16[16,128,64]{1,2,0:T(8,128)(2,1)}, u32[]{:S(2)}) copy-start(bf16[16,128,64]{1,2,0:T(8,128)(2,1)} %param.23) | copy-start | bytes 786436
  0.6 36.6 %copy-start.8 = (s32[4096]{0:T(1024)S(1)}, s32[4096]{0:T(1024)}, u32[]{:S(2)}) copy-start(s32[4096]{0:T(1024)} %param.22) | copy-start | bytes 49156
  5.4 8.2 %collective-permute-start = (f32[128,256]{1,0:T(8,128)}, f32[128,256]{1,0:T(8,128)S(1)}, u32[]{:S(2)}, u32[]{:S(2)}) collective-permute-start(f32[128,256]{1,0:T(8,128)} %get-tuple-element.26), channel_id=1, source_target_pairs={{0,8},{8,16},{16,24},{24,0},{1,9},{9,17},{17,25},{25,1},{2,10},{10... | collective-permute-start | bytes 393224 | tf_op jit(solution)/shard_map/ppermute | solution.py:252
  7.5 9.8 %collective-permute-start.1 = (f32[128,256]{1,0:T(8,128)}, f32[128,256]{1,0:T(8,128)S(1)}, u32[]{:S(2)}, u32[]{:S(2)}) collective-permute-start(f32[128,256]{1,0:T(8,128)} %get-tuple-element.26), channel_id=1, source_target_pairs={{0,16},{8,24},{16,0},{24,8},{1,17},{9,25},{17,1},{25,9},{2,18},{10... | collective-permute-start | bytes 393224 | tf_op jit(solution)/shard_map/ppermute | solution.py:252
  11.1 6.2 %collective-permute-start.2 = (f32[128,256]{1,0:T(8,128)}, f32[128,256]{1,0:T(8,128)S(1)}, u32[]{:S(2)}, u32[]{:S(2)}) collective-permute-start(f32[128,256]{1,0:T(8,128)} %get-tuple-element.26), channel_id=1, source_target_pairs={{0,24},{8,0},{16,8},{24,16},{1,25},{9,1},{17,9},{25,17},{2,26},{10... | collective-permute-start | bytes 393224 | tf_op jit(solution)/shard_map/ppermute | solution.py:252
  12.1 10.6 %collective-permute-start.4 = (bf16[1280,128]{1,0:T(8,128)(2,1)}, bf16[1280,128]{1,0:T(8,128)(2,1)S(1)}, u32[]{:S(2)}, u32[]{:S(2)}) collective-permute-start(bf16[1280,128]{1,0:T(8,128)(2,1)} %get-tuple-element.27), channel_id=1, source_target_pairs={{0,2},{1,33},{2,4},{3,35},{4,6},{5,37},{6,0},{7,39},{32,34},{33,65... | collective-permute-start | bytes 983048 | tf_op jit(solution)/shard_map/ppermute | solution.py:55
  13.6 10.6 %collective-permute-start.10 = (bf16[1280,128]{1,0:T(8,128)(2,1)}, bf16[1280,128]{1,0:T(8,128)(2,1)S(1)}, u32[]{:S(2)}, u32[]{:S(2)}) collective-permute-start(bf16[1280,128]{1,0:T(8,128)(2,1)} %get-tuple-element.34), channel_id=1, source_target_pairs={{0,97},{1,6},{2,99},{3,0},{4,101},{5,2},{6,103},{7,4},{32,1},{33,3... | collective-permute-start | bytes 983048 | tf_op jit(solution)/shard_map/ppermute | solution.py:59
  18.2 4.4 %collective-permute-start.3 = (bf16[128,256]{1,0:T(8,128)(2,1)S(1)}, bf16[128,256]{1,0:T(8,128)(2,1)S(1)}, u32[]{:S(2)}, u32[]{:S(2)}) collective-permute-start(bf16[128,256]{1,0:T(8,128)(2,1)S(1)} %add_convert_fusion), channel_id=1, source_target_pairs={{0,1},{1,0},{2,3},{3,2},{4,5},{5,4},{6,7},{7,6},{8,9},{9,8},{10,11... | collective-permute-start | bytes 196616 | tf_op jit(solution)/shard_map/ppermute | solution.py:254
  18.3 9.8 %collective-permute-start.5 = (bf16[1280,128]{1,0:T(8,128)(2,1)}, bf16[1280,128]{1,0:T(8,128)(2,1)S(1)}, u32[]{:S(2)}, u32[]{:S(2)}) collective-permute-start(bf16[1280,128]{1,0:T(8,128)(2,1)} %get-tuple-element.29), channel_id=1, source_target_pairs={{0,4},{1,65},{2,6},{3,67},{4,0},{5,69},{6,2},{7,71},{32,36},{33,97... | collective-permute-start | bytes 983048 | tf_op jit(solution)/shard_map/ppermute | solution.py:55
  21.6 12.4 %collective-permute-start.6 = (bf16[1280,128]{1,0:T(8,128)(2,1)}, bf16[1280,128]{1,0:T(8,128)(2,1)S(1)}, u32[]{:S(2)}, u32[]{:S(2)}) collective-permute-start(bf16[1280,128]{1,0:T(8,128)(2,1)} %get-tuple-element.30), channel_id=1, source_target_pairs={{0,6},{1,97},{2,0},{3,99},{4,2},{5,101},{6,4},{7,103},{32,38},{33,... | collective-permute-start | bytes 983048 | tf_op jit(solution)/shard_map/ppermute | solution.py:55
  22.7 12.6 %collective-permute-start.7 = (bf16[1280,128]{1,0:T(8,128)(2,1)}, bf16[1280,128]{1,0:T(8,128)(2,1)S(1)}, u32[]{:S(2)}, u32[]{:S(2)}) collective-permute-start(bf16[1280,128]{1,0:T(8,128)(2,1)} %get-tuple-element.31), channel_id=1, source_target_pairs={{0,1},{1,0},{2,3},{3,2},{4,5},{5,4},{6,7},{7,6},{32,33},{33,32},{3... | collective-permute-start | bytes 983048 | tf_op jit(solution)/shard_map/ppermute | solution.py:59
  22.7 19.2 %copy-start.11 = (bf16[1280,128]{1,0:T(8,128)(2,1)}, bf16[1280,128]{1,0:T(8,128)(2,1)S(1)}, u32[]{:S(2)}) copy-start(bf16[1280,128]{1,0:T(8,128)(2,1)S(1)} %collective-permute-done.4.rest_1_) | copy-start | bytes 983044
  22.7 15.2 %collective-permute-start.8 = (bf16[1280,128]{1,0:T(8,128)(2,1)}, bf16[1280,128]{1,0:T(8,128)(2,1)S(1)}, u32[]{:S(2)}, u32[]{:S(2)}) collective-permute-start(bf16[1280,128]{1,0:T(8,128)(2,1)} %get-tuple-element.32), channel_id=1, source_target_pairs={{0,33},{1,2},{2,35},{3,4},{4,37},{5,6},{6,39},{7,0},{32,65},{33,34... | collective-permute-start | bytes 983048 | tf_op jit(solution)/shard_map/ppermute | solution.py:59
  24.3 13.6 %collective-permute-start.9 = (bf16[1280,128]{1,0:T(8,128)(2,1)}, bf16[1280,128]{1,0:T(8,128)(2,1)S(1)}, u32[]{:S(2)}, u32[]{:S(2)}) collective-permute-start(bf16[1280,128]{1,0:T(8,128)(2,1)} %get-tuple-element.33), channel_id=1, source_target_pairs={{0,65},{1,4},{2,67},{3,6},{4,69},{5,0},{6,71},{7,2},{32,97},{33,36... | collective-permute-start | bytes 983048 | tf_op jit(solution)/shard_map/ppermute | solution.py:59
  28.1 9.8 %collective-permute-start.11 = (bf16[256,256]{1,0:T(8,128)(2,1)S(1)}, bf16[256,256]{1,0:T(8,128)(2,1)S(1)}, u32[]{:S(2)}, u32[]{:S(2)}) collective-permute-start(bf16[256,256]{1,0:T(8,128)(2,1)S(1)} %pad_maximum_fusion.rest_8_), channel_id=1, source_target_pairs={{0,2},{1,33},{2,4},{3,35},{4,6},{5,37},{6,0},{7,39},{32,34},{33,65... | collective-permute-start | bytes 393224 | tf_op jit(solution)/shard_map/ppermute | solution.py:55
  34.0 6.5 %collective-permute-start.12 = (bf16[256,256]{1,0:T(8,128)(2,1)S(1)}, bf16[256,256]{1,0:T(8,128)(2,1)S(1)}, u32[]{:S(2)}, u32[]{:S(2)}) collective-permute-start(bf16[256,256]{1,0:T(8,128)(2,1)S(1)} %pad_maximum_fusion.rest_8_), channel_id=1, source_target_pairs={{0,4},{1,65},{2,6},{3,67},{4,0},{5,69},{6,2},{7,71},{32,36},{33,97... | collective-permute-start | bytes 393224 | tf_op jit(solution)/shard_map/ppermute | solution.py:55
  35.2 6.6 %collective-permute-start.13 = (bf16[256,256]{1,0:T(8,128)(2,1)S(1)}, bf16[256,256]{1,0:T(8,128)(2,1)S(1)}, u32[]{:S(2)}, u32[]{:S(2)}) collective-permute-start(bf16[256,256]{1,0:T(8,128)(2,1)S(1)} %pad_maximum_fusion.rest_8_), channel_id=1, source_target_pairs={{0,6},{1,97},{2,0},{3,99},{4,2},{5,101},{6,4},{7,103},{32,38},{33,... | collective-permute-start | bytes 393224 | tf_op jit(solution)/shard_map/ppermute | solution.py:55
  42.5 19.0 %copy-start.2 = (f32[1,64,128]{2,1,0:T(8,128)S(1)}, f32[1,64,128]{2,1,0:T(8,128)}, u32[]{:S(2)}) copy-start(f32[1,64,128]{2,1,0:T(8,128)} %param.16) | copy-start | bytes 98308
  42.5 19.0 %copy-start.3 = (f32[1,64,128]{2,1,0:T(8,128)S(1)}, f32[1,64,128]{2,1,0:T(8,128)}, u32[]{:S(2)}) copy-start(f32[1,64,128]{2,1,0:T(8,128)} %param.17) | copy-start | bytes 98308
  48.0 8.6 %collective-permute-start.14 = (bf16[320,512]{1,0:T(8,128)(2,1)}, bf16[320,512]{1,0:T(8,128)(2,1)S(1)}, u32[]{:S(2)}, u32[]{:S(2)}) collective-permute-start(bf16[320,512]{1,0:T(8,128)(2,1)} %get-tuple-element.38), channel_id=1, source_target_pairs={{0,32},{1,3},{2,34},{3,5},{4,36},{5,7},{6,38},{7,1},{32,64},{33,35... | collective-permute-start | bytes 983048 | tf_op jit(solution)/shard_map/ppermute | solution.py:63
  50.2 11.3 %collective-permute-start.15 = (bf16[320,512]{1,0:T(8,128)(2,1)}, bf16[320,512]{1,0:T(8,128)(2,1)S(1)}, u32[]{:S(2)}, u32[]{:S(2)}) collective-permute-start(bf16[320,512]{1,0:T(8,128)(2,1)} %get-tuple-element.39), channel_id=1, source_target_pairs={{0,64},{1,5},{2,66},{3,7},{4,68},{5,1},{6,70},{7,3},{32,96},{33,37... | collective-permute-start | bytes 983048 | tf_op jit(solution)/shard_map/ppermute | solution.py:63
  52.7 8.8 %collective-permute-start.16 = (bf16[320,512]{1,0:T(8,128)(2,1)}, bf16[320,512]{1,0:T(8,128)(2,1)S(1)}, u32[]{:S(2)}, u32[]{:S(2)}) collective-permute-start(bf16[320,512]{1,0:T(8,128)(2,1)} %get-tuple-element.40), channel_id=1, source_target_pairs={{0,96},{1,7},{2,98},{3,1},{4,100},{5,3},{6,102},{7,5},{32,0},{33,3... | collective-permute-start | bytes 983048 | tf_op jit(solution)/shard_map/ppermute | solution.py:63
  63.9 1.2 %collective-permute-start.17 = (f32[8,512]{1,0:T(8,128)S(1)}, f32[8,512]{1,0:T(8,128)S(1)}, u32[]{:S(2)}, u32[]{:S(2)}) collective-permute-start(f32[8,512]{1,0:T(8,128)S(1)} %constant_dynamic-slice_fusion), channel_id=1, source_target_pairs={{0,1},{1,0},{2,3},{3,2},{4,5},{5,4},{6,7},{7,6},{8,9},{9,8},{10,11... | collective-permute-start | bytes 49160 | tf_op jit(solution)/shard_map/ppermute | solution.py:309
  89.2 1.3 %collective-permute-start.18 = (f32[8,512]{1,0:T(8,128)S(1)}, f32[8,512]{1,0:T(8,128)S(1)}, u32[]{:S(2)}, u32[]{:S(2)}) collective-permute-start(f32[8,512]{1,0:T(8,128)S(1)} %reduce_sum.29), channel_id=1, source_target_pairs={{0,1},{1,0},{2,3},{3,2},{4,5},{5,4},{6,7},{7,6},{8,9},{9,8},{10,11... | collective-permute-start | bytes 49160 | tf_op jit(solution)/shard_map/ppermute | solution.py:312
  (16 other events, 143.5 us)

commit v4 on v3

--- a/solution.py
+++ b/solution.py
@@ -55,27 +55,28 @@
     return lax.ppermute(value, PLANE, pairs(lambda p: along(p, shift)))
 
 
-def send_other(value, shift):
-    return lax.ppermute(value, PLANE, pairs(lambda p: along((p[0], p[1], 1 - p[2]), shift)))
-
-
 def send_across(value, shift):
     return lax.ppermute(value, PLANE, pairs(lambda p: across(p, shift)))
 
 
-def pack_kernel(where_ref, grad_hbm, tokens_hbm, down_hbm, up_hbm, *rest):
-    outs, portion_ref = rest[:8], rest[8]
-    grad, tokens, down, up, turned, loads, sent = rest[9:]
+def position():
+    return lax.axis_index("ex"), lax.axis_index("py"), lax.axis_index("co")
+
+
+def pack_kernel(grad_hbm, tokens_hbm, down_hbm, up_hbm, give_ref, own_ref, *rest):
+    sends, portion_ref = rest[:3], rest[3]
+    grad, tokens, down, up, turned, loads, sent = rest[4:]
     arrivals = [
         pltpu.make_async_copy(source, target, loads.at[i])
         for i, (source, target) in enumerate(((tokens_hbm, tokens), (grad_hbm, grad), (down_hbm, down), (up_hbm, up)))
     ]
     for arrival in arrivals:
         arrival.start()
-    x, y, c = where_ref[0], where_ref[1], where_ref[2]
+    x, y, c = position()
+    outs = [give_ref.at[k] for k in range(4)] + [own_ref] + [send.at[0] for send in sends]
     turned_copies, grad_copies = [], []
     for slot in range(8):
-        target = c if slot < 4 else 1 - c
+        target = 1 - c if slot < 4 else c
         k = slot % 4
         for i in range(4):
             to_x = lax.rem(x + jnp.where(target == 0, i, k), 4)
@@ -114,14 +115,33 @@
         copy.wait()
 
 
-def partial_kernel(where_ref, bounds_ref, *rest):
-    columns, inner, outs = rest[0:8], rest[8:12], rest[12:16]
-    left, side, right_h, right_u, own, sends, inner_sem, columns_sem, sent = rest[16:]
+def fill_kernel(taken_ref, a_in, b_in, c_in, a_ref, b_ref, c_ref, sent):
+    copies = [
+        pltpu.make_async_copy(taken_ref.at[k + 1], send.at[1], sent) for k, send in enumerate((a_ref, b_ref, c_ref))
+    ]
+    for copy in copies:
+        copy.start()
+    for copy in copies:
+        copy.wait()
+
+
+def partial_kernel(chunks, bounds_ref, own_ref, taken_ref, *rest):
+    count = len(chunks)
+    arrived, inner, outs = rest[0:3], rest[3:7], rest[7:7 + count]
+    left, side, right_h, right_u, done, inner_sem, columns_sem, sent = rest[7 + count:]
     inner_copies = [pltpu.make_async_copy(inner[k], side.at[k], inner_sem) for k in range(4)]
-    column_copies = [pltpu.make_async_copy(columns[s], left.at[2 * (s % 4) + s // 4], columns_sem) for s in range(8)]
+    column_copies = []
+    for s in range(8):
+        k, part = s // 2, s % 2
+        source = arrived[k - 1].at[part] if k else (taken_ref.at[0] if part else own_ref)
+        for n, j in enumerate(chunks):
+            for begin, at, size in ((j * WINDOW, n * WINDOW, WINDOW), (4 * WINDOW + j * DOWN_ROWS, count * WINDOW + n * DOWN_ROWS, DOWN_ROWS)):
+                column_copies.append(
+                    pltpu.make_async_copy(source.at[pl.ds(begin, size)], left.at[s, pl.ds(at, size)], columns_sem)
+                )
     for copy in inner_copies + column_copies:
         copy.start()
-    x, y, c = where_ref[0], where_ref[1], where_ref[2]
+    x, y, c = position()
     row = lax.broadcasted_iota(jnp.int32, (128, RANK), 0)
     for copy in inner_copies:
         copy.wait()
@@ -140,20 +160,41 @@
     for copy in column_copies:
         copy.wait()
 
-    def joined(begin, count):
-        return jnp.concatenate([left[s, begin:begin + count, :] for s in range(8)], axis=1)
-
-    down = jnp.dot(joined(4 * WINDOW, 4 * DOWN_ROWS), right_u[...], preferred_element_type=F32)
+    def joined(begin, size):
+        return jnp.concatenate([left[s, begin:begin + size, :] for s in range(8)], axis=1)
+
+    down = jnp.dot(joined(count * WINDOW, count * DOWN_ROWS), right_u[...], preferred_element_type=F32)
     out_copies = []
-    for j in (1, 2, 3, 0):
-        up = jnp.dot(joined(j * WINDOW, WINDOW), right_h[...], preferred_element_type=F32)
-        out = own if j == 0 else sends.at[j - 1]
-        out[:WINDOW, :] = up.astype(out.dtype)
-        out[WINDOW:, :] = down[j * DOWN_ROWS:(j + 1) * DOWN_ROWS].astype(out.dtype)
-        out_copies.append(pltpu.make_async_copy(out, outs[j], sent))
+    for n in range(count):
+        up = jnp.dot(joined(n * WINDOW, WINDOW), right_h[...], preferred_element_type=F32)
+        done[n, :WINDOW, :] = up.astype(BF)
+        done[n, WINDOW:, :] = down[n * DOWN_ROWS:(n + 1) * DOWN_ROWS].astype(BF)
+        out_copies.append(pltpu.make_async_copy(done.at[n], outs[n], sent))
         out_copies[-1].start()
     for copy in out_copies:
         copy.wait()
+
+
+def partial_call(chunks, *operands):
+    count = len(chunks)
+    return pl.pallas_call(
+        functools.partial(partial_kernel, chunks),
+        out_shape=[jax.ShapeDtypeStruct((ROWS, WIDE), BF)] * count,
+        in_specs=[SMEM] + [ANY] * 9,
+        out_specs=[ANY] * count,
+        scratch_shapes=[
+            pltpu.VMEM((8, count * ROWS, 128), BF),
+            pltpu.VMEM((4, PAIR, PAIR), BF),
+            pltpu.VMEM((1024, WIDE), BF),
+            pltpu.VMEM((1024, WIDE), BF),
+            pltpu.VMEM((count, ROWS, WIDE), BF),
+            pltpu.SemaphoreType.DMA,
+            pltpu.SemaphoreType.DMA,
+            pltpu.SemaphoreType.DMA,
+        ],
+        compiler_params=pltpu.CompilerParams(vmem_limit_bytes=60 << 20),
+        cost_estimate=pl.CostEstimate(flops=2 * count * ROWS * 1024 * WIDE, bytes_accessed=4 << 20, transcendentals=0),
+    )(*operands)
 
 
 def feature_kernel(
@@ -171,7 +212,7 @@
     for e in range(EXAMPLES):
         at = pl.ds(e * RANK, RANK)
         length = (bounds_ref[e + 1] - bounds_ref[e]).astype(F32)
-        total = own_ref[:, at] + a_ref[:, at].astype(F32) + b_ref[:, at].astype(F32) + c_ref[:, at].astype(F32)
+        total = (own_ref[:, at].astype(F32) + a_ref[:, at].astype(F32)) + (b_ref[:, at].astype(F32) + c_ref[:, at].astype(F32))
         grad = total / length
         feature = (first + 0.1 * grad) / (jnp.sqrt(second + 0.001 * grad * grad) + 1e-08)
         high = feature.astype(BF)
@@ -222,18 +263,22 @@
     segments,
     bank,
 ):
-    x, y, c = lax.axis_index("ex"), lax.axis_index("py"), lax.axis_index("co")
+    x, y, c = position()
     me = x * 8 + y * 2 + c
-    where = jnp.stack([x, y, c]).astype(jnp.int32)
     bounds = jnp.sum(
         (segments[None, :] < jnp.arange(EXAMPLES + 1, dtype=jnp.int32)[:, None]).astype(jnp.int32), axis=1
     )
 
     packed = pl.pallas_call(
         pack_kernel,
-        out_shape=[jax.ShapeDtypeStruct((4 * ROWS, 128), BF)] * 8 + [jax.ShapeDtypeStruct((128, PAIR), F32)],
-        in_specs=[SMEM, ANY, ANY, ANY, ANY],
-        out_specs=[ANY] * 8 + [VMEM],
+        out_shape=[
+            jax.ShapeDtypeStruct((4, 4 * ROWS, 128), BF),
+            jax.ShapeDtypeStruct((4 * ROWS, 128), BF),
+        ]
+        + [jax.ShapeDtypeStruct((2, 4 * ROWS, 128), BF)] * 3
+        + [jax.ShapeDtypeStruct((128, PAIR), F32)],
+        in_specs=[ANY, ANY, ANY, ANY],
+        out_specs=[ANY] * 5 + [VMEM],
         scratch_shapes=[
             pltpu.VMEM((LOCAL_UP, 128), BF),
             pltpu.VMEM((128, 2048), BF),
@@ -245,42 +290,35 @@
         ],
         compiler_params=pltpu.CompilerParams(vmem_limit_bytes=60 << 20),
         cost_estimate=pl.CostEstimate(flops=2 * 128 * 9440 * 128, bytes_accessed=8 << 20, transcendentals=0),
-    )(where, output_gradient.T, tokens, adapter_down_factor, adapter_up_factor)
-    portion = packed[8]
+    )(output_gradient.T, tokens, adapter_down_factor, adapter_up_factor)
+    give, own_columns, portion = packed[0], packed[1], packed[5]
+    taken = lax.ppermute(give, "co", [(0, 1), (1, 0)])
     whole = portion
     for shift in (1, 2, 3):
         whole = whole + lax.ppermute(portion, ("t1", "t0"), [(i, (i + shift) % 4) for i in range(4)])
     whole = whole.astype(BF)
     sibling = lax.ppermute(whole, "co", [(0, 1), (1, 0)])
     chip_inner = jnp.concatenate([whole, sibling], axis=0)
-    same = [packed[0]] + [send_same(packed[k], k) for k in (1, 2, 3)]
-    other = [send_other(packed[4 + k], k) for k in range(4)]
-    chip_inner, same[1] = lax.optimization_barrier((chip_inner, same[1]))
+    filled = pl.pallas_call(
+        fill_kernel,
+        out_shape=[jax.ShapeDtypeStruct((2, 4 * ROWS, 128), BF)] * 3,
+        in_specs=[ANY] * 4,
+        out_specs=[ANY] * 3,
+        scratch_shapes=[pltpu.SemaphoreType.DMA],
+        input_output_aliases={1: 0, 2: 1, 3: 2},
+        compiler_params=pltpu.CompilerParams(vmem_limit_bytes=60 << 20),
+        cost_estimate=pl.CostEstimate(flops=0, bytes_accessed=2 << 20, transcendentals=0),
+    )(taken, *packed[2:5])
+    arrived = [send_same(filled[k - 1], k) for k in (1, 2, 3)]
     inner = [chip_inner] + [send_same(chip_inner, k) for k in (1, 2, 3)]
 
-    sums = pl.pallas_call(
-        partial_kernel,
-        out_shape=[jax.ShapeDtypeStruct((ROWS, WIDE), F32)] + [jax.ShapeDtypeStruct((ROWS, WIDE), BF)] * 3,
-        in_specs=[SMEM, SMEM] + [ANY] * 12,
-        out_specs=[ANY] * 4,
-        scratch_shapes=[
-            pltpu.VMEM((8, 4 * ROWS, 128), BF),
-            pltpu.VMEM((4, PAIR, PAIR), BF),
-            pltpu.VMEM((1024, WIDE), BF),
-            pltpu.VMEM((1024, WIDE), BF),
-            pltpu.VMEM((ROWS, WIDE), F32),
-            pltpu.VMEM((3, ROWS, WIDE), BF),
-            pltpu.SemaphoreType.DMA,
-            pltpu.SemaphoreType.DMA,
-            pltpu.SemaphoreType.DMA,
-        ],
-        compiler_params=pltpu.CompilerParams(vmem_limit_bytes=60 << 20),
-        cost_estimate=pl.CostEstimate(flops=2 * 4 * ROWS * 1024 * WIDE, bytes_accessed=6 << 20, transcendentals=0),
-    )(where, bounds, *same, *other, *inner)
-    arrived = [send_across(sums[k], k) for k in (1, 2, 3)]
+    operands = (bounds, own_columns, taken, *arrived, *inner)
+    far, near = partial_call((2, 1), *operands)
+    last, own = partial_call((3, 0), *operands)
+    arrived = [send_across(near, 1), send_across(far, 2), send_across(last, 3)]
 
     kept = (first_moment_up, second_moment_up, up_row_seeds, down_row_seeds)
-    own, kept = lax.optimization_barrier((sums[0], kept))
+    own, kept = lax.optimization_barrier((own, kept))
     first_moment_up, second_moment_up, up_row_seeds, down_row_seeds = kept
     offset = me * UP_ROWS - window_start(me)
     seeds = jnp.concatenate(

time: 92.8 us -> 121 us (1.30)
  Pallas kernels: 11.6 us -> 45.2 us
  starting transfers between devices: 26.9 us -> 21.9 us
  other arithmetic: 2.26 us -> 0.76 us
    pallas_call x2 -> x4, Pallas kernels: 10.3 us -> 43.8 us  [the longest x1 30.9 us: on_device(): pl.pallas_call(fill_kernel, out_shape=[jax.ShapeDtypeStruct((2, 4 * ROWS,...]
    ppermute x4 -> x1, starting transfers between devices: 3.79 us -> 0.08 us  [on_device(): taken = lax.ppermute(give, 'co', [(0, 1), (1, 0)])]
    ppermute x3, waiting for transfers between devices: 3.64 us -> 0.01 us  [on_device(): lax.ppermute(portion, ('t1', 't0'), [(i, (i + shift) % 4) for i in range(...]
    ppermute x6, waiting for transfers between devices: 10.7 us -> 13 us  [send_same(): return lax.ppermute(value, PLANE, pairs(lambda p: along(p, shift)))]
    ppermute x1, waiting for transfers between devices: 0.01 us -> 1.24 us  [on_device(): sibling = lax.ppermute(whole, 'co', [(0, 1), (1, 0)])]
    unnamed x43 -> x41, local copies, waits for them, and re-layouts: 1.75 us -> 2.43 us
  transfers between devices with their start and end apart: 19 -> 16, of which waited for: 9 -> 8; matrix products, arithmetic and copies ran while one was open for 2% -> 1% of each run, Pallas kernels for 0% -> 26%
where the time goes in v4:
time: 121 us; the launch traced here: 119 us
  Pallas kernels  45.2 us (37%)
  blocking collectives  24 us (20%)
  waiting for transfers between devices  23.7 us (20%)
  starting transfers between devices  21.9 us (18%)
  local copies, waits for them, and re-layouts  2.66 us (2%)
    pallas_call x1, Pallas kernels, on_device(): pl.pallas_call(fill_kernel, out_shape=[jax.ShapeDtypeStruct((2, 4 * ROWS,...  30.9 us
    all_to_all x2, blocking collectives, spread_sum(): lax.all_to_all(copies, EVERY, split_axis=0, concat_axis=0, tiled=True, ax...  24 us
    ppermute x6, waiting for transfers between devices, send_same(): return lax.ppermute(value, PLANE, pairs(lambda p: along(p, shift)))  13 us
    ppermute x6, starting transfers between devices, send_same(): return lax.ppermute(value, PLANE, pairs(lambda p: along(p, shift)))  10.4 us
    pallas_call x2, Pallas kernels, partial_call(): pl.pallas_call(functools.partial(partial_kernel, chunks), out_shape=[jax....  8.9 us
    ppermute x3, waiting for transfers between devices, send_across(): return lax.ppermute(value, PLANE, pairs(lambda p: across(p, shift)))  7.07 us
    ppermute x3, starting transfers between devices, send_across(): return lax.ppermute(value, PLANE, pairs(lambda p: across(p, shift)))  5.73 us
    ppermute x3, starting transfers between devices, on_device(): lax.ppermute(portion, ('t1', 't0'), [(i, (i + shift) % 4) for i in range(...  5.45 us
  transfers between devices with their start and end apart: 16, of which 8 were waited for; matrix products, arithmetic and copies ran while one was open for 1% of the time, Pallas kernels for 26%

profile of v4, /device:TPU:0, one launch (start us, length us, event | category | flops | bytes accessed | tf_op | source)
XLA Modules:
  0.0 119.4 jit_solution(16507256823495433122)
XLA Ops:
  0.0 4.0 %shard_map.118 = (bf16[4,1280,128]{2,1,0:T(8,128)(2,1)}, bf16[1280,128]{1,0:T(8,128)(2,1)}, bf16[2,1280,128]{2,1,0:T(8,128)(2,1)}, bf16[2,1280,128]{2,1,0:T(8,12...) custom-call(bf16[7392,128]{1,0:T(8,128)(2,1)} %bitcast.18, bf16[128,2048]{1,0:T(8,128)(2,1)} %tokens_hbm.1, ...), custom_call_target="tpu_custom_call" | custom-call | flops 309329920 | bytes 8388608 | tf_op jit(solution)/shard_map/pallas_call | solution.py:272
  4.2 4.2 %collective-permute-start.6 = (f32[128,256]{1,0:T(8,128)}, f32[128,256]{1,0:T(8,128)S(1)}, u32[]{:S(2)}, u32[]{:S(2)}) collective-permute-start(f32[128,256]{1,0:T(8,128)} %get-tuple-element.31), channel_id=1, source_target_pairs={{0,24},{8,0},{16,8},{24,16},{1,25},{9,1},{17,9},{25,17},{2,26},{10... | collective-permute-start | bytes 393224 | tf_op jit(solution)/shard_map/ppermute | solution.py:298
  8.3 1.3 %collective-permute-start.4 = (f32[128,256]{1,0:T(8,128)}, f32[128,256]{1,0:T(8,128)S(1)}, u32[]{:S(2)}, u32[]{:S(2)}) collective-permute-start(f32[128,256]{1,0:T(8,128)} %get-tuple-element.31), channel_id=1, source_target_pairs={{0,8},{8,16},{16,24},{24,0},{1,9},{9,17},{17,25},{25,1},{2,10},{10... | collective-permute-start | bytes 393224 | tf_op jit(solution)/shard_map/ppermute | solution.py:298
  10.7 30.9 %shard_map.119 = (bf16[2,1280,128]{2,1,0:T(8,128)(2,1)}, bf16[2,1280,128]{2,1,0:T(8,128)(2,1)}, bf16[2,1280,128]{2,1,0:T(8,128)(2,1)}) custom-call(bf16[4,1280,128]{2,1,0:T(8,128)(2,1)} %copy-done.5, bf16[2,1280,128]{2,1,0:T(8,128)(2,1)} %get-tuple-element.25.a_in, ...), custom_call_target="tpu_custom_call", output_to_operand_aliasing={{0}: (1, {}), {1}: (2, {}), {2}: (3, {})} | custom-call | bytes 2097152 | tf_op jit(solution)/shard_map/pallas_call | solution.py:302
  41.6 1.6 %collective-permute-start.1 = (bf16[2,1280,128]{2,1,0:T(8,128)(2,1)}, bf16[2,1280,128]{2,1,0:T(8,128)(2,1)S(1)}, u32[]{:S(2)}, u32[]{:S(2)}) collective-permute-start(bf16[2,1280,128]{2,1,0:T(8,128)(2,1)} %get-tuple-element.28), channel_id=1, source_target_pairs={{0,2},{1,33},{2,4},{3,35},{4,6},{5,37},{6,0},{7,39},{32,34},{33,65... | collective-permute-start | bytes 1966088 | tf_op jit(solution)/shard_map/ppermute | solution.py:55
  43.2 2.9 %collective-permute-start.2 = (bf16[2,1280,128]{2,1,0:T(8,128)(2,1)}, bf16[2,1280,128]{2,1,0:T(8,128)(2,1)S(1)}, u32[]{:S(2)}, u32[]{:S(2)}) collective-permute-start(bf16[2,1280,128]{2,1,0:T(8,128)(2,1)} %get-tuple-element.29), channel_id=1, source_target_pairs={{0,4},{1,65},{2,6},{3,67},{4,0},{5,69},{6,2},{7,71},{32,36},{33,97... | collective-permute-start | bytes 1966088 | tf_op jit(solution)/shard_map/ppermute | solution.py:55
  46.1 1.3 %collective-permute-start.3 = (bf16[2,1280,128]{2,1,0:T(8,128)(2,1)}, bf16[2,1280,128]{2,1,0:T(8,128)(2,1)S(1)}, u32[]{:S(2)}, u32[]{:S(2)}) collective-permute-start(bf16[2,1280,128]{2,1,0:T(8,128)(2,1)} %get-tuple-element.30), channel_id=1, source_target_pairs={{0,6},{1,97},{2,0},{3,99},{4,2},{5,101},{6,4},{7,103},{32,38},{33,... | collective-permute-start | bytes 1966088 | tf_op jit(solution)/shard_map/ppermute | solution.py:55
  47.6 1.2 %collective-permute-done.7 = bf16[128,256]{1,0:T(8,128)(2,1)S(1)} collective-permute-done((bf16[128,256]{1,0:T(8,128)(2,1)S(1)}, bf16[128,256]{1,0:T(8,128)(2,1)S(1)}, u32[]{:S(2)}, u32[]{:S(2)}) %collective-permute-start.7) | collective-permute-done | bytes 65568 | tf_op jit(solution)/shard_map/ppermute | solution.py:300
  49.6 2.0 %collective-permute-start.9 = (bf16[256,256]{1,0:T(8,128)(2,1)S(1)}, bf16[256,256]{1,0:T(8,128)(2,1)S(1)}, u32[]{:S(2)}, u32[]{:S(2)}) collective-permute-start(bf16[256,256]{1,0:T(8,128)(2,1)S(1)} %pad_maximum_fusion.rest_3_), channel_id=1, source_target_pairs={{0,4},{1,65},{2,6},{3,67},{4,0},{5,69},{6,2},{7,71},{32,36},{33,97... | collective-permute-start | bytes 393224 | tf_op jit(solution)/shard_map/ppermute | solution.py:55
  51.7 10.5 %collective-permute-done.8.rest_4_ = bf16[256,256]{1,0:T(8,128)(2,1)S(1)} collective-permute-done((bf16[256,256]{1,0:T(8,128)(2,1)S(1)}, bf16[256,256]{1,0:T(8,128)(2,1)S(1)}, u32[]{:S(2)}, u32[]{:S(2)}) %collective-permute-start.8) | collective-permute-done | bytes 131104 | tf_op jit(solution)/shard_map/ppermute | solution.py:55
  62.2 1.8 %collective-permute-start.10 = (bf16[256,256]{1,0:T(8,128)(2,1)S(1)}, bf16[256,256]{1,0:T(8,128)(2,1)S(1)}, u32[]{:S(2)}, u32[]{:S(2)}) collective-permute-start(bf16[256,256]{1,0:T(8,128)(2,1)S(1)} %pad_maximum_fusion.rest_3_), channel_id=1, source_target_pairs={{0,6},{1,97},{2,0},{3,99},{4,2},{5,101},{6,4},{7,103},{32,38},{33,... | collective-permute-start | bytes 393224 | tf_op jit(solution)/shard_map/ppermute | solution.py:55
  64.8 2.4 %collective-permute-done.10.rest_6_ = bf16[256,256]{1,0:T(8,128)(2,1)S(1)} collective-permute-done((bf16[256,256]{1,0:T(8,128)(2,1)S(1)}, bf16[256,256]{1,0:T(8,128)(2,1)S(1)}, u32[]{:S(2)}, u32[]{:S(2)}) %collective-permute-start.10) | collective-permute-done | bytes 131104 | tf_op jit(solution)/shard_map/ppermute | solution.py:55
  68.4 4.4 %shard_map.120 = (bf16[320,512]{1,0:T(8,128)(2,1)}, bf16[320,512]{1,0:T(8,128)(2,1)}) custom-call(s32[5]{0:T(128)} %convert_reduce_fusion.bounds_ref, bf16[1280,128]{1,0:T(8,128)(2,1)} %get-tuple-element.23.own_ref, bf16[4,1280,128]{2,1,0:T(8,128)(2,1)} %copy-done.5, bf16[2,1280,128]{2,1,0:T(8,128)(2,1)} %copy-done.6, bf16[2,1280,128]{2,1,0:T(8,128)(2,1)} %copy-done.7, ...), custom_call_target="tpu_custom_call" | custom-call | flops 671088640 | bytes 4194304 | tf_op jit(solution)/shard_map/pallas_call | solution.py:180
  72.9 4.5 %shard_map.121 = (bf16[320,512]{1,0:T(8,128)(2,1)}, bf16[320,512]{1,0:T(8,128)(2,1)}) custom-call(s32[5]{0:T(128)} %convert_reduce_fusion.bounds_ref, bf16[1280,128]{1,0:T(8,128)(2,1)} %get-tuple-element.23.own_ref, bf16[4,1280,128]{2,1,0:T(8,128)(2,1)} %copy-done.5, bf16[2,1280,128]{2,1,0:T(8,128)(2,1)} %copy-done.6, bf16[2,1280,128]{2,1,0:T(8,128)(2,1)} %copy-done.7, ...), custom_call_target="tpu_custom_call" | custom-call | flops 671088640 | bytes 4194304 | tf_op jit(solution)/shard_map/pallas_call | solution.py:180
  77.5 1.6 %collective-permute-start.11 = (bf16[320,512]{1,0:T(8,128)(2,1)}, bf16[320,512]{1,0:T(8,128)(2,1)S(1)}, u32[]{:S(2)}, u32[]{:S(2)}) collective-permute-start(bf16[320,512]{1,0:T(8,128)(2,1)} %get-tuple-element.34), channel_id=1, source_target_pairs={{0,32},{1,3},{2,34},{3,5},{4,36},{5,7},{6,38},{7,1},{32,64},{33,35... | collective-permute-start | bytes 983048 | tf_op jit(solution)/shard_map/ppermute | solution.py:59
  79.0 2.7 %collective-permute-start.12 = (bf16[320,512]{1,0:T(8,128)(2,1)}, bf16[320,512]{1,0:T(8,128)(2,1)S(1)}, u32[]{:S(2)}, u32[]{:S(2)}) collective-permute-start(bf16[320,512]{1,0:T(8,128)(2,1)} %get-tuple-element.35), channel_id=1, source_target_pairs={{0,64},{1,5},{2,66},{3,7},{4,68},{5,1},{6,70},{7,3},{32,96},{33,37... | collective-permute-start | bytes 983048 | tf_op jit(solution)/shard_map/ppermute | solution.py:59
  81.8 1.4 %collective-permute-start.13 = (bf16[320,512]{1,0:T(8,128)(2,1)S(1)}, bf16[320,512]{1,0:T(8,128)(2,1)S(1)}, u32[]{:S(2)}, u32[]{:S(2)}) collective-permute-start(bf16[320,512]{1,0:T(8,128)(2,1)S(1)} %copy-done.19), channel_id=1, source_target_pairs={{0,96},{1,7},{2,98},{3,1},{4,100},{5,3},{6,102},{7,5},{32,0},{33,3... | collective-permute-start | bytes 983048 | tf_op jit(solution)/shard_map/ppermute | solution.py:59
  83.5 2.6 %collective-permute-done.11.a_ref = bf16[320,512]{1,0:T(8,128)(2,1)S(1)} collective-permute-done((bf16[320,512]{1,0:T(8,128)(2,1)}, bf16[320,512]{1,0:T(8,128)(2,1)S(1)}, u32[]{:S(2)}, u32[]{:S(2)}) %collective-permute-start.11) | collective-permute-done | bytes 327712 | tf_op jit(solution)/shard_map/ppermute | solution.py:59
  86.0 4.5 %collective-permute-done.12.b_ref = bf16[320,512]{1,0:T(8,128)(2,1)S(1)} collective-permute-done((bf16[320,512]{1,0:T(8,128)(2,1)}, bf16[320,512]{1,0:T(8,128)(2,1)S(1)}, u32[]{:S(2)}, u32[]{:S(2)}) %collective-permute-start.12) | collective-permute-done | bytes 327712 | tf_op jit(solution)/shard_map/ppermute | solution.py:59
  90.6 1.3 %shard_map.122 = f32[16,512]{1,0:T(8,128)S(1)} custom-call(bf16[320,512]{1,0:T(8,128)(2,1)S(1)} %copy-done.1, bf16[320,512]{1,0:T(8,128)(2,1)S(1)} %collective-permute-done.11.a_ref, bf16[320,512]{1,0:T(8,128)(2,1)S(1)} %collective-permute-done.12.b_ref, bf16[320,512]{1,0:T(8,128)(2,1)S(1)} %collective-permute-done.13.c_ref, s32[5]{0:T(128)S(1)} %copy-done.4, ...), custom_call_target="tpu_custom_call" | custom-call | bytes 3145728 | tf_op jit(solution)/shard_map/pallas_call | solution.py:331
  92.0 1.2 collective-permute-done.14
  93.2 12.1 %all_to_all.10 = f32[8,8,512]{2,1,0:T(8,128)S(1)} all-to-all(f32[8,8,512]{2,1,0:T(8,128)S(1)} %broadcast_in_dim.10), channel_id=1, replica_groups={{0,8,32,40,64,72,96,104},{16,24,48,56,80,88,112,120},{1,9,33,41,65,73,9..., dimensions={0} | all-to-all | bytes 262144 | tf_op jit(solution)/shard_map/all_to_all | solution.py:246
  105.3 11.9 %all_to_all.11 = f32[8,8,512]{2,1,0:T(8,128)S(1)} all-to-all(f32[8,8,512]{2,1,0:T(8,128)S(1)} %broadcast_in_dim.11), channel_id=1, replica_groups={{0,24,2,26,4,28,6,30},{8,16,10,18,12,20,14,22},{1,25,3,27,5,29,7,31},{9..., dimensions={0} | all-to-all | bytes 262144 | tf_op jit(solution)/shard_map/all_to_all | solution.py:246
  117.3 1.2 collective-permute-done.15
  (73 shorter events, 5.6 us)
Async XLA Ops:
  0.0 118.5 %copy-start = (bf16[16,128,64]{1,2,0:T(8,128)(2,1)S(1)}, bf16[16,128,64]{1,2,0:T(8,128)(2,1)}, u32[]{:S(2)}) copy-start(bf16[16,128,64]{1,2,0:T(8,128)(2,1)} %param.23) | copy-start | bytes 786436
  4.1 43.4 %copy-start.13 = (f32[128,256]{1,0:T(8,128)S(1)}, f32[128,256]{1,0:T(8,128)}, u32[]{:S(2)}) copy-start(f32[128,256]{1,0:T(8,128)} %get-tuple-element.31) | copy-start | bytes 393220
  4.1 5.5 %collective-permute-start = (bf16[4,1280,128]{2,1,0:T(8,128)(2,1)}, bf16[4,1280,128]{2,1,0:T(8,128)(2,1)S(1)}, u32[]{:S(2)}, u32[]{:S(2)}) collective-permute-start(bf16[4,1280,128]{2,1,0:T(8,128)(2,1)} %get-tuple-element.24), channel_id=1, source_target_pairs={{0,1},{1,0},{2,3},{3,2},{4,5},{5,4},{6,7},{7,6},{8,9},{9,8},{10,11... | collective-permute-start | bytes 3932168 | tf_op jit(solution)/shard_map/ppermute | solution.py:295
  4.2 42.0 %collective-permute-start.6 = (f32[128,256]{1,0:T(8,128)}, f32[128,256]{1,0:T(8,128)S(1)}, u32[]{:S(2)}, u32[]{:S(2)}) collective-permute-start(f32[128,256]{1,0:T(8,128)} %get-tuple-element.31), channel_id=1, source_target_pairs={{0,24},{8,0},{16,8},{24,16},{1,25},{9,1},{17,9},{25,17},{2,26},{10... | collective-permute-start | bytes 393224 | tf_op jit(solution)/shard_map/ppermute | solution.py:298
  8.3 39.1 %collective-permute-start.5 = (f32[128,256]{1,0:T(8,128)}, f32[128,256]{1,0:T(8,128)S(1)}, u32[]{:S(2)}, u32[]{:S(2)}) collective-permute-start(f32[128,256]{1,0:T(8,128)} %get-tuple-element.31), channel_id=1, source_target_pairs={{0,16},{8,24},{16,0},{24,8},{1,17},{9,25},{17,1},{25,9},{2,18},{10... | collective-permute-start | bytes 393224 | tf_op jit(solution)/shard_map/ppermute | solution.py:298
  8.3 39.1 %collective-permute-start.4 = (f32[128,256]{1,0:T(8,128)}, f32[128,256]{1,0:T(8,128)S(1)}, u32[]{:S(2)}, u32[]{:S(2)}) collective-permute-start(f32[128,256]{1,0:T(8,128)} %get-tuple-element.31), channel_id=1, source_target_pairs={{0,8},{8,16},{16,24},{24,0},{1,9},{9,17},{17,25},{25,1},{2,10},{10... | collective-permute-start | bytes 393224 | tf_op jit(solution)/shard_map/ppermute | solution.py:298
  10.7 53.3 %copy-start.16 = (s32[4096]{0:T(1024)S(1)}, s32[4096]{0:T(1024)}, u32[]{:S(2)}) copy-start(s32[4096]{0:T(1024)} %param.22) | copy-start | bytes 49156
  41.6 25.6 %collective-permute-start.1 = (bf16[2,1280,128]{2,1,0:T(8,128)(2,1)}, bf16[2,1280,128]{2,1,0:T(8,128)(2,1)S(1)}, u32[]{:S(2)}, u32[]{:S(2)}) collective-permute-start(bf16[2,1280,128]{2,1,0:T(8,128)(2,1)} %get-tuple-element.28), channel_id=1, source_target_pairs={{0,2},{1,33},{2,4},{3,35},{4,6},{5,37},{6,0},{7,39},{32,34},{33,65... | collective-permute-start | bytes 1966088 | tf_op jit(solution)/shard_map/ppermute | solution.py:55
  43.2 23.9 %collective-permute-start.2 = (bf16[2,1280,128]{2,1,0:T(8,128)(2,1)}, bf16[2,1280,128]{2,1,0:T(8,128)(2,1)S(1)}, u32[]{:S(2)}, u32[]{:S(2)}) collective-permute-start(bf16[2,1280,128]{2,1,0:T(8,128)(2,1)} %get-tuple-element.29), channel_id=1, source_target_pairs={{0,4},{1,65},{2,6},{3,67},{4,0},{5,69},{6,2},{7,71},{32,36},{33,97... | collective-permute-start | bytes 1966088 | tf_op jit(solution)/shard_map/ppermute | solution.py:55
  46.1 21.0 %collective-permute-start.3 = (bf16[2,1280,128]{2,1,0:T(8,128)(2,1)}, bf16[2,1280,128]{2,1,0:T(8,128)(2,1)S(1)}, u32[]{:S(2)}, u32[]{:S(2)}) collective-permute-start(bf16[2,1280,128]{2,1,0:T(8,128)(2,1)} %get-tuple-element.30), channel_id=1, source_target_pairs={{0,6},{1,97},{2,0},{3,99},{4,2},{5,101},{6,4},{7,103},{32,38},{33,... | collective-permute-start | bytes 1966088 | tf_op jit(solution)/shard_map/ppermute | solution.py:55
  47.5 1.3 %collective-permute-start.7 = (bf16[128,256]{1,0:T(8,128)(2,1)S(1)}, bf16[128,256]{1,0:T(8,128)(2,1)S(1)}, u32[]{:S(2)}, u32[]{:S(2)}) collective-permute-start(bf16[128,256]{1,0:T(8,128)(2,1)S(1)} %add_convert_fusion), channel_id=1, source_target_pairs={{0,1},{1,0},{2,3},{3,2},{4,5},{5,4},{6,7},{7,6},{8,9},{9,8},{10,11... | collective-permute-start | bytes 196616 | tf_op jit(solution)/shard_map/ppermute | solution.py:300
  48.9 18.3 %copy-start.9 = (bf16[256,256]{1,0:T(8,128)(2,1)}, bf16[256,256]{1,0:T(8,128)(2,1)S(1)}, u32[]{:S(2)}) copy-start(bf16[256,256]{1,0:T(8,128)(2,1)S(1)} %pad_maximum_fusion.rest_3_) | copy-start | bytes 393220
  48.9 13.3 %collective-permute-start.8 = (bf16[256,256]{1,0:T(8,128)(2,1)S(1)}, bf16[256,256]{1,0:T(8,128)(2,1)S(1)}, u32[]{:S(2)}, u32[]{:S(2)}) collective-permute-start(bf16[256,256]{1,0:T(8,128)(2,1)S(1)} %pad_maximum_fusion.rest_3_), channel_id=1, source_target_pairs={{0,2},{1,33},{2,4},{3,35},{4,6},{5,37},{6,0},{7,39},{32,34},{33,65... | collective-permute-start | bytes 393224 | tf_op jit(solution)/shard_map/ppermute | solution.py:55
  49.6 15.1 %collective-permute-start.9 = (bf16[256,256]{1,0:T(8,128)(2,1)S(1)}, bf16[256,256]{1,0:T(8,128)(2,1)S(1)}, u32[]{:S(2)}, u32[]{:S(2)}) collective-permute-start(bf16[256,256]{1,0:T(8,128)(2,1)S(1)} %pad_maximum_fusion.rest_3_), channel_id=1, source_target_pairs={{0,4},{1,65},{2,6},{3,67},{4,0},{5,69},{6,2},{7,71},{32,36},{33,97... | collective-permute-start | bytes 393224 | tf_op jit(solution)/shard_map/ppermute | solution.py:55
  62.2 5.0 %collective-permute-start.10 = (bf16[256,256]{1,0:T(8,128)(2,1)S(1)}, bf16[256,256]{1,0:T(8,128)(2,1)S(1)}, u32[]{:S(2)}, u32[]{:S(2)}) collective-permute-start(bf16[256,256]{1,0:T(8,128)(2,1)S(1)} %pad_maximum_fusion.rest_3_), channel_id=1, source_target_pairs={{0,6},{1,97},{2,0},{3,99},{4,2},{5,101},{6,4},{7,103},{32,38},{33,... | collective-permute-start | bytes 393224 | tf_op jit(solution)/shard_map/ppermute | solution.py:55
  72.9 17.7 %copy-start.1 = (bf16[320,512]{1,0:T(8,128)(2,1)S(1)}, bf16[320,512]{1,0:T(8,128)(2,1)}, u32[]{:S(2)}) copy-start(bf16[320,512]{1,0:T(8,128)(2,1)} %get-tuple-element.33.own_ref) | copy-start | bytes 983044
  72.9 17.6 %copy-start.2 = (f32[1,64,128]{2,1,0:T(8,128)S(1)}, f32[1,64,128]{2,1,0:T(8,128)}, u32[]{:S(2)}) copy-start(f32[1,64,128]{2,1,0:T(8,128)} %param.16) | copy-start | bytes 98308
  72.9 17.6 %copy-start.3 = (f32[1,64,128]{2,1,0:T(8,128)S(1)}, f32[1,64,128]{2,1,0:T(8,128)}, u32[]{:S(2)}) copy-start(f32[1,64,128]{2,1,0:T(8,128)} %param.17) | copy-start | bytes 98308
  72.9 17.6 %copy-start.4 = (s32[5]{0:T(128)S(1)}, s32[5]{0:T(128)}, u32[]{:S(2)}) copy-start(s32[5]{0:T(128)} %convert_reduce_fusion.bounds_ref) | copy-start | bytes 64
  77.5 8.6 %collective-permute-start.11 = (bf16[320,512]{1,0:T(8,128)(2,1)}, bf16[320,512]{1,0:T(8,128)(2,1)S(1)}, u32[]{:S(2)}, u32[]{:S(2)}) collective-permute-start(bf16[320,512]{1,0:T(8,128)(2,1)} %get-tuple-element.34), channel_id=1, source_target_pairs={{0,32},{1,3},{2,34},{3,5},{4,36},{5,7},{6,38},{7,1},{32,64},{33,35... | collective-permute-start | bytes 983048 | tf_op jit(solution)/shard_map/ppermute | solution.py:59
  79.0 11.5 %collective-permute-start.12 = (bf16[320,512]{1,0:T(8,128)(2,1)}, bf16[320,512]{1,0:T(8,128)(2,1)S(1)}, u32[]{:S(2)}, u32[]{:S(2)}) collective-permute-start(bf16[320,512]{1,0:T(8,128)(2,1)} %get-tuple-element.35), channel_id=1, source_target_pairs={{0,64},{1,5},{2,66},{3,7},{4,68},{5,1},{6,70},{7,3},{32,96},{33,37... | collective-permute-start | bytes 983048 | tf_op jit(solution)/shard_map/ppermute | solution.py:59
  81.8 8.8 %collective-permute-start.13 = (bf16[320,512]{1,0:T(8,128)(2,1)S(1)}, bf16[320,512]{1,0:T(8,128)(2,1)S(1)}, u32[]{:S(2)}, u32[]{:S(2)}) collective-permute-start(bf16[320,512]{1,0:T(8,128)(2,1)S(1)} %copy-done.19), channel_id=1, source_target_pairs={{0,96},{1,7},{2,98},{3,1},{4,100},{5,3},{6,102},{7,5},{32,0},{33,3... | collective-permute-start | bytes 983048 | tf_op jit(solution)/shard_map/ppermute | solution.py:59
  91.9 1.2 %collective-permute-start.14 = (f32[8,512]{1,0:T(8,128)S(1)}, f32[8,512]{1,0:T(8,128)S(1)}, u32[]{:S(2)}, u32[]{:S(2)}) collective-permute-start(f32[8,512]{1,0:T(8,128)S(1)} %constant_dynamic-slice_fusion), channel_id=1, source_target_pairs={{0,1},{1,0},{2,3},{3,2},{4,5},{5,4},{6,7},{7,6},{8,9},{9,8},{10,11... | collective-permute-start | bytes 49160 | tf_op jit(solution)/shard_map/ppermute | solution.py:347
  117.2 1.3 %collective-permute-start.15 = (f32[8,512]{1,0:T(8,128)S(1)}, f32[8,512]{1,0:T(8,128)S(1)}, u32[]{:S(2)}, u32[]{:S(2)}) collective-permute-start(f32[8,512]{1,0:T(8,128)S(1)} %reduce_sum.29), channel_id=1, source_target_pairs={{0,1},{1,0},{2,3},{3,2},{4,5},{5,4},{6,7},{7,6},{8,9},{9,8},{10,11... | collective-permute-start | bytes 49160 | tf_op jit(solution)/shard_map/ppermute | solution.py:350
  (12 other events, 63.4 us)

commit v5 on v3

--- a/solution.py
+++ b/solution.py
@@ -1,4 +1,3 @@
-import functools
 import math
 
 import jax
@@ -55,27 +54,28 @@
     return lax.ppermute(value, PLANE, pairs(lambda p: along(p, shift)))
 
 
-def send_other(value, shift):
-    return lax.ppermute(value, PLANE, pairs(lambda p: along((p[0], p[1], 1 - p[2]), shift)))
-
-
 def send_across(value, shift):
     return lax.ppermute(value, PLANE, pairs(lambda p: across(p, shift)))
 
 
-def pack_kernel(where_ref, grad_hbm, tokens_hbm, down_hbm, up_hbm, *rest):
-    outs, portion_ref = rest[:8], rest[8]
-    grad, tokens, down, up, turned, loads, sent = rest[9:]
+def position():
+    return lax.axis_index("ex"), lax.axis_index("py"), lax.axis_index("co")
+
+
+def pack_kernel(grad_hbm, tokens_hbm, down_hbm, up_hbm, give_ref, *rest):
+    sends, portion_ref = rest[:4], rest[4]
+    grad, tokens, down, up, turned, loads, sent = rest[5:]
     arrivals = [
         pltpu.make_async_copy(source, target, loads.at[i])
         for i, (source, target) in enumerate(((tokens_hbm, tokens), (grad_hbm, grad), (down_hbm, down), (up_hbm, up)))
     ]
     for arrival in arrivals:
         arrival.start()
-    x, y, c = where_ref[0], where_ref[1], where_ref[2]
+    x, y, c = position()
+    outs = [give_ref.at[k] for k in range(4)] + [send.at[0] for send in sends]
     turned_copies, grad_copies = [], []
     for slot in range(8):
-        target = c if slot < 4 else 1 - c
+        target = 1 - c if slot < 4 else c
         k = slot % 4
         for i in range(4):
             to_x = lax.rem(x + jnp.where(target == 0, i, k), 4)
@@ -114,14 +114,39 @@
         copy.wait()
 
 
-def partial_kernel(where_ref, bounds_ref, *rest):
-    columns, inner, outs = rest[0:8], rest[8:12], rest[12:16]
-    left, side, right_h, right_u, own, sends, inner_sem, columns_sem, sent = rest[16:]
+def fill_kernel(taken_ref, *rest):
+    sends, sent = rest[4:8], rest[8]
+    copies = [pltpu.make_async_copy(taken_ref.at[k], sends[k].at[1], sent) for k in range(4)]
+    for copy in copies:
+        copy.start()
+    for copy in copies:
+        copy.wait()
+
+
+def partial_kernel(bounds_ref, *rest):
+    columns, inner, outs = rest[0:4], rest[4:8], rest[8:12]
+    left, low, side, right_h, right_u, done, inner_sem, low_sem, left_sem, sent = rest[12:]
+    order = (1, 2, 3, 0)
     inner_copies = [pltpu.make_async_copy(inner[k], side.at[k], inner_sem) for k in range(4)]
-    column_copies = [pltpu.make_async_copy(columns[s], left.at[2 * (s % 4) + s // 4], columns_sem) for s in range(8)]
-    for copy in inner_copies + column_copies:
+    left_copies = {
+        j: [
+            pltpu.make_async_copy(
+                columns[s // 2].at[s % 2, pl.ds(j * WINDOW, WINDOW)], left.at[s, pl.ds(j * WINDOW, WINDOW)], left_sem.at[j]
+            )
+            for s in range(8)
+        ]
+        for j in order
+    }
+    low_copies = [
+        pltpu.make_async_copy(columns[s // 2].at[s % 2, pl.ds(4 * WINDOW, 4 * DOWN_ROWS)], low.at[s], low_sem)
+        for s in range(8)
+    ]
+    for copy in inner_copies + low_copies:
         copy.start()
-    x, y, c = where_ref[0], where_ref[1], where_ref[2]
+    for j in order:
+        for copy in left_copies[j]:
+            copy.start()
+    x, y, c = position()
     row = lax.broadcasted_iota(jnp.int32, (128, RANK), 0)
     for copy in inner_copies:
         copy.wait()
@@ -137,20 +162,19 @@
                 picked = jnp.where(inside, 1.0, 0.0).astype(BF)
                 right_h[rows, e * RANK:(e + 1) * RANK] = h * picked
                 right_u[rows, e * RANK:(e + 1) * RANK] = u * picked
-    for copy in column_copies:
-        copy.wait()
-
-    def joined(begin, count):
-        return jnp.concatenate([left[s, begin:begin + count, :] for s in range(8)], axis=1)
-
-    down = jnp.dot(joined(4 * WINDOW, 4 * DOWN_ROWS), right_u[...], preferred_element_type=F32)
+    for copy in low_copies:
+        copy.wait()
+    joined = jnp.concatenate([low[s] for s in range(8)], axis=1)
+    down = jnp.dot(joined, right_u[...], preferred_element_type=F32)
     out_copies = []
-    for j in (1, 2, 3, 0):
-        up = jnp.dot(joined(j * WINDOW, WINDOW), right_h[...], preferred_element_type=F32)
-        out = own if j == 0 else sends.at[j - 1]
-        out[:WINDOW, :] = up.astype(out.dtype)
-        out[WINDOW:, :] = down[j * DOWN_ROWS:(j + 1) * DOWN_ROWS].astype(out.dtype)
-        out_copies.append(pltpu.make_async_copy(out, outs[j], sent))
+    for j in order:
+        for copy in left_copies[j]:
+            copy.wait()
+        joined = jnp.concatenate([left[s, j * WINDOW:(j + 1) * WINDOW, :] for s in range(8)], axis=1)
+        up = jnp.dot(joined, right_h[...], preferred_element_type=F32)
+        done[j, :WINDOW, :] = up.astype(BF)
+        done[j, WINDOW:, :] = down[j * DOWN_ROWS:(j + 1) * DOWN_ROWS].astype(BF)
+        out_copies.append(pltpu.make_async_copy(done.at[j], outs[j], sent))
         out_copies[-1].start()
     for copy in out_copies:
         copy.wait()
@@ -171,7 +195,7 @@
     for e in range(EXAMPLES):
         at = pl.ds(e * RANK, RANK)
         length = (bounds_ref[e + 1] - bounds_ref[e]).astype(F32)
-        total = own_ref[:, at] + a_ref[:, at].astype(F32) + b_ref[:, at].astype(F32) + c_ref[:, at].astype(F32)
+        total = (own_ref[:, at].astype(F32) + a_ref[:, at].astype(F32)) + (b_ref[:, at].astype(F32) + c_ref[:, at].astype(F32))
         grad = total / length
         feature = (first + 0.1 * grad) / (jnp.sqrt(second + 0.001 * grad * grad) + 1e-08)
         high = feature.astype(BF)
@@ -222,18 +246,19 @@
     segments,
     bank,
 ):
-    x, y, c = lax.axis_index("ex"), lax.axis_index("py"), lax.axis_index("co")
+    x, y, c = position()
     me = x * 8 + y * 2 + c
-    where = jnp.stack([x, y, c]).astype(jnp.int32)
     bounds = jnp.sum(
         (segments[None, :] < jnp.arange(EXAMPLES + 1, dtype=jnp.int32)[:, None]).astype(jnp.int32), axis=1
     )
 
     packed = pl.pallas_call(
         pack_kernel,
-        out_shape=[jax.ShapeDtypeStruct((4 * ROWS, 128), BF)] * 8 + [jax.ShapeDtypeStruct((128, PAIR), F32)],
-        in_specs=[SMEM, ANY, ANY, ANY, ANY],
-        out_specs=[ANY] * 8 + [VMEM],
+        out_shape=[jax.ShapeDtypeStruct((4, 4 * ROWS, 128), BF)]
+        + [jax.ShapeDtypeStruct((2, 4 * ROWS, 128), BF)] * 4
+        + [jax.ShapeDtypeStruct((128, PAIR), F32)],
+        in_specs=[ANY, ANY, ANY, ANY],
+        out_specs=[ANY] * 5 + [VMEM],
         scratch_shapes=[
             pltpu.VMEM((LOCAL_UP, 128), BF),
             pltpu.VMEM((128, 2048), BF),
@@ -245,42 +270,52 @@
         ],
         compiler_params=pltpu.CompilerParams(vmem_limit_bytes=60 << 20),
         cost_estimate=pl.CostEstimate(flops=2 * 128 * 9440 * 128, bytes_accessed=8 << 20, transcendentals=0),
-    )(where, output_gradient.T, tokens, adapter_down_factor, adapter_up_factor)
-    portion = packed[8]
-    whole = portion
-    for shift in (1, 2, 3):
-        whole = whole + lax.ppermute(portion, ("t1", "t0"), [(i, (i + shift) % 4) for i in range(4)])
-    whole = whole.astype(BF)
+    )(output_gradient.T, tokens, adapter_down_factor, adapter_up_factor)
+    give, portion = packed[0], packed[5]
+    taken = lax.ppermute(give, "co", [(0, 1), (1, 0)])
+    peers = [lax.ppermute(portion, ("t1", "t0"), [(i, (i + shift) % 4) for i in range(4)]) for shift in (1, 2, 3)]
+    taken, peers[0] = lax.optimization_barrier((taken, peers[0]))
+    whole = ((portion + peers[0]) + (peers[1] + peers[2])).astype(BF)
     sibling = lax.ppermute(whole, "co", [(0, 1), (1, 0)])
     chip_inner = jnp.concatenate([whole, sibling], axis=0)
-    same = [packed[0]] + [send_same(packed[k], k) for k in (1, 2, 3)]
-    other = [send_other(packed[4 + k], k) for k in range(4)]
-    chip_inner, same[1] = lax.optimization_barrier((chip_inner, same[1]))
-    inner = [chip_inner] + [send_same(chip_inner, k) for k in (1, 2, 3)]
-
-    sums = pl.pallas_call(
+    filled = pl.pallas_call(
+        fill_kernel,
+        out_shape=[jax.ShapeDtypeStruct((2, 4 * ROWS, 128), BF)] * 4,
+        in_specs=[VMEM] + [ANY] * 4,
+        out_specs=[ANY] * 4,
+        scratch_shapes=[pltpu.SemaphoreType.DMA],
+        input_output_aliases={1: 0, 2: 1, 3: 2, 4: 3},
+        compiler_params=pltpu.CompilerParams(vmem_limit_bytes=60 << 20),
+        cost_estimate=pl.CostEstimate(flops=0, bytes_accessed=2 << 20, transcendentals=0),
+    )(taken, *packed[1:5])
+    columns = [filled[0]] + [send_same(filled[k], k) for k in (1, 2, 3)]
+    late_inner, columns[1] = lax.optimization_barrier((chip_inner, columns[1]))
+    inner = [chip_inner, send_same(chip_inner, 1), send_same(late_inner, 2), send_same(chip_inner, 3)]
+
+    own, *sums = pl.pallas_call(
         partial_kernel,
-        out_shape=[jax.ShapeDtypeStruct((ROWS, WIDE), F32)] + [jax.ShapeDtypeStruct((ROWS, WIDE), BF)] * 3,
-        in_specs=[SMEM, SMEM] + [ANY] * 12,
+        out_shape=[jax.ShapeDtypeStruct((ROWS, WIDE), BF)] * 4,
+        in_specs=[SMEM] + [ANY] * 8,
         out_specs=[ANY] * 4,
         scratch_shapes=[
-            pltpu.VMEM((8, 4 * ROWS, 128), BF),
+            pltpu.VMEM((8, 4 * WINDOW, 128), BF),
+            pltpu.VMEM((8, 4 * DOWN_ROWS, 128), BF),
             pltpu.VMEM((4, PAIR, PAIR), BF),
             pltpu.VMEM((1024, WIDE), BF),
             pltpu.VMEM((1024, WIDE), BF),
-            pltpu.VMEM((ROWS, WIDE), F32),
-            pltpu.VMEM((3, ROWS, WIDE), BF),
+            pltpu.VMEM((4, ROWS, WIDE), BF),
             pltpu.SemaphoreType.DMA,
             pltpu.SemaphoreType.DMA,
+            pltpu.SemaphoreType.DMA((4,)),
             pltpu.SemaphoreType.DMA,
         ],
         compiler_params=pltpu.CompilerParams(vmem_limit_bytes=60 << 20),
         cost_estimate=pl.CostEstimate(flops=2 * 4 * ROWS * 1024 * WIDE, bytes_accessed=6 << 20, transcendentals=0),
-    )(where, bounds, *same, *other, *inner)
-    arrived = [send_across(sums[k], k) for k in (1, 2, 3)]
+    )(bounds, *columns, *inner)
+    arrived = [send_across(sums[k - 1], k) for k in (1, 2, 3)]
 
     kept = (first_moment_up, second_moment_up, up_row_seeds, down_row_seeds)
-    own, kept = lax.optimization_barrier((sums[0], kept))
+    own, kept = lax.optimization_barrier((own, kept))
     first_moment_up, second_moment_up, up_row_seeds, down_row_seeds = kept
     offset = me * UP_ROWS - window_start(me)
     seeds = jnp.concatenate(

time: 92.8 us -> 92.6 us (level)
  Pallas kernels: 11.6 us -> 14 us
  waiting for transfers between devices: 23.5 us -> 21.5 us
  other arithmetic: 2.26 us -> 0.76 us
  starting transfers between devices: 26.9 us -> 25.6 us
  blocking collectives: 24 us -> 25.2 us
  local copies, waits for them, and re-layouts: 1.98 us -> 3.01 us
    ppermute x6, waiting for transfers between devices: 10.7 us -> 2.25 us  [send_same(): return lax.ppermute(value, PLANE, pairs(lambda p: along(p, shift)))]
    ppermute x6, starting transfers between devices: 9.85 us -> 15.7 us  [send_same(): return lax.ppermute(value, PLANE, pairs(lambda p: along(p, shift)))]
    ppermute x3, waiting for transfers between devices: 3.64 us -> 8.64 us  [on_device(): lax.ppermute(portion, ('t1', 't0'), [(i, (i + shift) % 4) for i in range(...]
    ppermute x4 -> x1, starting transfers between devices: 3.79 us -> 0.08 us  [on_device(): taken = lax.ppermute(give, 'co', [(0, 1), (1, 0)])]
    ppermute x3, starting transfers between devices: 6.66 us -> 3.83 us  [on_device(): lax.ppermute(portion, ('t1', 't0'), [(i, (i + shift) % 4) for i in range(...]
    pallas_call x1 -> x2, Pallas kernels: 4.79 us -> 6.48 us  [the longest x1 4.04 us: on_device(): pl.pallas_call(pack_kernel, out_shape=[jax.ShapeDtypeStruct((4, 4 * ROWS,...]
    ppermute x1, waiting for transfers between devices: 0.01 us -> 1.24 us  [on_device(): sibling = lax.ppermute(whole, 'co', [(0, 1), (1, 0)])]
    all_to_all x2, blocking collectives: 24 us -> 25.2 us  [spread_sum(): lax.all_to_all(copies, EVERY, split_axis=0, concat_axis=0, tiled=True, ax...]
  transfers between devices with their start and end apart: 19 -> 16, of which waited for: 9 -> 10; matrix products, arithmetic and copies ran while one was open for 2% -> 1% of each run, Pallas kernels for 0% -> 0%
where the time goes in v5:
time: 92.6 us; the launch traced here: 91.2 us
  starting transfers between devices  25.6 us (28%)
  blocking collectives  25.2 us (27%)
  waiting for transfers between devices  21.5 us (23%)
  Pallas kernels  14 us (15%)
  local copies, waits for them, and re-layouts  3.01 us (3%)
    all_to_all x2, blocking collectives, spread_sum(): lax.all_to_all(copies, EVERY, split_axis=0, concat_axis=0, tiled=True, ax...  25.2 us
    ppermute x6, starting transfers between devices, send_same(): return lax.ppermute(value, PLANE, pairs(lambda p: along(p, shift)))  15.7 us
    ppermute x3, waiting for transfers between devices, on_device(): lax.ppermute(portion, ('t1', 't0'), [(i, (i + shift) % 4) for i in range(...  8.64 us
    ppermute x3, waiting for transfers between devices, send_across(): return lax.ppermute(value, PLANE, pairs(lambda p: across(p, shift)))  7.07 us
    pallas_call x1, Pallas kernels, on_device(): pl.pallas_call(partial_kernel, out_shape=[jax.ShapeDtypeStruct((ROWS, WID...  6.23 us
    ppermute x3, starting transfers between devices, send_across(): return lax.ppermute(value, PLANE, pairs(lambda p: across(p, shift)))  5.73 us
    pallas_call x1, Pallas kernels, on_device(): pl.pallas_call(pack_kernel, out_shape=[jax.ShapeDtypeStruct((4, 4 * ROWS,...  4.04 us
    ppermute x3, starting transfers between devices, on_device(): lax.ppermute(portion, ('t1', 't0'), [(i, (i + shift) % 4) for i in range(...  3.83 us
  transfers between devices with their start and end apart: 16, of which 10 were waited for; matrix products, arithmetic and copies ran while one was open for 1% of the time, Pallas kernels for 0%

profile of v5, /device:TPU:0, one launch (start us, length us, event | category | flops | bytes accessed | tf_op | source)
XLA Modules:
  0.0 91.2 jit_solution(15750109217148891680)
XLA Ops:
  0.0 4.0 %shard_map.118 = (bf16[4,1280,128]{2,1,0:T(8,128)(2,1)}, bf16[2,1280,128]{2,1,0:T(8,128)(2,1)}, bf16[2,1280,128]{2,1,0:T(8,128)(2,1)}, bf16[2,1280,128]{2,1,0:T(...) custom-call(bf16[7392,128]{1,0:T(8,128)(2,1)} %bitcast.18, bf16[128,2048]{1,0:T(8,128)(2,1)} %tokens_hbm.1, ...), custom_call_target="tpu_custom_call" | custom-call | flops 309329920 | bytes 8388608 | tf_op jit(solution)/shard_map/pallas_call | solution.py:255
  4.1 2.1 %collective-permute-start.1 = (f32[128,256]{1,0:T(8,128)}, f32[128,256]{1,0:T(8,128)S(1)}, u32[]{:S(2)}, u32[]{:S(2)}) collective-permute-start(f32[128,256]{1,0:T(8,128)} %get-tuple-element.29), channel_id=1, source_target_pairs={{0,8},{8,16},{16,24},{24,0},{1,9},{9,17},{17,25},{25,1},{2,10},{10... | collective-permute-start | bytes 393224 | tf_op jit(solution)/shard_map/ppermute | solution.py:276
  6.2 6.4 %collective-permute-done.1 = f32[128,256]{1,0:T(8,128)S(1)} collective-permute-done((f32[128,256]{1,0:T(8,128)}, f32[128,256]{1,0:T(8,128)S(1)}, u32[]{:S(2)}, u32[]{:S(2)}) %collective-permute-start.1) | collective-permute-done | bytes 131104 | tf_op jit(solution)/shard_map/ppermute | solution.py:276
  13.7 2.4 %shard_map.119 = (bf16[2,1280,128]{2,1,0:T(8,128)(2,1)}, bf16[2,1280,128]{2,1,0:T(8,128)(2,1)}, bf16[2,1280,128]{2,1,0:T(8,128)(2,1)}, bf16[2,1280,128]{2,1,0:T(8,128)(2,1)}) custom-call(bf16[4,1280,128]{2,1,0:T(8,128)(2,1)} %copy-done.5, ...), custom_call_target="tpu_custom_call", output_to_operand_aliasing={{0}: (1, {}), {1}: (2, {}), {2}: (3, {}), {3}: (4, {})} | custom-call | bytes 2097152 | tf_op jit(solution)/shard_map/pallas_call | solution.py:281
  16.2 1.6 %collective-permute-start.5 = (bf16[2,1280,128]{2,1,0:T(8,128)(2,1)}, bf16[2,1280,128]{2,1,0:T(8,128)(2,1)S(1)}, u32[]{:S(2)}, u32[]{:S(2)}) collective-permute-start(bf16[2,1280,128]{2,1,0:T(8,128)(2,1)} %get-tuple-element.37), channel_id=1, source_target_pairs={{0,2},{1,33},{2,4},{3,35},{4,6},{5,37},{6,0},{7,39},{32,34},{33,65... | collective-permute-start | bytes 1966088 | tf_op jit(solution)/shard_map/ppermute | solution.py:54
  17.8 1.8 %collective-permute-start.3 = (f32[128,256]{1,0:T(8,128)S(1)}, f32[128,256]{1,0:T(8,128)S(1)}, u32[]{:S(2)}, u32[]{:S(2)}) collective-permute-start(f32[128,256]{1,0:T(8,128)S(1)} %copy-done.7), channel_id=1, source_target_pairs={{0,24},{8,0},{16,8},{24,16},{1,25},{9,1},{17,9},{25,17},{2,26},{10... | collective-permute-start | bytes 393224 | tf_op jit(solution)/shard_map/ppermute | solution.py:276
  19.6 2.9 %collective-permute-start.6 = (bf16[2,1280,128]{2,1,0:T(8,128)(2,1)}, bf16[2,1280,128]{2,1,0:T(8,128)(2,1)S(1)}, u32[]{:S(2)}, u32[]{:S(2)}) collective-permute-start(bf16[2,1280,128]{2,1,0:T(8,128)(2,1)} %get-tuple-element.39), channel_id=1, source_target_pairs={{0,4},{1,65},{2,6},{3,67},{4,0},{5,69},{6,2},{7,71},{32,36},{33,97... | collective-permute-start | bytes 1966088 | tf_op jit(solution)/shard_map/ppermute | solution.py:54
  22.5 1.3 %collective-permute-start.7 = (bf16[2,1280,128]{2,1,0:T(8,128)(2,1)}, bf16[2,1280,128]{2,1,0:T(8,128)(2,1)S(1)}, u32[]{:S(2)}, u32[]{:S(2)}) collective-permute-start(bf16[2,1280,128]{2,1,0:T(8,128)(2,1)} %get-tuple-element.40), channel_id=1, source_target_pairs={{0,6},{1,97},{2,0},{3,99},{4,2},{5,101},{6,4},{7,103},{32,38},{33,... | collective-permute-start | bytes 1966088 | tf_op jit(solution)/shard_map/ppermute | solution.py:54
  24.1 1.9 %collective-permute-done.2 = f32[128,256]{1,0:T(8,128)S(1)} collective-permute-done((f32[128,256]{1,0:T(8,128)S(1)}, f32[128,256]{1,0:T(8,128)S(1)}, u32[]{:S(2)}, u32[]{:S(2)}) %collective-permute-start.2) | collective-permute-done | bytes 131104 | tf_op jit(solution)/shard_map/ppermute | solution.py:276
  26.2 1.2 %collective-permute-done.4 = bf16[128,256]{1,0:T(8,128)(2,1)S(1)} collective-permute-done((bf16[128,256]{1,0:T(8,128)(2,1)S(1)}, bf16[128,256]{1,0:T(8,128)(2,1)S(1)}, u32[]{:S(2)}, u32[]{:S(2)}) %collective-permute-start.4) | collective-permute-done | bytes 65568 | tf_op jit(solution)/shard_map/ppermute | solution.py:279
  27.5 2.5 %collective-permute-start.10 = (bf16[256,256]{1,0:T(8,128)(2,1)S(1)}, bf16[256,256]{1,0:T(8,128)(2,1)S(1)}, u32[]{:S(2)}, u32[]{:S(2)}) collective-permute-start(bf16[256,256]{1,0:T(8,128)(2,1)S(1)} %pad_maximum_fusion.rest_4_), channel_id=1, source_target_pairs={{0,6},{1,97},{2,0},{3,99},{4,2},{5,101},{6,4},{7,103},{32,38},{33,... | collective-permute-start | bytes 393224 | tf_op jit(solution)/shard_map/ppermute | solution.py:54
  30.0 7.3 %collective-permute-start.9 = (bf16[256,256]{1,0:T(8,128)(2,1)S(1)}, bf16[256,256]{1,0:T(8,128)(2,1)S(1)}, u32[]{:S(2)}, u32[]{:S(2)}) collective-permute-start(bf16[256,256]{1,0:T(8,128)(2,1)S(1)} %pad_maximum_fusion.rest_4_), channel_id=1, source_target_pairs={{0,4},{1,65},{2,6},{3,67},{4,0},{5,69},{6,2},{7,71},{32,36},{33,97... | collective-permute-start | bytes 393224 | tf_op jit(solution)/shard_map/ppermute | solution.py:54
  37.9 1.4 %collective-permute-done.10.rest_7_ = bf16[256,256]{1,0:T(8,128)(2,1)S(1)} collective-permute-done((bf16[256,256]{1,0:T(8,128)(2,1)S(1)}, bf16[256,256]{1,0:T(8,128)(2,1)S(1)}, u32[]{:S(2)}, u32[]{:S(2)}) %collective-permute-start.10) | collective-permute-done | bytes 131104 | tf_op jit(solution)/shard_map/ppermute | solution.py:54
  40.9 6.2 %shard_map.120 = (bf16[320,512]{1,0:T(8,128)(2,1)}, bf16[320,512]{1,0:T(8,128)(2,1)}, bf16[320,512]{1,0:T(8,128)(2,1)}, bf16[320,512]{1,0:T(8,128)(2,1)}) custom-call(s32[5]{0:T(128)} %convert_reduce_fusion.bounds_ref, bf16[2,1280,128]{2,1,0:T(8,128)(2,1)} %get-tuple-element.35.rest_0_, bf16[2,1280,128]{2,1,0:T(8,128)(2,1)} %copy-done.13, ...), custom_call_target="tpu_custom_call" | custom-call | flops 1342177280 | bytes 6291456 | tf_op jit(solution)/shard_map/pallas_call | solution.py:295
  47.1 1.6 %collective-permute-start.11 = (bf16[320,512]{1,0:T(8,128)(2,1)}, bf16[320,512]{1,0:T(8,128)(2,1)S(1)}, u32[]{:S(2)}, u32[]{:S(2)}) collective-permute-start(bf16[320,512]{1,0:T(8,128)(2,1)} %get-tuple-element.44), channel_id=1, source_target_pairs={{0,32},{1,3},{2,34},{3,5},{4,36},{5,7},{6,38},{7,1},{32,64},{33,35... | collective-permute-start | bytes 983048 | tf_op jit(solution)/shard_map/ppermute | solution.py:58
  48.7 2.7 %collective-permute-start.12 = (bf16[320,512]{1,0:T(8,128)(2,1)}, bf16[320,512]{1,0:T(8,128)(2,1)S(1)}, u32[]{:S(2)}, u32[]{:S(2)}) collective-permute-start(bf16[320,512]{1,0:T(8,128)(2,1)} %get-tuple-element.45), channel_id=1, source_target_pairs={{0,64},{1,5},{2,66},{3,7},{4,68},{5,1},{6,70},{7,3},{32,96},{33,37... | collective-permute-start | bytes 983048 | tf_op jit(solution)/shard_map/ppermute | solution.py:58
  51.4 1.4 %collective-permute-start.13 = (bf16[320,512]{1,0:T(8,128)(2,1)}, bf16[320,512]{1,0:T(8,128)(2,1)S(1)}, u32[]{:S(2)}, u32[]{:S(2)}) collective-permute-start(bf16[320,512]{1,0:T(8,128)(2,1)} %get-tuple-element.46), channel_id=1, source_target_pairs={{0,96},{1,7},{2,98},{3,1},{4,100},{5,3},{6,102},{7,5},{32,0},{33,3... | collective-permute-start | bytes 983048 | tf_op jit(solution)/shard_map/ppermute | solution.py:58
  53.1 2.6 %collective-permute-done.11.a_ref = bf16[320,512]{1,0:T(8,128)(2,1)S(1)} collective-permute-done((bf16[320,512]{1,0:T(8,128)(2,1)}, bf16[320,512]{1,0:T(8,128)(2,1)S(1)}, u32[]{:S(2)}, u32[]{:S(2)}) %collective-permute-start.11) | collective-permute-done | bytes 327712 | tf_op jit(solution)/shard_map/ppermute | solution.py:58
  55.7 4.5 %collective-permute-done.12.b_ref = bf16[320,512]{1,0:T(8,128)(2,1)S(1)} collective-permute-done((bf16[320,512]{1,0:T(8,128)(2,1)}, bf16[320,512]{1,0:T(8,128)(2,1)S(1)}, u32[]{:S(2)}, u32[]{:S(2)}) %collective-permute-start.12) | collective-permute-done | bytes 327712 | tf_op jit(solution)/shard_map/ppermute | solution.py:58
  61.2 1.3 %shard_map.121 = f32[16,512]{1,0:T(8,128)S(1)} custom-call(bf16[320,512]{1,0:T(8,128)(2,1)S(1)} %copy-done.1, bf16[320,512]{1,0:T(8,128)(2,1)S(1)} %collective-permute-done.11.a_ref, bf16[320,512]{1,0:T(8,128)(2,1)S(1)} %collective-permute-done.12.b_ref, bf16[320,512]{1,0:T(8,128)(2,1)S(1)} %collective-permute-done.13.c_ref, s32[5]{0:T(128)S(1)} %copy-done.4, ...), custom_call_target="tpu_custom_call" | custom-call | bytes 3145728 | tf_op jit(solution)/shard_map/pallas_call | solution.py:328
  62.6 1.2 %collective-permute-done.14 = f32[8,512]{1,0:T(8,128)S(1)} collective-permute-done((f32[8,512]{1,0:T(8,128)S(1)}, f32[8,512]{1,0:T(8,128)S(1)}, u32[]{:S(2)}, u32[]{:S(2)}) %collective-permute-start.14) | collective-permute-done | bytes 16416 | tf_op jit(solution)/shard_map/ppermute | solution.py:344
  63.8 10.8 %all_to_all.10 = f32[8,8,512]{2,1,0:T(8,128)S(1)} all-to-all(f32[8,8,512]{2,1,0:T(8,128)S(1)} %broadcast_in_dim.10), channel_id=1, replica_groups={{0,8,32,40,64,72,96,104},{16,24,48,56,80,88,112,120},{1,9,33,41,65,73,9..., dimensions={0} | all-to-all | bytes 262144 | tf_op jit(solution)/shard_map/all_to_all | solution.py:229
  74.7 14.3 %all_to_all.11 = f32[8,8,512]{2,1,0:T(8,128)S(1)} all-to-all(f32[8,8,512]{2,1,0:T(8,128)S(1)} %broadcast_in_dim.11), channel_id=1, replica_groups={{0,24,2,26,4,28,6,30},{8,16,10,18,12,20,14,22},{1,25,3,27,5,29,7,31},{9..., dimensions={0} | all-to-all | bytes 262144 | tf_op jit(solution)/shard_map/all_to_all | solution.py:229
  89.1 1.2 %collective-permute-done.15 = f32[8,512]{1,0:T(8,128)S(1)} collective-permute-done((f32[8,512]{1,0:T(8,128)S(1)}, f32[8,512]{1,0:T(8,128)S(1)}, u32[]{:S(2)}, u32[]{:S(2)}) %collective-permute-start.15) | collective-permute-done | bytes 16416 | tf_op jit(solution)/shard_map/ppermute | solution.py:347
  (70 shorter events, 6.1 us)
Async XLA Ops:
  0.0 90.3 %copy-start = (bf16[16,128,64]{1,2,0:T(8,128)(2,1)S(1)}, bf16[16,128,64]{1,2,0:T(8,128)(2,1)}, u32[]{:S(2)}) copy-start(bf16[16,128,64]{1,2,0:T(8,128)(2,1)} %param.23) | copy-start | bytes 786436
  4.0 8.6 %collective-permute-start = (bf16[4,1280,128]{2,1,0:T(8,128)(2,1)}, bf16[4,1280,128]{2,1,0:T(8,128)(2,1)S(1)}, u32[]{:S(2)}, u32[]{:S(2)}) collective-permute-start(bf16[4,1280,128]{2,1,0:T(8,128)(2,1)} %get-tuple-element.28), channel_id=1, source_target_pairs={{0,1},{1,0},{2,3},{3,2},{4,5},{5,4},{6,7},{7,6},{8,9},{9,8},{10,11... | collective-permute-start | bytes 3932168 | tf_op jit(solution)/shard_map/ppermute | solution.py:275
  4.1 8.5 %collective-permute-start.1 = (f32[128,256]{1,0:T(8,128)}, f32[128,256]{1,0:T(8,128)S(1)}, u32[]{:S(2)}, u32[]{:S(2)}) collective-permute-start(f32[128,256]{1,0:T(8,128)} %get-tuple-element.29), channel_id=1, source_target_pairs={{0,8},{8,16},{16,24},{24,0},{1,9},{9,17},{17,25},{25,1},{2,10},{10... | collective-permute-start | bytes 393224 | tf_op jit(solution)/shard_map/ppermute | solution.py:276
  13.7 23.5 %copy-start.10 = (s32[4096]{0:T(1024)S(1)}, s32[4096]{0:T(1024)}, u32[]{:S(2)}) copy-start(s32[4096]{0:T(1024)} %param.22) | copy-start | bytes 49156
  16.2 13.8 %collective-permute-start.5 = (bf16[2,1280,128]{2,1,0:T(8,128)(2,1)}, bf16[2,1280,128]{2,1,0:T(8,128)(2,1)S(1)}, u32[]{:S(2)}, u32[]{:S(2)}) collective-permute-start(bf16[2,1280,128]{2,1,0:T(8,128)(2,1)} %get-tuple-element.37), channel_id=1, source_target_pairs={{0,2},{1,33},{2,4},{3,35},{4,6},{5,37},{6,0},{7,39},{32,34},{33,65... | collective-permute-start | bytes 1966088 | tf_op jit(solution)/shard_map/ppermute | solution.py:54
  17.8 6.3 %collective-permute-start.3 = (f32[128,256]{1,0:T(8,128)S(1)}, f32[128,256]{1,0:T(8,128)S(1)}, u32[]{:S(2)}, u32[]{:S(2)}) collective-permute-start(f32[128,256]{1,0:T(8,128)S(1)} %copy-done.7), channel_id=1, source_target_pairs={{0,24},{8,0},{16,8},{24,16},{1,25},{9,1},{17,9},{25,17},{2,26},{10... | collective-permute-start | bytes 393224 | tf_op jit(solution)/shard_map/ppermute | solution.py:276
  19.6 6.5 %collective-permute-start.2 = (f32[128,256]{1,0:T(8,128)S(1)}, f32[128,256]{1,0:T(8,128)S(1)}, u32[]{:S(2)}, u32[]{:S(2)}) collective-permute-start(f32[128,256]{1,0:T(8,128)S(1)} %copy-done.7), channel_id=1, source_target_pairs={{0,16},{8,24},{16,0},{24,8},{1,17},{9,25},{17,1},{25,9},{2,18},{10... | collective-permute-start | bytes 393224 | tf_op jit(solution)/shard_map/ppermute | solution.py:276
  19.6 19.8 %collective-permute-start.6 = (bf16[2,1280,128]{2,1,0:T(8,128)(2,1)}, bf16[2,1280,128]{2,1,0:T(8,128)(2,1)S(1)}, u32[]{:S(2)}, u32[]{:S(2)}) collective-permute-start(bf16[2,1280,128]{2,1,0:T(8,128)(2,1)} %get-tuple-element.39), channel_id=1, source_target_pairs={{0,4},{1,65},{2,6},{3,67},{4,0},{5,69},{6,2},{7,71},{32,36},{33,97... | collective-permute-start | bytes 1966088 | tf_op jit(solution)/shard_map/ppermute | solution.py:54
  22.5 16.9 %collective-permute-start.7 = (bf16[2,1280,128]{2,1,0:T(8,128)(2,1)}, bf16[2,1280,128]{2,1,0:T(8,128)(2,1)S(1)}, u32[]{:S(2)}, u32[]{:S(2)}) collective-permute-start(bf16[2,1280,128]{2,1,0:T(8,128)(2,1)} %get-tuple-element.40), channel_id=1, source_target_pairs={{0,6},{1,97},{2,0},{3,99},{4,2},{5,101},{6,4},{7,103},{32,38},{33,... | collective-permute-start | bytes 1966088 | tf_op jit(solution)/shard_map/ppermute | solution.py:54
  26.1 1.3 %collective-permute-start.4 = (bf16[128,256]{1,0:T(8,128)(2,1)S(1)}, bf16[128,256]{1,0:T(8,128)(2,1)S(1)}, u32[]{:S(2)}, u32[]{:S(2)}) collective-permute-start(bf16[128,256]{1,0:T(8,128)(2,1)S(1)} %add_convert_fusion), channel_id=1, source_target_pairs={{0,1},{1,0},{2,3},{3,2},{4,5},{5,4},{6,7},{7,6},{8,9},{9,8},{10,11... | collective-permute-start | bytes 196616 | tf_op jit(solution)/shard_map/ppermute | solution.py:279
  27.4 12.8 %copy-start.6 = (bf16[256,256]{1,0:T(8,128)(2,1)}, bf16[256,256]{1,0:T(8,128)(2,1)S(1)}, u32[]{:S(2)}) copy-start(bf16[256,256]{1,0:T(8,128)(2,1)S(1)} %pad_maximum_fusion.rest_4_) | copy-start | bytes 393220
  27.5 11.9 %collective-permute-start.10 = (bf16[256,256]{1,0:T(8,128)(2,1)S(1)}, bf16[256,256]{1,0:T(8,128)(2,1)S(1)}, u32[]{:S(2)}, u32[]{:S(2)}) collective-permute-start(bf16[256,256]{1,0:T(8,128)(2,1)S(1)} %pad_maximum_fusion.rest_4_), channel_id=1, source_target_pairs={{0,6},{1,97},{2,0},{3,99},{4,2},{5,101},{6,4},{7,103},{32,38},{33,... | collective-permute-start | bytes 393224 | tf_op jit(solution)/shard_map/ppermute | solution.py:54
  30.0 9.4 %collective-permute-start.8 = (bf16[256,256]{1,0:T(8,128)(2,1)S(1)}, bf16[256,256]{1,0:T(8,128)(2,1)S(1)}, u32[]{:S(2)}, u32[]{:S(2)}) collective-permute-start(bf16[256,256]{1,0:T(8,128)(2,1)S(1)} %pad_maximum_fusion.rest_4_), channel_id=1, source_target_pairs={{0,2},{1,33},{2,4},{3,35},{4,6},{5,37},{6,0},{7,39},{32,34},{33,65... | collective-permute-start | bytes 393224 | tf_op jit(solution)/shard_map/ppermute | solution.py:54
  30.0 10.2 %collective-permute-start.9 = (bf16[256,256]{1,0:T(8,128)(2,1)S(1)}, bf16[256,256]{1,0:T(8,128)(2,1)S(1)}, u32[]{:S(2)}, u32[]{:S(2)}) collective-permute-start(bf16[256,256]{1,0:T(8,128)(2,1)S(1)} %pad_maximum_fusion.rest_4_), channel_id=1, source_target_pairs={{0,4},{1,65},{2,6},{3,67},{4,0},{5,69},{6,2},{7,71},{32,36},{33,97... | collective-permute-start | bytes 393224 | tf_op jit(solution)/shard_map/ppermute | solution.py:54
  40.9 12.2 %copy-start.8 = (f32[1,231,128]{2,0,1:T(1,128)S(1)}, f32[1,231,128]{2,0,1:T(1,128)}, u32[]{:S(2)}) copy-start(f32[1,231,128]{2,0,1:T(1,128)} %param.19) | copy-start | bytes 354820
  40.9 12.2 %copy-start.9 = (f32[1,231,128]{2,0,1:T(1,128)S(1)}, f32[1,231,128]{2,0,1:T(1,128)}, u32[]{:S(2)}) copy-start(f32[1,231,128]{2,0,1:T(1,128)} %param.18) | copy-start | bytes 354820
  40.9 19.3 %copy-start.2 = (f32[1,64,128]{2,1,0:T(8,128)S(1)}, f32[1,64,128]{2,1,0:T(8,128)}, u32[]{:S(2)}) copy-start(f32[1,64,128]{2,1,0:T(8,128)} %param.16) | copy-start | bytes 98308
  40.9 19.3 %copy-start.3 = (f32[1,64,128]{2,1,0:T(8,128)S(1)}, f32[1,64,128]{2,1,0:T(8,128)}, u32[]{:S(2)}) copy-start(f32[1,64,128]{2,1,0:T(8,128)} %param.17) | copy-start | bytes 98308
  40.9 19.3 %copy-start.4 = (s32[5]{0:T(128)S(1)}, s32[5]{0:T(128)}, u32[]{:S(2)}) copy-start(s32[5]{0:T(128)} %convert_reduce_fusion.bounds_ref) | copy-start | bytes 64
  47.1 8.6 %collective-permute-start.11 = (bf16[320,512]{1,0:T(8,128)(2,1)}, bf16[320,512]{1,0:T(8,128)(2,1)S(1)}, u32[]{:S(2)}, u32[]{:S(2)}) collective-permute-start(bf16[320,512]{1,0:T(8,128)(2,1)} %get-tuple-element.44), channel_id=1, source_target_pairs={{0,32},{1,3},{2,34},{3,5},{4,36},{5,7},{6,38},{7,1},{32,64},{33,35... | collective-permute-start | bytes 983048 | tf_op jit(solution)/shard_map/ppermute | solution.py:58
  48.7 11.5 %collective-permute-start.12 = (bf16[320,512]{1,0:T(8,128)(2,1)}, bf16[320,512]{1,0:T(8,128)(2,1)S(1)}, u32[]{:S(2)}, u32[]{:S(2)}) collective-permute-start(bf16[320,512]{1,0:T(8,128)(2,1)} %get-tuple-element.45), channel_id=1, source_target_pairs={{0,64},{1,5},{2,66},{3,7},{4,68},{5,1},{6,70},{7,3},{32,96},{33,37... | collective-permute-start | bytes 983048 | tf_op jit(solution)/shard_map/ppermute | solution.py:58
  51.4 8.8 %collective-permute-start.13 = (bf16[320,512]{1,0:T(8,128)(2,1)}, bf16[320,512]{1,0:T(8,128)(2,1)S(1)}, u32[]{:S(2)}, u32[]{:S(2)}) collective-permute-start(bf16[320,512]{1,0:T(8,128)(2,1)} %get-tuple-element.46), channel_id=1, source_target_pairs={{0,96},{1,7},{2,98},{3,1},{4,100},{5,3},{6,102},{7,5},{32,0},{33,3... | collective-permute-start | bytes 983048 | tf_op jit(solution)/shard_map/ppermute | solution.py:58
  62.5 1.2 %collective-permute-start.14 = (f32[8,512]{1,0:T(8,128)S(1)}, f32[8,512]{1,0:T(8,128)S(1)}, u32[]{:S(2)}, u32[]{:S(2)}) collective-permute-start(f32[8,512]{1,0:T(8,128)S(1)} %constant_dynamic-slice_fusion), channel_id=1, source_target_pairs={{0,1},{1,0},{2,3},{3,2},{4,5},{5,4},{6,7},{7,6},{8,9},{9,8},{10,11... | collective-permute-start | bytes 49160 | tf_op jit(solution)/shard_map/ppermute | solution.py:344
  89.0 1.3 %collective-permute-start.15 = (f32[8,512]{1,0:T(8,128)S(1)}, f32[8,512]{1,0:T(8,128)S(1)}, u32[]{:S(2)}, u32[]{:S(2)}) collective-permute-start(f32[8,512]{1,0:T(8,128)S(1)} %reduce_sum.29), channel_id=1, source_target_pairs={{0,1},{1,0},{2,3},{3,2},{4,5},{5,4},{6,7},{7,6},{8,9},{9,8},{10,11... | collective-permute-start | bytes 49160 | tf_op jit(solution)/shard_map/ppermute | solution.py:347
  (11 other events, 45.1 us)

commit v6 on v4

--- a/solution.py
+++ b/solution.py
@@ -17,6 +17,7 @@
 DOWN_ROWS = 64
 WINDOW = 256
 ROWS = WINDOW + DOWN_ROWS
+FIRST = 3 * ROWS
 LOCAL_UP = 7392
 PAIR = 2 * RANK
 WIDE = EXAMPLES * RANK
@@ -63,9 +64,13 @@
     return lax.axis_index("ex"), lax.axis_index("py"), lax.axis_index("co")
 
 
-def pack_kernel(grad_hbm, tokens_hbm, down_hbm, up_hbm, give_ref, own_ref, *rest):
-    sends, portion_ref = rest[:3], rest[3]
-    grad, tokens, down, up, turned, loads, sent = rest[4:]
+def tie(value, arrived):
+    return lax.optimization_barrier((value, arrived))
+
+
+def pack_kernel(grad_hbm, tokens_hbm, down_hbm, up_hbm, give_ref, *rest):
+    firsts, seconds, portion_ref = rest[:4], rest[4:8], rest[8]
+    grad, tokens, down, up, turned, loads, sent = rest[9:]
     arrivals = [
         pltpu.make_async_copy(source, target, loads.at[i])
         for i, (source, target) in enumerate(((tokens_hbm, tokens), (grad_hbm, grad), (down_hbm, down), (up_hbm, up)))
@@ -73,7 +78,6 @@
     for arrival in arrivals:
         arrival.start()
     x, y, c = position()
-    outs = [give_ref.at[k] for k in range(4)] + [own_ref] + [send.at[0] for send in sends]
     turned_copies, grad_copies = [], []
     for slot in range(8):
         target = 1 - c if slot < 4 else c
@@ -84,15 +88,18 @@
             owner = to_x * 8 + to_y * 2 + target
             start = pl.multiple_of(window_start(owner), 16)
             column = pl.multiple_of(owner * DOWN_ROWS, DOWN_ROWS)
+            if i:
+                out = give_ref.at[k] if slot < 4 else firsts[k].at[0]
+                window_at, down_at = (i - 1) * WINDOW, 3 * WINDOW + (i - 1) * DOWN_ROWS
+            else:
+                out = give_ref.at[k] if slot < 4 else seconds[k].at[0]
+                window_at = FIRST if slot < 4 else 0
+                down_at = window_at + WINDOW
             grad_copies.append(
-                pltpu.make_async_copy(
-                    grad.at[pl.ds(start, WINDOW)], outs[slot].at[pl.ds(i * WINDOW, WINDOW)], sent
-                )
+                pltpu.make_async_copy(grad.at[pl.ds(start, WINDOW)], out.at[pl.ds(window_at, WINDOW)], sent)
             )
             turned_copies.append(
-                pltpu.make_async_copy(
-                    turned.at[pl.ds(column, DOWN_ROWS)], outs[slot].at[pl.ds(4 * WINDOW + i * DOWN_ROWS, DOWN_ROWS)], sent
-                )
+                pltpu.make_async_copy(turned.at[pl.ds(column, DOWN_ROWS)], out.at[pl.ds(down_at, DOWN_ROWS)], sent)
             )
     arrivals[0].wait()
     turned[...] = tokens[...].T
@@ -115,30 +122,28 @@
         copy.wait()
 
 
-def fill_kernel(taken_ref, a_in, b_in, c_in, a_ref, b_ref, c_ref, sent):
-    copies = [
-        pltpu.make_async_copy(taken_ref.at[k + 1], send.at[1], sent) for k, send in enumerate((a_ref, b_ref, c_ref))
-    ]
+def fill_kernel(taken_ref, *rest):
+    firsts, seconds, (held, load, sent) = rest[8:12], rest[12:16], rest[16:]
+    order = (1, 3, 2, 0)
+    loads = {k: pltpu.make_async_copy(taken_ref.at[k], held.at[k], load.at[k]) for k in order}
+    for k in order:
+        loads[k].start()
+    copies = []
+    for k in order:
+        loads[k].wait()
+        copies.append(pltpu.make_async_copy(held.at[k, pl.ds(0, FIRST)], firsts[k].at[1], sent))
+        copies.append(pltpu.make_async_copy(held.at[k, pl.ds(FIRST, ROWS)], seconds[k].at[1], sent))
+        copies[-2].start()
+        copies[-1].start()
     for copy in copies:
-        copy.start()
-    for copy in copies:
-        copy.wait()
-
-
-def partial_kernel(chunks, bounds_ref, own_ref, taken_ref, *rest):
-    count = len(chunks)
-    arrived, inner, outs = rest[0:3], rest[3:7], rest[7:7 + count]
-    left, side, right_h, right_u, done, inner_sem, columns_sem, sent = rest[7 + count:]
+        copy.wait()
+
+
+def partial_kernel(count, bounds_ref, *rest):
+    columns, inner, outs = rest[0:4], rest[4:8], rest[8:8 + count]
+    left, side, right_h, right_u, done, inner_sem, columns_sem, sent = rest[8 + count:]
     inner_copies = [pltpu.make_async_copy(inner[k], side.at[k], inner_sem) for k in range(4)]
-    column_copies = []
-    for s in range(8):
-        k, part = s // 2, s % 2
-        source = arrived[k - 1].at[part] if k else (taken_ref.at[0] if part else own_ref)
-        for n, j in enumerate(chunks):
-            for begin, at, size in ((j * WINDOW, n * WINDOW, WINDOW), (4 * WINDOW + j * DOWN_ROWS, count * WINDOW + n * DOWN_ROWS, DOWN_ROWS)):
-                column_copies.append(
-                    pltpu.make_async_copy(source.at[pl.ds(begin, size)], left.at[s, pl.ds(at, size)], columns_sem)
-                )
+    column_copies = [pltpu.make_async_copy(columns[k], left.at[k], columns_sem) for k in range(4)]
     for copy in inner_copies + column_copies:
         copy.start()
     x, y, c = position()
@@ -161,7 +166,7 @@
         copy.wait()
 
     def joined(begin, size):
-        return jnp.concatenate([left[s, begin:begin + size, :] for s in range(8)], axis=1)
+        return jnp.concatenate([left[s // 2, s % 2, begin:begin + size, :] for s in range(8)], axis=1)
 
     down = jnp.dot(joined(count * WINDOW, count * DOWN_ROWS), right_u[...], preferred_element_type=F32)
     out_copies = []
@@ -175,15 +180,14 @@
         copy.wait()
 
 
-def partial_call(chunks, *operands):
-    count = len(chunks)
+def partial_call(count, bounds, columns, inner):
     return pl.pallas_call(
-        functools.partial(partial_kernel, chunks),
+        functools.partial(partial_kernel, count),
         out_shape=[jax.ShapeDtypeStruct((ROWS, WIDE), BF)] * count,
-        in_specs=[SMEM] + [ANY] * 9,
+        in_specs=[SMEM] + [ANY] * 8,
         out_specs=[ANY] * count,
         scratch_shapes=[
-            pltpu.VMEM((8, count * ROWS, 128), BF),
+            pltpu.VMEM((4, 2, count * ROWS, 128), BF),
             pltpu.VMEM((4, PAIR, PAIR), BF),
             pltpu.VMEM((1024, WIDE), BF),
             pltpu.VMEM((1024, WIDE), BF),
@@ -193,8 +197,8 @@
             pltpu.SemaphoreType.DMA,
         ],
         compiler_params=pltpu.CompilerParams(vmem_limit_bytes=60 << 20),
-        cost_estimate=pl.CostEstimate(flops=2 * count * ROWS * 1024 * WIDE, bytes_accessed=4 << 20, transcendentals=0),
-    )(*operands)
+        cost_estimate=pl.CostEstimate(flops=2 * count * ROWS * 1024 * WIDE, bytes_accessed=6 << 20, transcendentals=0),
+    )(bounds, *columns, *inner)
 
 
 def feature_kernel(
@@ -269,16 +273,12 @@
         (segments[None, :] < jnp.arange(EXAMPLES + 1, dtype=jnp.int32)[:, None]).astype(jnp.int32), axis=1
     )
 
-    packed = pl.pallas_call(
+    shapes = [jax.ShapeDtypeStruct((2, FIRST, 128), BF)] * 4 + [jax.ShapeDtypeStruct((2, ROWS, 128), BF)] * 4
+    give, *packed, portion = pl.pallas_call(
         pack_kernel,
-        out_shape=[
-            jax.ShapeDtypeStruct((4, 4 * ROWS, 128), BF),
-            jax.ShapeDtypeStruct((4 * ROWS, 128), BF),
-        ]
-        + [jax.ShapeDtypeStruct((2, 4 * ROWS, 128), BF)] * 3
-        + [jax.ShapeDtypeStruct((128, PAIR), F32)],
-        in_specs=[ANY, ANY, ANY, ANY],
-        out_specs=[ANY] * 5 + [VMEM],
+        out_shape=[jax.ShapeDtypeStruct((4, 4 * ROWS, 128), BF)] + shapes + [jax.ShapeDtypeStruct((128, PAIR), F32)],
+        in_specs=[ANY] * 4,
+        out_specs=[ANY] * 9 + [VMEM],
         scratch_shapes=[
             pltpu.VMEM((LOCAL_UP, 128), BF),
             pltpu.VMEM((128, 2048), BF),
@@ -291,31 +291,42 @@
         compiler_params=pltpu.CompilerParams(vmem_limit_bytes=60 << 20),
         cost_estimate=pl.CostEstimate(flops=2 * 128 * 9440 * 128, bytes_accessed=8 << 20, transcendentals=0),
     )(output_gradient.T, tokens, adapter_down_factor, adapter_up_factor)
-    give, own_columns, portion = packed[0], packed[1], packed[5]
     taken = lax.ppermute(give, "co", [(0, 1), (1, 0)])
-    whole = portion
-    for shift in (1, 2, 3):
-        whole = whole + lax.ppermute(portion, ("t1", "t0"), [(i, (i + shift) % 4) for i in range(4)])
-    whole = whole.astype(BF)
+    filled = pl.pallas_call(
+        fill_kernel,
+        out_shape=shapes,
+        in_specs=[ANY] * 9,
+        out_specs=[ANY] * 8,
+        scratch_shapes=[
+            pltpu.VMEM((4, 4 * ROWS, 128), BF),
+            pltpu.SemaphoreType.DMA((4,)),
+            pltpu.SemaphoreType.DMA,
+        ],
+        input_output_aliases={k + 1: k for k in range(8)},
+        compiler_params=pltpu.CompilerParams(vmem_limit_bytes=60 << 20),
+        cost_estimate=pl.CostEstimate(flops=0, bytes_accessed=2 << 20, transcendentals=0),
+    )(taken, *packed)
+    first, second = list(filled[:4]), list(filled[4:])
+    peers = [lax.ppermute(portion, ("t1", "t0"), [(i, (i + shift) % 4) for i in range(4)]) for shift in (1, 2, 3)]
+    first[2], peers[0] = tie(first[2], peers[0])
+    first[1:] = [send_same(first[k], k) for k in (1, 2, 3)]
+    whole = ((portion + peers[0]) + (peers[1] + peers[2])).astype(BF)
     sibling = lax.ppermute(whole, "co", [(0, 1), (1, 0)])
     chip_inner = jnp.concatenate([whole, sibling], axis=0)
-    filled = pl.pallas_call(
-        fill_kernel,
-        out_shape=[jax.ShapeDtypeStruct((2, 4 * ROWS, 128), BF)] * 3,
-        in_specs=[ANY] * 4,
-        out_specs=[ANY] * 3,
-        scratch_shapes=[pltpu.SemaphoreType.DMA],
-        input_output_aliases={1: 0, 2: 1, 3: 2},
-        compiler_params=pltpu.CompilerParams(vmem_limit_bytes=60 << 20),
-        cost_estimate=pl.CostEstimate(flops=0, bytes_accessed=2 << 20, transcendentals=0),
-    )(taken, *packed[2:5])
-    arrived = [send_same(filled[k - 1], k) for k in (1, 2, 3)]
-    inner = [chip_inner] + [send_same(chip_inner, k) for k in (1, 2, 3)]
-
-    operands = (bounds, own_columns, taken, *arrived, *inner)
-    far, near = partial_call((2, 1), *operands)
-    last, own = partial_call((3, 0), *operands)
-    arrived = [send_across(near, 1), send_across(far, 2), send_across(last, 3)]
+    inner = [chip_inner, send_same(chip_inner, 1), None, send_same(chip_inner, 3)]
+    late, first[1] = tie(chip_inner, first[1])
+    inner[2] = send_same(late, 2)
+    second[1], first[3] = tie(second[1], first[3])
+    second[1] = send_same(second[1], 1)
+    second[3], first[2] = tie(second[3], first[2])
+    second[3] = send_same(second[3], 3)
+    second[2], inner[1] = tie(second[2], inner[1])
+    second[2] = send_same(second[2], 2)
+
+    sums = partial_call(3, bounds, first, inner)
+    arrived = [send_across(sums[k - 1], k) for k in (1, 2, 3)]
+    bounds_late, sums = tie(bounds, sums)
+    (own,) = partial_call(1, bounds_late, second, inner)
 
     kept = (first_moment_up, second_moment_up, up_row_seeds, down_row_seeds)
     own, kept = lax.optimization_barrier((own, kept))

time: 121 us -> 84.3 us (0.70)
  Pallas kernels: 45.2 us -> 16.2 us
  waiting for transfers between devices: 23.7 us -> 6.64 us
  starting transfers between devices: 21.9 us -> 31.7 us
  blocking collectives: 24 us -> 22.6 us
    pallas_call x3, Pallas kernels: 39.8 us -> 10.9 us  [the longest x2 8.72 us: partial_call(): pl.pallas_call(functools.partial(partial_kernel, count), out_shape=[jax.S...]
    ppermute x6 -> x9, waiting for transfers between devices: 13 us -> 0.68 us  [send_same(): return lax.ppermute(value, PLANE, pairs(lambda p: along(p, shift)))]
    ppermute x6 -> x9, starting transfers between devices: 10.4 us -> 19 us  [send_same(): return lax.ppermute(value, PLANE, pairs(lambda p: along(p, shift)))]
    ppermute x3, waiting for transfers between devices: 7.07 us -> 2.38 us  [send_across(): return lax.ppermute(value, PLANE, pairs(lambda p: across(p, shift)))]
    all_to_all x2, blocking collectives: 24 us -> 22.6 us  [spread_sum(): lax.all_to_all(copies, EVERY, split_axis=0, concat_axis=0, tiled=True, ax...]
    ppermute x3, starting transfers between devices: 5.45 us -> 6.66 us  [on_device(): lax.ppermute(portion, ('t1', 't0'), [(i, (i + shift) % 4) for i in range(...]
    unnamed x41 -> x45, local copies, waits for them, and re-layouts: 2.43 us -> 3.47 us
  transfers between devices with their start and end apart: 16 -> 19, of which waited for: 8 -> 5; matrix products, arithmetic and copies ran while one was open for 1% -> 1% of each run, Pallas kernels for 26% -> 13%
where the time goes in v6:
time: 84.3 us; the launch traced here: 82.9 us
  starting transfers between devices  31.7 us (38%)
  blocking collectives  22.6 us (27%)
  Pallas kernels  16.2 us (19%)
  waiting for transfers between devices  6.64 us (8%)
  local copies, waits for them, and re-layouts  3.76 us (4%)
  matrix products  0.91 us (1%)
    all_to_all x2, blocking collectives, spread_sum(): lax.all_to_all(copies, EVERY, split_axis=0, concat_axis=0, tiled=True, ax...  22.6 us
    ppermute x9, starting transfers between devices, send_same(): return lax.ppermute(value, PLANE, pairs(lambda p: along(p, shift)))  19 us
    pallas_call x2, Pallas kernels, partial_call(): pl.pallas_call(functools.partial(partial_kernel, count), out_shape=[jax.S...  8.72 us
    ppermute x3, starting transfers between devices, on_device(): lax.ppermute(portion, ('t1', 't0'), [(i, (i + shift) % 4) for i in range(...  6.66 us
    ppermute x3, starting transfers between devices, send_across(): return lax.ppermute(value, PLANE, pairs(lambda p: across(p, shift)))  5.72 us
    pallas_call x1, Pallas kernels, on_device(): pl.pallas_call(pack_kernel, out_shape=[jax.ShapeDtypeStruct((4, 4 * ROWS,...  4.03 us
    unnamed x45, local copies, waits for them, and re-layouts  3.47 us
    ppermute x3, waiting for transfers between devices, send_across(): return lax.ppermute(value, PLANE, pairs(lambda p: across(p, shift)))  2.38 us
  transfers between devices with their start and end apart: 19, of which 5 were waited for; matrix products, arithmetic and copies ran while one was open for 1% of the time, Pallas kernels for 13%

profile of v6, /device:TPU:0, one launch (start us, length us, event | category | flops | bytes accessed | tf_op | source)
XLA Modules:
  0.0 82.9 jit_solution(3418500540171690118)
XLA Ops:
  0.0 4.0 %shard_map.118 = (bf16[4,1280,128]{2,1,0:T(8,128)(2,1)}, bf16[2,960,128]{2,1,0:T(8,128)(2,1)}, bf16[2,960,128]{2,1,0:T(8,128)(2,1)}, bf16[2,960,128]{2,1,0:T(8,1...) custom-call(bf16[7392,128]{1,0:T(8,128)(2,1)} %bitcast.18, ...), custom_call_target="tpu_custom_call" | custom-call | flops 309329920 | bytes 8388608 | tf_op jit(solution)/shard_map/pallas_call | solution.py:277
  4.1 2.1 %collective-permute-start.1 = (f32[128,256]{1,0:T(8,128)}, f32[128,256]{1,0:T(8,128)S(1)}, u32[]{:S(2)}, u32[]{:S(2)}) collective-permute-start(f32[128,256]{1,0:T(8,128)} %get-tuple-element.52), channel_id=1, source_target_pairs={{0,8},{8,16},{16,24},{24,0},{1,9},{9,17},{17,25},{25,1},{2,10},{10... | collective-permute-start | bytes 393224 | tf_op jit(solution)/shard_map/ppermute | solution.py:310
  6.2 3.6 %collective-permute-start.2 = (f32[128,256]{1,0:T(8,128)}, f32[128,256]{1,0:T(8,128)S(1)}, u32[]{:S(2)}, u32[]{:S(2)}) collective-permute-start(f32[128,256]{1,0:T(8,128)} %get-tuple-element.52), channel_id=1, source_target_pairs={{0,16},{8,24},{16,0},{24,8},{1,17},{9,25},{17,1},{25,9},{2,18},{10... | collective-permute-start | bytes 393224 | tf_op jit(solution)/shard_map/ppermute | solution.py:310
  9.8 1.0 %collective-permute-start.3 = (f32[128,256]{1,0:T(8,128)}, f32[128,256]{1,0:T(8,128)S(1)}, u32[]{:S(2)}, u32[]{:S(2)}) collective-permute-start(f32[128,256]{1,0:T(8,128)} %get-tuple-element.52), channel_id=1, source_target_pairs={{0,24},{8,0},{16,8},{24,16},{1,25},{9,1},{17,9},{25,17},{2,26},{10... | collective-permute-start | bytes 393224 | tf_op jit(solution)/shard_map/ppermute | solution.py:310
  10.8 1.1 %copy-done.5 = bf16[4,1280,128]{2,1,0:T(8,128)(2,1)} copy-done((bf16[4,1280,128]{2,1,0:T(8,128)(2,1)}, bf16[4,1280,128]{2,1,0:T(8,128)(2,1)S(1)}, u32[]{:S(2)}) %copy-start.5) | copy-done | bytes 1310744
  11.9 2.1 %shard_map.119 = (bf16[2,960,128]{2,1,0:T(8,128)(2,1)}, bf16[2,960,128]{2,1,0:T(8,128)(2,1)}, bf16[2,960,128]{2,1,0:T(8,128)(2,1)}, bf16[2,960,128]{2,1,0:T(8,12...) custom-call(bf16[4,1280,128]{2,1,0:T(8,128)(2,1)} %copy-done.5, ...), custom_call_target="tpu_custom_call", output_to_operand_aliasing={{0}: (1, {}), {1}: (2, {}), {2}: (3, {}), {3}: (4, {}), {4}... | custom-call | bytes 2097152 | tf_op jit(solution)/shard_map/pallas_call | solution.py:295
  14.0 1.6 %collective-permute-start.5 = (bf16[2,960,128]{2,1,0:T(8,128)(2,1)}, bf16[2,960,128]{2,1,0:T(8,128)(2,1)S(1)}, u32[]{:S(2)}, u32[]{:S(2)}) collective-permute-start(bf16[2,960,128]{2,1,0:T(8,128)(2,1)} %get-tuple-element.55), channel_id=1, source_target_pairs={{0,2},{1,33},{2,4},{3,35},{4,6},{5,37},{6,0},{7,39},{32,34},{33,65... | collective-permute-start | bytes 1474568 | tf_op jit(solution)/shard_map/ppermute | solution.py:56
  15.7 2.9 %collective-permute-start.6 = (bf16[2,960,128]{2,1,0:T(8,128)(2,1)}, bf16[2,960,128]{2,1,0:T(8,128)(2,1)S(1)}, u32[]{:S(2)}, u32[]{:S(2)}) collective-permute-start(bf16[2,960,128]{2,1,0:T(8,128)(2,1)} %get-tuple-element.58), channel_id=1, source_target_pairs={{0,4},{1,65},{2,6},{3,67},{4,0},{5,69},{6,2},{7,71},{32,36},{33,97... | collective-permute-start | bytes 1474568 | tf_op jit(solution)/shard_map/ppermute | solution.py:56
  18.6 1.3 %collective-permute-start.7 = (bf16[2,960,128]{2,1,0:T(8,128)(2,1)}, bf16[2,960,128]{2,1,0:T(8,128)(2,1)S(1)}, u32[]{:S(2)}, u32[]{:S(2)}) collective-permute-start(bf16[2,960,128]{2,1,0:T(8,128)(2,1)} %get-tuple-element.61), channel_id=1, source_target_pairs={{0,6},{1,97},{2,0},{3,99},{4,2},{5,101},{6,4},{7,103},{32,38},{33,... | collective-permute-start | bytes 1474568 | tf_op jit(solution)/shard_map/ppermute | solution.py:56
  20.1 1.2 %collective-permute-done.4 = bf16[128,256]{1,0:T(8,128)(2,1)S(1)} collective-permute-done((bf16[128,256]{1,0:T(8,128)(2,1)S(1)}, bf16[128,256]{1,0:T(8,128)(2,1)S(1)}, u32[]{:S(2)}, u32[]{:S(2)}) %collective-permute-start.4) | collective-permute-done | bytes 65568 | tf_op jit(solution)/shard_map/ppermute | solution.py:314
  22.1 2.6 %collective-permute-start.10 = (bf16[256,256]{1,0:T(8,128)(2,1)S(1)}, bf16[256,256]{1,0:T(8,128)(2,1)S(1)}, u32[]{:S(2)}, u32[]{:S(2)}) collective-permute-start(bf16[256,256]{1,0:T(8,128)(2,1)S(1)} %pad_maximum_fusion.rest_4_), channel_id=1, source_target_pairs={{0,6},{1,97},{2,0},{3,99},{4,2},{5,101},{6,4},{7,103},{32,38},{33,... | collective-permute-start | bytes 393224 | tf_op jit(solution)/shard_map/ppermute | solution.py:56
  24.6 7.0 %collective-permute-start.9 = (bf16[256,256]{1,0:T(8,128)(2,1)S(1)}, bf16[256,256]{1,0:T(8,128)(2,1)S(1)}, u32[]{:S(2)}, u32[]{:S(2)}) collective-permute-start(bf16[256,256]{1,0:T(8,128)(2,1)S(1)} %pad_maximum_fusion.rest_4_), channel_id=1, source_target_pairs={{0,4},{1,65},{2,6},{3,67},{4,0},{5,69},{6,2},{7,71},{32,36},{33,97... | collective-permute-start | bytes 393224 | tf_op jit(solution)/shard_map/ppermute | solution.py:56
  33.0 1.2 %collective-permute-start.13 = (bf16[2,320,128]{2,1,0:T(8,128)(2,1)}, bf16[2,320,128]{2,1,0:T(8,128)(2,1)S(1)}, u32[]{:S(2)}, u32[]{:S(2)}) collective-permute-start(bf16[2,320,128]{2,1,0:T(8,128)(2,1)} %get-tuple-element.73), channel_id=1, source_target_pairs={{0,6},{1,97},{2,0},{3,99},{4,2},{5,101},{6,4},{7,103},{32,38},{33,... | collective-permute-start | bytes 491528 | tf_op jit(solution)/shard_map/ppermute | solution.py:56
  36.5 4.8 %shard_map.120 = (bf16[320,512]{1,0:T(8,128)(2,1)}, bf16[320,512]{1,0:T(8,128)(2,1)}, bf16[320,512]{1,0:T(8,128)(2,1)}) custom-call(s32[5]{0:T(128)} %convert_reduce_fusion.bounds_ref, bf16[2,960,128]{2,1,0:T(8,128)(2,1)} %get-tuple-element.51.rest_0_, bf16[2,960,128]{2,1,0:T(8,128)(2,1)} %copy-done.19, bf16[2,960,128]{2,1,0:T(8,128)(2,1)} %copy-done.20, ...), custom_call_target="tpu_custom_call" | custom-call | flops 1006632960 | bytes 6291456 | tf_op jit(solution)/shard_map/pallas_call | solution.py:184
  41.4 1.6 %collective-permute-start.14 = (bf16[320,512]{1,0:T(8,128)(2,1)}, bf16[320,512]{1,0:T(8,128)(2,1)S(1)}, u32[]{:S(2)}, u32[]{:S(2)}) collective-permute-start(bf16[320,512]{1,0:T(8,128)(2,1)} %get-tuple-element.66), channel_id=1, source_target_pairs={{0,32},{1,3},{2,34},{3,5},{4,36},{5,7},{6,38},{7,1},{32,64},{33,35... | collective-permute-start | bytes 983048 | tf_op jit(solution)/shard_map/ppermute | solution.py:60
  42.9 2.7 %collective-permute-start.15 = (bf16[320,512]{1,0:T(8,128)(2,1)}, bf16[320,512]{1,0:T(8,128)(2,1)S(1)}, u32[]{:S(2)}, u32[]{:S(2)}) collective-permute-start(bf16[320,512]{1,0:T(8,128)(2,1)} %get-tuple-element.67), channel_id=1, source_target_pairs={{0,64},{1,5},{2,66},{3,7},{4,68},{5,1},{6,70},{7,3},{32,96},{33,37... | collective-permute-start | bytes 983048 | tf_op jit(solution)/shard_map/ppermute | solution.py:60
  45.7 1.4 %collective-permute-start.16 = (bf16[320,512]{1,0:T(8,128)(2,1)}, bf16[320,512]{1,0:T(8,128)(2,1)S(1)}, u32[]{:S(2)}, u32[]{:S(2)}) collective-permute-start(bf16[320,512]{1,0:T(8,128)(2,1)} %get-tuple-element.68), channel_id=1, source_target_pairs={{0,96},{1,7},{2,98},{3,1},{4,100},{5,3},{6,102},{7,5},{32,0},{33,3... | collective-permute-start | bytes 983048 | tf_op jit(solution)/shard_map/ppermute | solution.py:60
  47.8 3.9 %shard_map.121.own_ref = bf16[320,512]{1,0:T(8,128)(2,1)} custom-call(s32[5]{0:T(128)} %convert_reduce_fusion.bounds_ref, bf16[2,320,128]{2,1,0:T(8,128)(2,1)} %get-tuple-element.70.rest_0_, bf16[2,320,128]{2,1,0:T(8,128)(2,1)} %copy-done.9, bf16[2,320,128]{2,1,0:T(8,128)(2,1)} %copy-done.7, bf16[2,320,128]{2,1,0:T(8,128)(2,1)} %copy-done.8, ...), custom_call_target="tpu_custom_call" | custom-call | flops 335544320 | bytes 6291456 | tf_op jit(solution)/shard_map/pallas_call | solution.py:184
  52.1 2.4 %collective-permute-done.15.b_ref = bf16[320,512]{1,0:T(8,128)(2,1)S(1)} collective-permute-done((bf16[320,512]{1,0:T(8,128)(2,1)}, bf16[320,512]{1,0:T(8,128)(2,1)S(1)}, u32[]{:S(2)}, u32[]{:S(2)}) %collective-permute-start.15) | collective-permute-done | bytes 327712 | tf_op jit(solution)/shard_map/ppermute | solution.py:60
  55.4 1.3 %shard_map.122 = f32[16,512]{1,0:T(8,128)S(1)} custom-call(bf16[320,512]{1,0:T(8,128)(2,1)S(1)} %copy-done.1, bf16[320,512]{1,0:T(8,128)(2,1)S(1)} %collective-permute-done.14.a_ref, bf16[320,512]{1,0:T(8,128)(2,1)S(1)} %collective-permute-done.15.b_ref, bf16[320,512]{1,0:T(8,128)(2,1)S(1)} %collective-permute-done.16.c_ref, s32[5]{0:T(128)S(1)} %copy-done.4, ...), custom_call_target="tpu_custom_call" | custom-call | bytes 3145728 | tf_op jit(solution)/shard_map/pallas_call | solution.py:342
  56.9 1.2 %collective-permute-done.17 = f32[8,512]{1,0:T(8,128)S(1)} collective-permute-done((f32[8,512]{1,0:T(8,128)S(1)}, f32[8,512]{1,0:T(8,128)S(1)}, u32[]{:S(2)}, u32[]{:S(2)}) %collective-permute-start.17) | collective-permute-done | bytes 16416 | tf_op jit(solution)/shard_map/ppermute | solution.py:358
  58.0 10.9 %all_to_all.10 = f32[8,8,512]{2,1,0:T(8,128)S(1)} all-to-all(f32[8,8,512]{2,1,0:T(8,128)S(1)} %broadcast_in_dim.10), channel_id=1, replica_groups={{0,8,32,40,64,72,96,104},{16,24,48,56,80,88,112,120},{1,9,33,41,65,73,9..., dimensions={0} | all-to-all | bytes 262144 | tf_op jit(solution)/shard_map/all_to_all | solution.py:250
  68.9 11.7 %all_to_all.11 = f32[8,8,512]{2,1,0:T(8,128)S(1)} all-to-all(f32[8,8,512]{2,1,0:T(8,128)S(1)} %broadcast_in_dim.11), channel_id=1, replica_groups={{0,24,2,26,4,28,6,30},{8,16,10,18,12,20,14,22},{1,25,3,27,5,29,7,31},{9..., dimensions={0} | all-to-all | bytes 262144 | tf_op jit(solution)/shard_map/all_to_all | solution.py:250
  80.7 1.2 %collective-permute-done.18 = f32[8,512]{1,0:T(8,128)S(1)} collective-permute-done((f32[8,512]{1,0:T(8,128)S(1)}, f32[8,512]{1,0:T(8,128)S(1)}, u32[]{:S(2)}, u32[]{:S(2)}) %collective-permute-start.18) | collective-permute-done | bytes 16416 | tf_op jit(solution)/shard_map/ppermute | solution.py:361
  (83 shorter events, 7.8 us)
Async XLA Ops:
  0.0 81.9 %copy-start = (bf16[16,128,64]{1,2,0:T(8,128)(2,1)S(1)}, bf16[16,128,64]{1,2,0:T(8,128)(2,1)}, u32[]{:S(2)}) copy-start(bf16[16,128,64]{1,2,0:T(8,128)(2,1)} %param.23) | copy-start | bytes 786436
  4.0 6.8 %collective-permute-start = (bf16[4,1280,128]{2,1,0:T(8,128)(2,1)}, bf16[4,1280,128]{2,1,0:T(8,128)(2,1)S(1)}, u32[]{:S(2)}, u32[]{:S(2)}) collective-permute-start(bf16[4,1280,128]{2,1,0:T(8,128)(2,1)} %get-tuple-element.42), channel_id=1, source_target_pairs={{0,1},{1,0},{2,3},{3,2},{4,5},{5,4},{6,7},{7,6},{8,9},{9,8},{10,11... | collective-permute-start | bytes 3932168 | tf_op jit(solution)/shard_map/ppermute | solution.py:294
  4.1 9.9 %collective-permute-start.1 = (f32[128,256]{1,0:T(8,128)}, f32[128,256]{1,0:T(8,128)S(1)}, u32[]{:S(2)}, u32[]{:S(2)}) collective-permute-start(f32[128,256]{1,0:T(8,128)} %get-tuple-element.52), channel_id=1, source_target_pairs={{0,8},{8,16},{16,24},{24,0},{1,9},{9,17},{17,25},{25,1},{2,10},{10... | collective-permute-start | bytes 393224 | tf_op jit(solution)/shard_map/ppermute | solution.py:310
  6.2 13.7 %collective-permute-start.2 = (f32[128,256]{1,0:T(8,128)}, f32[128,256]{1,0:T(8,128)S(1)}, u32[]{:S(2)}, u32[]{:S(2)}) collective-permute-start(f32[128,256]{1,0:T(8,128)} %get-tuple-element.52), channel_id=1, source_target_pairs={{0,16},{8,24},{16,0},{24,8},{1,17},{9,25},{17,1},{25,9},{2,18},{10... | collective-permute-start | bytes 393224 | tf_op jit(solution)/shard_map/ppermute | solution.py:310
  9.8 10.1 %collective-permute-start.3 = (f32[128,256]{1,0:T(8,128)}, f32[128,256]{1,0:T(8,128)S(1)}, u32[]{:S(2)}, u32[]{:S(2)}) collective-permute-start(f32[128,256]{1,0:T(8,128)} %get-tuple-element.52), channel_id=1, source_target_pairs={{0,24},{8,0},{16,8},{24,16},{1,25},{9,1},{17,9},{25,17},{2,26},{10... | collective-permute-start | bytes 393224 | tf_op jit(solution)/shard_map/ppermute | solution.py:310
  11.9 23.3 %copy-start.16 = (s32[4096]{0:T(1024)S(1)}, s32[4096]{0:T(1024)}, u32[]{:S(2)}) copy-start(s32[4096]{0:T(1024)} %param.22) | copy-start | bytes 49156
  14.0 10.6 %collective-permute-start.5 = (bf16[2,960,128]{2,1,0:T(8,128)(2,1)}, bf16[2,960,128]{2,1,0:T(8,128)(2,1)S(1)}, u32[]{:S(2)}, u32[]{:S(2)}) collective-permute-start(bf16[2,960,128]{2,1,0:T(8,128)(2,1)} %get-tuple-element.55), channel_id=1, source_target_pairs={{0,2},{1,33},{2,4},{3,35},{4,6},{5,37},{6,0},{7,39},{32,34},{33,65... | collective-permute-start | bytes 1474568 | tf_op jit(solution)/shard_map/ppermute | solution.py:56
  15.7 17.3 %collective-permute-start.6 = (bf16[2,960,128]{2,1,0:T(8,128)(2,1)}, bf16[2,960,128]{2,1,0:T(8,128)(2,1)S(1)}, u32[]{:S(2)}, u32[]{:S(2)}) collective-permute-start(bf16[2,960,128]{2,1,0:T(8,128)(2,1)} %get-tuple-element.58), channel_id=1, source_target_pairs={{0,4},{1,65},{2,6},{3,67},{4,0},{5,69},{6,2},{7,71},{32,36},{33,97... | collective-permute-start | bytes 1474568 | tf_op jit(solution)/shard_map/ppermute | solution.py:56
  18.6 14.4 %collective-permute-start.7 = (bf16[2,960,128]{2,1,0:T(8,128)(2,1)}, bf16[2,960,128]{2,1,0:T(8,128)(2,1)S(1)}, u32[]{:S(2)}, u32[]{:S(2)}) collective-permute-start(bf16[2,960,128]{2,1,0:T(8,128)(2,1)} %get-tuple-element.61), channel_id=1, source_target_pairs={{0,6},{1,97},{2,0},{3,99},{4,2},{5,101},{6,4},{7,103},{32,38},{33,... | collective-permute-start | bytes 1474568 | tf_op jit(solution)/shard_map/ppermute | solution.py:56
  20.0 1.3 %collective-permute-start.4 = (bf16[128,256]{1,0:T(8,128)(2,1)S(1)}, bf16[128,256]{1,0:T(8,128)(2,1)S(1)}, u32[]{:S(2)}, u32[]{:S(2)}) collective-permute-start(bf16[128,256]{1,0:T(8,128)(2,1)S(1)} %add_convert_fusion), channel_id=1, source_target_pairs={{0,1},{1,0},{2,3},{3,2},{4,5},{5,4},{6,7},{7,6},{8,9},{9,8},{10,11... | collective-permute-start | bytes 196616 | tf_op jit(solution)/shard_map/ppermute | solution.py:314
  21.3 10.9 %collective-permute-start.8 = (bf16[256,256]{1,0:T(8,128)(2,1)S(1)}, bf16[256,256]{1,0:T(8,128)(2,1)S(1)}, u32[]{:S(2)}, u32[]{:S(2)}) collective-permute-start(bf16[256,256]{1,0:T(8,128)(2,1)S(1)} %pad_maximum_fusion.rest_4_), channel_id=1, source_target_pairs={{0,2},{1,33},{2,4},{3,35},{4,6},{5,37},{6,0},{7,39},{32,34},{33,65... | collective-permute-start | bytes 393224 | tf_op jit(solution)/shard_map/ppermute | solution.py:56
  22.1 13.7 %collective-permute-start.10 = (bf16[256,256]{1,0:T(8,128)(2,1)S(1)}, bf16[256,256]{1,0:T(8,128)(2,1)S(1)}, u32[]{:S(2)}, u32[]{:S(2)}) collective-permute-start(bf16[256,256]{1,0:T(8,128)(2,1)S(1)} %pad_maximum_fusion.rest_4_), channel_id=1, source_target_pairs={{0,6},{1,97},{2,0},{3,99},{4,2},{5,101},{6,4},{7,103},{32,38},{33,... | collective-permute-start | bytes 393224 | tf_op jit(solution)/shard_map/ppermute | solution.py:56
  24.6 11.1 %collective-permute-start.9 = (bf16[256,256]{1,0:T(8,128)(2,1)S(1)}, bf16[256,256]{1,0:T(8,128)(2,1)S(1)}, u32[]{:S(2)}, u32[]{:S(2)}) collective-permute-start(bf16[256,256]{1,0:T(8,128)(2,1)S(1)} %pad_maximum_fusion.rest_4_), channel_id=1, source_target_pairs={{0,4},{1,65},{2,6},{3,67},{4,0},{5,69},{6,2},{7,71},{32,36},{33,97... | collective-permute-start | bytes 393224 | tf_op jit(solution)/shard_map/ppermute | solution.py:56
  32.3 13.4 %collective-permute-start.12 = (bf16[2,320,128]{2,1,0:T(8,128)(2,1)}, bf16[2,320,128]{2,1,0:T(8,128)(2,1)S(1)}, u32[]{:S(2)}, u32[]{:S(2)}) collective-permute-start(bf16[2,320,128]{2,1,0:T(8,128)(2,1)} %get-tuple-element.72), channel_id=1, source_target_pairs={{0,4},{1,65},{2,6},{3,67},{4,0},{5,69},{6,2},{7,71},{32,36},{33,97... | collective-permute-start | bytes 491528 | tf_op jit(solution)/shard_map/ppermute | solution.py:56
  33.0 14.1 %collective-permute-start.13 = (bf16[2,320,128]{2,1,0:T(8,128)(2,1)}, bf16[2,320,128]{2,1,0:T(8,128)(2,1)S(1)}, u32[]{:S(2)}, u32[]{:S(2)}) collective-permute-start(bf16[2,320,128]{2,1,0:T(8,128)(2,1)} %get-tuple-element.73), channel_id=1, source_target_pairs={{0,6},{1,97},{2,0},{3,99},{4,2},{5,101},{6,4},{7,103},{32,38},{33,... | collective-permute-start | bytes 491528 | tf_op jit(solution)/shard_map/ppermute | solution.py:56
  34.2 12.9 %collective-permute-start.11 = (bf16[2,320,128]{2,1,0:T(8,128)(2,1)}, bf16[2,320,128]{2,1,0:T(8,128)(2,1)S(1)}, u32[]{:S(2)}, u32[]{:S(2)}) collective-permute-start(bf16[2,320,128]{2,1,0:T(8,128)(2,1)} %get-tuple-element.71), channel_id=1, source_target_pairs={{0,2},{1,33},{2,4},{3,35},{4,6},{5,37},{6,0},{7,39},{32,34},{33,65... | collective-permute-start | bytes 491528 | tf_op jit(solution)/shard_map/ppermute | solution.py:56
  36.5 15.5 %copy-start.18 = (s32[1,64]{1,0:T(1,128)S(1)}, s32[1,64]{1,0:T(1,128)}, u32[]{:S(2)}) copy-start(s32[1,64]{1,0:T(1,128)} %param.20) | copy-start | bytes 772
  36.5 15.5 %copy-start.14 = (f32[1,231,128]{2,0,1:T(1,128)S(1)}, f32[1,231,128]{2,0,1:T(1,128)}, u32[]{:S(2)}) copy-start(f32[1,231,128]{2,0,1:T(1,128)} %param.19) | copy-start | bytes 354820
  36.5 15.5 %copy-start.15 = (f32[1,231,128]{2,0,1:T(1,128)S(1)}, f32[1,231,128]{2,0,1:T(1,128)}, u32[]{:S(2)}) copy-start(f32[1,231,128]{2,0,1:T(1,128)} %param.18) | copy-start | bytes 354820
  41.4 10.7 %collective-permute-start.14 = (bf16[320,512]{1,0:T(8,128)(2,1)}, bf16[320,512]{1,0:T(8,128)(2,1)S(1)}, u32[]{:S(2)}, u32[]{:S(2)}) collective-permute-start(bf16[320,512]{1,0:T(8,128)(2,1)} %get-tuple-element.66), channel_id=1, source_target_pairs={{0,32},{1,3},{2,34},{3,5},{4,36},{5,7},{6,38},{7,1},{32,64},{33,35... | collective-permute-start | bytes 983048 | tf_op jit(solution)/shard_map/ppermute | solution.py:60
  42.9 11.5 %collective-permute-start.15 = (bf16[320,512]{1,0:T(8,128)(2,1)}, bf16[320,512]{1,0:T(8,128)(2,1)S(1)}, u32[]{:S(2)}, u32[]{:S(2)}) collective-permute-start(bf16[320,512]{1,0:T(8,128)(2,1)} %get-tuple-element.67), channel_id=1, source_target_pairs={{0,64},{1,5},{2,66},{3,7},{4,68},{5,1},{6,70},{7,3},{32,96},{33,37... | collective-permute-start | bytes 983048 | tf_op jit(solution)/shard_map/ppermute | solution.py:60
  45.7 8.8 %collective-permute-start.16 = (bf16[320,512]{1,0:T(8,128)(2,1)}, bf16[320,512]{1,0:T(8,128)(2,1)S(1)}, u32[]{:S(2)}, u32[]{:S(2)}) collective-permute-start(bf16[320,512]{1,0:T(8,128)(2,1)} %get-tuple-element.68), channel_id=1, source_target_pairs={{0,96},{1,7},{2,98},{3,1},{4,100},{5,3},{6,102},{7,5},{32,0},{33,3... | collective-permute-start | bytes 983048 | tf_op jit(solution)/shard_map/ppermute | solution.py:60
  56.8 1.2 %collective-permute-start.17 = (f32[8,512]{1,0:T(8,128)S(1)}, f32[8,512]{1,0:T(8,128)S(1)}, u32[]{:S(2)}, u32[]{:S(2)}) collective-permute-start(f32[8,512]{1,0:T(8,128)S(1)} %constant_dynamic-slice_fusion), channel_id=1, source_target_pairs={{0,1},{1,0},{2,3},{3,2},{4,5},{5,4},{6,7},{7,6},{8,9},{9,8},{10,11... | collective-permute-start | bytes 49160 | tf_op jit(solution)/shard_map/ppermute | solution.py:358
  80.6 1.3 %collective-permute-start.18 = (f32[8,512]{1,0:T(8,128)S(1)}, f32[8,512]{1,0:T(8,128)S(1)}, u32[]{:S(2)}, u32[]{:S(2)}) collective-permute-start(f32[8,512]{1,0:T(8,128)S(1)} %reduce_sum.29), channel_id=1, source_target_pairs={{0,1},{1,0},{2,3},{3,2},{4,5},{5,4},{6,7},{7,6},{8,9},{9,8},{10,11... | collective-permute-start | bytes 49160 | tf_op jit(solution)/shard_map/ppermute | solution.py:361
  (17 other events, 103.6 us)

commit v7 on v6

--- a/solution.py
+++ b/solution.py
@@ -18,6 +18,7 @@
 WINDOW = 256
 ROWS = WINDOW + DOWN_ROWS
 FIRST = 3 * ROWS
+PARTED = (1, 3)
 LOCAL_UP = 7392
 PAIR = 2 * RANK
 WIDE = EXAMPLES * RANK
@@ -69,8 +70,8 @@
 
 
 def pack_kernel(grad_hbm, tokens_hbm, down_hbm, up_hbm, give_ref, *rest):
-    firsts, seconds, portion_ref = rest[:4], rest[4:8], rest[8]
-    grad, tokens, down, up, turned, loads, sent = rest[9:]
+    buffers, portion_ref = rest[:6], rest[6]
+    grad, tokens, down, up, turned, loads, sent = rest[7:]
     arrivals = [
         pltpu.make_async_copy(source, target, loads.at[i])
         for i, (source, target) in enumerate(((tokens_hbm, tokens), (grad_hbm, grad), (down_hbm, down), (up_hbm, up)))
@@ -88,13 +89,10 @@
             owner = to_x * 8 + to_y * 2 + target
             start = pl.multiple_of(window_start(owner), 16)
             column = pl.multiple_of(owner * DOWN_ROWS, DOWN_ROWS)
-            if i:
-                out = give_ref.at[k] if slot < 4 else firsts[k].at[0]
-                window_at, down_at = (i - 1) * WINDOW, 3 * WINDOW + (i - 1) * DOWN_ROWS
-            else:
-                out = give_ref.at[k] if slot < 4 else seconds[k].at[0]
-                window_at = FIRST if slot < 4 else 0
-                down_at = window_at + WINDOW
+            out = give_ref.at[k] if slot < 4 else buffers[k].at[0]
+            window_at, down_at = ((i - 1) * WINDOW, 3 * WINDOW + (i - 1) * DOWN_ROWS) if i else (FIRST, FIRST + WINDOW)
+            if slot >= 4 and i == 0 and k in PARTED:
+                out, window_at, down_at = buffers[4 + PARTED.index(k)].at[0], 0, WINDOW
             grad_copies.append(
                 pltpu.make_async_copy(grad.at[pl.ds(start, WINDOW)], out.at[pl.ds(window_at, WINDOW)], sent)
             )
@@ -123,82 +121,101 @@
 
 
 def fill_kernel(taken_ref, *rest):
-    firsts, seconds, (held, load, sent) = rest[8:12], rest[12:16], rest[16:]
-    order = (1, 3, 2, 0)
+    buffers, (held, load, sent) = rest[6:12], rest[12:]
+    order = (2, 1, 3, 0)
     loads = {k: pltpu.make_async_copy(taken_ref.at[k], held.at[k], load.at[k]) for k in order}
     for k in order:
         loads[k].start()
     copies = []
     for k in order:
         loads[k].wait()
-        copies.append(pltpu.make_async_copy(held.at[k, pl.ds(0, FIRST)], firsts[k].at[1], sent))
-        copies.append(pltpu.make_async_copy(held.at[k, pl.ds(FIRST, ROWS)], seconds[k].at[1], sent))
-        copies[-2].start()
+        if k in PARTED:
+            copies.append(pltpu.make_async_copy(held.at[k, pl.ds(0, FIRST)], buffers[k].at[1], sent))
+            copies[-1].start()
+            second = buffers[4 + PARTED.index(k)]
+            copies.append(pltpu.make_async_copy(held.at[k, pl.ds(FIRST, ROWS)], second.at[1], sent))
+        else:
+            copies.append(pltpu.make_async_copy(held.at[k], buffers[k].at[1], sent))
         copies[-1].start()
     for copy in copies:
         copy.wait()
 
 
-def partial_kernel(count, bounds_ref, *rest):
+def partial_kernel(count, segments_hbm, *rest):
     columns, inner, outs = rest[0:4], rest[4:8], rest[8:8 + count]
-    left, side, right_h, right_u, done, inner_sem, columns_sem, sent = rest[8 + count:]
+    left, side, segments, right_h, right_u, total, done, segments_sem, inner_sem, columns_sem, sent = rest[8 + count:]
+    segments_copy = pltpu.make_async_copy(segments_hbm, segments, segments_sem)
+    segments_copy.start()
     inner_copies = [pltpu.make_async_copy(inner[k], side.at[k], inner_sem) for k in range(4)]
-    column_copies = [pltpu.make_async_copy(columns[k], left.at[k], columns_sem) for k in range(4)]
+    column_copies = []
+    for k in range(4):
+        begin = FIRST if count == 1 and k not in PARTED else 0
+        for part in range(2):
+            source = columns[k].at[part, pl.ds(begin, count * ROWS)]
+            column_copies.append(pltpu.make_async_copy(source, left.at[k, part], columns_sem.at[k]))
     for copy in inner_copies + column_copies:
         copy.start()
     x, y, c = position()
-    row = lax.broadcasted_iota(jnp.int32, (128, RANK), 0)
-    for copy in inner_copies:
-        copy.wait()
+    segments_copy.wait()
+    masks = []
     for k in range(4):
         chip = jnp.where(c == 0, x * 4 + lax.rem(y - k + 4, 4), lax.rem(x - k + 4, 4) * 4 + y)
         for part in range(2):
-            token = row + (chip * PAIR + jnp.where(part == 0, c, 1 - c) * 128)
-            rows = pl.ds(k * PAIR + part * 128, 128)
-            h = side[k, part * 128:(part + 1) * 128, :RANK]
-            u = side[k, part * 128:(part + 1) * 128, RANK:]
-            for e in range(EXAMPLES):
-                inside = (token >= bounds_ref[e]) & (token < bounds_ref[e + 1])
-                picked = jnp.where(inside, 1.0, 0.0).astype(BF)
-                right_h[rows, e * RANK:(e + 1) * RANK] = h * picked
-                right_u[rows, e * RANK:(e + 1) * RANK] = u * picked
-    for copy in column_copies:
+            labels = segments[pl.ds(2 * chip + jnp.where(part == 0, c, 1 - c), 1), :]
+            labels = jnp.broadcast_to(labels.astype(F32), (128, RANK)).T
+            masks.append([jnp.where(labels == e, 1.0, 0.0).astype(BF) for e in range(EXAMPLES)])
+    for copy in inner_copies:
         copy.wait()
-
-    def joined(begin, size):
-        return jnp.concatenate([left[s // 2, s % 2, begin:begin + size, :] for s in range(8)], axis=1)
-
-    down = jnp.dot(joined(count * WINDOW, count * DOWN_ROWS), right_u[...], preferred_element_type=F32)
+    for s in range(8):
+        rows = pl.ds(s * 128, 128)
+        h = side[s // 2, s % 2 * 128:(s % 2 + 1) * 128, :RANK]
+        u = side[s // 2, s % 2 * 128:(s % 2 + 1) * 128, RANK:]
+        for e in range(EXAMPLES):
+            right_h[rows, e * RANK:(e + 1) * RANK] = h * masks[s][e]
+            right_u[rows, e * RANK:(e + 1) * RANK] = u * masks[s][e]
+    split = count * WINDOW
+    for k in range(4):
+        for copy in column_copies[2 * k:2 * k + 2]:
+            copy.wait()
+        both = pl.ds(k * PAIR, PAIR)
+        for n in range(count + 1):
+            rows = slice(n * WINDOW, (n + 1) * WINDOW) if n < count else slice(split, count * ROWS)
+            joined = jnp.concatenate([left[k, 0, rows, :], left[k, 1, rows, :]], axis=1)
+            right = (right_h if n < count else right_u)[both, :]
+            product = jnp.dot(joined, right, preferred_element_type=F32)
+            total[rows, :] = product if k == 0 else total[rows, :] + product
     out_copies = []
     for n in range(count):
-        up = jnp.dot(joined(n * WINDOW, WINDOW), right_h[...], preferred_element_type=F32)
-        done[n, :WINDOW, :] = up.astype(BF)
-        done[n, WINDOW:, :] = down[n * DOWN_ROWS:(n + 1) * DOWN_ROWS].astype(BF)
+        done[n, :WINDOW, :] = total[n * WINDOW:(n + 1) * WINDOW, :].astype(BF)
+        done[n, WINDOW:, :] = total[split + n * DOWN_ROWS:split + (n + 1) * DOWN_ROWS, :].astype(BF)
         out_copies.append(pltpu.make_async_copy(done.at[n], outs[n], sent))
         out_copies[-1].start()
     for copy in out_copies:
         copy.wait()
 
 
-def partial_call(count, bounds, columns, inner):
+def partial_call(count, labels, columns, inner):
     return pl.pallas_call(
         functools.partial(partial_kernel, count),
         out_shape=[jax.ShapeDtypeStruct((ROWS, WIDE), BF)] * count,
-        in_specs=[SMEM] + [ANY] * 8,
+        in_specs=[ANY] * 9,
         out_specs=[ANY] * count,
         scratch_shapes=[
             pltpu.VMEM((4, 2, count * ROWS, 128), BF),
             pltpu.VMEM((4, PAIR, PAIR), BF),
+            pltpu.VMEM((32, 128), jnp.int32),
             pltpu.VMEM((1024, WIDE), BF),
             pltpu.VMEM((1024, WIDE), BF),
+            pltpu.VMEM((count * ROWS, WIDE), F32),
             pltpu.VMEM((count, ROWS, WIDE), BF),
             pltpu.SemaphoreType.DMA,
             pltpu.SemaphoreType.DMA,
+            pltpu.SemaphoreType.DMA((4,)),
             pltpu.SemaphoreType.DMA,
         ],
         compiler_params=pltpu.CompilerParams(vmem_limit_bytes=60 << 20),
         cost_estimate=pl.CostEstimate(flops=2 * count * ROWS * 1024 * WIDE, bytes_accessed=6 << 20, transcendentals=0),
-    )(bounds, *columns, *inner)
+    )(labels, *columns, *inner)
 
 
 def feature_kernel(
@@ -269,16 +286,12 @@
 ):
     x, y, c = position()
     me = x * 8 + y * 2 + c
-    bounds = jnp.sum(
-        (segments[None, :] < jnp.arange(EXAMPLES + 1, dtype=jnp.int32)[:, None]).astype(jnp.int32), axis=1
-    )
-
-    shapes = [jax.ShapeDtypeStruct((2, FIRST, 128), BF)] * 4 + [jax.ShapeDtypeStruct((2, ROWS, 128), BF)] * 4
+    shapes = [jax.ShapeDtypeStruct((2, rows, 128), BF) for rows in (4 * ROWS, FIRST, 4 * ROWS, FIRST, ROWS, ROWS)]
     give, *packed, portion = pl.pallas_call(
         pack_kernel,
         out_shape=[jax.ShapeDtypeStruct((4, 4 * ROWS, 128), BF)] + shapes + [jax.ShapeDtypeStruct((128, PAIR), F32)],
         in_specs=[ANY] * 4,
-        out_specs=[ANY] * 9 + [VMEM],
+        out_specs=[ANY] * 7 + [VMEM],
         scratch_shapes=[
             pltpu.VMEM((LOCAL_UP, 128), BF),
             pltpu.VMEM((128, 2048), BF),
@@ -295,42 +308,48 @@
     filled = pl.pallas_call(
         fill_kernel,
         out_shape=shapes,
-        in_specs=[ANY] * 9,
-        out_specs=[ANY] * 8,
+        in_specs=[ANY] * 7,
+        out_specs=[ANY] * 6,
         scratch_shapes=[
             pltpu.VMEM((4, 4 * ROWS, 128), BF),
             pltpu.SemaphoreType.DMA((4,)),
             pltpu.SemaphoreType.DMA,
         ],
-        input_output_aliases={k + 1: k for k in range(8)},
+        input_output_aliases={k + 1: k for k in range(6)},
         compiler_params=pltpu.CompilerParams(vmem_limit_bytes=60 << 20),
         cost_estimate=pl.CostEstimate(flops=0, bytes_accessed=2 << 20, transcendentals=0),
     )(taken, *packed)
-    first, second = list(filled[:4]), list(filled[4:])
-    peers = [lax.ppermute(portion, ("t1", "t0"), [(i, (i + shift) % 4) for i in range(4)]) for shift in (1, 2, 3)]
-    first[2], peers[0] = tie(first[2], peers[0])
-    first[1:] = [send_same(first[k], k) for k in (1, 2, 3)]
-    whole = ((portion + peers[0]) + (peers[1] + peers[2])).astype(BF)
+    first, second = list(filled[:4]), dict(zip(PARTED, filled[4:]))
+    pair = portion + lax.ppermute(portion, ("t1", "t0"), [(0, 1), (1, 0), (2, 3), (3, 2)])
+    whole = pair + lax.ppermute(pair, ("t1", "t0"), [(0, 3), (3, 0), (1, 2), (2, 1)])
+    for k in (2, 1, 3):
+        first[k] = send_same(first[k], k)
+    whole = whole.astype(BF)
     sibling = lax.ppermute(whole, "co", [(0, 1), (1, 0)])
     chip_inner = jnp.concatenate([whole, sibling], axis=0)
-    inner = [chip_inner, send_same(chip_inner, 1), None, send_same(chip_inner, 3)]
-    late, first[1] = tie(chip_inner, first[1])
-    inner[2] = send_same(late, 2)
-    second[1], first[3] = tie(second[1], first[3])
-    second[1] = send_same(second[1], 1)
-    second[3], first[2] = tie(second[3], first[2])
-    second[3] = send_same(second[3], 3)
-    second[2], inner[1] = tie(second[2], inner[1])
-    second[2] = send_same(second[2], 2)
-
-    sums = partial_call(3, bounds, first, inner)
-    arrived = [send_across(sums[k - 1], k) for k in (1, 2, 3)]
-    bounds_late, sums = tie(bounds, sums)
-    (own,) = partial_call(1, bounds_late, second, inner)
-
-    kept = (first_moment_up, second_moment_up, up_row_seeds, down_row_seeds)
-    own, kept = lax.optimization_barrier((own, kept))
-    first_moment_up, second_moment_up, up_row_seeds, down_row_seeds = kept
+    inner = [chip_inner, None, None, None]
+    for k in (2, 1):
+        inner[k] = send_same(chip_inner, k)
+    late, first[2] = tie(chip_inner, first[2])
+    inner[3] = send_same(late, 3)
+    second[1], first[1] = tie(second[1], first[1])
+    second[3], first[3] = tie(second[3], first[3])
+    for k in PARTED:
+        second[k] = send_same(second[k], k)
+
+    labels = segments.reshape(32, 128)
+    sums = partial_call(3, labels, first, inner)
+    arrived = [send_across(sums[k - 1], k) for k in (2, 1, 3)]
+    kept = (labels, segments, first_moment_up, second_moment_up, up_row_seeds, down_row_seeds)
+    kept, sums = tie(kept, sums)
+    labels, segments, first_moment_up, second_moment_up, up_row_seeds, down_row_seeds = kept
+    (own,) = partial_call(1, labels, [first[0], second[1], first[2], second[3]], inner)
+    own = own.astype(F32)
+
+    bounds = jnp.sum(
+        (segments[None, :] < jnp.arange(EXAMPLES + 1, dtype=jnp.int32)[:, None]).astype(jnp.int32), axis=1
+    )
+
     offset = me * UP_ROWS - window_start(me)
     seeds = jnp.concatenate(
         [

time: 84.3 us -> 81.2 us (0.963)
  starting transfers between devices: 31.7 us -> 24.7 us
  blocking collectives: 22.6 us -> 25.2 us
  waiting for transfers between devices: 6.64 us -> 9.17 us
  Pallas kernels: 16.2 us -> 14.9 us
    ppermute x9 -> x8, starting transfers between devices: 19 us -> 11.8 us  [send_same(): return lax.ppermute(value, PLANE, pairs(lambda p: along(p, shift)))]
    all_to_all x2, blocking collectives: 22.6 us -> 25.2 us  [spread_sum(): lax.all_to_all(copies, EVERY, split_axis=0, concat_axis=0, tiled=True, ax...]
    ppermute x9 -> x8, waiting for transfers between devices: 0.68 us -> 2.95 us  [send_same(): return lax.ppermute(value, PLANE, pairs(lambda p: along(p, shift)))]
    ppermute x3, waiting for transfers between devices: 2.38 us -> 0.18 us  [send_across(): return lax.ppermute(value, PLANE, pairs(lambda p: across(p, shift)))]
    ppermute x3 -> x2, waiting for transfers between devices: 0.01 us -> 1.32 us  [the longest x1 1.32 us: on_device(): lax.ppermute(pair, ('t1', 't0'), [(0, 3), (3, 0), (1, 2), (2, 1)])]
    pallas_call x2, Pallas kernels: 8.72 us -> 7.42 us  [partial_call(): pl.pallas_call(functools.partial(partial_kernel, count), out_shape=[jax.S...]
    ppermute x1, waiting for transfers between devices: 0.01 us -> 1.15 us  [on_device(): taken = lax.ppermute(give, 'co', [(0, 1), (1, 0)])]
    convert_element_type x1 -> x2, other arithmetic: 0.04 us -> 1.06 us  [the longest x1 1.04 us: on_device(): own = own.astype(F32)]
  transfers between devices with their start and end apart: 19 -> 17, of which waited for: 5 -> 10; matrix products, arithmetic and copies ran while one was open for 1% -> 2% of each run, Pallas kernels for 13% -> 12%
where the time goes in v7:
time: 81.2 us; the launch traced here: 79.9 us
  blocking collectives  25.2 us (31%)
  starting transfers between devices  24.7 us (30%)
  Pallas kernels  14.9 us (18%)
  waiting for transfers between devices  9.17 us (11%)
  local copies, waits for them, and re-layouts  3.41 us (4%)
  other arithmetic  1.29 us (2%)
  matrix products  0.91 us (1%)
    all_to_all x2, blocking collectives, spread_sum(): lax.all_to_all(copies, EVERY, split_axis=0, concat_axis=0, tiled=True, ax...  25.2 us
    ppermute x8, starting transfers between devices, send_same(): return lax.ppermute(value, PLANE, pairs(lambda p: along(p, shift)))  11.8 us
    pallas_call x2, Pallas kernels, partial_call(): pl.pallas_call(functools.partial(partial_kernel, count), out_shape=[jax.S...  7.42 us
    ppermute x3, starting transfers between devices, send_across(): return lax.ppermute(value, PLANE, pairs(lambda p: across(p, shift)))  6.34 us
    ppermute x1, starting transfers between devices, on_device(): lax.ppermute(pair, ('t1', 't0'), [(0, 3), (3, 0), (1, 2), (2, 1)])  4.12 us
    pallas_call x1, Pallas kernels, on_device(): pl.pallas_call(pack_kernel, out_shape=[jax.ShapeDtypeStruct((4, 4 * ROWS,...  4.04 us
    unnamed x39, local copies, waits for them, and re-layouts  3.18 us
    ppermute x8, waiting for transfers between devices, send_same(): return lax.ppermute(value, PLANE, pairs(lambda p: along(p, shift)))  2.95 us
  transfers between devices with their start and end apart: 17, of which 10 were waited for; matrix products, arithmetic and copies ran while one was open for 2% of the time, Pallas kernels for 12%

profile of v7, /device:TPU:0, one launch (start us, length us, event | category | flops | bytes accessed | tf_op | source)
XLA Modules:
  0.0 79.9 jit_solution(1507389864854576988)
XLA Ops:
  0.0 4.0 %shard_map.118 = (bf16[4,1280,128]{2,1,0:T(8,128)(2,1)}, bf16[2,1280,128]{2,1,0:T(8,128)(2,1)}, bf16[2,960,128]{2,1,0:T(8,128)(2,1)}, bf16[2,1280,128]{2,1,0:T(8...) custom-call(bf16[7392,128]{1,0:T(8,128)(2,1)} %bitcast.19, ...), custom_call_target="tpu_custom_call" | custom-call | flops 309329920 | bytes 8388608 | tf_op jit(solution)/shard_map/pallas_call | solution.py:290
  4.1 2.1 %collective-permute-start.2 = (f32[128,256]{1,0:T(8,128)}, f32[128,256]{1,0:T(8,128)S(1)}, u32[]{:S(2)}, u32[]{:S(2)}) collective-permute-start(f32[128,256]{1,0:T(8,128)} %get-tuple-element.45), channel_id=1, source_target_pairs={{0,8},{8,0},{16,24},{24,16},{1,9},{9,1},{17,25},{25,17},{2,10},{10... | collective-permute-start | bytes 393224 | tf_op jit(solution)/shard_map/ppermute | solution.py:323
  6.2 1.2 %collective-permute-done.taken_ref = bf16[4,1280,128]{2,1,0:T(8,128)(2,1)S(1)} collective-permute-done((bf16[4,1280,128]{2,1,0:T(8,128)(2,1)}, bf16[4,1280,128]{2,1,0:T(8,128)(2,1)S(1)}, u32[]{:S(2)}, u32[]{:S(2)}) %collective-permute-start) | collective-permute-done | bytes 1310752 | tf_op jit(solution)/shard_map/ppermute | solution.py:307
  7.4 1.1 %copy-done.3 = bf16[4,1280,128]{2,1,0:T(8,128)(2,1)} copy-done((bf16[4,1280,128]{2,1,0:T(8,128)(2,1)}, bf16[4,1280,128]{2,1,0:T(8,128)(2,1)S(1)}, u32[]{:S(2)}) %copy-start.3) | copy-done | bytes 1310744
  8.4 2.1 %shard_map.119 = (bf16[2,1280,128]{2,1,0:T(8,128)(2,1)}, bf16[2,960,128]{2,1,0:T(8,128)(2,1)}, bf16[2,1280,128]{2,1,0:T(8,128)(2,1)}, bf16[2,960,128]{2,1,0:T(8,...) custom-call(bf16[4,1280,128]{2,1,0:T(8,128)(2,1)} %copy-done.3, ...), custom_call_target="tpu_custom_call", output_to_operand_aliasing={{0}: (1, {}), {1}: (2, {}), {2}: (3, {}), {3}: (4, {}), {4}... | custom-call | bytes 2097152 | tf_op jit(solution)/shard_map/pallas_call | solution.py:308
  10.6 3.4 %collective-permute-start.5 = (bf16[2,1280,128]{2,1,0:T(8,128)(2,1)}, bf16[2,1280,128]{2,1,0:T(8,128)(2,1)S(1)}, u32[]{:S(2)}, u32[]{:S(2)}) collective-permute-start(bf16[2,1280,128]{2,1,0:T(8,128)(2,1)} %get-tuple-element.46), channel_id=1, source_target_pairs={{0,4},{1,65},{2,6},{3,67},{4,0},{5,69},{6,2},{7,71},{32,36},{33,97... | collective-permute-start | bytes 1966088 | tf_op jit(solution)/shard_map/ppermute | solution.py:57
  14.0 4.1 %collective-permute-start.3 = (f32[128,256]{1,0:T(8,128)S(1)}, f32[128,256]{1,0:T(8,128)S(1)}, u32[]{:S(2)}, u32[]{:S(2)}) collective-permute-start(f32[128,256]{1,0:T(8,128)S(1)} %add.25), channel_id=1, source_target_pairs={{0,24},{24,0},{8,16},{16,8},{1,25},{25,1},{9,17},{17,9},{2,26},{26... | collective-permute-start | bytes 393224 | tf_op jit(solution)/shard_map/ppermute | solution.py:324
  18.1 1.1 %collective-permute-start.6 = (bf16[2,960,128]{2,1,0:T(8,128)(2,1)}, bf16[2,960,128]{2,1,0:T(8,128)(2,1)S(1)}, u32[]{:S(2)}, u32[]{:S(2)}) collective-permute-start(bf16[2,960,128]{2,1,0:T(8,128)(2,1)} %get-tuple-element.49), channel_id=1, source_target_pairs={{0,6},{1,97},{2,0},{3,99},{4,2},{5,101},{6,4},{7,103},{32,38},{33,... | collective-permute-start | bytes 1474568 | tf_op jit(solution)/shard_map/ppermute | solution.py:57
  20.1 1.3 %collective-permute-done.3 = f32[128,256]{1,0:T(8,128)S(1)} collective-permute-done((f32[128,256]{1,0:T(8,128)S(1)}, f32[128,256]{1,0:T(8,128)S(1)}, u32[]{:S(2)}, u32[]{:S(2)}) %collective-permute-start.3) | collective-permute-done | bytes 131104 | tf_op jit(solution)/shard_map/ppermute | solution.py:324
  21.5 1.2 %collective-permute-done.4 = bf16[128,256]{1,0:T(8,128)(2,1)S(1)} collective-permute-done((bf16[128,256]{1,0:T(8,128)(2,1)S(1)}, bf16[128,256]{1,0:T(8,128)(2,1)S(1)}, u32[]{:S(2)}, u32[]{:S(2)}) %collective-permute-start.4) | collective-permute-done | bytes 65568 | tf_op jit(solution)/shard_map/ppermute | solution.py:328
  22.8 1.6 %collective-permute-start.7 = (bf16[256,256]{1,0:T(8,128)(2,1)S(1)}, bf16[256,256]{1,0:T(8,128)(2,1)S(1)}, u32[]{:S(2)}, u32[]{:S(2)}) collective-permute-start(bf16[256,256]{1,0:T(8,128)(2,1)S(1)} %pad_maximum_fusion.rest_4_), channel_id=1, source_target_pairs={{0,2},{1,33},{2,4},{3,35},{4,6},{5,37},{6,0},{7,39},{32,34},{33,65... | collective-permute-start | bytes 393224 | tf_op jit(solution)/shard_map/ppermute | solution.py:57
  24.5 1.7 %collective-permute-start.8 = (bf16[256,256]{1,0:T(8,128)(2,1)S(1)}, bf16[256,256]{1,0:T(8,128)(2,1)S(1)}, u32[]{:S(2)}, u32[]{:S(2)}) collective-permute-start(bf16[256,256]{1,0:T(8,128)(2,1)S(1)} %pad_maximum_fusion.rest_4_), channel_id=1, source_target_pairs={{0,4},{1,65},{2,6},{3,67},{4,0},{5,69},{6,2},{7,71},{32,36},{33,97... | collective-permute-start | bytes 393224 | tf_op jit(solution)/shard_map/ppermute | solution.py:57
  26.2 1.1 %collective-permute-start.9 = (bf16[256,256]{1,0:T(8,128)(2,1)S(1)}, bf16[256,256]{1,0:T(8,128)(2,1)S(1)}, u32[]{:S(2)}, u32[]{:S(2)}) collective-permute-start(bf16[256,256]{1,0:T(8,128)(2,1)S(1)} %pad_maximum_fusion.rest_4_), channel_id=1, source_target_pairs={{0,6},{1,97},{2,0},{3,99},{4,2},{5,101},{6,4},{7,103},{32,38},{33,... | collective-permute-start | bytes 393224 | tf_op jit(solution)/shard_map/ppermute | solution.py:57
  27.2 1.5 %collective-permute-done.6.rest_3_ = bf16[2,960,128]{2,1,0:T(8,128)(2,1)S(1)} collective-permute-done((bf16[2,960,128]{2,1,0:T(8,128)(2,1)}, bf16[2,960,128]{2,1,0:T(8,128)(2,1)S(1)}, u32[]{:S(2)}, u32[]{:S(2)}) %collective-permute-start.6) | collective-permute-done | bytes 491552 | tf_op jit(solution)/shard_map/ppermute | solution.py:57
  29.4 2.0 %collective-permute-start.11 = (bf16[2,320,128]{2,1,0:T(8,128)(2,1)}, bf16[2,320,128]{2,1,0:T(8,128)(2,1)S(1)}, u32[]{:S(2)}, u32[]{:S(2)}) collective-permute-start(bf16[2,320,128]{2,1,0:T(8,128)(2,1)} %get-tuple-element.57), channel_id=1, source_target_pairs={{0,6},{1,97},{2,0},{3,99},{4,2},{5,101},{6,4},{7,103},{32,38},{33,... | collective-permute-start | bytes 491528 | tf_op jit(solution)/shard_map/ppermute | solution.py:57
  32.9 4.3 %shard_map.120 = (bf16[320,512]{1,0:T(8,128)(2,1)}, bf16[320,512]{1,0:T(8,128)(2,1)}, bf16[320,512]{1,0:T(8,128)(2,1)}) custom-call(s32[32,128]{1,0:T(8,128)} %bitcast.20, bf16[2,1280,128]{2,1,0:T(8,128)(2,1)} %get-tuple-element.41.rest_0_, bf16[2,960,128]{2,1,0:T(8,128)(2,1)} %copy-done.18, bf16[2,1280,128]{2,1,0:T(8,128)(2,1)} %copy-done.4, ...), custom_call_target="tpu_custom_call" | custom-call | flops 1006632960 | bytes 6291456 | tf_op jit(solution)/shard_map/pallas_call | solution.py:198
  37.3 3.1 %collective-permute-start.12 = (bf16[320,512]{1,0:T(8,128)(2,1)}, bf16[320,512]{1,0:T(8,128)(2,1)S(1)}, u32[]{:S(2)}, u32[]{:S(2)}) collective-permute-start(bf16[320,512]{1,0:T(8,128)(2,1)} %get-tuple-element.53), channel_id=1, source_target_pairs={{0,64},{1,5},{2,66},{3,7},{4,68},{5,1},{6,70},{7,3},{32,96},{33,37... | collective-permute-start | bytes 983048 | tf_op jit(solution)/shard_map/ppermute | solution.py:61
  41.0 2.6 %collective-permute-start.14 = (bf16[320,512]{1,0:T(8,128)(2,1)}, bf16[320,512]{1,0:T(8,128)(2,1)S(1)}, u32[]{:S(2)}, u32[]{:S(2)}) collective-permute-start(bf16[320,512]{1,0:T(8,128)(2,1)} %get-tuple-element.54), channel_id=1, source_target_pairs={{0,96},{1,7},{2,98},{3,1},{4,100},{5,3},{6,102},{7,5},{32,0},{33,3... | collective-permute-start | bytes 983048 | tf_op jit(solution)/shard_map/ppermute | solution.py:61
  45.3 3.1 %shard_map.121 = bf16[320,512]{1,0:T(8,128)(2,1)} custom-call(s32[32,128]{1,0:T(8,128)} %bitcast.21, bf16[2,1280,128]{2,1,0:T(8,128)(2,1)} %get-tuple-element.41.rest_0_, bf16[2,320,128]{2,1,0:T(8,128)(2,1)} %copy-done.7, bf16[2,1280,128]{2,1,0:T(8,128)(2,1)} %copy-done.4, bf16[2,320,128]{2,1,0:T(8,128)(2,1)} %copy-done.6, bf16[256,256]{1,0:T(8,128)(2,1)} %copy-done.5, ...), custom_call_target="tpu_custom_call" | custom-call | flops 335544320 | bytes 6291456 | tf_op jit(solution)/shard_map/pallas_call | solution.py:198
  49.8 1.3 %shard_map.122 = f32[16,512]{1,0:T(8,128)S(1)} custom-call(f32[320,512]{1,0:T(8,128)S(1)} %convert_element_type.14.own_ref, bf16[320,512]{1,0:T(8,128)(2,1)S(1)} %collective-permute-done.12.a_ref, bf16[320,512]{1,0:T(8,128)(2,1)S(1)} %collective-permute-done.13.b_ref, bf16[320,512]{1,0:T(8,128)(2,1)S(1)} %collective-permute-done.14.c_ref, ...), custom_call_target="tpu_custom_call" | custom-call | bytes 3145728 | tf_op jit(solution)/shard_map/pallas_call | solution.py:361
  51.2 1.2 %collective-permute-done.15 = f32[8,512]{1,0:T(8,128)S(1)} collective-permute-done((f32[8,512]{1,0:T(8,128)S(1)}, f32[8,512]{1,0:T(8,128)S(1)}, u32[]{:S(2)}, u32[]{:S(2)}) %collective-permute-start.15) | collective-permute-done | bytes 16416 | tf_op jit(solution)/shard_map/ppermute | solution.py:377
  52.4 10.8 %all_to_all.10 = f32[8,8,512]{2,1,0:T(8,128)S(1)} all-to-all(f32[8,8,512]{2,1,0:T(8,128)S(1)} %broadcast_in_dim.10), channel_id=1, replica_groups={{0,8,32,40,64,72,96,104},{16,24,48,56,80,88,112,120},{1,9,33,41,65,73,9..., dimensions={0} | all-to-all | bytes 262144 | tf_op jit(solution)/shard_map/all_to_all | solution.py:267
  63.2 14.5 %all_to_all.11 = f32[8,8,512]{2,1,0:T(8,128)S(1)} all-to-all(f32[8,8,512]{2,1,0:T(8,128)S(1)} %broadcast_in_dim.11), channel_id=1, replica_groups={{0,24,2,26,4,28,6,30},{8,16,10,18,12,20,14,22},{1,25,3,27,5,29,7,31},{9..., dimensions={0} | all-to-all | bytes 262144 | tf_op jit(solution)/shard_map/all_to_all | solution.py:267
  77.7 1.2 %collective-permute-done.16 = f32[8,512]{1,0:T(8,128)S(1)} collective-permute-done((f32[8,512]{1,0:T(8,128)S(1)}, f32[8,512]{1,0:T(8,128)S(1)}, u32[]{:S(2)}, u32[]{:S(2)}) %collective-permute-start.16) | collective-permute-done | bytes 16416 | tf_op jit(solution)/shard_map/ppermute | solution.py:380
  (75 shorter events, 8.1 us)
Async XLA Ops:
  0.0 78.9 %copy-start = (bf16[16,128,64]{1,2,0:T(8,128)(2,1)S(1)}, bf16[16,128,64]{1,2,0:T(8,128)(2,1)}, u32[]{:S(2)}) copy-start(bf16[16,128,64]{1,2,0:T(8,128)(2,1)} %param.23) | copy-start | bytes 786436
  4.0 3.3 %collective-permute-start = (bf16[4,1280,128]{2,1,0:T(8,128)(2,1)}, bf16[4,1280,128]{2,1,0:T(8,128)(2,1)S(1)}, u32[]{:S(2)}, u32[]{:S(2)}) collective-permute-start(bf16[4,1280,128]{2,1,0:T(8,128)(2,1)} %get-tuple-element.34), channel_id=1, source_target_pairs={{0,1},{1,0},{2,3},{3,2},{4,5},{5,4},{6,7},{7,6},{8,9},{9,8},{10,11... | collective-permute-start | bytes 3932168 | tf_op jit(solution)/shard_map/ppermute | solution.py:307
  4.1 9.8 %collective-permute-start.2 = (f32[128,256]{1,0:T(8,128)}, f32[128,256]{1,0:T(8,128)S(1)}, u32[]{:S(2)}, u32[]{:S(2)}) collective-permute-start(f32[128,256]{1,0:T(8,128)} %get-tuple-element.45), channel_id=1, source_target_pairs={{0,8},{8,0},{16,24},{24,16},{1,9},{9,1},{17,25},{25,17},{2,10},{10... | collective-permute-start | bytes 393224 | tf_op jit(solution)/shard_map/ppermute | solution.py:323
  10.6 15.6 %collective-permute-start.5 = (bf16[2,1280,128]{2,1,0:T(8,128)(2,1)}, bf16[2,1280,128]{2,1,0:T(8,128)(2,1)S(1)}, u32[]{:S(2)}, u32[]{:S(2)}) collective-permute-start(bf16[2,1280,128]{2,1,0:T(8,128)(2,1)} %get-tuple-element.46), channel_id=1, source_target_pairs={{0,4},{1,65},{2,6},{3,67},{4,0},{5,69},{6,2},{7,71},{32,36},{33,97... | collective-permute-start | bytes 1966088 | tf_op jit(solution)/shard_map/ppermute | solution.py:57
  14.0 7.5 %collective-permute-start.3 = (f32[128,256]{1,0:T(8,128)S(1)}, f32[128,256]{1,0:T(8,128)S(1)}, u32[]{:S(2)}, u32[]{:S(2)}) collective-permute-start(f32[128,256]{1,0:T(8,128)S(1)} %add.25), channel_id=1, source_target_pairs={{0,24},{24,0},{8,16},{16,8},{1,25},{25,1},{9,17},{17,9},{2,26},{26... | collective-permute-start | bytes 393224 | tf_op jit(solution)/shard_map/ppermute | solution.py:324
  18.1 10.6 %collective-permute-start.6 = (bf16[2,960,128]{2,1,0:T(8,128)(2,1)}, bf16[2,960,128]{2,1,0:T(8,128)(2,1)S(1)}, u32[]{:S(2)}, u32[]{:S(2)}) collective-permute-start(bf16[2,960,128]{2,1,0:T(8,128)(2,1)} %get-tuple-element.49), channel_id=1, source_target_pairs={{0,6},{1,97},{2,0},{3,99},{4,2},{5,101},{6,4},{7,103},{32,38},{33,... | collective-permute-start | bytes 1474568 | tf_op jit(solution)/shard_map/ppermute | solution.py:57
  19.1 10.3 %collective-permute-start.1 = (bf16[2,960,128]{2,1,0:T(8,128)(2,1)}, bf16[2,960,128]{2,1,0:T(8,128)(2,1)S(1)}, u32[]{:S(2)}, u32[]{:S(2)}) collective-permute-start(bf16[2,960,128]{2,1,0:T(8,128)(2,1)} %get-tuple-element.43), channel_id=1, source_target_pairs={{0,2},{1,33},{2,4},{3,35},{4,6},{5,37},{6,0},{7,39},{32,34},{33,65... | collective-permute-start | bytes 1474568 | tf_op jit(solution)/shard_map/ppermute | solution.py:57
  21.4 1.3 %collective-permute-start.4 = (bf16[128,256]{1,0:T(8,128)(2,1)S(1)}, bf16[128,256]{1,0:T(8,128)(2,1)S(1)}, u32[]{:S(2)}, u32[]{:S(2)}) collective-permute-start(bf16[128,256]{1,0:T(8,128)(2,1)S(1)} %add_convert_fusion), channel_id=1, source_target_pairs={{0,1},{1,0},{2,3},{3,2},{4,5},{5,4},{6,7},{7,6},{8,9},{9,8},{10,11... | collective-permute-start | bytes 196616 | tf_op jit(solution)/shard_map/ppermute | solution.py:328
  22.8 9.4 %copy-start.5 = (bf16[256,256]{1,0:T(8,128)(2,1)}, bf16[256,256]{1,0:T(8,128)(2,1)S(1)}, u32[]{:S(2)}) copy-start(bf16[256,256]{1,0:T(8,128)(2,1)S(1)} %pad_maximum_fusion.rest_4_) | copy-start | bytes 393220
  22.8 9.4 %collective-permute-start.7 = (bf16[256,256]{1,0:T(8,128)(2,1)S(1)}, bf16[256,256]{1,0:T(8,128)(2,1)S(1)}, u32[]{:S(2)}, u32[]{:S(2)}) collective-permute-start(bf16[256,256]{1,0:T(8,128)(2,1)S(1)} %pad_maximum_fusion.rest_4_), channel_id=1, source_target_pairs={{0,2},{1,33},{2,4},{3,35},{4,6},{5,37},{6,0},{7,39},{32,34},{33,65... | collective-permute-start | bytes 393224 | tf_op jit(solution)/shard_map/ppermute | solution.py:57
  24.5 7.8 %collective-permute-start.8 = (bf16[256,256]{1,0:T(8,128)(2,1)S(1)}, bf16[256,256]{1,0:T(8,128)(2,1)S(1)}, u32[]{:S(2)}, u32[]{:S(2)}) collective-permute-start(bf16[256,256]{1,0:T(8,128)(2,1)S(1)} %pad_maximum_fusion.rest_4_), channel_id=1, source_target_pairs={{0,4},{1,65},{2,6},{3,67},{4,0},{5,69},{6,2},{7,71},{32,36},{33,97... | collective-permute-start | bytes 393224 | tf_op jit(solution)/shard_map/ppermute | solution.py:57
  26.2 6.0 %collective-permute-start.9 = (bf16[256,256]{1,0:T(8,128)(2,1)S(1)}, bf16[256,256]{1,0:T(8,128)(2,1)S(1)}, u32[]{:S(2)}, u32[]{:S(2)}) collective-permute-start(bf16[256,256]{1,0:T(8,128)(2,1)S(1)} %pad_maximum_fusion.rest_4_), channel_id=1, source_target_pairs={{0,6},{1,97},{2,0},{3,99},{4,2},{5,101},{6,4},{7,103},{32,38},{33,... | collective-permute-start | bytes 393224 | tf_op jit(solution)/shard_map/ppermute | solution.py:57
  27.2 16.4 %copy-start.15 = (s32[1,231]{1,0:T(1,128)S(1)}, s32[1,231]{1,0:T(1,128)}, u32[]{:S(2)}) copy-start(s32[1,231]{1,0:T(1,128)} %param.21) | copy-start | bytes 2776
  27.2 16.6 %copy-start.16 = (s32[1,64]{1,0:T(1,128)S(1)}, s32[1,64]{1,0:T(1,128)}, u32[]{:S(2)}) copy-start(s32[1,64]{1,0:T(1,128)} %param.20) | copy-start | bytes 772
  29.4 14.5 %collective-permute-start.11 = (bf16[2,320,128]{2,1,0:T(8,128)(2,1)}, bf16[2,320,128]{2,1,0:T(8,128)(2,1)S(1)}, u32[]{:S(2)}, u32[]{:S(2)}) collective-permute-start(bf16[2,320,128]{2,1,0:T(8,128)(2,1)} %get-tuple-element.57), channel_id=1, source_target_pairs={{0,6},{1,97},{2,0},{3,99},{4,2},{5,101},{6,4},{7,103},{32,38},{33,... | collective-permute-start | bytes 491528 | tf_op jit(solution)/shard_map/ppermute | solution.py:57
  31.4 12.5 %collective-permute-start.10 = (bf16[2,320,128]{2,1,0:T(8,128)(2,1)}, bf16[2,320,128]{2,1,0:T(8,128)(2,1)S(1)}, u32[]{:S(2)}, u32[]{:S(2)}) collective-permute-start(bf16[2,320,128]{2,1,0:T(8,128)(2,1)} %get-tuple-element.56), channel_id=1, source_target_pairs={{0,2},{1,33},{2,4},{3,35},{4,6},{5,37},{6,0},{7,39},{32,34},{33,65... | collective-permute-start | bytes 491528 | tf_op jit(solution)/shard_map/ppermute | solution.py:57
  37.3 12.1 %copy-start.14 = (s32[4096]{0:T(1024)S(1)}, s32[4096]{0:T(1024)}, u32[]{:S(2)}) copy-start(s32[4096]{0:T(1024)} %param.22) | copy-start | bytes 49156
  37.3 12.3 %copy-start.12 = (f32[1,231,128]{2,0,1:T(1,128)S(1)}, f32[1,231,128]{2,0,1:T(1,128)}, u32[]{:S(2)}) copy-start(f32[1,231,128]{2,0,1:T(1,128)} %param.19) | copy-start | bytes 354820
  37.3 12.3 %copy-start.13 = (f32[1,231,128]{2,0,1:T(1,128)S(1)}, f32[1,231,128]{2,0,1:T(1,128)}, u32[]{:S(2)}) copy-start(f32[1,231,128]{2,0,1:T(1,128)} %param.18) | copy-start | bytes 354820
  37.3 12.3 %collective-permute-start.12 = (bf16[320,512]{1,0:T(8,128)(2,1)}, bf16[320,512]{1,0:T(8,128)(2,1)S(1)}, u32[]{:S(2)}, u32[]{:S(2)}) collective-permute-start(bf16[320,512]{1,0:T(8,128)(2,1)} %get-tuple-element.53), channel_id=1, source_target_pairs={{0,64},{1,5},{2,66},{3,7},{4,68},{5,1},{6,70},{7,3},{32,96},{33,37... | collective-permute-start | bytes 983048 | tf_op jit(solution)/shard_map/ppermute | solution.py:61
  40.4 9.3 %collective-permute-start.13 = (bf16[320,512]{1,0:T(8,128)(2,1)}, bf16[320,512]{1,0:T(8,128)(2,1)S(1)}, u32[]{:S(2)}, u32[]{:S(2)}) collective-permute-start(bf16[320,512]{1,0:T(8,128)(2,1)} %get-tuple-element.52), channel_id=1, source_target_pairs={{0,32},{1,3},{2,34},{3,5},{4,36},{5,7},{6,38},{7,1},{32,64},{33,35... | collective-permute-start | bytes 983048 | tf_op jit(solution)/shard_map/ppermute | solution.py:61
  41.0 8.8 %collective-permute-start.14 = (bf16[320,512]{1,0:T(8,128)(2,1)}, bf16[320,512]{1,0:T(8,128)(2,1)S(1)}, u32[]{:S(2)}, u32[]{:S(2)}) collective-permute-start(bf16[320,512]{1,0:T(8,128)(2,1)} %get-tuple-element.54), channel_id=1, source_target_pairs={{0,96},{1,7},{2,98},{3,1},{4,100},{5,3},{6,102},{7,5},{32,0},{33,3... | collective-permute-start | bytes 983048 | tf_op jit(solution)/shard_map/ppermute | solution.py:61
  51.1 1.2 %collective-permute-start.15 = (f32[8,512]{1,0:T(8,128)S(1)}, f32[8,512]{1,0:T(8,128)S(1)}, u32[]{:S(2)}, u32[]{:S(2)}) collective-permute-start(f32[8,512]{1,0:T(8,128)S(1)} %constant_dynamic-slice_fusion), channel_id=1, source_target_pairs={{0,1},{1,0},{2,3},{3,2},{4,5},{5,4},{6,7},{7,6},{8,9},{9,8},{10,11... | collective-permute-start | bytes 49160 | tf_op jit(solution)/shard_map/ppermute | solution.py:377
  77.6 1.3 %collective-permute-start.16 = (f32[8,512]{1,0:T(8,128)S(1)}, f32[8,512]{1,0:T(8,128)S(1)}, u32[]{:S(2)}, u32[]{:S(2)}) collective-permute-start(f32[8,512]{1,0:T(8,128)S(1)} %reduce_sum.29), channel_id=1, source_target_pairs={{0,1},{1,0},{2,3},{3,2},{4,5},{5,4},{6,7},{7,6},{8,9},{9,8},{10,11... | collective-permute-start | bytes 49160 | tf_op jit(solution)/shard_map/ppermute | solution.py:380
  (12 other events, 34.3 us)

commit v8 on v7

--- a/solution.py
+++ b/solution.py
@@ -18,6 +18,7 @@
 WINDOW = 256
 ROWS = WINDOW + DOWN_ROWS
 FIRST = 3 * ROWS
+EARLY = {2: (0, 0), 1: (0, 1), 3: (1, 0), 0: (1, 1)}
 PARTED = (1, 3)
 LOCAL_UP = 7392
 PAIR = 2 * RANK
@@ -69,7 +70,8 @@
     return lax.optimization_barrier((value, arrived))
 
 
-def pack_kernel(grad_hbm, tokens_hbm, down_hbm, up_hbm, give_ref, *rest):
+def pack_kernel(grad_hbm, tokens_hbm, down_hbm, up_hbm, *rest):
+    gives, rest = rest[:2], rest[2:]
     buffers, portion_ref = rest[:6], rest[6]
     grad, tokens, down, up, turned, loads, sent = rest[7:]
     arrivals = [
@@ -89,7 +91,7 @@
             owner = to_x * 8 + to_y * 2 + target
             start = pl.multiple_of(window_start(owner), 16)
             column = pl.multiple_of(owner * DOWN_ROWS, DOWN_ROWS)
-            out = give_ref.at[k] if slot < 4 else buffers[k].at[0]
+            out = gives[EARLY[k][0]].at[EARLY[k][1]] if slot < 4 else buffers[k].at[0]
             window_at, down_at = ((i - 1) * WINDOW, 3 * WINDOW + (i - 1) * DOWN_ROWS) if i else (FIRST, FIRST + WINDOW)
             if slot >= 4 and i == 0 and k in PARTED:
                 out, window_at, down_at = buffers[4 + PARTED.index(k)].at[0], 0, WINDOW
@@ -120,25 +122,38 @@
         copy.wait()
 
 
-def fill_kernel(taken_ref, *rest):
-    buffers, (held, load, sent) = rest[6:12], rest[12:]
-    order = (2, 1, 3, 0)
-    loads = {k: pltpu.make_async_copy(taken_ref.at[k], held.at[k], load.at[k]) for k in order}
-    for k in order:
-        loads[k].start()
-    copies = []
-    for k in order:
-        loads[k].wait()
-        if k in PARTED:
-            copies.append(pltpu.make_async_copy(held.at[k, pl.ds(0, FIRST)], buffers[k].at[1], sent))
+def fill_kernel(shifts, taken_ref, *rest):
+    count = sum(2 if k in PARTED else 1 for k in shifts)
+    buffers, (held, load, sent) = rest[count:2 * count], rest[2 * count:]
+    loads = [pltpu.make_async_copy(taken_ref.at[n], held.at[n], load.at[n]) for n in range(len(shifts))]
+    for copy in loads:
+        copy.start()
+    copies, at = [], 0
+    for n, k in enumerate(shifts):
+        loads[n].wait()
+        for begin, size in ((0, FIRST), (FIRST, ROWS)) if k in PARTED else ((0, 4 * ROWS),):
+            copies.append(pltpu.make_async_copy(held.at[n, pl.ds(begin, size)], buffers[at].at[1], sent))
             copies[-1].start()
-            second = buffers[4 + PARTED.index(k)]
-            copies.append(pltpu.make_async_copy(held.at[k, pl.ds(FIRST, ROWS)], second.at[1], sent))
-        else:
-            copies.append(pltpu.make_async_copy(held.at[k], buffers[k].at[1], sent))
-        copies[-1].start()
+            at += 1
     for copy in copies:
         copy.wait()
+
+
+def fill_call(shifts, taken, buffers):
+    return pl.pallas_call(
+        functools.partial(fill_kernel, shifts),
+        out_shape=[jax.ShapeDtypeStruct(buffer.shape, BF) for buffer in buffers],
+        in_specs=[ANY] * (1 + len(buffers)),
+        out_specs=[ANY] * len(buffers),
+        scratch_shapes=[
+            pltpu.VMEM((len(shifts), 4 * ROWS, 128), BF),
+            pltpu.SemaphoreType.DMA((len(shifts),)),
+            pltpu.SemaphoreType.DMA,
+        ],
+        input_output_aliases={k + 1: k for k in range(len(buffers))},
+        compiler_params=pltpu.CompilerParams(vmem_limit_bytes=60 << 20),
+        cost_estimate=pl.CostEstimate(flops=0, bytes_accessed=1 << 20, transcendentals=0),
+    )(taken, *buffers)
 
 
 def partial_kernel(count, segments_hbm, *rest):
@@ -287,11 +302,11 @@
     x, y, c = position()
     me = x * 8 + y * 2 + c
     shapes = [jax.ShapeDtypeStruct((2, rows, 128), BF) for rows in (4 * ROWS, FIRST, 4 * ROWS, FIRST, ROWS, ROWS)]
-    give, *packed, portion = pl.pallas_call(
+    give, give_late, *packed, portion = pl.pallas_call(
         pack_kernel,
-        out_shape=[jax.ShapeDtypeStruct((4, 4 * ROWS, 128), BF)] + shapes + [jax.ShapeDtypeStruct((128, PAIR), F32)],
+        out_shape=[jax.ShapeDtypeStruct((2, 4 * ROWS, 128), BF)] * 2 + shapes + [jax.ShapeDtypeStruct((128, PAIR), F32)],
         in_specs=[ANY] * 4,
-        out_specs=[ANY] * 7 + [VMEM],
+        out_specs=[ANY] * 8 + [VMEM],
         scratch_shapes=[
             pltpu.VMEM((LOCAL_UP, 128), BF),
             pltpu.VMEM((128, 2048), BF),
@@ -305,21 +320,12 @@
         cost_estimate=pl.CostEstimate(flops=2 * 128 * 9440 * 128, bytes_accessed=8 << 20, transcendentals=0),
     )(output_gradient.T, tokens, adapter_down_factor, adapter_up_factor)
     taken = lax.ppermute(give, "co", [(0, 1), (1, 0)])
-    filled = pl.pallas_call(
-        fill_kernel,
-        out_shape=shapes,
-        in_specs=[ANY] * 7,
-        out_specs=[ANY] * 6,
-        scratch_shapes=[
-            pltpu.VMEM((4, 4 * ROWS, 128), BF),
-            pltpu.SemaphoreType.DMA((4,)),
-            pltpu.SemaphoreType.DMA,
-        ],
-        input_output_aliases={k + 1: k for k in range(6)},
-        compiler_params=pltpu.CompilerParams(vmem_limit_bytes=60 << 20),
-        cost_estimate=pl.CostEstimate(flops=0, bytes_accessed=2 << 20, transcendentals=0),
-    )(taken, *packed)
-    first, second = list(filled[:4]), dict(zip(PARTED, filled[4:]))
+    give_late, taken = tie(give_late, taken)
+    taken_late = lax.ppermute(give_late, "co", [(0, 1), (1, 0)])
+    first, second = {}, {}
+    first[2], first[1], second[1] = fill_call((2, 1), taken, (packed[2], packed[1], packed[4]))
+    taken_late, first[2] = tie(taken_late, first[2])
+    first[3], second[3], first[0] = fill_call((3, 0), taken_late, (packed[3], packed[5], packed[0]))
     pair = portion + lax.ppermute(portion, ("t1", "t0"), [(0, 1), (1, 0), (2, 3), (3, 2)])
     whole = pair + lax.ppermute(pair, ("t1", "t0"), [(0, 3), (3, 0), (1, 2), (2, 1)])
     for k in (2, 1, 3):
@@ -338,7 +344,7 @@
         second[k] = send_same(second[k], k)
 
     labels = segments.reshape(32, 128)
-    sums = partial_call(3, labels, first, inner)
+    sums = partial_call(3, labels, [first[k] for k in range(4)], inner)
     arrived = [send_across(sums[k - 1], k) for k in (2, 1, 3)]
     kept = (labels, segments, first_moment_up, second_moment_up, up_row_seeds, down_row_seeds)
     kept, sums = tie(kept, sums)
@@ -371,14 +377,9 @@
         first_moment_up[0], first_moment_down[0], second_moment_up[0], second_moment_down[0],
     )
 
-    half = BANK // 2
-    kept = lax.dynamic_slice_in_dim(blocks, c * half, half, 0)
-    given = lax.dynamic_slice_in_dim(blocks, (1 - c) * half, half, 0)
-    total = kept + lax.ppermute(given, "co", [(0, 1), (1, 0)])
-    total = spread_sum(total, True)
-    total = spread_sum(total, False)
-    theirs = lax.ppermute(total, "co", [(0, 1), (1, 0)])
-    summed = jnp.concatenate([jnp.where(c == 0, total, theirs), jnp.where(c == 0, theirs, total)], axis=0)
+    summed = blocks + lax.ppermute(blocks, "co", [(0, 1), (1, 0)])
+    summed = spread_sum(summed, True)
+    summed = spread_sum(summed, False)
     inverse = 1.0 / math.sqrt((MODEL_WIDTH + HIDDEN_WIDTH) * RANK)
     sketch = jnp.einsum(
         "jer,jrk->ek", summed.reshape(BANK, EXAMPLES, RANK), bank.astype(F32), precision=lax.Precision.HIGHEST

time: 81.2 us -> 78.8 us (0.970); the launches traced: 79.9 us -> 78.5 us
  waiting for transfers between devices: 9.17 us -> 5.02 us
  starting transfers between devices: 24.7 us -> 28.4 us
  Pallas kernels: 14.9 us -> 16.5 us
  blocking collectives: 25.2 us -> 23.6 us
  local copies, waits for them, and re-layouts: 3.41 us -> 2.41 us
    ppermute x8, starting transfers between devices: 11.8 us -> 16.7 us  [send_same(): return lax.ppermute(value, PLANE, pairs(lambda p: along(p, shift)))]
    ppermute x8, waiting for transfers between devices: 2.95 us -> 0.14 us  [send_same(): return lax.ppermute(value, PLANE, pairs(lambda p: along(p, shift)))]
    all_to_all x2, blocking collectives: 25.2 us -> 23.6 us  [spread_sum(): lax.all_to_all(copies, EVERY, split_axis=0, concat_axis=0, tiled=True, ax...]
    pallas_call x2 -> x3, Pallas kernels: 6.16 us -> 7.68 us  [the longest x1 4.04 us: on_device(): pl.pallas_call(pack_kernel, out_shape=[jax.ShapeDtypeStruct((2, 4 * ROWS,...]
    ppermute x1, waiting for transfers between devices: 1.32 us -> 0.01 us  [on_device(): lax.ppermute(pair, ('t1', 't0'), [(0, 3), (3, 0), (1, 2), (2, 1)])]
    ppermute x1, waiting for transfers between devices: 1.15 us -> 2.3 us  [on_device(): taken = lax.ppermute(give, 'co', [(0, 1), (1, 0)])]
    ppermute x2, waiting for transfers between devices: 2.33 us -> 1.2 us  [the longest x1 1.19 us: on_device(): summed = blocks + lax.ppermute(blocks, 'co', [(0, 1), (1, 0)])]
    ppermute x1, starting transfers between devices: 4.12 us -> 3.03 us  [on_device(): lax.ppermute(pair, ('t1', 't0'), [(0, 3), (3, 0), (1, 2), (2, 1)])]
  transfers between devices with their start and end apart: 17 -> 17, of which waited for: 10 -> 6; matrix products, arithmetic and copies ran while one was open for 2% -> 2% of each run, Pallas kernels for 12% -> 14%
where the time goes in v8:
time: 78.8 us; the launch traced here: 78.5 us
  starting transfers between devices  28.4 us (36%)
  blocking collectives  23.6 us (30%)
  Pallas kernels  16.5 us (21%)
  waiting for transfers between devices  5.02 us (6%)
  local copies, waits for them, and re-layouts  2.41 us (3%)
  other arithmetic  1.29 us (2%)
  matrix products  0.91 us (1%)
    all_to_all x2, blocking collectives, spread_sum(): lax.all_to_all(copies, EVERY, split_axis=0, concat_axis=0, tiled=True, ax...  23.6 us
    ppermute x8, starting transfers between devices, send_same(): return lax.ppermute(value, PLANE, pairs(lambda p: along(p, shift)))  16.7 us
    pallas_call x2, Pallas kernels, partial_call(): pl.pallas_call(functools.partial(partial_kernel, count), out_shape=[jax.S...  7.47 us
    ppermute x3, starting transfers between devices, send_across(): return lax.ppermute(value, PLANE, pairs(lambda p: across(p, shift)))  6.34 us
    pallas_call x1, Pallas kernels, on_device(): pl.pallas_call(pack_kernel, out_shape=[jax.ShapeDtypeStruct((2, 4 * ROWS,...  4.04 us
    pallas_call x2, Pallas kernels, fill_call(): pl.pallas_call(functools.partial(fill_kernel, shifts), out_shape=[jax.Sha...  3.64 us
    ppermute x1, starting transfers between devices, on_device(): lax.ppermute(pair, ('t1', 't0'), [(0, 3), (3, 0), (1, 2), (2, 1)])  3.03 us
    ppermute x1, waiting for transfers between devices, on_device(): taken = lax.ppermute(give, 'co', [(0, 1), (1, 0)])  2.3 us
  transfers between devices with their start and end apart: 17, of which 6 were waited for; matrix products, arithmetic and copies ran while one was open for 2% of the time, Pallas kernels for 14%

profile of v8, /device:TPU:0, one launch (start us, length us, event | category | flops | bytes accessed | tf_op | source)
XLA Modules:
  0.0 78.5 jit_solution(4853436146099784175)
XLA Ops:
  0.0 4.0 %shard_map.118 = (bf16[2,1280,128]{2,1,0:T(8,128)(2,1)}, bf16[2,1280,128]{2,1,0:T(8,128)(2,1)}, bf16[2,1280,128]{2,1,0:T(8,128)(2,1)}, bf16[2,960,128]{2,1,0:T(8...) custom-call(bf16[7392,128]{1,0:T(8,128)(2,1)} %bitcast.19, ...), custom_call_target="tpu_custom_call" | custom-call | flops 309329920 | bytes 8388608 | tf_op jit(solution)/shard_map/pallas_call | solution.py:305
  4.1 2.3 %collective-permute-done.taken_ref = bf16[2,1280,128]{2,1,0:T(8,128)(2,1)S(1)} collective-permute-done((bf16[2,1280,128]{2,1,0:T(8,128)(2,1)}, bf16[2,1280,128]{2,1,0:T(8,128)(2,1)S(1)}, u32[]{:S(2)}, u32[]{:S(2)}) %collective-permute-start) | collective-permute-done | bytes 655392 | tf_op jit(solution)/shard_map/ppermute | solution.py:322
  6.6 2.0 %collective-permute-start.3 = (f32[128,256]{1,0:T(8,128)}, f32[128,256]{1,0:T(8,128)S(1)}, u32[]{:S(2)}, u32[]{:S(2)}) collective-permute-start(f32[128,256]{1,0:T(8,128)} %get-tuple-element.55), channel_id=1, source_target_pairs={{0,8},{8,0},{16,24},{24,16},{1,9},{9,1},{17,25},{25,17},{2,10},{10... | collective-permute-start | bytes 393224 | tf_op jit(solution)/shard_map/ppermute | solution.py:329
  8.6 1.8 %shard_map.119 = (bf16[2,1280,128]{2,1,0:T(8,128)(2,1)}, bf16[2,960,128]{2,1,0:T(8,128)(2,1)}, bf16[2,320,128]{2,1,0:T(8,128)(2,1)}) custom-call(bf16[2,1280,128]{2,1,0:T(8,128)(2,1)} %copy-done.5, bf16[2,1280,128]{2,1,0:T(8,128)(2,1)} %get-tuple-element.43.rest_0_, ...), custom_call_target="tpu_custom_call", output_to_operand_aliasing={{0}: (1, {}), {1}: (2, {}), {2}: (3, {})} | custom-call | bytes 1048576 | tf_op jit(solution)/shard_map/pallas_call | solution.py:143
  10.5 3.3 %collective-permute-start.6 = (bf16[2,1280,128]{2,1,0:T(8,128)(2,1)}, bf16[2,1280,128]{2,1,0:T(8,128)(2,1)S(1)}, u32[]{:S(2)}, u32[]{:S(2)}) collective-permute-start(bf16[2,1280,128]{2,1,0:T(8,128)(2,1)} %get-tuple-element.56), channel_id=1, source_target_pairs={{0,4},{1,65},{2,6},{3,67},{4,0},{5,69},{6,2},{7,71},{32,36},{33,97... | collective-permute-start | bytes 1966088 | tf_op jit(solution)/shard_map/ppermute | solution.py:58
  13.8 3.0 %collective-permute-start.4 = (f32[128,256]{1,0:T(8,128)S(1)}, f32[128,256]{1,0:T(8,128)S(1)}, u32[]{:S(2)}, u32[]{:S(2)}) collective-permute-start(f32[128,256]{1,0:T(8,128)S(1)} %add.19), channel_id=1, source_target_pairs={{0,24},{24,0},{8,16},{16,8},{1,25},{25,1},{9,17},{17,9},{2,26},{26... | collective-permute-start | bytes 393224 | tf_op jit(solution)/shard_map/ppermute | solution.py:330
  16.8 1.6 %collective-permute-start.2 = (bf16[2,960,128]{2,1,0:T(8,128)(2,1)}, bf16[2,960,128]{2,1,0:T(8,128)(2,1)S(1)}, u32[]{:S(2)}, u32[]{:S(2)}) collective-permute-start(bf16[2,960,128]{2,1,0:T(8,128)(2,1)} %get-tuple-element.53), channel_id=1, source_target_pairs={{0,2},{1,33},{2,4},{3,35},{4,6},{5,37},{6,0},{7,39},{32,34},{33,65... | collective-permute-start | bytes 1474568 | tf_op jit(solution)/shard_map/ppermute | solution.py:58
  18.4 1.8 %shard_map.120 = (bf16[2,960,128]{2,1,0:T(8,128)(2,1)}, bf16[2,320,128]{2,1,0:T(8,128)(2,1)}, bf16[2,1280,128]{2,1,0:T(8,128)(2,1)}) custom-call(bf16[2,1280,128]{2,1,0:T(8,128)(2,1)} %copy-done.4, bf16[2,960,128]{2,1,0:T(8,128)(2,1)} %get-tuple-element.48.rest_0_, ...), custom_call_target="tpu_custom_call", output_to_operand_aliasing={{0}: (1, {}), {1}: (2, {}), {2}: (3, {})} | custom-call | bytes 1048576 | tf_op jit(solution)/shard_map/pallas_call | solution.py:143
  20.2 1.7 %collective-permute-start.7 = (bf16[2,960,128]{2,1,0:T(8,128)(2,1)}, bf16[2,960,128]{2,1,0:T(8,128)(2,1)S(1)}, u32[]{:S(2)}, u32[]{:S(2)}) collective-permute-start(bf16[2,960,128]{2,1,0:T(8,128)(2,1)} %get-tuple-element.59), channel_id=1, source_target_pairs={{0,6},{1,97},{2,0},{3,99},{4,2},{5,101},{6,4},{7,103},{32,38},{33,... | collective-permute-start | bytes 1474568 | tf_op jit(solution)/shard_map/ppermute | solution.py:58
  22.0 1.2 %collective-permute-done.5 = bf16[128,256]{1,0:T(8,128)(2,1)S(1)} collective-permute-done((bf16[128,256]{1,0:T(8,128)(2,1)S(1)}, bf16[128,256]{1,0:T(8,128)(2,1)S(1)}, u32[]{:S(2)}, u32[]{:S(2)}) %collective-permute-start.5) | collective-permute-done | bytes 65568 | tf_op jit(solution)/shard_map/ppermute | solution.py:334
  23.7 2.9 %collective-permute-start.9 = (bf16[256,256]{1,0:T(8,128)(2,1)S(1)}, bf16[256,256]{1,0:T(8,128)(2,1)S(1)}, u32[]{:S(2)}, u32[]{:S(2)}) collective-permute-start(bf16[256,256]{1,0:T(8,128)(2,1)S(1)} %pad_maximum_fusion.rest_4_), channel_id=1, source_target_pairs={{0,4},{1,65},{2,6},{3,67},{4,0},{5,69},{6,2},{7,71},{32,36},{33,97... | collective-permute-start | bytes 393224 | tf_op jit(solution)/shard_map/ppermute | solution.py:58
  26.6 1.3 %collective-permute-start.10 = (bf16[256,256]{1,0:T(8,128)(2,1)S(1)}, bf16[256,256]{1,0:T(8,128)(2,1)S(1)}, u32[]{:S(2)}, u32[]{:S(2)}) collective-permute-start(bf16[256,256]{1,0:T(8,128)(2,1)S(1)} %pad_maximum_fusion.rest_4_), channel_id=1, source_target_pairs={{0,6},{1,97},{2,0},{3,99},{4,2},{5,101},{6,4},{7,103},{32,38},{33,... | collective-permute-start | bytes 393224 | tf_op jit(solution)/shard_map/ppermute | solution.py:58
  28.1 1.7 %collective-permute-start.11 = (bf16[2,320,128]{2,1,0:T(8,128)(2,1)S(1)}, bf16[2,320,128]{2,1,0:T(8,128)(2,1)S(1)}, u32[]{:S(2)}, u32[]{:S(2)}) collective-permute-start(bf16[2,320,128]{2,1,0:T(8,128)(2,1)S(1)} %copy-done.9), channel_id=1, source_target_pairs={{0,2},{1,33},{2,4},{3,35},{4,6},{5,37},{6,0},{7,39},{32,34},{33,65... | collective-permute-start | bytes 491528 | tf_op jit(solution)/shard_map/ppermute | solution.py:58
  29.9 3.7 %collective-permute-start.12 = (bf16[2,320,128]{2,1,0:T(8,128)(2,1)}, bf16[2,320,128]{2,1,0:T(8,128)(2,1)S(1)}, u32[]{:S(2)}, u32[]{:S(2)}) collective-permute-start(bf16[2,320,128]{2,1,0:T(8,128)(2,1)} %get-tuple-element.67), channel_id=1, source_target_pairs={{0,6},{1,97},{2,0},{3,99},{4,2},{5,101},{6,4},{7,103},{32,38},{33,... | collective-permute-start | bytes 491528 | tf_op jit(solution)/shard_map/ppermute | solution.py:58
  34.3 4.4 %shard_map.121 = (bf16[320,512]{1,0:T(8,128)(2,1)}, bf16[320,512]{1,0:T(8,128)(2,1)}, bf16[320,512]{1,0:T(8,128)(2,1)}) custom-call(s32[32,128]{1,0:T(8,128)} %bitcast.20, bf16[2,1280,128]{2,1,0:T(8,128)(2,1)} %get-tuple-element.51.rest_0_, bf16[2,960,128]{2,1,0:T(8,128)(2,1)} %copy-done.19, bf16[2,1280,128]{2,1,0:T(8,128)(2,1)} %copy-done.3, ...), custom_call_target="tpu_custom_call" | custom-call | flops 1006632960 | bytes 6291456 | tf_op jit(solution)/shard_map/pallas_call | solution.py:213
  38.8 3.1 %collective-permute-start.13 = (bf16[320,512]{1,0:T(8,128)(2,1)}, bf16[320,512]{1,0:T(8,128)(2,1)S(1)}, u32[]{:S(2)}, u32[]{:S(2)}) collective-permute-start(bf16[320,512]{1,0:T(8,128)(2,1)} %get-tuple-element.63), channel_id=1, source_target_pairs={{0,64},{1,5},{2,66},{3,7},{4,68},{5,1},{6,70},{7,3},{32,96},{33,37... | collective-permute-start | bytes 983048 | tf_op jit(solution)/shard_map/ppermute | solution.py:62
  42.5 2.6 %collective-permute-start.15 = (bf16[320,512]{1,0:T(8,128)(2,1)}, bf16[320,512]{1,0:T(8,128)(2,1)S(1)}, u32[]{:S(2)}, u32[]{:S(2)}) collective-permute-start(bf16[320,512]{1,0:T(8,128)(2,1)} %get-tuple-element.64), channel_id=1, source_target_pairs={{0,96},{1,7},{2,98},{3,1},{4,100},{5,3},{6,102},{7,5},{32,0},{33,3... | collective-permute-start | bytes 983048 | tf_op jit(solution)/shard_map/ppermute | solution.py:62
  46.5 3.1 %shard_map.122 = bf16[320,512]{1,0:T(8,128)(2,1)} custom-call(s32[32,128]{1,0:T(8,128)} %bitcast.21, bf16[2,1280,128]{2,1,0:T(8,128)(2,1)} %get-tuple-element.51.rest_0_, bf16[2,320,128]{2,1,0:T(8,128)(2,1)} %copy-done.7, bf16[2,1280,128]{2,1,0:T(8,128)(2,1)} %copy-done.3, bf16[2,320,128]{2,1,0:T(8,128)(2,1)} %copy-done.8, bf16[256,256]{1,0:T(8,128)(2,1)} %copy-done.6, ...), custom_call_target="tpu_custom_call" | custom-call | flops 335544320 | bytes 6291456 | tf_op jit(solution)/shard_map/pallas_call | solution.py:213
  49.6 1.0 %convert_element_type.14.own_ref = f32[320,512]{1,0:T(8,128)S(1)} convert(bf16[320,512]{1,0:T(8,128)(2,1)} %shard_map.122) | non-fusion elementwise | flops 163840 | bytes 983040 | tf_op jit(solution)/shard_map/convert_element_type | solution.py:353
  51.3 1.3 %shard_map.123 = f32[16,512]{1,0:T(8,128)S(1)} custom-call(f32[320,512]{1,0:T(8,128)S(1)} %convert_element_type.14.own_ref, bf16[320,512]{1,0:T(8,128)(2,1)S(1)} %collective-permute-done.13.a_ref, bf16[320,512]{1,0:T(8,128)(2,1)S(1)} %collective-permute-done.14.b_ref, bf16[320,512]{1,0:T(8,128)(2,1)S(1)} %collective-permute-done.15.c_ref, ...), custom_call_target="tpu_custom_call" | custom-call | bytes 3145728 | tf_op jit(solution)/shard_map/pallas_call | solution.py:367
  52.6 1.2 %collective-permute-done.16 = f32[16,512]{1,0:T(8,128)S(1)} collective-permute-done((f32[16,512]{1,0:T(8,128)S(1)}, f32[16,512]{1,0:T(8,128)S(1)}, u32[]{:S(2)}, u32[]{:S(2)}) %collective-permute-start.16) | collective-permute-done | bytes 32800 | tf_op jit(solution)/shard_map/ppermute | solution.py:380
  53.9 11.1 %all_to_all.10 = f32[8,16,512]{2,1,0:T(8,128)S(1)} all-to-all(f32[8,16,512]{2,1,0:T(8,128)S(1)} %broadcast_in_dim.10), channel_id=1, replica_groups={{0,8,32,40,64,72,96,104},{16,24,48,56,80,88,112,120},{1,9,33,41,65,73,9..., dimensions={0} | all-to-all | bytes 524288 | tf_op jit(solution)/shard_map/all_to_all | solution.py:282
  65.0 12.5 %all_to_all.11 = f32[8,16,512]{2,1,0:T(8,128)S(1)} all-to-all(f32[8,16,512]{2,1,0:T(8,128)S(1)} %broadcast_in_dim.11), channel_id=1, replica_groups={{0,24,2,26,4,28,6,30},{8,16,10,18,12,20,14,22},{1,25,3,27,5,29,7,31},{9..., dimensions={0} | all-to-all | bytes 524288 | tf_op jit(solution)/shard_map/all_to_all | solution.py:282
  77.6 0.9 %fusion = f32[4,64]{1,0:T(4,128)} fusion(f32[16,4,128]{2,1,0:T(4,128)S(1)} %reshape.11, bf16[16,128,64]{1,2,0:T(8,128)(2,1)S(1)} %copy-done), kind=kOutput, calls=%fused_computation.1 | convolution fusion | flops 6291712 | bytes 295936 | tf_op jit(solution)/shard_map/jer,jrk->ek/dot_general | solution.py:384
  (77 shorter events, 4.3 us)
Async XLA Ops:
  0.0 77.5 %copy-start = (bf16[16,128,64]{1,2,0:T(8,128)(2,1)S(1)}, bf16[16,128,64]{1,2,0:T(8,128)(2,1)}, u32[]{:S(2)}) copy-start(bf16[16,128,64]{1,2,0:T(8,128)(2,1)} %param.23) | copy-start | bytes 786436
  4.1 2.4 %collective-permute-start = (bf16[2,1280,128]{2,1,0:T(8,128)(2,1)}, bf16[2,1280,128]{2,1,0:T(8,128)(2,1)S(1)}, u32[]{:S(2)}, u32[]{:S(2)}) collective-permute-start(bf16[2,1280,128]{2,1,0:T(8,128)(2,1)} %get-tuple-element.40), channel_id=1, source_target_pairs={{0,1},{1,0},{2,3},{3,2},{4,5},{5,4},{6,7},{7,6},{8,9},{9,8},{10,11... | collective-permute-start | bytes 1966088 | tf_op jit(solution)/shard_map/ppermute | solution.py:322
  6.4 4.0 %collective-permute-start.1 = (bf16[2,1280,128]{2,1,0:T(8,128)(2,1)}, bf16[2,1280,128]{2,1,0:T(8,128)(2,1)S(1)}, u32[]{:S(2)}, u32[]{:S(2)}) collective-permute-start(bf16[2,1280,128]{2,1,0:T(8,128)(2,1)} %get-tuple-element.41), channel_id=1, source_target_pairs={{0,1},{1,0},{2,3},{3,2},{4,5},{5,4},{6,7},{7,6},{8,9},{9,8},{10,11... | collective-permute-start | bytes 1966088 | tf_op jit(solution)/shard_map/ppermute | solution.py:324
  6.6 7.2 %collective-permute-start.3 = (f32[128,256]{1,0:T(8,128)}, f32[128,256]{1,0:T(8,128)S(1)}, u32[]{:S(2)}, u32[]{:S(2)}) collective-permute-start(f32[128,256]{1,0:T(8,128)} %get-tuple-element.55), channel_id=1, source_target_pairs={{0,8},{8,0},{16,24},{24,16},{1,9},{9,1},{17,25},{25,17},{2,10},{10... | collective-permute-start | bytes 393224 | tf_op jit(solution)/shard_map/ppermute | solution.py:329
  10.4 17.7 %copy-start.9 = (bf16[2,320,128]{2,1,0:T(8,128)(2,1)S(1)}, bf16[2,320,128]{2,1,0:T(8,128)(2,1)}, u32[]{:S(2)}) copy-start(bf16[2,320,128]{2,1,0:T(8,128)(2,1)} %get-tuple-element.66) | copy-start | bytes 491524
  10.5 16.2 %collective-permute-start.6 = (bf16[2,1280,128]{2,1,0:T(8,128)(2,1)}, bf16[2,1280,128]{2,1,0:T(8,128)(2,1)S(1)}, u32[]{:S(2)}, u32[]{:S(2)}) collective-permute-start(bf16[2,1280,128]{2,1,0:T(8,128)(2,1)} %get-tuple-element.56), channel_id=1, source_target_pairs={{0,4},{1,65},{2,6},{3,67},{4,0},{5,69},{6,2},{7,71},{32,36},{33,97... | collective-permute-start | bytes 1966088 | tf_op jit(solution)/shard_map/ppermute | solution.py:58
  13.8 8.2 %collective-permute-start.4 = (f32[128,256]{1,0:T(8,128)S(1)}, f32[128,256]{1,0:T(8,128)S(1)}, u32[]{:S(2)}, u32[]{:S(2)}) collective-permute-start(f32[128,256]{1,0:T(8,128)S(1)} %add.19), channel_id=1, source_target_pairs={{0,24},{24,0},{8,16},{16,8},{1,25},{25,1},{9,17},{17,9},{2,26},{26... | collective-permute-start | bytes 393224 | tf_op jit(solution)/shard_map/ppermute | solution.py:330
  16.8 11.3 %collective-permute-start.2 = (bf16[2,960,128]{2,1,0:T(8,128)(2,1)}, bf16[2,960,128]{2,1,0:T(8,128)(2,1)S(1)}, u32[]{:S(2)}, u32[]{:S(2)}) collective-permute-start(bf16[2,960,128]{2,1,0:T(8,128)(2,1)} %get-tuple-element.53), channel_id=1, source_target_pairs={{0,2},{1,33},{2,4},{3,35},{4,6},{5,37},{6,0},{7,39},{32,34},{33,65... | collective-permute-start | bytes 1474568 | tf_op jit(solution)/shard_map/ppermute | solution.py:58
  20.2 9.7 %collective-permute-start.7 = (bf16[2,960,128]{2,1,0:T(8,128)(2,1)}, bf16[2,960,128]{2,1,0:T(8,128)(2,1)S(1)}, u32[]{:S(2)}, u32[]{:S(2)}) collective-permute-start(bf16[2,960,128]{2,1,0:T(8,128)(2,1)} %get-tuple-element.59), channel_id=1, source_target_pairs={{0,6},{1,97},{2,0},{3,99},{4,2},{5,101},{6,4},{7,103},{32,38},{33,... | collective-permute-start | bytes 1474568 | tf_op jit(solution)/shard_map/ppermute | solution.py:58
  22.0 1.3 %collective-permute-start.5 = (bf16[128,256]{1,0:T(8,128)(2,1)S(1)}, bf16[128,256]{1,0:T(8,128)(2,1)S(1)}, u32[]{:S(2)}, u32[]{:S(2)}) collective-permute-start(bf16[128,256]{1,0:T(8,128)(2,1)S(1)} %add_convert_fusion), channel_id=1, source_target_pairs={{0,1},{1,0},{2,3},{3,2},{4,5},{5,4},{6,7},{7,6},{8,9},{9,8},{10,11... | collective-permute-start | bytes 196616 | tf_op jit(solution)/shard_map/ppermute | solution.py:334
  23.3 10.3 %collective-permute-start.8 = (bf16[256,256]{1,0:T(8,128)(2,1)S(1)}, bf16[256,256]{1,0:T(8,128)(2,1)S(1)}, u32[]{:S(2)}, u32[]{:S(2)}) collective-permute-start(bf16[256,256]{1,0:T(8,128)(2,1)S(1)} %pad_maximum_fusion.rest_4_), channel_id=1, source_target_pairs={{0,2},{1,33},{2,4},{3,35},{4,6},{5,37},{6,0},{7,39},{32,34},{33,65... | collective-permute-start | bytes 393224 | tf_op jit(solution)/shard_map/ppermute | solution.py:58
  23.7 9.9 %collective-permute-start.9 = (bf16[256,256]{1,0:T(8,128)(2,1)S(1)}, bf16[256,256]{1,0:T(8,128)(2,1)S(1)}, u32[]{:S(2)}, u32[]{:S(2)}) collective-permute-start(bf16[256,256]{1,0:T(8,128)(2,1)S(1)} %pad_maximum_fusion.rest_4_), channel_id=1, source_target_pairs={{0,4},{1,65},{2,6},{3,67},{4,0},{5,69},{6,2},{7,71},{32,36},{33,97... | collective-permute-start | bytes 393224 | tf_op jit(solution)/shard_map/ppermute | solution.py:58
  26.6 7.0 %collective-permute-start.10 = (bf16[256,256]{1,0:T(8,128)(2,1)S(1)}, bf16[256,256]{1,0:T(8,128)(2,1)S(1)}, u32[]{:S(2)}, u32[]{:S(2)}) collective-permute-start(bf16[256,256]{1,0:T(8,128)(2,1)S(1)} %pad_maximum_fusion.rest_4_), channel_id=1, source_target_pairs={{0,6},{1,97},{2,0},{3,99},{4,2},{5,101},{6,4},{7,103},{32,38},{33,... | collective-permute-start | bytes 393224 | tf_op jit(solution)/shard_map/ppermute | solution.py:58
  28.1 17.0 %collective-permute-start.11 = (bf16[2,320,128]{2,1,0:T(8,128)(2,1)S(1)}, bf16[2,320,128]{2,1,0:T(8,128)(2,1)S(1)}, u32[]{:S(2)}, u32[]{:S(2)}) collective-permute-start(bf16[2,320,128]{2,1,0:T(8,128)(2,1)S(1)} %copy-done.9), channel_id=1, source_target_pairs={{0,2},{1,33},{2,4},{3,35},{4,6},{5,37},{6,0},{7,39},{32,34},{33,65... | collective-permute-start | bytes 491528 | tf_op jit(solution)/shard_map/ppermute | solution.py:58
  29.9 15.3 %collective-permute-start.12 = (bf16[2,320,128]{2,1,0:T(8,128)(2,1)}, bf16[2,320,128]{2,1,0:T(8,128)(2,1)S(1)}, u32[]{:S(2)}, u32[]{:S(2)}) collective-permute-start(bf16[2,320,128]{2,1,0:T(8,128)(2,1)} %get-tuple-element.67), channel_id=1, source_target_pairs={{0,6},{1,97},{2,0},{3,99},{4,2},{5,101},{6,4},{7,103},{32,38},{33,... | collective-permute-start | bytes 491528 | tf_op jit(solution)/shard_map/ppermute | solution.py:58
  38.7 11.9 %copy-start.17 = (s32[1,231]{1,0:T(1,128)S(1)}, s32[1,231]{1,0:T(1,128)}, u32[]{:S(2)}) copy-start(s32[1,231]{1,0:T(1,128)} %param.21) | copy-start | bytes 2776
  38.8 12.1 %copy-start.18 = (s32[1,64]{1,0:T(1,128)S(1)}, s32[1,64]{1,0:T(1,128)}, u32[]{:S(2)}) copy-start(s32[1,64]{1,0:T(1,128)} %param.20) | copy-start | bytes 772
  38.8 12.2 %copy-start.16 = (s32[4096]{0:T(1024)S(1)}, s32[4096]{0:T(1024)}, u32[]{:S(2)}) copy-start(s32[4096]{0:T(1024)} %param.22) | copy-start | bytes 49156
  38.8 12.3 %copy-start.14 = (f32[1,231,128]{2,0,1:T(1,128)S(1)}, f32[1,231,128]{2,0,1:T(1,128)}, u32[]{:S(2)}) copy-start(f32[1,231,128]{2,0,1:T(1,128)} %param.19) | copy-start | bytes 354820
  38.8 12.3 %copy-start.15 = (f32[1,231,128]{2,0,1:T(1,128)S(1)}, f32[1,231,128]{2,0,1:T(1,128)}, u32[]{:S(2)}) copy-start(f32[1,231,128]{2,0,1:T(1,128)} %param.18) | copy-start | bytes 354820
  38.8 12.3 %collective-permute-start.13 = (bf16[320,512]{1,0:T(8,128)(2,1)}, bf16[320,512]{1,0:T(8,128)(2,1)S(1)}, u32[]{:S(2)}, u32[]{:S(2)}) collective-permute-start(bf16[320,512]{1,0:T(8,128)(2,1)} %get-tuple-element.63), channel_id=1, source_target_pairs={{0,64},{1,5},{2,66},{3,7},{4,68},{5,1},{6,70},{7,3},{32,96},{33,37... | collective-permute-start | bytes 983048 | tf_op jit(solution)/shard_map/ppermute | solution.py:62
  41.9 9.3 %collective-permute-start.14 = (bf16[320,512]{1,0:T(8,128)(2,1)}, bf16[320,512]{1,0:T(8,128)(2,1)S(1)}, u32[]{:S(2)}, u32[]{:S(2)}) collective-permute-start(bf16[320,512]{1,0:T(8,128)(2,1)} %get-tuple-element.62), channel_id=1, source_target_pairs={{0,32},{1,3},{2,34},{3,5},{4,36},{5,7},{6,38},{7,1},{32,64},{33,35... | collective-permute-start | bytes 983048 | tf_op jit(solution)/shard_map/ppermute | solution.py:62
  42.5 8.8 %collective-permute-start.15 = (bf16[320,512]{1,0:T(8,128)(2,1)}, bf16[320,512]{1,0:T(8,128)(2,1)S(1)}, u32[]{:S(2)}, u32[]{:S(2)}) collective-permute-start(bf16[320,512]{1,0:T(8,128)(2,1)} %get-tuple-element.64), channel_id=1, source_target_pairs={{0,96},{1,7},{2,98},{3,1},{4,100},{5,3},{6,102},{7,5},{32,0},{33,3... | collective-permute-start | bytes 983048 | tf_op jit(solution)/shard_map/ppermute | solution.py:62
  52.6 1.2 %collective-permute-start.16 = (f32[16,512]{1,0:T(8,128)S(1)}, f32[16,512]{1,0:T(8,128)S(1)}, u32[]{:S(2)}, u32[]{:S(2)}) collective-permute-start(f32[16,512]{1,0:T(8,128)S(1)} %shard_map.123), channel_id=1, source_target_pairs={{0,1},{1,0},{2,3},{3,2},{4,5},{5,4},{6,7},{7,6},{8,9},{9,8},{10,11... | collective-permute-start | bytes 98312 | tf_op jit(solution)/shard_map/ppermute | solution.py:380
  (14 other events, 67.4 us)

commit v9 on v8

--- a/solution.py
+++ b/solution.py
@@ -16,7 +16,8 @@
 UP_ROWS = 231
 DOWN_ROWS = 64
 WINDOW = 256
-ROWS = WINDOW + DOWN_ROWS
+HELD = 240
+ROWS = HELD + DOWN_ROWS
 FIRST = 3 * ROWS
 EARLY = {2: (0, 0), 1: (0, 1), 3: (1, 0), 0: (1, 1)}
 PARTED = (1, 3)
@@ -73,7 +74,7 @@
 def pack_kernel(grad_hbm, tokens_hbm, down_hbm, up_hbm, *rest):
     gives, rest = rest[:2], rest[2:]
     buffers, portion_ref = rest[:6], rest[6]
-    grad, tokens, down, up, turned, loads, sent = rest[7:]
+    grad, tokens, down, up, turned, staged, loads, sent = rest[7:]
     arrivals = [
         pltpu.make_async_copy(source, target, loads.at[i])
         for i, (source, target) in enumerate(((tokens_hbm, tokens), (grad_hbm, grad), (down_hbm, down), (up_hbm, up)))
@@ -81,8 +82,11 @@
     for arrival in arrivals:
         arrival.start()
     x, y, c = position()
-    turned_copies, grad_copies = [], []
-    for slot in range(8):
+    arrivals[0].wait()
+    turned[...] = tokens[...].T
+    arrivals[1].wait()
+    copies = []
+    for slot in (2, 6, 1, 5, 3, 7, 0, 4):
         target = 1 - c if slot < 4 else c
         k = slot % 4
         for i in range(4):
@@ -91,23 +95,19 @@
             owner = to_x * 8 + to_y * 2 + target
             start = pl.multiple_of(window_start(owner), 16)
             column = pl.multiple_of(owner * DOWN_ROWS, DOWN_ROWS)
-            out = gives[EARLY[k][0]].at[EARLY[k][1]] if slot < 4 else buffers[k].at[0]
-            window_at, down_at = ((i - 1) * WINDOW, 3 * WINDOW + (i - 1) * DOWN_ROWS) if i else (FIRST, FIRST + WINDOW)
-            if slot >= 4 and i == 0 and k in PARTED:
-                out, window_at, down_at = buffers[4 + PARTED.index(k)].at[0], 0, WINDOW
-            grad_copies.append(
-                pltpu.make_async_copy(grad.at[pl.ds(start, WINDOW)], out.at[pl.ds(window_at, WINDOW)], sent)
-            )
-            turned_copies.append(
-                pltpu.make_async_copy(turned.at[pl.ds(column, DOWN_ROWS)], out.at[pl.ds(down_at, DOWN_ROWS)], sent)
-            )
-    arrivals[0].wait()
-    turned[...] = tokens[...].T
-    for copy in turned_copies:
-        copy.start()
-    arrivals[1].wait()
-    for copy in grad_copies:
-        copy.start()
+            window_at, down_at = ((i - 1) * HELD, 3 * HELD + (i - 1) * DOWN_ROWS) if i else (FIRST, FIRST + HELD)
+            window = pltpu.roll(grad[pl.ds(start, WINDOW), :].astype(F32), WINDOW + start - owner * UP_ROWS, 0)
+            staged[slot, window_at:window_at + HELD, :] = window[:HELD].astype(BF)
+            staged[slot, down_at:down_at + DOWN_ROWS, :] = turned[pl.ds(column, DOWN_ROWS), :]
+        if slot < 4:
+            parts = [(0, 4 * ROWS, gives[EARLY[k][0]].at[EARLY[k][1]])]
+        elif k in PARTED:
+            parts = [(0, FIRST, buffers[k].at[0]), (FIRST, ROWS, buffers[4 + PARTED.index(k)].at[0])]
+        else:
+            parts = [(0, 4 * ROWS, buffers[k].at[0])]
+        for begin, size, out in parts:
+            copies.append(pltpu.make_async_copy(staged.at[slot, pl.ds(begin, size)], out, sent))
+            copies[-1].start()
     arrivals[2].wait()
     portion_ref[:, :RANK] = jnp.dot(tokens[...], down[...], preferred_element_type=F32)
     arrivals[3].wait()
@@ -118,7 +118,7 @@
             grad[begin:end, :], up[begin:end, :], (((0,), (0,)), ((), ())), preferred_element_type=F32
         )
     portion_ref[:, RANK:] = product
-    for copy in turned_copies + grad_copies:
+    for copy in copies:
         copy.wait()
 
 
@@ -188,21 +188,21 @@
         for e in range(EXAMPLES):
             right_h[rows, e * RANK:(e + 1) * RANK] = h * masks[s][e]
             right_u[rows, e * RANK:(e + 1) * RANK] = u * masks[s][e]
-    split = count * WINDOW
+    split = count * HELD
     for k in range(4):
         for copy in column_copies[2 * k:2 * k + 2]:
             copy.wait()
         both = pl.ds(k * PAIR, PAIR)
         for n in range(count + 1):
-            rows = slice(n * WINDOW, (n + 1) * WINDOW) if n < count else slice(split, count * ROWS)
+            rows = slice(n * HELD, (n + 1) * HELD) if n < count else slice(split, count * ROWS)
             joined = jnp.concatenate([left[k, 0, rows, :], left[k, 1, rows, :]], axis=1)
             right = (right_h if n < count else right_u)[both, :]
             product = jnp.dot(joined, right, preferred_element_type=F32)
             total[rows, :] = product if k == 0 else total[rows, :] + product
     out_copies = []
     for n in range(count):
-        done[n, :WINDOW, :] = total[n * WINDOW:(n + 1) * WINDOW, :].astype(BF)
-        done[n, WINDOW:, :] = total[split + n * DOWN_ROWS:split + (n + 1) * DOWN_ROWS, :].astype(BF)
+        done[n, :HELD, :] = total[n * HELD:(n + 1) * HELD, :].astype(BF)
+        done[n, HELD:, :] = total[split + n * DOWN_ROWS:split + (n + 1) * DOWN_ROWS, :].astype(BF)
         out_copies.append(pltpu.make_async_copy(done.at[n], outs[n], sent))
         out_copies[-1].start()
     for copy in out_copies:
@@ -234,14 +234,13 @@
 
 
 def feature_kernel(
-    own_ref, a_ref, b_ref, c_ref, bounds_ref, offset_ref, select_ref,
+    own_ref, a_ref, b_ref, c_ref, bounds_ref, select_ref,
     first_up, first_down, second_up, second_down, out_ref, first_ref, second_ref,
 ):
     for up, down, space in ((first_up, first_down, first_ref), (second_up, second_down, second_ref)):
-        space[:WINDOW, :] = jnp.zeros((WINDOW, RANK), F32)
+        space[HELD - 16:HELD, :] = jnp.zeros((16, RANK), F32)
         space[:UP_ROWS, :] = up[...]
-        space[:WINDOW, :] = pltpu.roll(space[:WINDOW, :], offset_ref[0], 0)
-        space[WINDOW:, :] = down[...]
+        space[HELD:, :] = down[...]
     first = 0.9 * first_ref[...]
     second = 0.999 * second_ref[...]
     select = select_ref[...]
@@ -299,8 +298,6 @@
     segments,
     bank,
 ):
-    x, y, c = position()
-    me = x * 8 + y * 2 + c
     shapes = [jax.ShapeDtypeStruct((2, rows, 128), BF) for rows in (4 * ROWS, FIRST, 4 * ROWS, FIRST, ROWS, ROWS)]
     give, give_late, *packed, portion = pl.pallas_call(
         pack_kernel,
@@ -313,6 +310,7 @@
             pltpu.VMEM((2048, 128), BF),
             pltpu.VMEM((LOCAL_UP, 128), BF),
             pltpu.VMEM((2048, 128), BF),
+            pltpu.VMEM((8, 4 * ROWS, 128), BF),
             pltpu.SemaphoreType.DMA((4,)),
             pltpu.SemaphoreType.DMA,
         ],
@@ -356,30 +354,24 @@
         (segments[None, :] < jnp.arange(EXAMPLES + 1, dtype=jnp.int32)[:, None]).astype(jnp.int32), axis=1
     )
 
-    offset = me * UP_ROWS - window_start(me)
-    seeds = jnp.concatenate(
-        [
-            lax.dynamic_update_slice_in_dim(jnp.full((WINDOW,), -1, jnp.int32), up_row_seeds[0], offset, 0),
-            down_row_seeds[0],
-        ]
-    )
+    seeds = jnp.concatenate([up_row_seeds[0], jnp.full((HELD - UP_ROWS,), -1, jnp.int32), down_row_seeds[0]])
     select = (jnp.arange(BANK, dtype=jnp.int32)[:, None] == seeds[None, :]).astype(BF)
     blocks = pl.pallas_call(
         feature_kernel,
         out_shape=jax.ShapeDtypeStruct((BANK, WIDE), F32),
-        in_specs=[VMEM] * 4 + [SMEM] * 2 + [VMEM] * 5,
+        in_specs=[VMEM] * 4 + [SMEM] + [VMEM] * 5,
         out_specs=VMEM,
         scratch_shapes=[pltpu.VMEM((ROWS, RANK), F32), pltpu.VMEM((ROWS, RANK), F32)],
         compiler_params=pltpu.CompilerParams(vmem_limit_bytes=24 << 20),
         cost_estimate=pl.CostEstimate(flops=0, bytes_accessed=3 << 20, transcendentals=0),
     )(
-        own, *arrived, bounds, offset.astype(jnp.int32)[None], select,
+        own, *arrived, bounds, select,
         first_moment_up[0], first_moment_down[0], second_moment_up[0], second_moment_down[0],
     )
 
     summed = blocks + lax.ppermute(blocks, "co", [(0, 1), (1, 0)])
+    summed = spread_sum(summed, False)
     summed = spread_sum(summed, True)
-    summed = spread_sum(summed, False)
     inverse = 1.0 / math.sqrt((MODEL_WIDTH + HIDDEN_WIDTH) * RANK)
     sketch = jnp.einsum(
         "jer,jrk->ek", summed.reshape(BANK, EXAMPLES, RANK), bank.astype(F32), precision=lax.Precision.HIGHEST

time: 78.8 us -> 77.6 us (0.985)
  blocking collectives: 23.6 us -> 22.6 us
    all_to_all x2, blocking collectives: 23.6 us -> 22.6 us  [spread_sum(): lax.all_to_all(copies, EVERY, split_axis=0, concat_axis=0, tiled=True, ax...]
  transfers between devices with their start and end apart: 17 -> 17, of which waited for: 6 -> 3; matrix products, arithmetic and copies ran while one was open for 2% -> 2% of each run, Pallas kernels for 14% -> 14%
where the time goes in v9:
time: 77.6 us; the launch traced here: 77.3 us
  starting transfers between devices  28.3 us (36%)
  blocking collectives  22.6 us (29%)
  Pallas kernels  16.9 us (22%)
  waiting for transfers between devices  4.72 us (6%)
  local copies, waits for them, and re-layouts  2.15 us (3%)
  other arithmetic  1.35 us (2%)
  matrix products  0.91 us (1%)
    all_to_all x2, blocking collectives, spread_sum(): lax.all_to_all(copies, EVERY, split_axis=0, concat_axis=0, tiled=True, ax...  22.6 us
    ppermute x8, starting transfers between devices, send_same(): return lax.ppermute(value, PLANE, pairs(lambda p: along(p, shift)))  16.6 us
    pallas_call x2, Pallas kernels, partial_call(): pl.pallas_call(functools.partial(partial_kernel, count), out_shape=[jax.S...  7.37 us
    ppermute x3, starting transfers between devices, send_across(): return lax.ppermute(value, PLANE, pairs(lambda p: across(p, shift)))  6.34 us
    pallas_call x1, Pallas kernels, on_device(): pl.pallas_call(pack_kernel, out_shape=[jax.ShapeDtypeStruct((2, 4 * ROWS,...  4.65 us
    pallas_call x2, Pallas kernels, fill_call(): pl.pallas_call(functools.partial(fill_kernel, shifts), out_shape=[jax.Sha...  3.66 us
    ppermute x1, starting transfers between devices, on_device(): lax.ppermute(pair, ('t1', 't0'), [(0, 3), (3, 0), (1, 2), (2, 1)])  3.02 us
    ppermute x1, waiting for transfers between devices, on_device(): taken = lax.ppermute(give, 'co', [(0, 1), (1, 0)])  2.25 us
  transfers between devices with their start and end apart: 17, of which 3 were waited for; matrix products, arithmetic and copies ran while one was open for 2% of the time, Pallas kernels for 14%

profile of v9, /device:TPU:0, one launch (start us, length us, event | category | flops | bytes accessed | tf_op | source)
XLA Modules:
  0.0 77.3 jit_solution(10793145674318492250)
XLA Ops:
  0.0 4.6 %shard_map.118 = (bf16[2,1216,128]{2,1,0:T(8,128)(2,1)}, bf16[2,1216,128]{2,1,0:T(8,128)(2,1)}, bf16[2,1216,128]{2,1,0:T(8,128)(2,1)}, bf16[2,912,128]{2,1,0:T(8...) custom-call(bf16[7392,128]{1,0:T(8,128)(2,1)} %bitcast.18, ...), custom_call_target="tpu_custom_call" | custom-call | flops 309329920 | bytes 8388608 | tf_op jit(solution)/shard_map/pallas_call | solution.py:302
  4.8 2.2 %collective-permute-done.taken_ref = bf16[2,1216,128]{2,1,0:T(8,128)(2,1)S(1)} collective-permute-done((bf16[2,1216,128]{2,1,0:T(8,128)(2,1)}, bf16[2,1216,128]{2,1,0:T(8,128)(2,1)S(1)}, u32[]{:S(2)}, u32[]{:S(2)}) %collective-permute-start) | collective-permute-done | bytes 622624 | tf_op jit(solution)/shard_map/ppermute | solution.py:320
  7.2 2.0 %collective-permute-start.3 = (f32[128,256]{1,0:T(8,128)}, f32[128,256]{1,0:T(8,128)S(1)}, u32[]{:S(2)}, u32[]{:S(2)}) collective-permute-start(f32[128,256]{1,0:T(8,128)} %get-tuple-element.55), channel_id=1, source_target_pairs={{0,8},{8,0},{16,24},{24,16},{1,9},{9,1},{17,25},{25,17},{2,10},{10... | collective-permute-start | bytes 393224 | tf_op jit(solution)/shard_map/ppermute | solution.py:327
  9.2 1.8 %shard_map.119 = (bf16[2,1216,128]{2,1,0:T(8,128)(2,1)}, bf16[2,912,128]{2,1,0:T(8,128)(2,1)}, bf16[2,304,128]{2,1,0:T(8,128)(2,1)}) custom-call(bf16[2,1216,128]{2,1,0:T(8,128)(2,1)} %copy-done.5, bf16[2,1216,128]{2,1,0:T(8,128)(2,1)} %get-tuple-element.43.rest_0_, ...), custom_call_target="tpu_custom_call", output_to_operand_aliasing={{0}: (1, {}), {1}: (2, {}), {2}: (3, {})} | custom-call | bytes 1048576 | tf_op jit(solution)/shard_map/pallas_call | solution.py:143
  11.0 3.3 %collective-permute-start.6 = (bf16[2,1216,128]{2,1,0:T(8,128)(2,1)}, bf16[2,1216,128]{2,1,0:T(8,128)(2,1)S(1)}, u32[]{:S(2)}, u32[]{:S(2)}) collective-permute-start(bf16[2,1216,128]{2,1,0:T(8,128)(2,1)} %get-tuple-element.56), channel_id=1, source_target_pairs={{0,4},{1,65},{2,6},{3,67},{4,0},{5,69},{6,2},{7,71},{32,36},{33,97... | collective-permute-start | bytes 1867784 | tf_op jit(solution)/shard_map/ppermute | solution.py:59
  14.3 3.0 %collective-permute-start.4 = (f32[128,256]{1,0:T(8,128)S(1)}, f32[128,256]{1,0:T(8,128)S(1)}, u32[]{:S(2)}, u32[]{:S(2)}) collective-permute-start(f32[128,256]{1,0:T(8,128)S(1)} %add.9), channel_id=1, source_target_pairs={{0,24},{24,0},{8,16},{16,8},{1,25},{25,1},{9,17},{17,9},{2,26},{26... | collective-permute-start | bytes 393224 | tf_op jit(solution)/shard_map/ppermute | solution.py:328
  17.4 1.6 %collective-permute-start.2 = (bf16[2,912,128]{2,1,0:T(8,128)(2,1)}, bf16[2,912,128]{2,1,0:T(8,128)(2,1)S(1)}, u32[]{:S(2)}, u32[]{:S(2)}) collective-permute-start(bf16[2,912,128]{2,1,0:T(8,128)(2,1)} %get-tuple-element.53), channel_id=1, source_target_pairs={{0,2},{1,33},{2,4},{3,35},{4,6},{5,37},{6,0},{7,39},{32,34},{33,65... | collective-permute-start | bytes 1400840 | tf_op jit(solution)/shard_map/ppermute | solution.py:59
  18.9 1.8 %shard_map.120 = (bf16[2,912,128]{2,1,0:T(8,128)(2,1)}, bf16[2,304,128]{2,1,0:T(8,128)(2,1)}, bf16[2,1216,128]{2,1,0:T(8,128)(2,1)}) custom-call(bf16[2,1216,128]{2,1,0:T(8,128)(2,1)} %copy-done.4, bf16[2,912,128]{2,1,0:T(8,128)(2,1)} %get-tuple-element.48.rest_0_, ...), custom_call_target="tpu_custom_call", output_to_operand_aliasing={{0}: (1, {}), {1}: (2, {}), {2}: (3, {})} | custom-call | bytes 1048576 | tf_op jit(solution)/shard_map/pallas_call | solution.py:143
  20.8 1.7 %collective-permute-start.7 = (bf16[2,912,128]{2,1,0:T(8,128)(2,1)}, bf16[2,912,128]{2,1,0:T(8,128)(2,1)S(1)}, u32[]{:S(2)}, u32[]{:S(2)}) collective-permute-start(bf16[2,912,128]{2,1,0:T(8,128)(2,1)} %get-tuple-element.59), channel_id=1, source_target_pairs={{0,6},{1,97},{2,0},{3,99},{4,2},{5,101},{6,4},{7,103},{32,38},{33,... | collective-permute-start | bytes 1400840 | tf_op jit(solution)/shard_map/ppermute | solution.py:59
  22.6 1.2 %collective-permute-done.5 = bf16[128,256]{1,0:T(8,128)(2,1)S(1)} collective-permute-done((bf16[128,256]{1,0:T(8,128)(2,1)S(1)}, bf16[128,256]{1,0:T(8,128)(2,1)S(1)}, u32[]{:S(2)}, u32[]{:S(2)}) %collective-permute-start.5) | collective-permute-done | bytes 65568 | tf_op jit(solution)/shard_map/ppermute | solution.py:332
  24.3 2.9 %collective-permute-start.9 = (bf16[256,256]{1,0:T(8,128)(2,1)S(1)}, bf16[256,256]{1,0:T(8,128)(2,1)S(1)}, u32[]{:S(2)}, u32[]{:S(2)}) collective-permute-start(bf16[256,256]{1,0:T(8,128)(2,1)S(1)} %pad_maximum_fusion.rest_4_), channel_id=1, source_target_pairs={{0,4},{1,65},{2,6},{3,67},{4,0},{5,69},{6,2},{7,71},{32,36},{33,97... | collective-permute-start | bytes 393224 | tf_op jit(solution)/shard_map/ppermute | solution.py:59
  27.2 1.3 %collective-permute-start.10 = (bf16[256,256]{1,0:T(8,128)(2,1)S(1)}, bf16[256,256]{1,0:T(8,128)(2,1)S(1)}, u32[]{:S(2)}, u32[]{:S(2)}) collective-permute-start(bf16[256,256]{1,0:T(8,128)(2,1)S(1)} %pad_maximum_fusion.rest_4_), channel_id=1, source_target_pairs={{0,6},{1,97},{2,0},{3,99},{4,2},{5,101},{6,4},{7,103},{32,38},{33,... | collective-permute-start | bytes 393224 | tf_op jit(solution)/shard_map/ppermute | solution.py:59
  28.6 1.2 %collective-permute-start.11 = (bf16[2,304,128]{2,1,0:T(8,128)(2,1)S(1)}, bf16[2,304,128]{2,1,0:T(8,128)(2,1)S(1)}, u32[]{:S(2)}, u32[]{:S(2)}) collective-permute-start(bf16[2,304,128]{2,1,0:T(8,128)(2,1)S(1)} %copy-done.9), channel_id=1, source_target_pairs={{0,2},{1,33},{2,4},{3,35},{4,6},{5,37},{6,0},{7,39},{32,34},{33,65... | collective-permute-start | bytes 466952 | tf_op jit(solution)/shard_map/ppermute | solution.py:59
  29.8 4.1 %collective-permute-start.12 = (bf16[2,304,128]{2,1,0:T(8,128)(2,1)}, bf16[2,304,128]{2,1,0:T(8,128)(2,1)S(1)}, u32[]{:S(2)}, u32[]{:S(2)}) collective-permute-start(bf16[2,304,128]{2,1,0:T(8,128)(2,1)} %get-tuple-element.67), channel_id=1, source_target_pairs={{0,6},{1,97},{2,0},{3,99},{4,2},{5,101},{6,4},{7,103},{32,38},{33,... | collective-permute-start | bytes 466952 | tf_op jit(solution)/shard_map/ppermute | solution.py:59
  34.7 4.3 %shard_map.121 = (bf16[304,512]{1,0:T(8,128)(2,1)}, bf16[304,512]{1,0:T(8,128)(2,1)}, bf16[304,512]{1,0:T(8,128)(2,1)}) custom-call(s32[32,128]{1,0:T(8,128)} %bitcast.19, bf16[2,1216,128]{2,1,0:T(8,128)(2,1)} %get-tuple-element.51.rest_0_, bf16[2,912,128]{2,1,0:T(8,128)(2,1)} %copy-done.19, bf16[2,1216,128]{2,1,0:T(8,128)(2,1)} %copy-done.3, ...), custom_call_target="tpu_custom_call" | custom-call | flops 956301312 | bytes 6291456 | tf_op jit(solution)/shard_map/pallas_call | solution.py:213
  39.0 3.1 %collective-permute-start.13 = (bf16[304,512]{1,0:T(8,128)(2,1)}, bf16[304,512]{1,0:T(8,128)(2,1)S(1)}, u32[]{:S(2)}, u32[]{:S(2)}) collective-permute-start(bf16[304,512]{1,0:T(8,128)(2,1)} %get-tuple-element.63), channel_id=1, source_target_pairs={{0,64},{1,5},{2,66},{3,7},{4,68},{5,1},{6,70},{7,3},{32,96},{33,37... | collective-permute-start | bytes 933896 | tf_op jit(solution)/shard_map/ppermute | solution.py:63
  42.7 2.6 %collective-permute-start.15 = (bf16[304,512]{1,0:T(8,128)(2,1)}, bf16[304,512]{1,0:T(8,128)(2,1)S(1)}, u32[]{:S(2)}, u32[]{:S(2)}) collective-permute-start(bf16[304,512]{1,0:T(8,128)(2,1)} %get-tuple-element.64), channel_id=1, source_target_pairs={{0,96},{1,7},{2,98},{3,1},{4,100},{5,3},{6,102},{7,5},{32,0},{33,3... | collective-permute-start | bytes 933896 | tf_op jit(solution)/shard_map/ppermute | solution.py:63
  46.7 3.1 %shard_map.122 = bf16[304,512]{1,0:T(8,128)(2,1)} custom-call(s32[32,128]{1,0:T(8,128)} %bitcast.20, bf16[2,1216,128]{2,1,0:T(8,128)(2,1)} %get-tuple-element.51.rest_0_, bf16[2,304,128]{2,1,0:T(8,128)(2,1)} %copy-done.7, bf16[2,1216,128]{2,1,0:T(8,128)(2,1)} %copy-done.3, bf16[2,304,128]{2,1,0:T(8,128)(2,1)} %copy-done.8, bf16[256,256]{1,0:T(8,128)(2,1)} %copy-done.6, ...), custom_call_target="tpu_custom_call" | custom-call | flops 318767104 | bytes 6291456 | tf_op jit(solution)/shard_map/pallas_call | solution.py:213
  49.8 1.0 %convert_element_type.14.own_ref = f32[304,512]{1,0:T(8,128)S(1)} convert(bf16[304,512]{1,0:T(8,128)(2,1)} %shard_map.122) | non-fusion elementwise | flops 155648 | bytes 933888 | tf_op jit(solution)/shard_map/convert_element_type | solution.py:351
  51.2 1.2 %shard_map.123 = f32[16,512]{1,0:T(8,128)S(1)} custom-call(f32[304,512]{1,0:T(8,128)S(1)} %convert_element_type.14.own_ref, bf16[304,512]{1,0:T(8,128)(2,1)S(1)} %collective-permute-done.13.a_ref, bf16[304,512]{1,0:T(8,128)(2,1)S(1)} %collective-permute-done.14.b_ref, bf16[304,512]{1,0:T(8,128)(2,1)S(1)} %collective-permute-done.15.c_ref, ...), custom_call_target="tpu_custom_call" | custom-call | bytes 3145728 | tf_op jit(solution)/shard_map/pallas_call | solution.py:359
  52.4 1.2 %collective-permute-done.16 = f32[16,512]{1,0:T(8,128)S(1)} collective-permute-done((f32[16,512]{1,0:T(8,128)S(1)}, f32[16,512]{1,0:T(8,128)S(1)}, u32[]{:S(2)}, u32[]{:S(2)}) %collective-permute-start.16) | collective-permute-done | bytes 32800 | tf_op jit(solution)/shard_map/ppermute | solution.py:372
  53.7 12.0 %all_to_all.10 = f32[8,16,512]{2,1,0:T(8,128)S(1)} all-to-all(f32[8,16,512]{2,1,0:T(8,128)S(1)} %broadcast_in_dim.4), channel_id=1, replica_groups={{0,24,2,26,4,28,6,30},{8,16,10,18,12,20,14,22},{1,25,3,27,5,29,7,31},{9..., dimensions={0} | all-to-all | bytes 524288 | tf_op jit(solution)/shard_map/all_to_all | solution.py:281
  65.7 10.6 %all_to_all.11 = f32[8,16,512]{2,1,0:T(8,128)S(1)} all-to-all(f32[8,16,512]{2,1,0:T(8,128)S(1)} %broadcast_in_dim.5), channel_id=1, replica_groups={{0,8,32,40,64,72,96,104},{16,24,48,56,80,88,112,120},{1,9,33,41,65,73,9..., dimensions={0} | all-to-all | bytes 524288 | tf_op jit(solution)/shard_map/all_to_all | solution.py:281
  76.4 0.9 %fusion = f32[4,64]{1,0:T(4,128)} fusion(f32[16,4,128]{2,1,0:T(4,128)S(1)} %reshape.11, bf16[16,128,64]{1,2,0:T(8,128)(2,1)S(1)} %copy-done), kind=kOutput, calls=%fused_computation.1 | convolution fusion | flops 6291712 | bytes 295936 | tf_op jit(solution)/shard_map/jer,jrk->ek/dot_general | solution.py:376
  (76 shorter events, 3.9 us)
Async XLA Ops:
  0.0 76.4 %copy-start = (bf16[16,128,64]{1,2,0:T(8,128)(2,1)S(1)}, bf16[16,128,64]{1,2,0:T(8,128)(2,1)}, u32[]{:S(2)}) copy-start(bf16[16,128,64]{1,2,0:T(8,128)(2,1)} %param.23) | copy-start | bytes 786436
  4.7 2.3 %collective-permute-start = (bf16[2,1216,128]{2,1,0:T(8,128)(2,1)}, bf16[2,1216,128]{2,1,0:T(8,128)(2,1)S(1)}, u32[]{:S(2)}, u32[]{:S(2)}) collective-permute-start(bf16[2,1216,128]{2,1,0:T(8,128)(2,1)} %get-tuple-element.40), channel_id=1, source_target_pairs={{0,1},{1,0},{2,3},{3,2},{4,5},{5,4},{6,7},{7,6},{8,9},{9,8},{10,11... | collective-permute-start | bytes 1867784 | tf_op jit(solution)/shard_map/ppermute | solution.py:320
  7.0 4.0 %collective-permute-start.1 = (bf16[2,1216,128]{2,1,0:T(8,128)(2,1)}, bf16[2,1216,128]{2,1,0:T(8,128)(2,1)S(1)}, u32[]{:S(2)}, u32[]{:S(2)}) collective-permute-start(bf16[2,1216,128]{2,1,0:T(8,128)(2,1)} %get-tuple-element.41), channel_id=1, source_target_pairs={{0,1},{1,0},{2,3},{3,2},{4,5},{5,4},{6,7},{7,6},{8,9},{9,8},{10,11... | collective-permute-start | bytes 1867784 | tf_op jit(solution)/shard_map/ppermute | solution.py:322
  7.2 7.2 %collective-permute-start.3 = (f32[128,256]{1,0:T(8,128)}, f32[128,256]{1,0:T(8,128)S(1)}, u32[]{:S(2)}, u32[]{:S(2)}) collective-permute-start(f32[128,256]{1,0:T(8,128)} %get-tuple-element.55), channel_id=1, source_target_pairs={{0,8},{8,0},{16,24},{24,16},{1,9},{9,1},{17,25},{25,17},{2,10},{10... | collective-permute-start | bytes 393224 | tf_op jit(solution)/shard_map/ppermute | solution.py:327
  11.0 17.6 %copy-start.9 = (bf16[2,304,128]{2,1,0:T(8,128)(2,1)S(1)}, bf16[2,304,128]{2,1,0:T(8,128)(2,1)}, u32[]{:S(2)}) copy-start(bf16[2,304,128]{2,1,0:T(8,128)(2,1)} %get-tuple-element.66) | copy-start | bytes 466948
  11.0 16.2 %collective-permute-start.6 = (bf16[2,1216,128]{2,1,0:T(8,128)(2,1)}, bf16[2,1216,128]{2,1,0:T(8,128)(2,1)S(1)}, u32[]{:S(2)}, u32[]{:S(2)}) collective-permute-start(bf16[2,1216,128]{2,1,0:T(8,128)(2,1)} %get-tuple-element.56), channel_id=1, source_target_pairs={{0,4},{1,65},{2,6},{3,67},{4,0},{5,69},{6,2},{7,71},{32,36},{33,97... | collective-permute-start | bytes 1867784 | tf_op jit(solution)/shard_map/ppermute | solution.py:59
  14.3 8.2 %collective-permute-start.4 = (f32[128,256]{1,0:T(8,128)S(1)}, f32[128,256]{1,0:T(8,128)S(1)}, u32[]{:S(2)}, u32[]{:S(2)}) collective-permute-start(f32[128,256]{1,0:T(8,128)S(1)} %add.9), channel_id=1, source_target_pairs={{0,24},{24,0},{8,16},{16,8},{1,25},{25,1},{9,17},{17,9},{2,26},{26... | collective-permute-start | bytes 393224 | tf_op jit(solution)/shard_map/ppermute | solution.py:328
  17.4 11.2 %collective-permute-start.2 = (bf16[2,912,128]{2,1,0:T(8,128)(2,1)}, bf16[2,912,128]{2,1,0:T(8,128)(2,1)S(1)}, u32[]{:S(2)}, u32[]{:S(2)}) collective-permute-start(bf16[2,912,128]{2,1,0:T(8,128)(2,1)} %get-tuple-element.53), channel_id=1, source_target_pairs={{0,2},{1,33},{2,4},{3,35},{4,6},{5,37},{6,0},{7,39},{32,34},{33,65... | collective-permute-start | bytes 1400840 | tf_op jit(solution)/shard_map/ppermute | solution.py:59
  20.8 9.0 %collective-permute-start.7 = (bf16[2,912,128]{2,1,0:T(8,128)(2,1)}, bf16[2,912,128]{2,1,0:T(8,128)(2,1)S(1)}, u32[]{:S(2)}, u32[]{:S(2)}) collective-permute-start(bf16[2,912,128]{2,1,0:T(8,128)(2,1)} %get-tuple-element.59), channel_id=1, source_target_pairs={{0,6},{1,97},{2,0},{3,99},{4,2},{5,101},{6,4},{7,103},{32,38},{33,... | collective-permute-start | bytes 1400840 | tf_op jit(solution)/shard_map/ppermute | solution.py:59
  22.5 1.3 %collective-permute-start.5 = (bf16[128,256]{1,0:T(8,128)(2,1)S(1)}, bf16[128,256]{1,0:T(8,128)(2,1)S(1)}, u32[]{:S(2)}, u32[]{:S(2)}) collective-permute-start(bf16[128,256]{1,0:T(8,128)(2,1)S(1)} %add_convert_fusion), channel_id=1, source_target_pairs={{0,1},{1,0},{2,3},{3,2},{4,5},{5,4},{6,7},{7,6},{8,9},{9,8},{10,11... | collective-permute-start | bytes 196616 | tf_op jit(solution)/shard_map/ppermute | solution.py:332
  23.9 10.0 %collective-permute-start.8 = (bf16[256,256]{1,0:T(8,128)(2,1)S(1)}, bf16[256,256]{1,0:T(8,128)(2,1)S(1)}, u32[]{:S(2)}, u32[]{:S(2)}) collective-permute-start(bf16[256,256]{1,0:T(8,128)(2,1)S(1)} %pad_maximum_fusion.rest_4_), channel_id=1, source_target_pairs={{0,2},{1,33},{2,4},{3,35},{4,6},{5,37},{6,0},{7,39},{32,34},{33,65... | collective-permute-start | bytes 393224 | tf_op jit(solution)/shard_map/ppermute | solution.py:59
  24.3 9.6 %collective-permute-start.9 = (bf16[256,256]{1,0:T(8,128)(2,1)S(1)}, bf16[256,256]{1,0:T(8,128)(2,1)S(1)}, u32[]{:S(2)}, u32[]{:S(2)}) collective-permute-start(bf16[256,256]{1,0:T(8,128)(2,1)S(1)} %pad_maximum_fusion.rest_4_), channel_id=1, source_target_pairs={{0,4},{1,65},{2,6},{3,67},{4,0},{5,69},{6,2},{7,71},{32,36},{33,97... | collective-permute-start | bytes 393224 | tf_op jit(solution)/shard_map/ppermute | solution.py:59
  27.2 6.7 %collective-permute-start.10 = (bf16[256,256]{1,0:T(8,128)(2,1)S(1)}, bf16[256,256]{1,0:T(8,128)(2,1)S(1)}, u32[]{:S(2)}, u32[]{:S(2)}) collective-permute-start(bf16[256,256]{1,0:T(8,128)(2,1)S(1)} %pad_maximum_fusion.rest_4_), channel_id=1, source_target_pairs={{0,6},{1,97},{2,0},{3,99},{4,2},{5,101},{6,4},{7,103},{32,38},{33,... | collective-permute-start | bytes 393224 | tf_op jit(solution)/shard_map/ppermute | solution.py:59
  28.6 16.8 %collective-permute-start.11 = (bf16[2,304,128]{2,1,0:T(8,128)(2,1)S(1)}, bf16[2,304,128]{2,1,0:T(8,128)(2,1)S(1)}, u32[]{:S(2)}, u32[]{:S(2)}) collective-permute-start(bf16[2,304,128]{2,1,0:T(8,128)(2,1)S(1)} %copy-done.9), channel_id=1, source_target_pairs={{0,2},{1,33},{2,4},{3,35},{4,6},{5,37},{6,0},{7,39},{32,34},{33,65... | collective-permute-start | bytes 466952 | tf_op jit(solution)/shard_map/ppermute | solution.py:59
  29.8 15.6 %collective-permute-start.12 = (bf16[2,304,128]{2,1,0:T(8,128)(2,1)}, bf16[2,304,128]{2,1,0:T(8,128)(2,1)S(1)}, u32[]{:S(2)}, u32[]{:S(2)}) collective-permute-start(bf16[2,304,128]{2,1,0:T(8,128)(2,1)} %get-tuple-element.67), channel_id=1, source_target_pairs={{0,6},{1,97},{2,0},{3,99},{4,2},{5,101},{6,4},{7,103},{32,38},{33,... | collective-permute-start | bytes 466952 | tf_op jit(solution)/shard_map/ppermute | solution.py:59
  39.0 11.9 %copy-start.17 = (s32[1,231]{1,0:T(1,128)S(1)}, s32[1,231]{1,0:T(1,128)}, u32[]{:S(2)}) copy-start(s32[1,231]{1,0:T(1,128)} %param.21) | copy-start | bytes 2776
  39.0 11.9 %copy-start.18 = (s32[1,64]{1,0:T(1,128)S(1)}, s32[1,64]{1,0:T(1,128)}, u32[]{:S(2)}) copy-start(s32[1,64]{1,0:T(1,128)} %param.20) | copy-start | bytes 772
  39.0 12.0 %copy-start.16 = (s32[4096]{0:T(1024)S(1)}, s32[4096]{0:T(1024)}, u32[]{:S(2)}) copy-start(s32[4096]{0:T(1024)} %param.22) | copy-start | bytes 49156
  39.0 12.1 %copy-start.14 = (f32[1,231,128]{2,0,1:T(1,128)S(1)}, f32[1,231,128]{2,0,1:T(1,128)}, u32[]{:S(2)}) copy-start(f32[1,231,128]{2,0,1:T(1,128)} %param.19) | copy-start | bytes 354820
  39.0 12.1 %copy-start.15 = (f32[1,231,128]{2,0,1:T(1,128)S(1)}, f32[1,231,128]{2,0,1:T(1,128)}, u32[]{:S(2)}) copy-start(f32[1,231,128]{2,0,1:T(1,128)} %param.18) | copy-start | bytes 354820
  39.0 12.1 %collective-permute-start.13 = (bf16[304,512]{1,0:T(8,128)(2,1)}, bf16[304,512]{1,0:T(8,128)(2,1)S(1)}, u32[]{:S(2)}, u32[]{:S(2)}) collective-permute-start(bf16[304,512]{1,0:T(8,128)(2,1)} %get-tuple-element.63), channel_id=1, source_target_pairs={{0,64},{1,5},{2,66},{3,7},{4,68},{5,1},{6,70},{7,3},{32,96},{33,37... | collective-permute-start | bytes 933896 | tf_op jit(solution)/shard_map/ppermute | solution.py:63
  42.1 9.0 %collective-permute-start.14 = (bf16[304,512]{1,0:T(8,128)(2,1)}, bf16[304,512]{1,0:T(8,128)(2,1)S(1)}, u32[]{:S(2)}, u32[]{:S(2)}) collective-permute-start(bf16[304,512]{1,0:T(8,128)(2,1)} %get-tuple-element.62), channel_id=1, source_target_pairs={{0,32},{1,3},{2,34},{3,5},{4,36},{5,7},{6,38},{7,1},{32,64},{33,35... | collective-permute-start | bytes 933896 | tf_op jit(solution)/shard_map/ppermute | solution.py:63
  42.7 8.4 %collective-permute-start.15 = (bf16[304,512]{1,0:T(8,128)(2,1)}, bf16[304,512]{1,0:T(8,128)(2,1)S(1)}, u32[]{:S(2)}, u32[]{:S(2)}) collective-permute-start(bf16[304,512]{1,0:T(8,128)(2,1)} %get-tuple-element.64), channel_id=1, source_target_pairs={{0,96},{1,7},{2,98},{3,1},{4,100},{5,3},{6,102},{7,5},{32,0},{33,3... | collective-permute-start | bytes 933896 | tf_op jit(solution)/shard_map/ppermute | solution.py:63
  52.4 1.2 %collective-permute-start.16 = (f32[16,512]{1,0:T(8,128)S(1)}, f32[16,512]{1,0:T(8,128)S(1)}, u32[]{:S(2)}, u32[]{:S(2)}) collective-permute-start(f32[16,512]{1,0:T(8,128)S(1)} %shard_map.123), channel_id=1, source_target_pairs={{0,1},{1,0},{2,3},{3,2},{4,5},{5,4},{6,7},{7,6},{8,9},{9,8},{10,11... | collective-permute-start | bytes 98312 | tf_op jit(solution)/shard_map/ppermute | solution.py:372
  (14 other events, 66.3 us)

commit v10 on v9

v10 whole, which is shorter than its diff:
```python
import functools
import math

import jax
import jax.numpy as jnp
from jax import lax
from jax.experimental import pallas as pl
from jax.experimental.pallas import tpu as pltpu
from jax.sharding import Mesh, PartitionSpec as P

MODEL_WIDTH = 8192
HIDDEN_WIDTH = 29568
RANK = 128
BANK = 16
EXAMPLES = 4
UP_ROWS = 231
DOWN_ROWS = 64
WINDOW = 256
HELD = 240
ROWS = HELD + DOWN_ROWS
FIRST = 3 * ROWS
PARTED = (1, 3)
LOCAL_UP = 7392
PAIR = 2 * RANK
WIDE = EXAMPLES * RANK
BF = jnp.bfloat16
F32 = jnp.float32
VMEM = pl.BlockSpec(memory_space=pltpu.VMEM)
ANY = pl.BlockSpec(memory_space=pl.ANY)
SMEM = pl.BlockSpec(memory_space=pltpu.SMEM)
PLANE = ("ex", "py", "co")


def window_start(owner):
    return jnp.minimum((owner * UP_ROWS) // 16 * 16, LOCAL_UP - WINDOW)


def along(position, shift):
    x, y, c = position
    return (x, (y + shift) % 4, 0) if c == 0 else ((x + shift) % 4, y, 1)


def across(position, shift):
    x, y, c = position
    return ((x + shift) % 4, y, 0) if c == 0 else (x, (y + shift) % 4, 1)


def flat(position):
    return position[0] * 8 + position[1] * 2 + position[2]


def pairs(move):
    everyone = [(x, y, c) for x in range(4) for y in range(4) for c in range(2)]
    return [(flat(p), flat(move(p))) for p in everyone]


def send_same(value, shift):
    return lax.ppermute(value, PLANE, pairs(lambda p: along(p, shift)))


def send_across(value, shift):
    return lax.ppermute(value, PLANE, pairs(lambda p: across(p, shift)))


def position():
    return lax.axis_index("ex"), lax.axis_index("py"), lax.axis_index("co")


def tie(value, arrived):
    return lax.optimization_barrier((value, arrived))


def pack_kernel(grad, tokens, *rest):
    give, mine, turned = rest[0], rest[1:5], rest[5]
    x, y, c = position()
    turned[...] = tokens[...].T
    for slot in (2, 6, 1, 5, 3, 7, 0, 4):
        target = 1 - c if slot < 4 else c
        k = slot % 4
        for i in range(4):
            to_x = lax.rem(x + jnp.where(target == 0, i, k), 4)
            to_y = lax.rem(y + jnp.where(target == 0, k, i), 4)
            owner = to_x * 8 + to_y * 2 + target
            start = pl.multiple_of(window_start(owner), 16)
            column = pl.multiple_of(owner * DOWN_ROWS, DOWN_ROWS)
            window_at, down_at = ((i - 1) * HELD, 3 * HELD + (i - 1) * DOWN_ROWS) if i else (FIRST, FIRST + HELD)
            out = give.at[k] if slot < 4 else mine[k]
            window = pltpu.roll(grad[pl.ds(start, WINDOW), :].astype(F32), WINDOW + start - owner * UP_ROWS, 0)
            out[window_at:window_at + HELD, :] = window[:HELD].astype(BF)
            out[down_at:down_at + DOWN_ROWS, :] = turned[pl.ds(column, DOWN_ROWS), :]


def product_kernel(grad, tokens, down, up, portion_ref):
    portion_ref[:, :RANK] = jnp.dot(tokens[...], down[...], preferred_element_type=F32)
    product = jnp.zeros((128, RANK), F32)
    for begin in range(0, LOCAL_UP, 1024):
        end = min(begin + 1024, LOCAL_UP)
        product += lax.dot_general(
            grad[begin:end, :], up[begin:end, :], (((0,), (0,)), ((), ())), preferred_element_type=F32
        )
    portion_ref[:, RANK:] = product


def fill_kernel(shifts, taken_ref, *rest):
    mine, buffers = rest[:len(shifts)], rest[len(shifts):]
    at = 0
    for n, k in enumerate(shifts):
        for begin, size in ((0, FIRST), (FIRST, ROWS)) if k in PARTED else ((0, 4 * ROWS),):
            buffers[at][0] = mine[n][begin:begin + size, :]
            buffers[at][1] = taken_ref[k, begin:begin + size, :]
            at += 1


def fill_call(shifts, taken, mine):
    sizes = [size for k in shifts for size in ((FIRST, ROWS) if k in PARTED else (4 * ROWS,))]
    return pl.pallas_call(
        functools.partial(fill_kernel, shifts),
        out_shape=[jax.ShapeDtypeStruct((2, size, 128), BF) for size in sizes],
        in_specs=[VMEM] * (1 + len(shifts)),
        out_specs=[VMEM] * len(sizes),
        compiler_params=pltpu.CompilerParams(vmem_limit_bytes=16 << 20),
        cost_estimate=pl.CostEstimate(flops=0, bytes_accessed=1 << 20, transcendentals=0),
    )(taken, *mine)


def partial_kernel(count, segments, *rest):
    columns, inner, outs = rest[0:4], rest[4:8], rest[8:8 + count]
    right_h, right_u, total = rest[8 + count:]
    x, y, c = position()
    split = count * HELD
    for k in range(4):
        chip = jnp.where(c == 0, x * 4 + lax.rem(y - k + 4, 4), lax.rem(x - k + 4, 4) * 4 + y)
        for part in range(2):
            labels = segments[pl.ds(2 * chip + jnp.where(part == 0, c, 1 - c), 1), :]
            labels = jnp.broadcast_to(labels.astype(F32), (128, RANK)).T
            rows = pl.ds(k * PAIR + part * 128, 128)
            h = inner[k][part * 128:(part + 1) * 128, :RANK]
            u = inner[k][part * 128:(part + 1) * 128, RANK:]
            for e in range(EXAMPLES):
                mask = jnp.where(labels == e, 1.0, 0.0).astype(BF)
                right_h[rows, e * RANK:(e + 1) * RANK] = h * mask
                right_u[rows, e * RANK:(e + 1) * RANK] = u * mask
        begin = FIRST if count == 1 and k not in PARTED else 0
        both = pl.ds(k * PAIR, PAIR)
        for n in range(count + 1):
            at, size = (n * HELD, HELD) if n < count else (split, count * DOWN_ROWS)
            pieces = [columns[k][part, begin + at:begin + at + size, :] for part in range(2)]
            right = (right_h if n < count else right_u)[both, :]
            product = jnp.dot(jnp.concatenate(pieces, axis=1), right, preferred_element_type=F32)
            total[at:at + size, :] = product if k == 0 else total[at:at + size, :] + product
    for n in range(count):
        outs[n][:HELD, :] = total[n * HELD:(n + 1) * HELD, :].astype(BF)
        outs[n][HELD:, :] = total[split + n * DOWN_ROWS:split + (n + 1) * DOWN_ROWS, :].astype(BF)


def partial_call(count, labels, columns, inner):
    return pl.pallas_call(
        functools.partial(partial_kernel, count),
        out_shape=[jax.ShapeDtypeStruct((ROWS, WIDE), BF)] * count,
        in_specs=[VMEM] * 9,
        out_specs=[VMEM] * count,
        scratch_shapes=[
            pltpu.VMEM((1024, WIDE), BF),
            pltpu.VMEM((1024, WIDE), BF),
            pltpu.VMEM((count * ROWS, WIDE), F32),
        ],
        compiler_params=pltpu.CompilerParams(vmem_limit_bytes=24 << 20),
        cost_estimate=pl.CostEstimate(flops=2 * count * ROWS * 1024 * WIDE, bytes_accessed=6 << 20, transcendentals=0),
    )(labels, *columns, *inner)


def feature_kernel(
    own_ref, a_ref, b_ref, c_ref, bounds_ref, select_ref,
    first_up, first_down, second_up, second_down, out_ref, first_ref, second_ref,
):
    for up, down, space in ((first_up, first_down, first_ref), (second_up, second_down, second_ref)):
        space[HELD - 16:HELD, :] = jnp.zeros((16, RANK), F32)
        space[:UP_ROWS, :] = up[...]
        space[HELD:, :] = down[...]
    first = 0.9 * first_ref[...]
    second = 0.999 * second_ref[...]
    select = select_ref[...]
    for e in range(EXAMPLES):
        at = pl.ds(e * RANK, RANK)
        length = (bounds_ref[e + 1] - bounds_ref[e]).astype(F32)
        total = (own_ref[:, at].astype(F32) + a_ref[:, at].astype(F32)) + (b_ref[:, at].astype(F32) + c_ref[:, at].astype(F32))
        grad = total / length
        feature = (first + 0.1 * grad) / (jnp.sqrt(second + 0.001 * grad * grad) + 1e-08)
        high = feature.astype(BF)
        low = (feature - high.astype(F32)).astype(BF)
        out_ref[:, at] = jnp.dot(select, high, preferred_element_type=F32) + jnp.dot(
            select, low, preferred_element_type=F32
        )


EVERY = ("ex", "t1", "t0", "py", "co")


def groups(along_x):
    found = []
    for fixed in range(4):
        for c in range(2):
            for zs in ((0, 1), (2, 3)) if along_x else ((0, 3), (1, 2)):
                found.append(
                    [
                        (((x * 4 + z) * 4) + y) * 2 + c
                        for w in range(4)
                        for z in zs
                        for x, y in [(w, fixed) if along_x else (fixed, w)]
                    ]
                )
    return found


def spread_sum(value, along_x):
    copies = jnp.broadcast_to(value[None], (8,) + value.shape)
    arrived = lax.all_to_all(
        copies, EVERY, split_axis=0, concat_axis=0, tiled=True, axis_index_groups=groups(along_x)
    )
    return jnp.sum(arrived, axis=0)


def on_device(
    tokens,
    output_gradient,
    adapter_down_factor,
    adapter_up_factor,
    first_moment_down,
    second_moment_down,
    first_moment_up,
    second_moment_up,
    down_row_seeds,
    up_row_seeds,
    segments,
    bank,
):
    turned_grad = output_gradient.T
    give, *mine = pl.pallas_call(
        pack_kernel,
        out_shape=[jax.ShapeDtypeStruct((4, 4 * ROWS, 128), BF)] + [jax.ShapeDtypeStruct((4 * ROWS, 128), BF)] * 4,
        in_specs=[VMEM] * 2,
        out_specs=[VMEM] * 5,
        scratch_shapes=[pltpu.VMEM((2048, 128), BF)],
        compiler_params=pltpu.CompilerParams(vmem_limit_bytes=24 << 20),
        cost_estimate=pl.CostEstimate(flops=0, bytes_accessed=5 << 20, transcendentals=0),
    )(turned_grad, tokens)
    portion = pl.pallas_call(
        product_kernel,
        out_shape=jax.ShapeDtypeStruct((128, PAIR), F32),
        in_specs=[VMEM] * 4,
        out_specs=VMEM,
        compiler_params=pltpu.CompilerParams(vmem_limit_bytes=24 << 20),
        cost_estimate=pl.CostEstimate(flops=2 * 128 * 9440 * 128, bytes_accessed=5 << 20, transcendentals=0),
    )(turned_grad, tokens, adapter_down_factor, adapter_up_factor)
    taken = lax.ppermute(give, "co", [(0, 1), (1, 0)])
    taken, portion = tie(taken, portion)
    first, second = {}, {}
    (first[2],) = fill_call((2,), taken, (mine[2],))
    first[1], second[1], first[3], second[3], first[0] = fill_call((1, 3, 0), taken, (mine[1], mine[3], mine[0]))
    peers = [lax.ppermute(portion, ("t1", "t0"), [(i, (i + shift) % 4) for i in range(4)]) for shift in (2, 1, 3)]
    for k in (2, 1, 3):
        first[k] = send_same(first[k], k)
    whole = ((portion + peers[0]) + (peers[1] + peers[2])).astype(BF)
    sibling = lax.ppermute(whole, "co", [(0, 1), (1, 0)])
    chip_inner = jnp.concatenate([whole, sibling], axis=0)
    inner = [chip_inner, None, None, None]
    for k in (2, 1):
        inner[k] = send_same(chip_inner, k)
    late, first[2] = tie(chip_inner, first[2])
    inner[3] = send_same(late, 3)
    second[1], first[1] = tie(second[1], first[1])
    second[3], first[3] = tie(second[3], first[3])
    for k in PARTED:
        second[k] = send_same(second[k], k)

    labels = segments.reshape(32, 128)
    sums = partial_call(3, labels, [first[k] for k in range(4)], inner)
    arrived = [send_across(sums[k - 1], k) for k in (2, 1, 3)]
    kept = (labels, segments, first_moment_up, second_moment_up, up_row_seeds, down_row_seeds)
    kept, sums = tie(kept, sums)
    labels, segments, first_moment_up, second_moment_up, up_row_seeds, down_row_seeds = kept
    (own,) = partial_call(1, labels, [first[0], second[1], first[2], second[3]], inner)
    own = own.astype(F32)

    bounds = jnp.sum(
        (segments[None, :] < jnp.arange(EXAMPLES + 1, dtype=jnp.int32)[:, None]).astype(jnp.int32), axis=1
    )

    seeds = jnp.concatenate([up_row_seeds[0], jnp.full((HELD - UP_ROWS,), -1, jnp.int32), down_row_seeds[0]])
    select = (jnp.arange(BANK, dtype=jnp.int32)[:, None] == seeds[None, :]).astype(BF)
    blocks = pl.pallas_call(
        feature_kernel,
        out_shape=jax.ShapeDtypeStruct((BANK, WIDE), F32),
        in_specs=[VMEM] * 4 + [SMEM] + [VMEM] * 5,
        out_specs=VMEM,
        scratch_shapes=[pltpu.VMEM((ROWS, RANK), F32), pltpu.VMEM((ROWS, RANK), F32)],
        compiler_params=pltpu.CompilerParams(vmem_limit_bytes=24 << 20),
        cost_estimate=pl.CostEstimate(flops=0, bytes_accessed=3 << 20, transcendentals=0),
    )(
        own, *arrived, bounds, select,
        first_moment_up[0], first_moment_down[0], second_moment_up[0], second_moment_down[0],
    )

    summed = blocks + lax.ppermute(blocks, "co", [(0, 1), (1, 0)])
    summed = spread_sum(summed, False)
    summed = spread_sum(summed, True)
    inverse = 1.0 / math.sqrt((MODEL_WIDTH + HIDDEN_WIDTH) * RANK)
    sketch = jnp.einsum(
        "jer,jrk->ek", summed.reshape(BANK, EXAMPLES, RANK), bank.astype(F32), precision=lax.Precision.HIGHEST
    )
    return sketch * inverse


def solution(mesh):
    rows = ("ex", "py", "co")
    tp = ("t1", "t0")
    split = Mesh(mesh.devices.reshape(4, 2, 2, 4, 2), ("ex", "t1", "t0", "py", "co"))
    return jax.shard_map(
        on_device,
        mesh=split,
        in_specs=(
            P(rows, tp),
            P(rows, tp),
            P(tp, None),
            P(tp, None),
            P(tp, rows, None),
            P(tp, rows, None),
            P(tp, rows, None),
            P(tp, rows, None),
            P(tp, rows),
            P(tp, rows),
            P(),
            P(None, None, ("ex", "t1", "t0", "py", "co")),
        ),
        out_specs=P(None, ("ex", "t1", "t0", "py", "co")),
        check_vma=False,
    )
```

time: 77.6 us -> 72.4 us (0.933)
  Pallas kernels: 16.9 us -> 5.86 us
  waiting for transfers between devices: 4.72 us -> 13.1 us
  starting transfers between devices: 28.3 us -> 25.3 us
  blocking collectives: 22.6 us -> 23.6 us
  other arithmetic: 1.35 us -> 0.39 us
    pallas_call x2, Pallas kernels: 7.37 us -> 2.16 us  [partial_call(): pl.pallas_call(functools.partial(partial_kernel, count), out_shape=[jax.S...]
    ppermute x3, waiting for transfers between devices: 0.01 us -> 5.08 us  [send_across(): return lax.ppermute(value, PLANE, pairs(lambda p: across(p, shift)))]
    pallas_call x2, Pallas kernels: 3.66 us -> 0.16 us  [fill_call(): pl.pallas_call(functools.partial(fill_kernel, shifts), out_shape=[jax.Sha...]
    ppermute x8, starting transfers between devices: 16.6 us -> 13.7 us  [send_same(): return lax.ppermute(value, PLANE, pairs(lambda p: along(p, shift)))]
    ppermute x3, waiting for transfers between devices: 0.01 us -> 2.64 us  [on_device(): lax.ppermute(portion, ('t1', 't0'), [(i, (i + shift) % 4) for i in range(...]
    pallas_call x1 -> x2, Pallas kernels: 4.65 us -> 2.31 us  [the longest x1 1.51 us: on_device(): pl.pallas_call(pack_kernel, out_shape=[jax.ShapeDtypeStruct((4, 4 * ROWS,...]
    all_to_all x2, blocking collectives: 22.6 us -> 23.6 us  [spread_sum(): lax.all_to_all(copies, EVERY, split_axis=0, concat_axis=0, tiled=True, ax...]
    convert_element_type x1, other arithmetic: 1.03 us -> 0.06 us  [on_device(): own = own.astype(F32)]
  transfers between devices with their start and end apart: 17 -> 17, of which waited for: 3 -> 10; matrix products, arithmetic and copies ran while one was open for 2% -> 1% of each run, Pallas kernels for 14% -> 4%
where the time goes in v10:
time: 72.4 us; the launch traced here: 72.1 us
  starting transfers between devices  25.3 us (35%)
  blocking collectives  23.6 us (33%)
  waiting for transfers between devices  13.1 us (18%)
  Pallas kernels  5.86 us (8%)
  local copies, waits for them, and re-layouts  2.73 us (4%)
  matrix products  0.91 us (1%)
    all_to_all x2, blocking collectives, spread_sum(): lax.all_to_all(copies, EVERY, split_axis=0, concat_axis=0, tiled=True, ax...  23.6 us
    ppermute x8, starting transfers between devices, send_same(): return lax.ppermute(value, PLANE, pairs(lambda p: along(p, shift)))  13.7 us
    ppermute x3, starting transfers between devices, on_device(): lax.ppermute(portion, ('t1', 't0'), [(i, (i + shift) % 4) for i in range(...  5.9 us
    ppermute x3, starting transfers between devices, send_across(): return lax.ppermute(value, PLANE, pairs(lambda p: across(p, shift)))  5.47 us
    ppermute x3, waiting for transfers between devices, send_across(): return lax.ppermute(value, PLANE, pairs(lambda p: across(p, shift)))  5.08 us
    unnamed x25, local copies, waits for them, and re-layouts  2.67 us
    ppermute x3, waiting for transfers between devices, on_device(): lax.ppermute(portion, ('t1', 't0'), [(i, (i + shift) % 4) for i in range(...  2.64 us
    pallas_call x2, Pallas kernels, partial_call(): pl.pallas_call(functools.partial(partial_kernel, count), out_shape=[jax.S...  2.16 us
  transfers between devices with their start and end apart: 17, of which 10 were waited for; matrix products, arithmetic and copies ran while one was open for 1% of the time, Pallas kernels for 4%

profile of v10, /device:TPU:0, one launch (start us, length us, event | category | flops | bytes accessed | tf_op | source)
XLA Modules:
  0.0 72.1 jit_solution(18433879288556204207)
XLA Ops:
  0.0 1.6 %copy-done.1 = bf16[128,7392]{0,1:T(8,128)(2,1)S(1)} copy-done((bf16[128,7392]{0,1:T(8,128)(2,1)S(1)}, bf16[128,7392]{0,1:T(8,128)(2,1)}, u32[]{:S(2)}) %copy-start.1) | copy-done | bytes 1892376
  1.6 1.0 %copy-done.2 = bf16[128,2048]{1,0:T(8,128)(2,1)S(1)} copy-done((bf16[128,2048]{1,0:T(8,128)(2,1)S(1)}, bf16[128,2048]{1,0:T(8,128)(2,1)}, u32[]{:S(2)}) %copy-start.2) | copy-done | bytes 524312
  2.6 1.5 %shard_map.118 = (bf16[4,1216,128]{2,1,0:T(8,128)(2,1)S(1)}, bf16[1216,128]{1,0:T(8,128)(2,1)S(1)}, bf16[1216,128]{1,0:T(8,128)(2,1)S(1)}, bf16[1216,128]{1,0:T(8,128)(2,1)S(1)}, bf16[1216,128]{1,0:T(8,128)(2,1)S(1)}) custom-call(bf16[7392,128]{1,0:T(8,128)(2,1)S(1)} %bitcast.16, bf16[128,2048]{1,0:T(8,128)(2,1)S(1)} %copy-done.2), custom_call_target="tpu_custom_call" | custom-call | bytes 5242880 | tf_op jit(solution)/shard_map/pallas_call | solution.py:238
  5.1 2.1 %collective-permute-done.taken_ref = bf16[4,1216,128]{2,1,0:T(8,128)(2,1)S(1)} collective-permute-done((bf16[4,1216,128]{2,1,0:T(8,128)(2,1)S(1)}, bf16[4,1216,128]{2,1,0:T(8,128)(2,1)S(1)}, u32[]{:S(2)}, u32[]{:S(2)}) %collective-permute-start) | collective-permute-done | bytes 1245216 | tf_op jit(solution)/shard_map/ppermute | solution.py:255
  7.2 3.4 %collective-permute-start.6 = (bf16[2,1216,128]{2,1,0:T(8,128)(2,1)S(1)}, bf16[2,1216,128]{2,1,0:T(8,128)(2,1)S(1)}, u32[]{:S(2)}, u32[]{:S(2)}) collective-permute-start(bf16[2,1216,128]{2,1,0:T(8,128)(2,1)S(1)} %shard_map.121), channel_id=1, source_target_pairs={{0,4},{1,65},{2,6},{3,67},{4,0},{5,69},{6,2},{7,71},{32,36},{33,97... | collective-permute-start | bytes 1867784 | tf_op jit(solution)/shard_map/ppermute | solution.py:58
  10.6 1.9 %collective-permute-start.3 = (f32[128,256]{1,0:T(8,128)S(1)}, f32[128,256]{1,0:T(8,128)S(1)}, u32[]{:S(2)}, u32[]{:S(2)}) collective-permute-start(f32[128,256]{1,0:T(8,128)S(1)} %shard_map.119), channel_id=1, source_target_pairs={{0,8},{8,16},{16,24},{24,0},{1,9},{9,17},{17,25},{25,1},{2,10},{10... | collective-permute-start | bytes 393224 | tf_op jit(solution)/shard_map/ppermute | solution.py:260
  12.5 2.1 %collective-permute-start.4 = (f32[128,256]{1,0:T(8,128)S(1)}, f32[128,256]{1,0:T(8,128)S(1)}, u32[]{:S(2)}, u32[]{:S(2)}) collective-permute-start(f32[128,256]{1,0:T(8,128)S(1)} %shard_map.119), channel_id=1, source_target_pairs={{0,24},{8,0},{16,8},{24,16},{1,25},{9,1},{17,9},{25,17},{2,26},{10... | collective-permute-start | bytes 393224 | tf_op jit(solution)/shard_map/ppermute | solution.py:260
  14.6 1.9 %collective-permute-start.2 = (f32[128,256]{1,0:T(8,128)S(1)}, f32[128,256]{1,0:T(8,128)S(1)}, u32[]{:S(2)}, u32[]{:S(2)}) collective-permute-start(f32[128,256]{1,0:T(8,128)S(1)} %shard_map.119), channel_id=1, source_target_pairs={{0,16},{8,24},{16,0},{24,8},{1,17},{9,25},{17,1},{25,9},{2,18},{10... | collective-permute-start | bytes 393224 | tf_op jit(solution)/shard_map/ppermute | solution.py:260
  18.0 2.0 %collective-permute-start.7 = (bf16[2,912,128]{2,1,0:T(8,128)(2,1)S(1)}, bf16[2,912,128]{2,1,0:T(8,128)(2,1)S(1)}, u32[]{:S(2)}, u32[]{:S(2)}) collective-permute-start(bf16[2,912,128]{2,1,0:T(8,128)(2,1)S(1)} %get-tuple-element.45), channel_id=1, source_target_pairs={{0,6},{1,97},{2,0},{3,99},{4,2},{5,101},{6,4},{7,103},{32,38},{33,... | collective-permute-start | bytes 1400840 | tf_op jit(solution)/shard_map/ppermute | solution.py:58
  20.1 1.9 %collective-permute-done.2 = f32[128,256]{1,0:T(8,128)S(1)} collective-permute-done((f32[128,256]{1,0:T(8,128)S(1)}, f32[128,256]{1,0:T(8,128)S(1)}, u32[]{:S(2)}, u32[]{:S(2)}) %collective-permute-start.2) | collective-permute-done | bytes 131104 | tf_op jit(solution)/shard_map/ppermute | solution.py:260
  22.1 1.2 %collective-permute-done.5 = bf16[128,256]{1,0:T(8,128)(2,1)S(1)} collective-permute-done((bf16[128,256]{1,0:T(8,128)(2,1)S(1)}, bf16[128,256]{1,0:T(8,128)(2,1)S(1)}, u32[]{:S(2)}, u32[]{:S(2)}) %collective-permute-start.5) | collective-permute-done | bytes 65568 | tf_op jit(solution)/shard_map/ppermute | solution.py:264
  23.3 1.6 %collective-permute-start.8 = (bf16[256,256]{1,0:T(8,128)(2,1)S(1)}, bf16[256,256]{1,0:T(8,128)(2,1)S(1)}, u32[]{:S(2)}, u32[]{:S(2)}) collective-permute-start(bf16[256,256]{1,0:T(8,128)(2,1)S(1)} %pad_maximum_fusion.rest_4_), channel_id=1, source_target_pairs={{0,2},{1,33},{2,4},{3,35},{4,6},{5,37},{6,0},{7,39},{32,34},{33,65... | collective-permute-start | bytes 393224 | tf_op jit(solution)/shard_map/ppermute | solution.py:58
  25.0 1.7 %collective-permute-start.9 = (bf16[256,256]{1,0:T(8,128)(2,1)S(1)}, bf16[256,256]{1,0:T(8,128)(2,1)S(1)}, u32[]{:S(2)}, u32[]{:S(2)}) collective-permute-start(bf16[256,256]{1,0:T(8,128)(2,1)S(1)} %pad_maximum_fusion.rest_4_), channel_id=1, source_target_pairs={{0,4},{1,65},{2,6},{3,67},{4,0},{5,69},{6,2},{7,71},{32,36},{33,97... | collective-permute-start | bytes 393224 | tf_op jit(solution)/shard_map/ppermute | solution.py:58
  26.7 1.1 %collective-permute-start.10 = (bf16[256,256]{1,0:T(8,128)(2,1)S(1)}, bf16[256,256]{1,0:T(8,128)(2,1)S(1)}, u32[]{:S(2)}, u32[]{:S(2)}) collective-permute-start(bf16[256,256]{1,0:T(8,128)(2,1)S(1)} %pad_maximum_fusion.rest_4_), channel_id=1, source_target_pairs={{0,6},{1,97},{2,0},{3,99},{4,2},{5,101},{6,4},{7,103},{32,38},{33,... | collective-permute-start | bytes 393224 | tf_op jit(solution)/shard_map/ppermute | solution.py:58
  28.7 2.3 %collective-permute-start.12 = (bf16[2,304,128]{2,1,0:T(8,128)(2,1)S(1)}, bf16[2,304,128]{2,1,0:T(8,128)(2,1)S(1)}, u32[]{:S(2)}, u32[]{:S(2)}) collective-permute-start(bf16[2,304,128]{2,1,0:T(8,128)(2,1)S(1)} %get-tuple-element.53), channel_id=1, source_target_pairs={{0,6},{1,97},{2,0},{3,99},{4,2},{5,101},{6,4},{7,103},{32,38},{33,... | collective-permute-start | bytes 466952 | tf_op jit(solution)/shard_map/ppermute | solution.py:58
  31.8 1.3 %shard_map.122 = (bf16[304,512]{1,0:T(8,128)(2,1)S(1)}, bf16[304,512]{1,0:T(8,128)(2,1)S(1)}, bf16[304,512]{1,0:T(8,128)(2,1)S(1)}) custom-call(s32[32,128]{1,0:T(8,128)S(1)} %bitcast.18, bf16[2,1216,128]{2,1,0:T(8,128)(2,1)S(1)} %get-tuple-element.37.rest_0_, bf16[2,912,128]{2,1,0:T(8,128)(2,1)S(1)} %collective-permute-done.1.rest_1_, ...), custom_call_target="tpu_custom_call" | custom-call | flops 956301312 | bytes 6291456 | tf_op jit(solution)/shard_map/pallas_call | solution.py:157
  33.2 2.2 %collective-permute-start.13 = (bf16[304,512]{1,0:T(8,128)(2,1)S(1)}, bf16[304,512]{1,0:T(8,128)(2,1)S(1)}, u32[]{:S(2)}, u32[]{:S(2)}) collective-permute-start(bf16[304,512]{1,0:T(8,128)(2,1)S(1)} %get-tuple-element.49), channel_id=1, source_target_pairs={{0,64},{1,5},{2,66},{3,7},{4,68},{5,1},{6,70},{7,3},{32,96},{33,37... | collective-permute-start | bytes 933896 | tf_op jit(solution)/shard_map/ppermute | solution.py:62
  36.3 2.4 %collective-permute-start.15 = (bf16[304,512]{1,0:T(8,128)(2,1)S(1)}, bf16[304,512]{1,0:T(8,128)(2,1)S(1)}, u32[]{:S(2)}, u32[]{:S(2)}) collective-permute-start(bf16[304,512]{1,0:T(8,128)(2,1)S(1)} %get-tuple-element.50), channel_id=1, source_target_pairs={{0,96},{1,7},{2,98},{3,1},{4,100},{5,3},{6,102},{7,5},{32,0},{33,3... | collective-permute-start | bytes 933896 | tf_op jit(solution)/shard_map/ppermute | solution.py:62
  39.9 1.9 %collective-permute-done.13.a_ref = bf16[304,512]{1,0:T(8,128)(2,1)S(1)} collective-permute-done((bf16[304,512]{1,0:T(8,128)(2,1)S(1)}, bf16[304,512]{1,0:T(8,128)(2,1)S(1)}, u32[]{:S(2)}, u32[]{:S(2)}) %collective-permute-start.13) | collective-permute-done | bytes 311328 | tf_op jit(solution)/shard_map/ppermute | solution.py:62
  41.8 3.2 %collective-permute-done.14.b_ref = bf16[304,512]{1,0:T(8,128)(2,1)S(1)} collective-permute-done((bf16[304,512]{1,0:T(8,128)(2,1)S(1)}, bf16[304,512]{1,0:T(8,128)(2,1)S(1)}, u32[]{:S(2)}, u32[]{:S(2)}) %collective-permute-start.14) | collective-permute-done | bytes 311328 | tf_op jit(solution)/shard_map/ppermute | solution.py:62
  45.0 1.2 %shard_map.124 = f32[16,512]{1,0:T(8,128)S(1)} custom-call(f32[304,512]{1,0:T(8,128)S(1)} %convert_element_type.14.own_ref, bf16[304,512]{1,0:T(8,128)(2,1)S(1)} %collective-permute-done.13.a_ref, bf16[304,512]{1,0:T(8,128)(2,1)S(1)} %collective-permute-done.14.b_ref, bf16[304,512]{1,0:T(8,128)(2,1)S(1)} %collective-permute-done.15.c_ref, ...), custom_call_target="tpu_custom_call" | custom-call | bytes 3145728 | tf_op jit(solution)/shard_map/pallas_call | solution.py:291
  46.3 1.2 %collective-permute-done.16 = f32[16,512]{1,0:T(8,128)S(1)} collective-permute-done((f32[16,512]{1,0:T(8,128)S(1)}, f32[16,512]{1,0:T(8,128)S(1)}, u32[]{:S(2)}, u32[]{:S(2)}) %collective-permute-start.16) | collective-permute-done | bytes 32800 | tf_op jit(solution)/shard_map/ppermute | solution.py:304
  47.5 13.5 %all_to_all.10 = f32[8,16,512]{2,1,0:T(8,128)S(1)} all-to-all(f32[8,16,512]{2,1,0:T(8,128)S(1)} %broadcast_in_dim.4), channel_id=1, replica_groups={{0,24,2,26,4,28,6,30},{8,16,10,18,12,20,14,22},{1,25,3,27,5,29,7,31},{9..., dimensions={0} | all-to-all | bytes 524288 | tf_op jit(solution)/shard_map/all_to_all | solution.py:217
  61.0 10.1 %all_to_all.11 = f32[8,16,512]{2,1,0:T(8,128)S(1)} all-to-all(f32[8,16,512]{2,1,0:T(8,128)S(1)} %broadcast_in_dim.5), channel_id=1, replica_groups={{0,8,32,40,64,72,96,104},{16,24,48,56,80,88,112,120},{1,9,33,41,65,73,9..., dimensions={0} | all-to-all | bytes 524288 | tf_op jit(solution)/shard_map/all_to_all | solution.py:217
  (58 shorter events, 7.6 us)
Async XLA Ops:
  0.0 71.2 %copy-start = (bf16[16,128,64]{1,2,0:T(8,128)(2,1)S(1)}, bf16[16,128,64]{1,2,0:T(8,128)(2,1)}, u32[]{:S(2)}) copy-start(bf16[16,128,64]{1,2,0:T(8,128)(2,1)} %param.23) | copy-start | bytes 786436
  4.1 3.0 %collective-permute-start = (bf16[4,1216,128]{2,1,0:T(8,128)(2,1)S(1)}, bf16[4,1216,128]{2,1,0:T(8,128)(2,1)S(1)}, u32[]{:S(2)}, u32[]{:S(2)}) collective-permute-start(bf16[4,1216,128]{2,1,0:T(8,128)(2,1)S(1)} %get-tuple-element.32), channel_id=1, source_target_pairs={{0,1},{1,0},{2,3},{3,2},{4,5},{5,4},{6,7},{7,6},{8,9},{9,8},{10,11... | collective-permute-start | bytes 3735560 | tf_op jit(solution)/shard_map/ppermute | solution.py:255
  7.2 24.6 %copy-start.5 = (s32[4096]{0:T(1024)S(1)}, s32[4096]{0:T(1024)}, u32[]{:S(2)}) copy-start(s32[4096]{0:T(1024)} %param.22) | copy-start | bytes 49156
  7.2 19.5 %collective-permute-start.6 = (bf16[2,1216,128]{2,1,0:T(8,128)(2,1)S(1)}, bf16[2,1216,128]{2,1,0:T(8,128)(2,1)S(1)}, u32[]{:S(2)}, u32[]{:S(2)}) collective-permute-start(bf16[2,1216,128]{2,1,0:T(8,128)(2,1)S(1)} %shard_map.121), channel_id=1, source_target_pairs={{0,4},{1,65},{2,6},{3,67},{4,0},{5,69},{6,2},{7,71},{32,36},{33,97... | collective-permute-start | bytes 1867784 | tf_op jit(solution)/shard_map/ppermute | solution.py:58
  10.6 7.4 %collective-permute-start.3 = (f32[128,256]{1,0:T(8,128)S(1)}, f32[128,256]{1,0:T(8,128)S(1)}, u32[]{:S(2)}, u32[]{:S(2)}) collective-permute-start(f32[128,256]{1,0:T(8,128)S(1)} %shard_map.119), channel_id=1, source_target_pairs={{0,8},{8,16},{16,24},{24,0},{1,9},{9,17},{17,25},{25,1},{2,10},{10... | collective-permute-start | bytes 393224 | tf_op jit(solution)/shard_map/ppermute | solution.py:260
  12.5 7.6 %collective-permute-start.4 = (f32[128,256]{1,0:T(8,128)S(1)}, f32[128,256]{1,0:T(8,128)S(1)}, u32[]{:S(2)}, u32[]{:S(2)}) collective-permute-start(f32[128,256]{1,0:T(8,128)S(1)} %shard_map.119), channel_id=1, source_target_pairs={{0,24},{8,0},{16,8},{24,16},{1,25},{9,1},{17,9},{25,17},{2,26},{10... | collective-permute-start | bytes 393224 | tf_op jit(solution)/shard_map/ppermute | solution.py:260
  14.6 7.3 %collective-permute-start.2 = (f32[128,256]{1,0:T(8,128)S(1)}, f32[128,256]{1,0:T(8,128)S(1)}, u32[]{:S(2)}, u32[]{:S(2)}) collective-permute-start(f32[128,256]{1,0:T(8,128)S(1)} %shard_map.119), channel_id=1, source_target_pairs={{0,16},{8,24},{16,0},{24,8},{1,17},{9,25},{17,1},{25,9},{2,18},{10... | collective-permute-start | bytes 393224 | tf_op jit(solution)/shard_map/ppermute | solution.py:260
  16.6 11.2 %collective-permute-start.1 = (bf16[2,912,128]{2,1,0:T(8,128)(2,1)S(1)}, bf16[2,912,128]{2,1,0:T(8,128)(2,1)S(1)}, u32[]{:S(2)}, u32[]{:S(2)}) collective-permute-start(bf16[2,912,128]{2,1,0:T(8,128)(2,1)S(1)} %get-tuple-element.39), channel_id=1, source_target_pairs={{0,2},{1,33},{2,4},{3,35},{4,6},{5,37},{6,0},{7,39},{32,34},{33,65... | collective-permute-start | bytes 1400840 | tf_op jit(solution)/shard_map/ppermute | solution.py:58
  18.0 9.8 %collective-permute-start.7 = (bf16[2,912,128]{2,1,0:T(8,128)(2,1)S(1)}, bf16[2,912,128]{2,1,0:T(8,128)(2,1)S(1)}, u32[]{:S(2)}, u32[]{:S(2)}) collective-permute-start(bf16[2,912,128]{2,1,0:T(8,128)(2,1)S(1)} %get-tuple-element.45), channel_id=1, source_target_pairs={{0,6},{1,97},{2,0},{3,99},{4,2},{5,101},{6,4},{7,103},{32,38},{33,... | collective-permute-start | bytes 1400840 | tf_op jit(solution)/shard_map/ppermute | solution.py:58
  22.0 1.3 %collective-permute-start.5 = (bf16[128,256]{1,0:T(8,128)(2,1)S(1)}, bf16[128,256]{1,0:T(8,128)(2,1)S(1)}, u32[]{:S(2)}, u32[]{:S(2)}) collective-permute-start(bf16[128,256]{1,0:T(8,128)(2,1)S(1)} %add_convert_fusion), channel_id=1, source_target_pairs={{0,1},{1,0},{2,3},{3,2},{4,5},{5,4},{6,7},{7,6},{8,9},{9,8},{10,11... | collective-permute-start | bytes 196616 | tf_op jit(solution)/shard_map/ppermute | solution.py:264
  23.3 7.7 %collective-permute-start.8 = (bf16[256,256]{1,0:T(8,128)(2,1)S(1)}, bf16[256,256]{1,0:T(8,128)(2,1)S(1)}, u32[]{:S(2)}, u32[]{:S(2)}) collective-permute-start(bf16[256,256]{1,0:T(8,128)(2,1)S(1)} %pad_maximum_fusion.rest_4_), channel_id=1, source_target_pairs={{0,2},{1,33},{2,4},{3,35},{4,6},{5,37},{6,0},{7,39},{32,34},{33,65... | collective-permute-start | bytes 393224 | tf_op jit(solution)/shard_map/ppermute | solution.py:58
  25.0 6.5 %collective-permute-start.9 = (bf16[256,256]{1,0:T(8,128)(2,1)S(1)}, bf16[256,256]{1,0:T(8,128)(2,1)S(1)}, u32[]{:S(2)}, u32[]{:S(2)}) collective-permute-start(bf16[256,256]{1,0:T(8,128)(2,1)S(1)} %pad_maximum_fusion.rest_4_), channel_id=1, source_target_pairs={{0,4},{1,65},{2,6},{3,67},{4,0},{5,69},{6,2},{7,71},{32,36},{33,97... | collective-permute-start | bytes 393224 | tf_op jit(solution)/shard_map/ppermute | solution.py:58
  26.7 5.2 %collective-permute-start.10 = (bf16[256,256]{1,0:T(8,128)(2,1)S(1)}, bf16[256,256]{1,0:T(8,128)(2,1)S(1)}, u32[]{:S(2)}, u32[]{:S(2)}) collective-permute-start(bf16[256,256]{1,0:T(8,128)(2,1)S(1)} %pad_maximum_fusion.rest_4_), channel_id=1, source_target_pairs={{0,6},{1,97},{2,0},{3,99},{4,2},{5,101},{6,4},{7,103},{32,38},{33,... | collective-permute-start | bytes 393224 | tf_op jit(solution)/shard_map/ppermute | solution.py:58
  27.8 10.9 %collective-permute-start.11 = (bf16[2,304,128]{2,1,0:T(8,128)(2,1)S(1)}, bf16[2,304,128]{2,1,0:T(8,128)(2,1)S(1)}, u32[]{:S(2)}, u32[]{:S(2)}) collective-permute-start(bf16[2,304,128]{2,1,0:T(8,128)(2,1)S(1)} %get-tuple-element.52), channel_id=1, source_target_pairs={{0,2},{1,33},{2,4},{3,35},{4,6},{5,37},{6,0},{7,39},{32,34},{33,65... | collective-permute-start | bytes 466952 | tf_op jit(solution)/shard_map/ppermute | solution.py:58
  28.7 10.0 %collective-permute-start.12 = (bf16[2,304,128]{2,1,0:T(8,128)(2,1)S(1)}, bf16[2,304,128]{2,1,0:T(8,128)(2,1)S(1)}, u32[]{:S(2)}, u32[]{:S(2)}) collective-permute-start(bf16[2,304,128]{2,1,0:T(8,128)(2,1)S(1)} %get-tuple-element.53), channel_id=1, source_target_pairs={{0,6},{1,97},{2,0},{3,99},{4,2},{5,101},{6,4},{7,103},{32,38},{33,... | collective-permute-start | bytes 466952 | tf_op jit(solution)/shard_map/ppermute | solution.py:58
  33.1 6.5 %copy-start.10 = (s32[1,231]{1,0:T(1,128)S(1)}, s32[1,231]{1,0:T(1,128)}, u32[]{:S(2)}) copy-start(s32[1,231]{1,0:T(1,128)} %param.21) | copy-start | bytes 2776
  33.2 6.7 %copy-start.8 = (f32[1,231,128]{2,0,1:T(1,128)S(1)}, f32[1,231,128]{2,0,1:T(1,128)}, u32[]{:S(2)}) copy-start(f32[1,231,128]{2,0,1:T(1,128)} %param.19) | copy-start | bytes 354820
  33.2 6.7 %copy-start.9 = (f32[1,231,128]{2,0,1:T(1,128)S(1)}, f32[1,231,128]{2,0,1:T(1,128)}, u32[]{:S(2)}) copy-start(f32[1,231,128]{2,0,1:T(1,128)} %param.18) | copy-start | bytes 354820
  33.2 8.6 %collective-permute-start.13 = (bf16[304,512]{1,0:T(8,128)(2,1)S(1)}, bf16[304,512]{1,0:T(8,128)(2,1)S(1)}, u32[]{:S(2)}, u32[]{:S(2)}) collective-permute-start(bf16[304,512]{1,0:T(8,128)(2,1)S(1)} %get-tuple-element.49), channel_id=1, source_target_pairs={{0,64},{1,5},{2,66},{3,7},{4,68},{5,1},{6,70},{7,3},{32,96},{33,37... | collective-permute-start | bytes 933896 | tf_op jit(solution)/shard_map/ppermute | solution.py:62
  35.4 9.6 %collective-permute-start.14 = (bf16[304,512]{1,0:T(8,128)(2,1)S(1)}, bf16[304,512]{1,0:T(8,128)(2,1)S(1)}, u32[]{:S(2)}, u32[]{:S(2)}) collective-permute-start(bf16[304,512]{1,0:T(8,128)(2,1)S(1)} %get-tuple-element.48), channel_id=1, source_target_pairs={{0,32},{1,3},{2,34},{3,5},{4,36},{5,7},{6,38},{7,1},{32,64},{33,35... | collective-permute-start | bytes 933896 | tf_op jit(solution)/shard_map/ppermute | solution.py:62
  36.3 8.7 %copy-start.6 = (f32[1,64,128]{2,1,0:T(8,128)S(1)}, f32[1,64,128]{2,1,0:T(8,128)}, u32[]{:S(2)}) copy-start(f32[1,64,128]{2,1,0:T(8,128)} %param.16) | copy-start | bytes 98308
  36.3 8.7 %copy-start.7 = (f32[1,64,128]{2,1,0:T(8,128)S(1)}, f32[1,64,128]{2,1,0:T(8,128)}, u32[]{:S(2)}) copy-start(f32[1,64,128]{2,1,0:T(8,128)} %param.17) | copy-start | bytes 98308
  36.3 8.7 %collective-permute-start.15 = (bf16[304,512]{1,0:T(8,128)(2,1)S(1)}, bf16[304,512]{1,0:T(8,128)(2,1)S(1)}, u32[]{:S(2)}, u32[]{:S(2)}) collective-permute-start(bf16[304,512]{1,0:T(8,128)(2,1)S(1)} %get-tuple-element.50), channel_id=1, source_target_pairs={{0,96},{1,7},{2,98},{3,1},{4,100},{5,3},{6,102},{7,5},{32,0},{33,3... | collective-permute-start | bytes 933896 | tf_op jit(solution)/shard_map/ppermute | solution.py:62
  46.2 1.2 %collective-permute-start.16 = (f32[16,512]{1,0:T(8,128)S(1)}, f32[16,512]{1,0:T(8,128)S(1)}, u32[]{:S(2)}, u32[]{:S(2)}) collective-permute-start(f32[16,512]{1,0:T(8,128)S(1)} %shard_map.124), channel_id=1, source_target_pairs={{0,1},{1,0},{2,3},{3,2},{4,5},{5,4},{6,7},{7,6},{8,9},{9,8},{10,11... | collective-permute-start | bytes 98312 | tf_op jit(solution)/shard_map/ppermute | solution.py:304
  (5 other events, 12.3 us)

commit v11 on v10

--- a/solution.py
+++ b/solution.py
@@ -213,11 +213,11 @@
 
 
 def spread_sum(value, along_x):
-    copies = jnp.broadcast_to(value[None], (8,) + value.shape)
+    copies = jnp.broadcast_to(value.astype(BF)[None], (8,) + value.shape)
     arrived = lax.all_to_all(
         copies, EVERY, split_axis=0, concat_axis=0, tiled=True, axis_index_groups=groups(along_x)
     )
-    return jnp.sum(arrived, axis=0)
+    return jnp.sum(arrived.astype(F32), axis=0)
 
 
 def on_device(

time: 72.4 us -> 71 us (0.981)
  blocking collectives: 23.6 us -> 22.2 us
    all_to_all x2, blocking collectives: 23.6 us -> 22.2 us  [spread_sum(): lax.all_to_all(copies, EVERY, split_axis=0, concat_axis=0, tiled=True, ax...]
where the time goes in v11:
time: 71 us; the launch traced here: 70.7 us
  starting transfers between devices  25.3 us (36%)
  blocking collectives  22.2 us (31%)
  waiting for transfers between devices  13.1 us (18%)
  Pallas kernels  5.86 us (8%)
  local copies, waits for them, and re-layouts  2.71 us (4%)
  matrix products  0.91 us (1%)
    all_to_all x2, blocking collectives, spread_sum(): lax.all_to_all(copies, EVERY, split_axis=0, concat_axis=0, tiled=True, ax...  22.2 us
    ppermute x8, starting transfers between devices, send_same(): return lax.ppermute(value, PLANE, pairs(lambda p: along(p, shift)))  13.7 us
    ppermute x3, starting transfers between devices, on_device(): lax.ppermute(portion, ('t1', 't0'), [(i, (i + shift) % 4) for i in range(...  5.9 us
    ppermute x3, starting transfers between devices, send_across(): return lax.ppermute(value, PLANE, pairs(lambda p: across(p, shift)))  5.47 us
    ppermute x3, waiting for transfers between devices, send_across(): return lax.ppermute(value, PLANE, pairs(lambda p: across(p, shift)))  5.08 us
    unnamed x25, local copies, waits for them, and re-layouts  2.67 us
    ppermute x3, waiting for transfers between devices, on_device(): lax.ppermute(portion, ('t1', 't0'), [(i, (i + shift) % 4) for i in range(...  2.64 us
    pallas_call x2, Pallas kernels, partial_call(): pl.pallas_call(functools.partial(partial_kernel, count), out_shape=[jax.S...  2.16 us
  transfers between devices with their start and end apart: 17, of which 10 were waited for; matrix products, arithmetic and copies ran while one was open for 1% of the time, Pallas kernels for 4%

profile of v11, /device:TPU:0, one launch (start us, length us, event | category | flops | bytes accessed | tf_op | source)
XLA Modules:
  0.0 70.7 jit_solution(2931996316963398256)
XLA Ops:
  0.0 1.6 %copy-done.1 = bf16[128,7392]{0,1:T(8,128)(2,1)S(1)} copy-done((bf16[128,7392]{0,1:T(8,128)(2,1)S(1)}, bf16[128,7392]{0,1:T(8,128)(2,1)}, u32[]{:S(2)}) %copy-start.1) | copy-done | bytes 1892376
  1.6 1.0 %copy-done.2 = bf16[128,2048]{1,0:T(8,128)(2,1)S(1)} copy-done((bf16[128,2048]{1,0:T(8,128)(2,1)S(1)}, bf16[128,2048]{1,0:T(8,128)(2,1)}, u32[]{:S(2)}) %copy-start.2) | copy-done | bytes 524312
  2.6 1.5 %shard_map.118 = (bf16[4,1216,128]{2,1,0:T(8,128)(2,1)S(1)}, bf16[1216,128]{1,0:T(8,128)(2,1)S(1)}, bf16[1216,128]{1,0:T(8,128)(2,1)S(1)}, bf16[1216,128]{1,0:T(8,128)(2,1)S(1)}, bf16[1216,128]{1,0:T(8,128)(2,1)S(1)}) custom-call(bf16[7392,128]{1,0:T(8,128)(2,1)S(1)} %bitcast.16, bf16[128,2048]{1,0:T(8,128)(2,1)S(1)} %copy-done.2), custom_call_target="tpu_custom_call" | custom-call | bytes 5242880 | tf_op jit(solution)/shard_map/pallas_call | solution.py:238
  5.1 2.1 %collective-permute-done.taken_ref = bf16[4,1216,128]{2,1,0:T(8,128)(2,1)S(1)} collective-permute-done((bf16[4,1216,128]{2,1,0:T(8,128)(2,1)S(1)}, bf16[4,1216,128]{2,1,0:T(8,128)(2,1)S(1)}, u32[]{:S(2)}, u32[]{:S(2)}) %collective-permute-start) | collective-permute-done | bytes 1245216 | tf_op jit(solution)/shard_map/ppermute | solution.py:255
  7.2 3.4 %collective-permute-start.6 = (bf16[2,1216,128]{2,1,0:T(8,128)(2,1)S(1)}, bf16[2,1216,128]{2,1,0:T(8,128)(2,1)S(1)}, u32[]{:S(2)}, u32[]{:S(2)}) collective-permute-start(bf16[2,1216,128]{2,1,0:T(8,128)(2,1)S(1)} %shard_map.121), channel_id=1, source_target_pairs={{0,4},{1,65},{2,6},{3,67},{4,0},{5,69},{6,2},{7,71},{32,36},{33,97... | collective-permute-start | bytes 1867784 | tf_op jit(solution)/shard_map/ppermute | solution.py:58
  10.6 1.9 %collective-permute-start.3 = (f32[128,256]{1,0:T(8,128)S(1)}, f32[128,256]{1,0:T(8,128)S(1)}, u32[]{:S(2)}, u32[]{:S(2)}) collective-permute-start(f32[128,256]{1,0:T(8,128)S(1)} %shard_map.119), channel_id=1, source_target_pairs={{0,8},{8,16},{16,24},{24,0},{1,9},{9,17},{17,25},{25,1},{2,10},{10... | collective-permute-start | bytes 393224 | tf_op jit(solution)/shard_map/ppermute | solution.py:260
  12.5 2.1 %collective-permute-start.4 = (f32[128,256]{1,0:T(8,128)S(1)}, f32[128,256]{1,0:T(8,128)S(1)}, u32[]{:S(2)}, u32[]{:S(2)}) collective-permute-start(f32[128,256]{1,0:T(8,128)S(1)} %shard_map.119), channel_id=1, source_target_pairs={{0,24},{8,0},{16,8},{24,16},{1,25},{9,1},{17,9},{25,17},{2,26},{10... | collective-permute-start | bytes 393224 | tf_op jit(solution)/shard_map/ppermute | solution.py:260
  14.6 1.9 %collective-permute-start.2 = (f32[128,256]{1,0:T(8,128)S(1)}, f32[128,256]{1,0:T(8,128)S(1)}, u32[]{:S(2)}, u32[]{:S(2)}) collective-permute-start(f32[128,256]{1,0:T(8,128)S(1)} %shard_map.119), channel_id=1, source_target_pairs={{0,16},{8,24},{16,0},{24,8},{1,17},{9,25},{17,1},{25,9},{2,18},{10... | collective-permute-start | bytes 393224 | tf_op jit(solution)/shard_map/ppermute | solution.py:260
  18.0 2.0 %collective-permute-start.7 = (bf16[2,912,128]{2,1,0:T(8,128)(2,1)S(1)}, bf16[2,912,128]{2,1,0:T(8,128)(2,1)S(1)}, u32[]{:S(2)}, u32[]{:S(2)}) collective-permute-start(bf16[2,912,128]{2,1,0:T(8,128)(2,1)S(1)} %get-tuple-element.45), channel_id=1, source_target_pairs={{0,6},{1,97},{2,0},{3,99},{4,2},{5,101},{6,4},{7,103},{32,38},{33,... | collective-permute-start | bytes 1400840 | tf_op jit(solution)/shard_map/ppermute | solution.py:58
  20.1 1.9 %collective-permute-done.2 = f32[128,256]{1,0:T(8,128)S(1)} collective-permute-done((f32[128,256]{1,0:T(8,128)S(1)}, f32[128,256]{1,0:T(8,128)S(1)}, u32[]{:S(2)}, u32[]{:S(2)}) %collective-permute-start.2) | collective-permute-done | bytes 131104 | tf_op jit(solution)/shard_map/ppermute | solution.py:260
  22.1 1.2 %collective-permute-done.5 = bf16[128,256]{1,0:T(8,128)(2,1)S(1)} collective-permute-done((bf16[128,256]{1,0:T(8,128)(2,1)S(1)}, bf16[128,256]{1,0:T(8,128)(2,1)S(1)}, u32[]{:S(2)}, u32[]{:S(2)}) %collective-permute-start.5) | collective-permute-done | bytes 65568 | tf_op jit(solution)/shard_map/ppermute | solution.py:264
  23.3 1.6 %collective-permute-start.8 = (bf16[256,256]{1,0:T(8,128)(2,1)S(1)}, bf16[256,256]{1,0:T(8,128)(2,1)S(1)}, u32[]{:S(2)}, u32[]{:S(2)}) collective-permute-start(bf16[256,256]{1,0:T(8,128)(2,1)S(1)} %pad_maximum_fusion.rest_4_), channel_id=1, source_target_pairs={{0,2},{1,33},{2,4},{3,35},{4,6},{5,37},{6,0},{7,39},{32,34},{33,65... | collective-permute-start | bytes 393224 | tf_op jit(solution)/shard_map/ppermute | solution.py:58
  25.0 1.7 %collective-permute-start.9 = (bf16[256,256]{1,0:T(8,128)(2,1)S(1)}, bf16[256,256]{1,0:T(8,128)(2,1)S(1)}, u32[]{:S(2)}, u32[]{:S(2)}) collective-permute-start(bf16[256,256]{1,0:T(8,128)(2,1)S(1)} %pad_maximum_fusion.rest_4_), channel_id=1, source_target_pairs={{0,4},{1,65},{2,6},{3,67},{4,0},{5,69},{6,2},{7,71},{32,36},{33,97... | collective-permute-start | bytes 393224 | tf_op jit(solution)/shard_map/ppermute | solution.py:58
  26.7 1.1 %collective-permute-start.10 = (bf16[256,256]{1,0:T(8,128)(2,1)S(1)}, bf16[256,256]{1,0:T(8,128)(2,1)S(1)}, u32[]{:S(2)}, u32[]{:S(2)}) collective-permute-start(bf16[256,256]{1,0:T(8,128)(2,1)S(1)} %pad_maximum_fusion.rest_4_), channel_id=1, source_target_pairs={{0,6},{1,97},{2,0},{3,99},{4,2},{5,101},{6,4},{7,103},{32,38},{33,... | collective-permute-start | bytes 393224 | tf_op jit(solution)/shard_map/ppermute | solution.py:58
  28.7 2.3 %collective-permute-start.12 = (bf16[2,304,128]{2,1,0:T(8,128)(2,1)S(1)}, bf16[2,304,128]{2,1,0:T(8,128)(2,1)S(1)}, u32[]{:S(2)}, u32[]{:S(2)}) collective-permute-start(bf16[2,304,128]{2,1,0:T(8,128)(2,1)S(1)} %get-tuple-element.53), channel_id=1, source_target_pairs={{0,6},{1,97},{2,0},{3,99},{4,2},{5,101},{6,4},{7,103},{32,38},{33,... | collective-permute-start | bytes 466952 | tf_op jit(solution)/shard_map/ppermute | solution.py:58
  31.8 1.3 %shard_map.122 = (bf16[304,512]{1,0:T(8,128)(2,1)S(1)}, bf16[304,512]{1,0:T(8,128)(2,1)S(1)}, bf16[304,512]{1,0:T(8,128)(2,1)S(1)}) custom-call(s32[32,128]{1,0:T(8,128)S(1)} %bitcast.18, bf16[2,1216,128]{2,1,0:T(8,128)(2,1)S(1)} %get-tuple-element.37.rest_0_, bf16[2,912,128]{2,1,0:T(8,128)(2,1)S(1)} %collective-permute-done.1.rest_1_, ...), custom_call_target="tpu_custom_call" | custom-call | flops 956301312 | bytes 6291456 | tf_op jit(solution)/shard_map/pallas_call | solution.py:157
  33.2 2.2 %collective-permute-start.13 = (bf16[304,512]{1,0:T(8,128)(2,1)S(1)}, bf16[304,512]{1,0:T(8,128)(2,1)S(1)}, u32[]{:S(2)}, u32[]{:S(2)}) collective-permute-start(bf16[304,512]{1,0:T(8,128)(2,1)S(1)} %get-tuple-element.49), channel_id=1, source_target_pairs={{0,64},{1,5},{2,66},{3,7},{4,68},{5,1},{6,70},{7,3},{32,96},{33,37... | collective-permute-start | bytes 933896 | tf_op jit(solution)/shard_map/ppermute | solution.py:62
  36.3 2.4 %collective-permute-start.15 = (bf16[304,512]{1,0:T(8,128)(2,1)S(1)}, bf16[304,512]{1,0:T(8,128)(2,1)S(1)}, u32[]{:S(2)}, u32[]{:S(2)}) collective-permute-start(bf16[304,512]{1,0:T(8,128)(2,1)S(1)} %get-tuple-element.50), channel_id=1, source_target_pairs={{0,96},{1,7},{2,98},{3,1},{4,100},{5,3},{6,102},{7,5},{32,0},{33,3... | collective-permute-start | bytes 933896 | tf_op jit(solution)/shard_map/ppermute | solution.py:62
  39.9 1.9 %collective-permute-done.13.a_ref = bf16[304,512]{1,0:T(8,128)(2,1)S(1)} collective-permute-done((bf16[304,512]{1,0:T(8,128)(2,1)S(1)}, bf16[304,512]{1,0:T(8,128)(2,1)S(1)}, u32[]{:S(2)}, u32[]{:S(2)}) %collective-permute-start.13) | collective-permute-done | bytes 311328 | tf_op jit(solution)/shard_map/ppermute | solution.py:62
  41.8 3.2 %collective-permute-done.14.b_ref = bf16[304,512]{1,0:T(8,128)(2,1)S(1)} collective-permute-done((bf16[304,512]{1,0:T(8,128)(2,1)S(1)}, bf16[304,512]{1,0:T(8,128)(2,1)S(1)}, u32[]{:S(2)}, u32[]{:S(2)}) %collective-permute-start.14) | collective-permute-done | bytes 311328 | tf_op jit(solution)/shard_map/ppermute | solution.py:62
  45.0 1.2 %shard_map.124 = f32[16,512]{1,0:T(8,128)S(1)} custom-call(f32[304,512]{1,0:T(8,128)S(1)} %convert_element_type.22.own_ref, bf16[304,512]{1,0:T(8,128)(2,1)S(1)} %collective-permute-done.13.a_ref, bf16[304,512]{1,0:T(8,128)(2,1)S(1)} %collective-permute-done.14.b_ref, bf16[304,512]{1,0:T(8,128)(2,1)S(1)} %collective-permute-done.15.c_ref, ...), custom_call_target="tpu_custom_call" | custom-call | bytes 3145728 | tf_op jit(solution)/shard_map/pallas_call | solution.py:291
  46.3 1.2 %collective-permute-done.16 = f32[16,512]{1,0:T(8,128)S(1)} collective-permute-done((f32[16,512]{1,0:T(8,128)S(1)}, f32[16,512]{1,0:T(8,128)S(1)}, u32[]{:S(2)}, u32[]{:S(2)}) %collective-permute-start.16) | collective-permute-done | bytes 32800 | tf_op jit(solution)/shard_map/ppermute | solution.py:304
  47.5 12.6 %all_to_all.10 = bf16[8,16,512]{2,1,0:T(8,128)(2,1)S(1)} all-to-all(bf16[8,16,512]{2,1,0:T(8,128)(2,1)S(1)} %broadcast_in_dim.4), channel_id=1, replica_groups={{0,24,2,26,4,28,6,30},{8,16,10,18,12,20,14,22},{1,25,3,27,5,29,7,31},{9..., dimensions={0} | all-to-all | bytes 262144 | tf_op jit(solution)/shard_map/all_to_all | solution.py:217
  60.1 9.6 %all_to_all.11 = bf16[8,16,512]{2,1,0:T(8,128)(2,1)S(1)} all-to-all(bf16[8,16,512]{2,1,0:T(8,128)(2,1)S(1)} %broadcast_in_dim.5), channel_id=1, replica_groups={{0,8,32,40,64,72,96,104},{16,24,48,56,80,88,112,120},{1,9,33,41,65,73,9..., dimensions={0} | all-to-all | bytes 262144 | tf_op jit(solution)/shard_map/all_to_all | solution.py:217
  (58 shorter events, 7.6 us)
Async XLA Ops:
  0.0 69.8 %copy-start = (bf16[16,128,64]{1,2,0:T(8,128)(2,1)S(1)}, bf16[16,128,64]{1,2,0:T(8,128)(2,1)}, u32[]{:S(2)}) copy-start(bf16[16,128,64]{1,2,0:T(8,128)(2,1)} %param.23) | copy-start | bytes 786436
  4.1 3.0 %collective-permute-start = (bf16[4,1216,128]{2,1,0:T(8,128)(2,1)S(1)}, bf16[4,1216,128]{2,1,0:T(8,128)(2,1)S(1)}, u32[]{:S(2)}, u32[]{:S(2)}) collective-permute-start(bf16[4,1216,128]{2,1,0:T(8,128)(2,1)S(1)} %get-tuple-element.32), channel_id=1, source_target_pairs={{0,1},{1,0},{2,3},{3,2},{4,5},{5,4},{6,7},{7,6},{8,9},{9,8},{10,11... | collective-permute-start | bytes 3735560 | tf_op jit(solution)/shard_map/ppermute | solution.py:255
  7.2 24.6 %copy-start.5 = (s32[4096]{0:T(1024)S(1)}, s32[4096]{0:T(1024)}, u32[]{:S(2)}) copy-start(s32[4096]{0:T(1024)} %param.22) | copy-start | bytes 49156
  7.2 19.5 %collective-permute-start.6 = (bf16[2,1216,128]{2,1,0:T(8,128)(2,1)S(1)}, bf16[2,1216,128]{2,1,0:T(8,128)(2,1)S(1)}, u32[]{:S(2)}, u32[]{:S(2)}) collective-permute-start(bf16[2,1216,128]{2,1,0:T(8,128)(2,1)S(1)} %shard_map.121), channel_id=1, source_target_pairs={{0,4},{1,65},{2,6},{3,67},{4,0},{5,69},{6,2},{7,71},{32,36},{33,97... | collective-permute-start | bytes 1867784 | tf_op jit(solution)/shard_map/ppermute | solution.py:58
  10.6 7.4 %collective-permute-start.3 = (f32[128,256]{1,0:T(8,128)S(1)}, f32[128,256]{1,0:T(8,128)S(1)}, u32[]{:S(2)}, u32[]{:S(2)}) collective-permute-start(f32[128,256]{1,0:T(8,128)S(1)} %shard_map.119), channel_id=1, source_target_pairs={{0,8},{8,16},{16,24},{24,0},{1,9},{9,17},{17,25},{25,1},{2,10},{10... | collective-permute-start | bytes 393224 | tf_op jit(solution)/shard_map/ppermute | solution.py:260
  12.5 7.6 %collective-permute-start.4 = (f32[128,256]{1,0:T(8,128)S(1)}, f32[128,256]{1,0:T(8,128)S(1)}, u32[]{:S(2)}, u32[]{:S(2)}) collective-permute-start(f32[128,256]{1,0:T(8,128)S(1)} %shard_map.119), channel_id=1, source_target_pairs={{0,24},{8,0},{16,8},{24,16},{1,25},{9,1},{17,9},{25,17},{2,26},{10... | collective-permute-start | bytes 393224 | tf_op jit(solution)/shard_map/ppermute | solution.py:260
  14.6 7.3 %collective-permute-start.2 = (f32[128,256]{1,0:T(8,128)S(1)}, f32[128,256]{1,0:T(8,128)S(1)}, u32[]{:S(2)}, u32[]{:S(2)}) collective-permute-start(f32[128,256]{1,0:T(8,128)S(1)} %shard_map.119), channel_id=1, source_target_pairs={{0,16},{8,24},{16,0},{24,8},{1,17},{9,25},{17,1},{25,9},{2,18},{10... | collective-permute-start | bytes 393224 | tf_op jit(solution)/shard_map/ppermute | solution.py:260
  16.6 11.2 %collective-permute-start.1 = (bf16[2,912,128]{2,1,0:T(8,128)(2,1)S(1)}, bf16[2,912,128]{2,1,0:T(8,128)(2,1)S(1)}, u32[]{:S(2)}, u32[]{:S(2)}) collective-permute-start(bf16[2,912,128]{2,1,0:T(8,128)(2,1)S(1)} %get-tuple-element.39), channel_id=1, source_target_pairs={{0,2},{1,33},{2,4},{3,35},{4,6},{5,37},{6,0},{7,39},{32,34},{33,65... | collective-permute-start | bytes 1400840 | tf_op jit(solution)/shard_map/ppermute | solution.py:58
  18.0 9.8 %collective-permute-start.7 = (bf16[2,912,128]{2,1,0:T(8,128)(2,1)S(1)}, bf16[2,912,128]{2,1,0:T(8,128)(2,1)S(1)}, u32[]{:S(2)}, u32[]{:S(2)}) collective-permute-start(bf16[2,912,128]{2,1,0:T(8,128)(2,1)S(1)} %get-tuple-element.45), channel_id=1, source_target_pairs={{0,6},{1,97},{2,0},{3,99},{4,2},{5,101},{6,4},{7,103},{32,38},{33,... | collective-permute-start | bytes 1400840 | tf_op jit(solution)/shard_map/ppermute | solution.py:58
  22.0 1.3 %collective-permute-start.5 = (bf16[128,256]{1,0:T(8,128)(2,1)S(1)}, bf16[128,256]{1,0:T(8,128)(2,1)S(1)}, u32[]{:S(2)}, u32[]{:S(2)}) collective-permute-start(bf16[128,256]{1,0:T(8,128)(2,1)S(1)} %add_convert_fusion), channel_id=1, source_target_pairs={{0,1},{1,0},{2,3},{3,2},{4,5},{5,4},{6,7},{7,6},{8,9},{9,8},{10,11... | collective-permute-start | bytes 196616 | tf_op jit(solution)/shard_map/ppermute | solution.py:264
  23.3 7.7 %collective-permute-start.8 = (bf16[256,256]{1,0:T(8,128)(2,1)S(1)}, bf16[256,256]{1,0:T(8,128)(2,1)S(1)}, u32[]{:S(2)}, u32[]{:S(2)}) collective-permute-start(bf16[256,256]{1,0:T(8,128)(2,1)S(1)} %pad_maximum_fusion.rest_4_), channel_id=1, source_target_pairs={{0,2},{1,33},{2,4},{3,35},{4,6},{5,37},{6,0},{7,39},{32,34},{33,65... | collective-permute-start | bytes 393224 | tf_op jit(solution)/shard_map/ppermute | solution.py:58
  25.0 6.5 %collective-permute-start.9 = (bf16[256,256]{1,0:T(8,128)(2,1)S(1)}, bf16[256,256]{1,0:T(8,128)(2,1)S(1)}, u32[]{:S(2)}, u32[]{:S(2)}) collective-permute-start(bf16[256,256]{1,0:T(8,128)(2,1)S(1)} %pad_maximum_fusion.rest_4_), channel_id=1, source_target_pairs={{0,4},{1,65},{2,6},{3,67},{4,0},{5,69},{6,2},{7,71},{32,36},{33,97... | collective-permute-start | bytes 393224 | tf_op jit(solution)/shard_map/ppermute | solution.py:58
  26.7 5.2 %collective-permute-start.10 = (bf16[256,256]{1,0:T(8,128)(2,1)S(1)}, bf16[256,256]{1,0:T(8,128)(2,1)S(1)}, u32[]{:S(2)}, u32[]{:S(2)}) collective-permute-start(bf16[256,256]{1,0:T(8,128)(2,1)S(1)} %pad_maximum_fusion.rest_4_), channel_id=1, source_target_pairs={{0,6},{1,97},{2,0},{3,99},{4,2},{5,101},{6,4},{7,103},{32,38},{33,... | collective-permute-start | bytes 393224 | tf_op jit(solution)/shard_map/ppermute | solution.py:58
  27.8 10.9 %collective-permute-start.11 = (bf16[2,304,128]{2,1,0:T(8,128)(2,1)S(1)}, bf16[2,304,128]{2,1,0:T(8,128)(2,1)S(1)}, u32[]{:S(2)}, u32[]{:S(2)}) collective-permute-start(bf16[2,304,128]{2,1,0:T(8,128)(2,1)S(1)} %get-tuple-element.52), channel_id=1, source_target_pairs={{0,2},{1,33},{2,4},{3,35},{4,6},{5,37},{6,0},{7,39},{32,34},{33,65... | collective-permute-start | bytes 466952 | tf_op jit(solution)/shard_map/ppermute | solution.py:58
  28.7 10.0 %collective-permute-start.12 = (bf16[2,304,128]{2,1,0:T(8,128)(2,1)S(1)}, bf16[2,304,128]{2,1,0:T(8,128)(2,1)S(1)}, u32[]{:S(2)}, u32[]{:S(2)}) collective-permute-start(bf16[2,304,128]{2,1,0:T(8,128)(2,1)S(1)} %get-tuple-element.53), channel_id=1, source_target_pairs={{0,6},{1,97},{2,0},{3,99},{4,2},{5,101},{6,4},{7,103},{32,38},{33,... | collective-permute-start | bytes 466952 | tf_op jit(solution)/shard_map/ppermute | solution.py:58
  33.1 6.5 %copy-start.10 = (s32[1,231]{1,0:T(1,128)S(1)}, s32[1,231]{1,0:T(1,128)}, u32[]{:S(2)}) copy-start(s32[1,231]{1,0:T(1,128)} %param.21) | copy-start | bytes 2776
  33.2 6.7 %copy-start.8 = (f32[1,231,128]{2,0,1:T(1,128)S(1)}, f32[1,231,128]{2,0,1:T(1,128)}, u32[]{:S(2)}) copy-start(f32[1,231,128]{2,0,1:T(1,128)} %param.19) | copy-start | bytes 354820
  33.2 6.7 %copy-start.9 = (f32[1,231,128]{2,0,1:T(1,128)S(1)}, f32[1,231,128]{2,0,1:T(1,128)}, u32[]{:S(2)}) copy-start(f32[1,231,128]{2,0,1:T(1,128)} %param.18) | copy-start | bytes 354820
  33.2 8.6 %collective-permute-start.13 = (bf16[304,512]{1,0:T(8,128)(2,1)S(1)}, bf16[304,512]{1,0:T(8,128)(2,1)S(1)}, u32[]{:S(2)}, u32[]{:S(2)}) collective-permute-start(bf16[304,512]{1,0:T(8,128)(2,1)S(1)} %get-tuple-element.49), channel_id=1, source_target_pairs={{0,64},{1,5},{2,66},{3,7},{4,68},{5,1},{6,70},{7,3},{32,96},{33,37... | collective-permute-start | bytes 933896 | tf_op jit(solution)/shard_map/ppermute | solution.py:62
  35.4 9.6 %collective-permute-start.14 = (bf16[304,512]{1,0:T(8,128)(2,1)S(1)}, bf16[304,512]{1,0:T(8,128)(2,1)S(1)}, u32[]{:S(2)}, u32[]{:S(2)}) collective-permute-start(bf16[304,512]{1,0:T(8,128)(2,1)S(1)} %get-tuple-element.48), channel_id=1, source_target_pairs={{0,32},{1,3},{2,34},{3,5},{4,36},{5,7},{6,38},{7,1},{32,64},{33,35... | collective-permute-start | bytes 933896 | tf_op jit(solution)/shard_map/ppermute | solution.py:62
  36.3 8.7 %copy-start.6 = (f32[1,64,128]{2,1,0:T(8,128)S(1)}, f32[1,64,128]{2,1,0:T(8,128)}, u32[]{:S(2)}) copy-start(f32[1,64,128]{2,1,0:T(8,128)} %param.16) | copy-start | bytes 98308
  36.3 8.7 %copy-start.7 = (f32[1,64,128]{2,1,0:T(8,128)S(1)}, f32[1,64,128]{2,1,0:T(8,128)}, u32[]{:S(2)}) copy-start(f32[1,64,128]{2,1,0:T(8,128)} %param.17) | copy-start | bytes 98308
  36.3 8.7 %collective-permute-start.15 = (bf16[304,512]{1,0:T(8,128)(2,1)S(1)}, bf16[304,512]{1,0:T(8,128)(2,1)S(1)}, u32[]{:S(2)}, u32[]{:S(2)}) collective-permute-start(bf16[304,512]{1,0:T(8,128)(2,1)S(1)} %get-tuple-element.50), channel_id=1, source_target_pairs={{0,96},{1,7},{2,98},{3,1},{4,100},{5,3},{6,102},{7,5},{32,0},{33,3... | collective-permute-start | bytes 933896 | tf_op jit(solution)/shard_map/ppermute | solution.py:62
  46.2 1.2 %collective-permute-start.16 = (f32[16,512]{1,0:T(8,128)S(1)}, f32[16,512]{1,0:T(8,128)S(1)}, u32[]{:S(2)}, u32[]{:S(2)}) collective-permute-start(f32[16,512]{1,0:T(8,128)S(1)} %shard_map.124), channel_id=1, source_target_pairs={{0,1},{1,0},{2,3},{3,2},{4,5},{5,4},{6,7},{7,6},{8,9},{9,8},{10,11... | collective-permute-start | bytes 98312 | tf_op jit(solution)/shard_map/ppermute | solution.py:304
  (5 other events, 12.3 us)

commit v12 on v10

--- a/solution.py
+++ b/solution.py
@@ -212,12 +212,25 @@
     return found
 
 
-def spread_sum(value, along_x):
+def spread(value, along_x):
     copies = jnp.broadcast_to(value[None], (8,) + value.shape)
-    arrived = lax.all_to_all(
+    return lax.all_to_all(
         copies, EVERY, split_axis=0, concat_axis=0, tiled=True, axis_index_groups=groups(along_x)
     )
-    return jnp.sum(arrived, axis=0)
+
+
+def sketch_kernel(arrived_ref, bank_ref, out_ref):
+    summed = arrived_ref[0].astype(F32)
+    for i in range(1, 8):
+        summed = summed + arrived_ref[i].astype(F32)
+    total = jnp.zeros((2 * EXAMPLES, bank_ref.shape[1]), F32)
+    for j in range(BANK):
+        rows = jnp.concatenate([summed[j:j + 1, e * RANK:(e + 1) * RANK] for e in range(EXAMPLES)], axis=0)
+        high = rows.astype(BF).astype(F32)
+        left = jnp.concatenate([high, rows - high], axis=0).astype(BF)
+        total += lax.dot_general(left, bank_ref[j], (((1,), (1,)), ((), ())), preferred_element_type=F32)
+    inverse = 1.0 / math.sqrt((MODEL_WIDTH + HIDDEN_WIDTH) * RANK)
+    out_ref[...] = (total[:EXAMPLES] + total[EXAMPLES:]) * inverse
 
 
 def on_device(
@@ -302,13 +315,16 @@
     )
 
     summed = blocks + lax.ppermute(blocks, "co", [(0, 1), (1, 0)])
-    summed = spread_sum(summed, False)
-    summed = spread_sum(summed, True)
-    inverse = 1.0 / math.sqrt((MODEL_WIDTH + HIDDEN_WIDTH) * RANK)
-    sketch = jnp.einsum(
-        "jer,jrk->ek", summed.reshape(BANK, EXAMPLES, RANK), bank.astype(F32), precision=lax.Precision.HIGHEST
-    )
-    return sketch * inverse
+    summed = jnp.sum(spread(summed, False), axis=0)
+    arrived = spread(summed.astype(F32), True)
+    return pl.pallas_call(
+        sketch_kernel,
+        out_shape=jax.ShapeDtypeStruct((EXAMPLES, bank.shape[2]), F32),
+        in_specs=[VMEM] * 2,
+        out_specs=VMEM,
+        compiler_params=pltpu.CompilerParams(vmem_limit_bytes=24 << 20),
+        cost_estimate=pl.CostEstimate(flops=1 << 22, bytes_accessed=1 << 20, transcendentals=0),
+    )(arrived, jnp.transpose(bank, (0, 2, 1)))
 
 
 def solution(mesh):

time: 72.4 us -> 72.2 us (level)
  matrix products: 0.91 us -> 0 us
  Pallas kernels: 5.86 us -> 6.68 us
    dot_general x1 -> x0, matrix products: 0.91 us -> none  [on_device(): jnp.einsum('jer,jrk->ek', summed.reshape(BANK, EXAMPLES, RANK), bank.asty...]
    pallas_call x0 -> x1, Pallas kernels: none -> 0.84 us  [on_device(): pl.pallas_call(sketch_kernel, out_shape=jax.ShapeDtypeStruct((EXAMPLES, b...]
where the time goes in v12:
time: 72.2 us; the launch traced here: 72 us
  starting transfers between devices  25.3 us (35%)
  blocking collectives  23.6 us (33%)
  waiting for transfers between devices  13.1 us (18%)
  Pallas kernels  6.68 us (9%)
  local copies, waits for them, and re-layouts  2.67 us (4%)
    all_to_all x2, blocking collectives, spread(): lax.all_to_all(copies, EVERY, split_axis=0, concat_axis=0, tiled=True, ax...  23.6 us
    ppermute x8, starting transfers between devices, send_same(): return lax.ppermute(value, PLANE, pairs(lambda p: along(p, shift)))  13.7 us
    ppermute x3, starting transfers between devices, on_device(): lax.ppermute(portion, ('t1', 't0'), [(i, (i + shift) % 4) for i in range(...  5.9 us
    ppermute x3, starting transfers between devices, send_across(): return lax.ppermute(value, PLANE, pairs(lambda p: across(p, shift)))  5.49 us
    ppermute x3, waiting for transfers between devices, send_across(): return lax.ppermute(value, PLANE, pairs(lambda p: across(p, shift)))  5.08 us
    ppermute x3, waiting for transfers between devices, on_device(): lax.ppermute(portion, ('t1', 't0'), [(i, (i + shift) % 4) for i in range(...  2.64 us
    unnamed x25, local copies, waits for them, and re-layouts  2.63 us
    pallas_call x2, Pallas kernels, partial_call(): pl.pallas_call(functools.partial(partial_kernel, count), out_shape=[jax.S...  2.14 us
  transfers between devices with their start and end apart: 17, of which 10 were waited for; matrix products, arithmetic and copies ran while one was open for 1% of the time, Pallas kernels for 4%

profile of v12, /device:TPU:0, one launch (start us, length us, event | category | flops | bytes accessed | tf_op | source)
XLA Modules:
  0.0 72.0 jit_solution(179844584902657369)
XLA Ops:
  0.0 1.5 %copy-done = bf16[128,7392]{0,1:T(8,128)(2,1)S(1)} copy-done((bf16[128,7392]{0,1:T(8,128)(2,1)S(1)}, bf16[128,7392]{0,1:T(8,128)(2,1)}, u32[]{:S(2)}) %copy-start) | copy-done | bytes 1892376
  1.5 1.0 %copy-done.1 = bf16[128,2048]{1,0:T(8,128)(2,1)S(1)} copy-done((bf16[128,2048]{1,0:T(8,128)(2,1)S(1)}, bf16[128,2048]{1,0:T(8,128)(2,1)}, u32[]{:S(2)}) %copy-start.1) | copy-done | bytes 524312
  2.6 1.5 %shard_map.118 = (bf16[4,1216,128]{2,1,0:T(8,128)(2,1)S(1)}, bf16[1216,128]{1,0:T(8,128)(2,1)S(1)}, bf16[1216,128]{1,0:T(8,128)(2,1)S(1)}, bf16[1216,128]{1,0:T(8,128)(2,1)S(1)}, bf16[1216,128]{1,0:T(8,128)(2,1)S(1)}) custom-call(bf16[7392,128]{1,0:T(8,128)(2,1)S(1)} %bitcast.11, bf16[128,2048]{1,0:T(8,128)(2,1)S(1)} %copy-done.1), custom_call_target="tpu_custom_call" | custom-call | bytes 5242880 | tf_op jit(solution)/shard_map/pallas_call | solution.py:251
  5.0 2.1 %collective-permute-done.taken_ref = bf16[4,1216,128]{2,1,0:T(8,128)(2,1)S(1)} collective-permute-done((bf16[4,1216,128]{2,1,0:T(8,128)(2,1)S(1)}, bf16[4,1216,128]{2,1,0:T(8,128)(2,1)S(1)}, u32[]{:S(2)}, u32[]{:S(2)}) %collective-permute-start) | collective-permute-done | bytes 1245216 | tf_op jit(solution)/shard_map/ppermute | solution.py:268
  7.2 3.4 %collective-permute-start.6 = (bf16[2,1216,128]{2,1,0:T(8,128)(2,1)S(1)}, bf16[2,1216,128]{2,1,0:T(8,128)(2,1)S(1)}, u32[]{:S(2)}, u32[]{:S(2)}) collective-permute-start(bf16[2,1216,128]{2,1,0:T(8,128)(2,1)S(1)} %shard_map.121), channel_id=1, source_target_pairs={{0,4},{1,65},{2,6},{3,67},{4,0},{5,69},{6,2},{7,71},{32,36},{33,97... | collective-permute-start | bytes 1867784 | tf_op jit(solution)/shard_map/ppermute | solution.py:58
  10.5 1.9 %collective-permute-start.3 = (f32[128,256]{1,0:T(8,128)S(1)}, f32[128,256]{1,0:T(8,128)S(1)}, u32[]{:S(2)}, u32[]{:S(2)}) collective-permute-start(f32[128,256]{1,0:T(8,128)S(1)} %shard_map.119), channel_id=1, source_target_pairs={{0,8},{8,16},{16,24},{24,0},{1,9},{9,17},{17,25},{25,1},{2,10},{10... | collective-permute-start | bytes 393224 | tf_op jit(solution)/shard_map/ppermute | solution.py:273
  12.4 2.1 %collective-permute-start.4 = (f32[128,256]{1,0:T(8,128)S(1)}, f32[128,256]{1,0:T(8,128)S(1)}, u32[]{:S(2)}, u32[]{:S(2)}) collective-permute-start(f32[128,256]{1,0:T(8,128)S(1)} %shard_map.119), channel_id=1, source_target_pairs={{0,24},{8,0},{16,8},{24,16},{1,25},{9,1},{17,9},{25,17},{2,26},{10... | collective-permute-start | bytes 393224 | tf_op jit(solution)/shard_map/ppermute | solution.py:273
  14.6 1.9 %collective-permute-start.2 = (f32[128,256]{1,0:T(8,128)S(1)}, f32[128,256]{1,0:T(8,128)S(1)}, u32[]{:S(2)}, u32[]{:S(2)}) collective-permute-start(f32[128,256]{1,0:T(8,128)S(1)} %shard_map.119), channel_id=1, source_target_pairs={{0,16},{8,24},{16,0},{24,8},{1,17},{9,25},{17,1},{25,9},{2,18},{10... | collective-permute-start | bytes 393224 | tf_op jit(solution)/shard_map/ppermute | solution.py:273
  17.9 2.0 %collective-permute-start.7 = (bf16[2,912,128]{2,1,0:T(8,128)(2,1)S(1)}, bf16[2,912,128]{2,1,0:T(8,128)(2,1)S(1)}, u32[]{:S(2)}, u32[]{:S(2)}) collective-permute-start(bf16[2,912,128]{2,1,0:T(8,128)(2,1)S(1)} %get-tuple-element.45), channel_id=1, source_target_pairs={{0,6},{1,97},{2,0},{3,99},{4,2},{5,101},{6,4},{7,103},{32,38},{33,... | collective-permute-start | bytes 1400840 | tf_op jit(solution)/shard_map/ppermute | solution.py:58
  20.0 1.9 %collective-permute-done.2 = f32[128,256]{1,0:T(8,128)S(1)} collective-permute-done((f32[128,256]{1,0:T(8,128)S(1)}, f32[128,256]{1,0:T(8,128)S(1)}, u32[]{:S(2)}, u32[]{:S(2)}) %collective-permute-start.2) | collective-permute-done | bytes 131104 | tf_op jit(solution)/shard_map/ppermute | solution.py:273
  22.0 1.2 %collective-permute-done.5 = bf16[128,256]{1,0:T(8,128)(2,1)S(1)} collective-permute-done((bf16[128,256]{1,0:T(8,128)(2,1)S(1)}, bf16[128,256]{1,0:T(8,128)(2,1)S(1)}, u32[]{:S(2)}, u32[]{:S(2)}) %collective-permute-start.5) | collective-permute-done | bytes 65568 | tf_op jit(solution)/shard_map/ppermute | solution.py:277
  23.3 1.6 %collective-permute-start.8 = (bf16[256,256]{1,0:T(8,128)(2,1)S(1)}, bf16[256,256]{1,0:T(8,128)(2,1)S(1)}, u32[]{:S(2)}, u32[]{:S(2)}) collective-permute-start(bf16[256,256]{1,0:T(8,128)(2,1)S(1)} %pad_maximum_fusion.rest_4_), channel_id=1, source_target_pairs={{0,2},{1,33},{2,4},{3,35},{4,6},{5,37},{6,0},{7,39},{32,34},{33,65... | collective-permute-start | bytes 393224 | tf_op jit(solution)/shard_map/ppermute | solution.py:58
  24.9 1.7 %collective-permute-start.9 = (bf16[256,256]{1,0:T(8,128)(2,1)S(1)}, bf16[256,256]{1,0:T(8,128)(2,1)S(1)}, u32[]{:S(2)}, u32[]{:S(2)}) collective-permute-start(bf16[256,256]{1,0:T(8,128)(2,1)S(1)} %pad_maximum_fusion.rest_4_), channel_id=1, source_target_pairs={{0,4},{1,65},{2,6},{3,67},{4,0},{5,69},{6,2},{7,71},{32,36},{33,97... | collective-permute-start | bytes 393224 | tf_op jit(solution)/shard_map/ppermute | solution.py:58
  26.6 1.1 %collective-permute-start.10 = (bf16[256,256]{1,0:T(8,128)(2,1)S(1)}, bf16[256,256]{1,0:T(8,128)(2,1)S(1)}, u32[]{:S(2)}, u32[]{:S(2)}) collective-permute-start(bf16[256,256]{1,0:T(8,128)(2,1)S(1)} %pad_maximum_fusion.rest_4_), channel_id=1, source_target_pairs={{0,6},{1,97},{2,0},{3,99},{4,2},{5,101},{6,4},{7,103},{32,38},{33,... | collective-permute-start | bytes 393224 | tf_op jit(solution)/shard_map/ppermute | solution.py:58
  28.7 2.3 %collective-permute-start.12 = (bf16[2,304,128]{2,1,0:T(8,128)(2,1)S(1)}, bf16[2,304,128]{2,1,0:T(8,128)(2,1)S(1)}, u32[]{:S(2)}, u32[]{:S(2)}) collective-permute-start(bf16[2,304,128]{2,1,0:T(8,128)(2,1)S(1)} %get-tuple-element.53), channel_id=1, source_target_pairs={{0,6},{1,97},{2,0},{3,99},{4,2},{5,101},{6,4},{7,103},{32,38},{33,... | collective-permute-start | bytes 466952 | tf_op jit(solution)/shard_map/ppermute | solution.py:58
  31.8 1.3 %shard_map.122 = (bf16[304,512]{1,0:T(8,128)(2,1)S(1)}, bf16[304,512]{1,0:T(8,128)(2,1)S(1)}, bf16[304,512]{1,0:T(8,128)(2,1)S(1)}) custom-call(s32[32,128]{1,0:T(8,128)S(1)} %bitcast.14, bf16[2,1216,128]{2,1,0:T(8,128)(2,1)S(1)} %get-tuple-element.37.rest_0_, bf16[2,912,128]{2,1,0:T(8,128)(2,1)S(1)} %collective-permute-done.1.rest_1_, ...), custom_call_target="tpu_custom_call" | custom-call | flops 956301312 | bytes 6291456 | tf_op jit(solution)/shard_map/pallas_call | solution.py:157
  33.1 2.3 %collective-permute-start.13 = (bf16[304,512]{1,0:T(8,128)(2,1)S(1)}, bf16[304,512]{1,0:T(8,128)(2,1)S(1)}, u32[]{:S(2)}, u32[]{:S(2)}) collective-permute-start(bf16[304,512]{1,0:T(8,128)(2,1)S(1)} %get-tuple-element.49), channel_id=1, source_target_pairs={{0,64},{1,5},{2,66},{3,7},{4,68},{5,1},{6,70},{7,3},{32,96},{33,37... | collective-permute-start | bytes 933896 | tf_op jit(solution)/shard_map/ppermute | solution.py:62
  36.2 2.4 %collective-permute-start.15 = (bf16[304,512]{1,0:T(8,128)(2,1)S(1)}, bf16[304,512]{1,0:T(8,128)(2,1)S(1)}, u32[]{:S(2)}, u32[]{:S(2)}) collective-permute-start(bf16[304,512]{1,0:T(8,128)(2,1)S(1)} %get-tuple-element.50), channel_id=1, source_target_pairs={{0,96},{1,7},{2,98},{3,1},{4,100},{5,3},{6,102},{7,5},{32,0},{33,3... | collective-permute-start | bytes 933896 | tf_op jit(solution)/shard_map/ppermute | solution.py:62
  39.9 1.8 %collective-permute-done.13.a_ref = bf16[304,512]{1,0:T(8,128)(2,1)S(1)} collective-permute-done((bf16[304,512]{1,0:T(8,128)(2,1)S(1)}, bf16[304,512]{1,0:T(8,128)(2,1)S(1)}, u32[]{:S(2)}, u32[]{:S(2)}) %collective-permute-start.13) | collective-permute-done | bytes 311328 | tf_op jit(solution)/shard_map/ppermute | solution.py:62
  41.7 3.2 %collective-permute-done.14.b_ref = bf16[304,512]{1,0:T(8,128)(2,1)S(1)} collective-permute-done((bf16[304,512]{1,0:T(8,128)(2,1)S(1)}, bf16[304,512]{1,0:T(8,128)(2,1)S(1)}, u32[]{:S(2)}, u32[]{:S(2)}) %collective-permute-start.14) | collective-permute-done | bytes 311328 | tf_op jit(solution)/shard_map/ppermute | solution.py:62
  45.0 1.2 %shard_map.124 = f32[16,512]{1,0:T(8,128)S(1)} custom-call(f32[304,512]{1,0:T(8,128)S(1)} %convert_element_type.13.own_ref, bf16[304,512]{1,0:T(8,128)(2,1)S(1)} %collective-permute-done.13.a_ref, bf16[304,512]{1,0:T(8,128)(2,1)S(1)} %collective-permute-done.14.b_ref, bf16[304,512]{1,0:T(8,128)(2,1)S(1)} %collective-permute-done.15.c_ref, ...), custom_call_target="tpu_custom_call" | custom-call | bytes 3145728 | tf_op jit(solution)/shard_map/pallas_call | solution.py:304
  46.3 1.2 %collective-permute-done.16 = f32[16,512]{1,0:T(8,128)S(1)} collective-permute-done((f32[16,512]{1,0:T(8,128)S(1)}, f32[16,512]{1,0:T(8,128)S(1)}, u32[]{:S(2)}, u32[]{:S(2)}) %collective-permute-start.16) | collective-permute-done | bytes 32800 | tf_op jit(solution)/shard_map/ppermute | solution.py:317
  47.5 13.5 %all_to_all.10 = f32[8,16,512]{2,1,0:T(8,128)S(1)} all-to-all(f32[8,16,512]{2,1,0:T(8,128)S(1)} %broadcast_in_dim.4), channel_id=1, replica_groups={{0,24,2,26,4,28,6,30},{8,16,10,18,12,20,14,22},{1,25,3,27,5,29,7,31},{9..., dimensions={0} | all-to-all | bytes 524288 | tf_op jit(solution)/shard_map/all_to_all | solution.py:217
  61.0 10.1 %all_to_all.11.arrived_ref = f32[8,16,512]{2,1,0:T(8,128)S(1)} all-to-all(f32[8,16,512]{2,1,0:T(8,128)S(1)} %broadcast_in_dim.5), channel_id=1, replica_groups={{0,8,32,40,64,72,96,104},{16,24,48,56,80,88,112,120},{1,9,33,41,65,73,9..., dimensions={0} | all-to-all | bytes 524288 | tf_op jit(solution)/shard_map/all_to_all | solution.py:217
  (56 shorter events, 7.5 us)
Async XLA Ops:
  4.1 3.0 %collective-permute-start = (bf16[4,1216,128]{2,1,0:T(8,128)(2,1)S(1)}, bf16[4,1216,128]{2,1,0:T(8,128)(2,1)S(1)}, u32[]{:S(2)}, u32[]{:S(2)}) collective-permute-start(bf16[4,1216,128]{2,1,0:T(8,128)(2,1)S(1)} %get-tuple-element.32), channel_id=1, source_target_pairs={{0,1},{1,0},{2,3},{3,2},{4,5},{5,4},{6,7},{7,6},{8,9},{9,8},{10,11... | collective-permute-start | bytes 3735560 | tf_op jit(solution)/shard_map/ppermute | solution.py:268
  7.2 24.6 %copy-start.5 = (s32[4096]{0:T(1024)S(1)}, s32[4096]{0:T(1024)}, u32[]{:S(2)}) copy-start(s32[4096]{0:T(1024)} %param.22) | copy-start | bytes 49156
  7.2 19.5 %collective-permute-start.6 = (bf16[2,1216,128]{2,1,0:T(8,128)(2,1)S(1)}, bf16[2,1216,128]{2,1,0:T(8,128)(2,1)S(1)}, u32[]{:S(2)}, u32[]{:S(2)}) collective-permute-start(bf16[2,1216,128]{2,1,0:T(8,128)(2,1)S(1)} %shard_map.121), channel_id=1, source_target_pairs={{0,4},{1,65},{2,6},{3,67},{4,0},{5,69},{6,2},{7,71},{32,36},{33,97... | collective-permute-start | bytes 1867784 | tf_op jit(solution)/shard_map/ppermute | solution.py:58
  10.5 7.4 %collective-permute-start.3 = (f32[128,256]{1,0:T(8,128)S(1)}, f32[128,256]{1,0:T(8,128)S(1)}, u32[]{:S(2)}, u32[]{:S(2)}) collective-permute-start(f32[128,256]{1,0:T(8,128)S(1)} %shard_map.119), channel_id=1, source_target_pairs={{0,8},{8,16},{16,24},{24,0},{1,9},{9,17},{17,25},{25,1},{2,10},{10... | collective-permute-start | bytes 393224 | tf_op jit(solution)/shard_map/ppermute | solution.py:273
  12.4 7.6 %collective-permute-start.4 = (f32[128,256]{1,0:T(8,128)S(1)}, f32[128,256]{1,0:T(8,128)S(1)}, u32[]{:S(2)}, u32[]{:S(2)}) collective-permute-start(f32[128,256]{1,0:T(8,128)S(1)} %shard_map.119), channel_id=1, source_target_pairs={{0,24},{8,0},{16,8},{24,16},{1,25},{9,1},{17,9},{25,17},{2,26},{10... | collective-permute-start | bytes 393224 | tf_op jit(solution)/shard_map/ppermute | solution.py:273
  14.6 7.3 %collective-permute-start.2 = (f32[128,256]{1,0:T(8,128)S(1)}, f32[128,256]{1,0:T(8,128)S(1)}, u32[]{:S(2)}, u32[]{:S(2)}) collective-permute-start(f32[128,256]{1,0:T(8,128)S(1)} %shard_map.119), channel_id=1, source_target_pairs={{0,16},{8,24},{16,0},{24,8},{1,17},{9,25},{17,1},{25,9},{2,18},{10... | collective-permute-start | bytes 393224 | tf_op jit(solution)/shard_map/ppermute | solution.py:273
  16.6 11.2 %collective-permute-start.1 = (bf16[2,912,128]{2,1,0:T(8,128)(2,1)S(1)}, bf16[2,912,128]{2,1,0:T(8,128)(2,1)S(1)}, u32[]{:S(2)}, u32[]{:S(2)}) collective-permute-start(bf16[2,912,128]{2,1,0:T(8,128)(2,1)S(1)} %get-tuple-element.39), channel_id=1, source_target_pairs={{0,2},{1,33},{2,4},{3,35},{4,6},{5,37},{6,0},{7,39},{32,34},{33,65... | collective-permute-start | bytes 1400840 | tf_op jit(solution)/shard_map/ppermute | solution.py:58
  17.9 9.8 %collective-permute-start.7 = (bf16[2,912,128]{2,1,0:T(8,128)(2,1)S(1)}, bf16[2,912,128]{2,1,0:T(8,128)(2,1)S(1)}, u32[]{:S(2)}, u32[]{:S(2)}) collective-permute-start(bf16[2,912,128]{2,1,0:T(8,128)(2,1)S(1)} %get-tuple-element.45), channel_id=1, source_target_pairs={{0,6},{1,97},{2,0},{3,99},{4,2},{5,101},{6,4},{7,103},{32,38},{33,... | collective-permute-start | bytes 1400840 | tf_op jit(solution)/shard_map/ppermute | solution.py:58
  21.9 1.3 %collective-permute-start.5 = (bf16[128,256]{1,0:T(8,128)(2,1)S(1)}, bf16[128,256]{1,0:T(8,128)(2,1)S(1)}, u32[]{:S(2)}, u32[]{:S(2)}) collective-permute-start(bf16[128,256]{1,0:T(8,128)(2,1)S(1)} %add_convert_fusion), channel_id=1, source_target_pairs={{0,1},{1,0},{2,3},{3,2},{4,5},{5,4},{6,7},{7,6},{8,9},{9,8},{10,11... | collective-permute-start | bytes 196616 | tf_op jit(solution)/shard_map/ppermute | solution.py:277
  23.3 7.7 %collective-permute-start.8 = (bf16[256,256]{1,0:T(8,128)(2,1)S(1)}, bf16[256,256]{1,0:T(8,128)(2,1)S(1)}, u32[]{:S(2)}, u32[]{:S(2)}) collective-permute-start(bf16[256,256]{1,0:T(8,128)(2,1)S(1)} %pad_maximum_fusion.rest_4_), channel_id=1, source_target_pairs={{0,2},{1,33},{2,4},{3,35},{4,6},{5,37},{6,0},{7,39},{32,34},{33,65... | collective-permute-start | bytes 393224 | tf_op jit(solution)/shard_map/ppermute | solution.py:58
  24.9 6.5 %collective-permute-start.9 = (bf16[256,256]{1,0:T(8,128)(2,1)S(1)}, bf16[256,256]{1,0:T(8,128)(2,1)S(1)}, u32[]{:S(2)}, u32[]{:S(2)}) collective-permute-start(bf16[256,256]{1,0:T(8,128)(2,1)S(1)} %pad_maximum_fusion.rest_4_), channel_id=1, source_target_pairs={{0,4},{1,65},{2,6},{3,67},{4,0},{5,69},{6,2},{7,71},{32,36},{33,97... | collective-permute-start | bytes 393224 | tf_op jit(solution)/shard_map/ppermute | solution.py:58
  26.6 5.2 %collective-permute-start.10 = (bf16[256,256]{1,0:T(8,128)(2,1)S(1)}, bf16[256,256]{1,0:T(8,128)(2,1)S(1)}, u32[]{:S(2)}, u32[]{:S(2)}) collective-permute-start(bf16[256,256]{1,0:T(8,128)(2,1)S(1)} %pad_maximum_fusion.rest_4_), channel_id=1, source_target_pairs={{0,6},{1,97},{2,0},{3,99},{4,2},{5,101},{6,4},{7,103},{32,38},{33,... | collective-permute-start | bytes 393224 | tf_op jit(solution)/shard_map/ppermute | solution.py:58
  27.7 10.9 %collective-permute-start.11 = (bf16[2,304,128]{2,1,0:T(8,128)(2,1)S(1)}, bf16[2,304,128]{2,1,0:T(8,128)(2,1)S(1)}, u32[]{:S(2)}, u32[]{:S(2)}) collective-permute-start(bf16[2,304,128]{2,1,0:T(8,128)(2,1)S(1)} %get-tuple-element.52), channel_id=1, source_target_pairs={{0,2},{1,33},{2,4},{3,35},{4,6},{5,37},{6,0},{7,39},{32,34},{33,65... | collective-permute-start | bytes 466952 | tf_op jit(solution)/shard_map/ppermute | solution.py:58
  28.7 10.0 %collective-permute-start.12 = (bf16[2,304,128]{2,1,0:T(8,128)(2,1)S(1)}, bf16[2,304,128]{2,1,0:T(8,128)(2,1)S(1)}, u32[]{:S(2)}, u32[]{:S(2)}) collective-permute-start(bf16[2,304,128]{2,1,0:T(8,128)(2,1)S(1)} %get-tuple-element.53), channel_id=1, source_target_pairs={{0,6},{1,97},{2,0},{3,99},{4,2},{5,101},{6,4},{7,103},{32,38},{33,... | collective-permute-start | bytes 466952 | tf_op jit(solution)/shard_map/ppermute | solution.py:58
  33.1 6.5 %copy-start.10 = (s32[1,231]{1,0:T(1,128)S(1)}, s32[1,231]{1,0:T(1,128)}, u32[]{:S(2)}) copy-start(s32[1,231]{1,0:T(1,128)} %param.21) | copy-start | bytes 2776
  33.1 6.7 %copy-start.8 = (f32[1,231,128]{2,0,1:T(1,128)S(1)}, f32[1,231,128]{2,0,1:T(1,128)}, u32[]{:S(2)}) copy-start(f32[1,231,128]{2,0,1:T(1,128)} %param.19) | copy-start | bytes 354820
  33.1 6.7 %copy-start.9 = (f32[1,231,128]{2,0,1:T(1,128)S(1)}, f32[1,231,128]{2,0,1:T(1,128)}, u32[]{:S(2)}) copy-start(f32[1,231,128]{2,0,1:T(1,128)} %param.18) | copy-start | bytes 354820
  33.1 8.6 %collective-permute-start.13 = (bf16[304,512]{1,0:T(8,128)(2,1)S(1)}, bf16[304,512]{1,0:T(8,128)(2,1)S(1)}, u32[]{:S(2)}, u32[]{:S(2)}) collective-permute-start(bf16[304,512]{1,0:T(8,128)(2,1)S(1)} %get-tuple-element.49), channel_id=1, source_target_pairs={{0,64},{1,5},{2,66},{3,7},{4,68},{5,1},{6,70},{7,3},{32,96},{33,37... | collective-permute-start | bytes 933896 | tf_op jit(solution)/shard_map/ppermute | solution.py:62
  35.4 9.6 %collective-permute-start.14 = (bf16[304,512]{1,0:T(8,128)(2,1)S(1)}, bf16[304,512]{1,0:T(8,128)(2,1)S(1)}, u32[]{:S(2)}, u32[]{:S(2)}) collective-permute-start(bf16[304,512]{1,0:T(8,128)(2,1)S(1)} %get-tuple-element.48), channel_id=1, source_target_pairs={{0,32},{1,3},{2,34},{3,5},{4,36},{5,7},{6,38},{7,1},{32,64},{33,35... | collective-permute-start | bytes 933896 | tf_op jit(solution)/shard_map/ppermute | solution.py:62
  36.2 8.7 %copy-start.6 = (f32[1,64,128]{2,1,0:T(8,128)S(1)}, f32[1,64,128]{2,1,0:T(8,128)}, u32[]{:S(2)}) copy-start(f32[1,64,128]{2,1,0:T(8,128)} %param.16) | copy-start | bytes 98308
  36.2 8.7 %copy-start.7 = (f32[1,64,128]{2,1,0:T(8,128)S(1)}, f32[1,64,128]{2,1,0:T(8,128)}, u32[]{:S(2)}) copy-start(f32[1,64,128]{2,1,0:T(8,128)} %param.17) | copy-start | bytes 98308
  36.2 8.7 %collective-permute-start.15 = (bf16[304,512]{1,0:T(8,128)(2,1)S(1)}, bf16[304,512]{1,0:T(8,128)(2,1)S(1)}, u32[]{:S(2)}, u32[]{:S(2)}) collective-permute-start(bf16[304,512]{1,0:T(8,128)(2,1)S(1)} %get-tuple-element.50), channel_id=1, source_target_pairs={{0,96},{1,7},{2,98},{3,1},{4,100},{5,3},{6,102},{7,5},{32,0},{33,3... | collective-permute-start | bytes 933896 | tf_op jit(solution)/shard_map/ppermute | solution.py:62
  45.0 26.2 %copy-start.4 = (bf16[16,128,64]{1,2,0:T(8,128)(2,1)S(1)}, bf16[16,128,64]{1,2,0:T(8,128)(2,1)}, u32[]{:S(2)}) copy-start(bf16[16,128,64]{1,2,0:T(8,128)(2,1)} %param.23) | copy-start | bytes 786436
  46.2 1.2 %collective-permute-start.16 = (f32[16,512]{1,0:T(8,128)S(1)}, f32[16,512]{1,0:T(8,128)S(1)}, u32[]{:S(2)}, u32[]{:S(2)}) collective-permute-start(f32[16,512]{1,0:T(8,128)S(1)} %shard_map.124), channel_id=1, source_target_pairs={{0,1},{1,0},{2,3},{3,2},{4,5},{5,4},{6,7},{7,6},{8,9},{9,8},{10,11... | collective-permute-start | bytes 98312 | tf_op jit(solution)/shard_map/ppermute | solution.py:317
  (5 other events, 12.3 us)

commit v13 on v12

--- a/solution.py
+++ b/solution.py
@@ -70,10 +70,9 @@
     return lax.optimization_barrier((value, arrived))
 
 
-def pack_kernel(grad, tokens, *rest):
-    give, mine, turned = rest[0], rest[1:5], rest[5]
+def pack_kernel(grad, turned, *rest):
+    give, mine = rest[0], rest[1:5]
     x, y, c = position()
-    turned[...] = tokens[...].T
     for slot in (2, 6, 1, 5, 3, 7, 0, 4):
         target = 1 - c if slot < 4 else c
         k = slot % 4
@@ -253,10 +252,9 @@
         out_shape=[jax.ShapeDtypeStruct((4, 4 * ROWS, 128), BF)] + [jax.ShapeDtypeStruct((4 * ROWS, 128), BF)] * 4,
         in_specs=[VMEM] * 2,
         out_specs=[VMEM] * 5,
-        scratch_shapes=[pltpu.VMEM((2048, 128), BF)],
         compiler_params=pltpu.CompilerParams(vmem_limit_bytes=24 << 20),
         cost_estimate=pl.CostEstimate(flops=0, bytes_accessed=5 << 20, transcendentals=0),
-    )(turned_grad, tokens)
+    )(turned_grad, tokens.T)
     portion = pl.pallas_call(
         product_kernel,
         out_shape=jax.ShapeDtypeStruct((128, PAIR), F32),

time: 72.2 us -> 72.3 us (level)
    unnamed x25 -> x26, local copies, waits for them, and re-layouts: 2.63 us -> 3.19 us
where the time goes in v13:
time: 72.3 us; the launch traced here: 72 us
  starting transfers between devices  25.3 us (35%)
  blocking collectives  23.6 us (33%)
  waiting for transfers between devices  12.9 us (18%)
  Pallas kernels  6.38 us (9%)
  local copies, waits for them, and re-layouts  3.23 us (4%)
    all_to_all x2, blocking collectives, spread(): lax.all_to_all(copies, EVERY, split_axis=0, concat_axis=0, tiled=True, ax...  23.6 us
    ppermute x8, starting transfers between devices, send_same(): return lax.ppermute(value, PLANE, pairs(lambda p: along(p, shift)))  13.7 us
    ppermute x3, starting transfers between devices, on_device(): lax.ppermute(portion, ('t1', 't0'), [(i, (i + shift) % 4) for i in range(...  5.9 us
    ppermute x3, starting transfers between devices, send_across(): return lax.ppermute(value, PLANE, pairs(lambda p: across(p, shift)))  5.47 us
    ppermute x3, waiting for transfers between devices, send_across(): return lax.ppermute(value, PLANE, pairs(lambda p: across(p, shift)))  5.08 us
    unnamed x26, local copies, waits for them, and re-layouts  3.19 us
    ppermute x3, waiting for transfers between devices, on_device(): lax.ppermute(portion, ('t1', 't0'), [(i, (i + shift) % 4) for i in range(...  2.64 us
    pallas_call x2, Pallas kernels, partial_call(): pl.pallas_call(functools.partial(partial_kernel, count), out_shape=[jax.S...  2.16 us
  transfers between devices with their start and end apart: 17, of which 10 were waited for; matrix products, arithmetic and copies ran while one was open for 1% of the time, Pallas kernels for 4%

profile of v13, /device:TPU:0, one launch (start us, length us, event | category | flops | bytes accessed | tf_op | source)
XLA Modules:
  0.0 72.0 jit_solution(12616885952569701546)
XLA Ops:
  0.0 1.4 %copy.14 = bf16[128,2048]{0,1:T(8,128)(2,1)S(1)} copy(bf16[128,2048]{1,0:T(8,128)(2,1)} %tokens.1) | data formatting | bytes 1048576 | tf_op args[0]
  1.4 1.5 %copy-done = bf16[128,7392]{0,1:T(8,128)(2,1)S(1)} copy-done((bf16[128,7392]{0,1:T(8,128)(2,1)S(1)}, bf16[128,7392]{0,1:T(8,128)(2,1)}, u32[]{:S(2)}) %copy-start) | copy-done | bytes 1892376
  2.9 1.2 %shard_map.118 = (bf16[4,1216,128]{2,1,0:T(8,128)(2,1)S(1)}, bf16[1216,128]{1,0:T(8,128)(2,1)S(1)}, bf16[1216,128]{1,0:T(8,128)(2,1)S(1)}, bf16[1216,128]{1,0:T(8,128)(2,1)S(1)}, bf16[1216,128]{1,0:T(8,128)(2,1)S(1)}) custom-call(bf16[7392,128]{1,0:T(8,128)(2,1)S(1)} %bitcast.12, bf16[2048,128]{1,0:T(8,128)(2,1)S(1)} %bitcast.14), custom_call_target="tpu_custom_call" | custom-call | bytes 5242880 | tf_op jit(solution)/shard_map/pallas_call | solution.py:250
  5.3 1.9 %collective-permute-done.taken_ref = bf16[4,1216,128]{2,1,0:T(8,128)(2,1)S(1)} collective-permute-done((bf16[4,1216,128]{2,1,0:T(8,128)(2,1)S(1)}, bf16[4,1216,128]{2,1,0:T(8,128)(2,1)S(1)}, u32[]{:S(2)}, u32[]{:S(2)}) %collective-permute-start) | collective-permute-done | bytes 1245216 | tf_op jit(solution)/shard_map/ppermute | solution.py:266
  7.2 3.4 %collective-permute-start.6 = (bf16[2,1216,128]{2,1,0:T(8,128)(2,1)S(1)}, bf16[2,1216,128]{2,1,0:T(8,128)(2,1)S(1)}, u32[]{:S(2)}, u32[]{:S(2)}) collective-permute-start(bf16[2,1216,128]{2,1,0:T(8,128)(2,1)S(1)} %shard_map.121), channel_id=1, source_target_pairs={{0,4},{1,65},{2,6},{3,67},{4,0},{5,69},{6,2},{7,71},{32,36},{33,97... | collective-permute-start | bytes 1867784 | tf_op jit(solution)/shard_map/ppermute | solution.py:58
  10.6 1.9 %collective-permute-start.3 = (f32[128,256]{1,0:T(8,128)S(1)}, f32[128,256]{1,0:T(8,128)S(1)}, u32[]{:S(2)}, u32[]{:S(2)}) collective-permute-start(f32[128,256]{1,0:T(8,128)S(1)} %shard_map.119), channel_id=1, source_target_pairs={{0,8},{8,16},{16,24},{24,0},{1,9},{9,17},{17,25},{25,1},{2,10},{10... | collective-permute-start | bytes 393224 | tf_op jit(solution)/shard_map/ppermute | solution.py:271
  12.5 2.1 %collective-permute-start.4 = (f32[128,256]{1,0:T(8,128)S(1)}, f32[128,256]{1,0:T(8,128)S(1)}, u32[]{:S(2)}, u32[]{:S(2)}) collective-permute-start(f32[128,256]{1,0:T(8,128)S(1)} %shard_map.119), channel_id=1, source_target_pairs={{0,24},{8,0},{16,8},{24,16},{1,25},{9,1},{17,9},{25,17},{2,26},{10... | collective-permute-start | bytes 393224 | tf_op jit(solution)/shard_map/ppermute | solution.py:271
  14.6 1.9 %collective-permute-start.2 = (f32[128,256]{1,0:T(8,128)S(1)}, f32[128,256]{1,0:T(8,128)S(1)}, u32[]{:S(2)}, u32[]{:S(2)}) collective-permute-start(f32[128,256]{1,0:T(8,128)S(1)} %shard_map.119), channel_id=1, source_target_pairs={{0,16},{8,24},{16,0},{24,8},{1,17},{9,25},{17,1},{25,9},{2,18},{10... | collective-permute-start | bytes 393224 | tf_op jit(solution)/shard_map/ppermute | solution.py:271
  18.0 2.0 %collective-permute-start.7 = (bf16[2,912,128]{2,1,0:T(8,128)(2,1)S(1)}, bf16[2,912,128]{2,1,0:T(8,128)(2,1)S(1)}, u32[]{:S(2)}, u32[]{:S(2)}) collective-permute-start(bf16[2,912,128]{2,1,0:T(8,128)(2,1)S(1)} %get-tuple-element.45), channel_id=1, source_target_pairs={{0,6},{1,97},{2,0},{3,99},{4,2},{5,101},{6,4},{7,103},{32,38},{33,... | collective-permute-start | bytes 1400840 | tf_op jit(solution)/shard_map/ppermute | solution.py:58
  20.1 1.9 %collective-permute-done.2 = f32[128,256]{1,0:T(8,128)S(1)} collective-permute-done((f32[128,256]{1,0:T(8,128)S(1)}, f32[128,256]{1,0:T(8,128)S(1)}, u32[]{:S(2)}, u32[]{:S(2)}) %collective-permute-start.2) | collective-permute-done | bytes 131104 | tf_op jit(solution)/shard_map/ppermute | solution.py:271
  22.1 1.2 %collective-permute-done.5 = bf16[128,256]{1,0:T(8,128)(2,1)S(1)} collective-permute-done((bf16[128,256]{1,0:T(8,128)(2,1)S(1)}, bf16[128,256]{1,0:T(8,128)(2,1)S(1)}, u32[]{:S(2)}, u32[]{:S(2)}) %collective-permute-start.5) | collective-permute-done | bytes 65568 | tf_op jit(solution)/shard_map/ppermute | solution.py:275
  23.3 1.6 %collective-permute-start.8 = (bf16[256,256]{1,0:T(8,128)(2,1)S(1)}, bf16[256,256]{1,0:T(8,128)(2,1)S(1)}, u32[]{:S(2)}, u32[]{:S(2)}) collective-permute-start(bf16[256,256]{1,0:T(8,128)(2,1)S(1)} %pad_maximum_fusion.rest_4_), channel_id=1, source_target_pairs={{0,2},{1,33},{2,4},{3,35},{4,6},{5,37},{6,0},{7,39},{32,34},{33,65... | collective-permute-start | bytes 393224 | tf_op jit(solution)/shard_map/ppermute | solution.py:58
  25.0 1.7 %collective-permute-start.9 = (bf16[256,256]{1,0:T(8,128)(2,1)S(1)}, bf16[256,256]{1,0:T(8,128)(2,1)S(1)}, u32[]{:S(2)}, u32[]{:S(2)}) collective-permute-start(bf16[256,256]{1,0:T(8,128)(2,1)S(1)} %pad_maximum_fusion.rest_4_), channel_id=1, source_target_pairs={{0,4},{1,65},{2,6},{3,67},{4,0},{5,69},{6,2},{7,71},{32,36},{33,97... | collective-permute-start | bytes 393224 | tf_op jit(solution)/shard_map/ppermute | solution.py:58
  26.7 1.1 %collective-permute-start.10 = (bf16[256,256]{1,0:T(8,128)(2,1)S(1)}, bf16[256,256]{1,0:T(8,128)(2,1)S(1)}, u32[]{:S(2)}, u32[]{:S(2)}) collective-permute-start(bf16[256,256]{1,0:T(8,128)(2,1)S(1)} %pad_maximum_fusion.rest_4_), channel_id=1, source_target_pairs={{0,6},{1,97},{2,0},{3,99},{4,2},{5,101},{6,4},{7,103},{32,38},{33,... | collective-permute-start | bytes 393224 | tf_op jit(solution)/shard_map/ppermute | solution.py:58
  28.7 2.3 %collective-permute-start.12 = (bf16[2,304,128]{2,1,0:T(8,128)(2,1)S(1)}, bf16[2,304,128]{2,1,0:T(8,128)(2,1)S(1)}, u32[]{:S(2)}, u32[]{:S(2)}) collective-permute-start(bf16[2,304,128]{2,1,0:T(8,128)(2,1)S(1)} %get-tuple-element.53), channel_id=1, source_target_pairs={{0,6},{1,97},{2,0},{3,99},{4,2},{5,101},{6,4},{7,103},{32,38},{33,... | collective-permute-start | bytes 466952 | tf_op jit(solution)/shard_map/ppermute | solution.py:58
  31.9 1.3 %shard_map.122 = (bf16[304,512]{1,0:T(8,128)(2,1)S(1)}, bf16[304,512]{1,0:T(8,128)(2,1)S(1)}, bf16[304,512]{1,0:T(8,128)(2,1)S(1)}) custom-call(s32[32,128]{1,0:T(8,128)S(1)} %bitcast.16, bf16[2,1216,128]{2,1,0:T(8,128)(2,1)S(1)} %get-tuple-element.37.rest_0_, bf16[2,912,128]{2,1,0:T(8,128)(2,1)S(1)} %collective-permute-done.1.rest_1_, ...), custom_call_target="tpu_custom_call" | custom-call | flops 956301312 | bytes 6291456 | tf_op jit(solution)/shard_map/pallas_call | solution.py:156
  33.2 2.2 %collective-permute-start.13 = (bf16[304,512]{1,0:T(8,128)(2,1)S(1)}, bf16[304,512]{1,0:T(8,128)(2,1)S(1)}, u32[]{:S(2)}, u32[]{:S(2)}) collective-permute-start(bf16[304,512]{1,0:T(8,128)(2,1)S(1)} %get-tuple-element.49), channel_id=1, source_target_pairs={{0,64},{1,5},{2,66},{3,7},{4,68},{5,1},{6,70},{7,3},{32,96},{33,37... | collective-permute-start | bytes 933896 | tf_op jit(solution)/shard_map/ppermute | solution.py:62
  36.3 2.4 %collective-permute-start.15 = (bf16[304,512]{1,0:T(8,128)(2,1)S(1)}, bf16[304,512]{1,0:T(8,128)(2,1)S(1)}, u32[]{:S(2)}, u32[]{:S(2)}) collective-permute-start(bf16[304,512]{1,0:T(8,128)(2,1)S(1)} %get-tuple-element.50), channel_id=1, source_target_pairs={{0,96},{1,7},{2,98},{3,1},{4,100},{5,3},{6,102},{7,5},{32,0},{33,3... | collective-permute-start | bytes 933896 | tf_op jit(solution)/shard_map/ppermute | solution.py:62
  39.9 1.9 %collective-permute-done.13.a_ref = bf16[304,512]{1,0:T(8,128)(2,1)S(1)} collective-permute-done((bf16[304,512]{1,0:T(8,128)(2,1)S(1)}, bf16[304,512]{1,0:T(8,128)(2,1)S(1)}, u32[]{:S(2)}, u32[]{:S(2)}) %collective-permute-start.13) | collective-permute-done | bytes 311328 | tf_op jit(solution)/shard_map/ppermute | solution.py:62
  41.8 3.2 %collective-permute-done.14.b_ref = bf16[304,512]{1,0:T(8,128)(2,1)S(1)} collective-permute-done((bf16[304,512]{1,0:T(8,128)(2,1)S(1)}, bf16[304,512]{1,0:T(8,128)(2,1)S(1)}, u32[]{:S(2)}, u32[]{:S(2)}) %collective-permute-start.14) | collective-permute-done | bytes 311328 | tf_op jit(solution)/shard_map/ppermute | solution.py:62
  45.0 1.2 %shard_map.124 = f32[16,512]{1,0:T(8,128)S(1)} custom-call(f32[304,512]{1,0:T(8,128)S(1)} %convert_element_type.13.own_ref, bf16[304,512]{1,0:T(8,128)(2,1)S(1)} %collective-permute-done.13.a_ref, bf16[304,512]{1,0:T(8,128)(2,1)S(1)} %collective-permute-done.14.b_ref, bf16[304,512]{1,0:T(8,128)(2,1)S(1)} %collective-permute-done.15.c_ref, ...), custom_call_target="tpu_custom_call" | custom-call | bytes 3145728 | tf_op jit(solution)/shard_map/pallas_call | solution.py:302
  46.3 1.2 %collective-permute-done.16 = f32[16,512]{1,0:T(8,128)S(1)} collective-permute-done((f32[16,512]{1,0:T(8,128)S(1)}, f32[16,512]{1,0:T(8,128)S(1)}, u32[]{:S(2)}, u32[]{:S(2)}) %collective-permute-start.16) | collective-permute-done | bytes 32800 | tf_op jit(solution)/shard_map/ppermute | solution.py:315
  47.5 13.5 %all_to_all.10 = f32[8,16,512]{2,1,0:T(8,128)S(1)} all-to-all(f32[8,16,512]{2,1,0:T(8,128)S(1)} %broadcast_in_dim.4), channel_id=1, replica_groups={{0,24,2,26,4,28,6,30},{8,16,10,18,12,20,14,22},{1,25,3,27,5,29,7,31},{9..., dimensions={0} | all-to-all | bytes 524288 | tf_op jit(solution)/shard_map/all_to_all | solution.py:216
  61.0 10.1 %all_to_all.11.arrived_ref = f32[8,16,512]{2,1,0:T(8,128)S(1)} all-to-all(f32[8,16,512]{2,1,0:T(8,128)S(1)} %broadcast_in_dim.5), channel_id=1, replica_groups={{0,8,32,40,64,72,96,104},{16,24,48,56,80,88,112,120},{1,9,33,41,65,73,9..., dimensions={0} | all-to-all | bytes 524288 | tf_op jit(solution)/shard_map/all_to_all | solution.py:216
  (57 shorter events, 7.7 us)
Async XLA Ops:
  4.1 3.0 %collective-permute-start = (bf16[4,1216,128]{2,1,0:T(8,128)(2,1)S(1)}, bf16[4,1216,128]{2,1,0:T(8,128)(2,1)S(1)}, u32[]{:S(2)}, u32[]{:S(2)}) collective-permute-start(bf16[4,1216,128]{2,1,0:T(8,128)(2,1)S(1)} %get-tuple-element.32), channel_id=1, source_target_pairs={{0,1},{1,0},{2,3},{3,2},{4,5},{5,4},{6,7},{7,6},{8,9},{9,8},{10,11... | collective-permute-start | bytes 3735560 | tf_op jit(solution)/shard_map/ppermute | solution.py:266
  7.2 24.6 %copy-start.5 = (s32[4096]{0:T(1024)S(1)}, s32[4096]{0:T(1024)}, u32[]{:S(2)}) copy-start(s32[4096]{0:T(1024)} %param.22) | copy-start | bytes 49156
  7.2 19.5 %collective-permute-start.6 = (bf16[2,1216,128]{2,1,0:T(8,128)(2,1)S(1)}, bf16[2,1216,128]{2,1,0:T(8,128)(2,1)S(1)}, u32[]{:S(2)}, u32[]{:S(2)}) collective-permute-start(bf16[2,1216,128]{2,1,0:T(8,128)(2,1)S(1)} %shard_map.121), channel_id=1, source_target_pairs={{0,4},{1,65},{2,6},{3,67},{4,0},{5,69},{6,2},{7,71},{32,36},{33,97... | collective-permute-start | bytes 1867784 | tf_op jit(solution)/shard_map/ppermute | solution.py:58
  10.6 7.4 %collective-permute-start.3 = (f32[128,256]{1,0:T(8,128)S(1)}, f32[128,256]{1,0:T(8,128)S(1)}, u32[]{:S(2)}, u32[]{:S(2)}) collective-permute-start(f32[128,256]{1,0:T(8,128)S(1)} %shard_map.119), channel_id=1, source_target_pairs={{0,8},{8,16},{16,24},{24,0},{1,9},{9,17},{17,25},{25,1},{2,10},{10... | collective-permute-start | bytes 393224 | tf_op jit(solution)/shard_map/ppermute | solution.py:271
  12.5 7.6 %collective-permute-start.4 = (f32[128,256]{1,0:T(8,128)S(1)}, f32[128,256]{1,0:T(8,128)S(1)}, u32[]{:S(2)}, u32[]{:S(2)}) collective-permute-start(f32[128,256]{1,0:T(8,128)S(1)} %shard_map.119), channel_id=1, source_target_pairs={{0,24},{8,0},{16,8},{24,16},{1,25},{9,1},{17,9},{25,17},{2,26},{10... | collective-permute-start | bytes 393224 | tf_op jit(solution)/shard_map/ppermute | solution.py:271
  14.6 7.3 %collective-permute-start.2 = (f32[128,256]{1,0:T(8,128)S(1)}, f32[128,256]{1,0:T(8,128)S(1)}, u32[]{:S(2)}, u32[]{:S(2)}) collective-permute-start(f32[128,256]{1,0:T(8,128)S(1)} %shard_map.119), channel_id=1, source_target_pairs={{0,16},{8,24},{16,0},{24,8},{1,17},{9,25},{17,1},{25,9},{2,18},{10... | collective-permute-start | bytes 393224 | tf_op jit(solution)/shard_map/ppermute | solution.py:271
  16.6 11.2 %collective-permute-start.1 = (bf16[2,912,128]{2,1,0:T(8,128)(2,1)S(1)}, bf16[2,912,128]{2,1,0:T(8,128)(2,1)S(1)}, u32[]{:S(2)}, u32[]{:S(2)}) collective-permute-start(bf16[2,912,128]{2,1,0:T(8,128)(2,1)S(1)} %get-tuple-element.39), channel_id=1, source_target_pairs={{0,2},{1,33},{2,4},{3,35},{4,6},{5,37},{6,0},{7,39},{32,34},{33,65... | collective-permute-start | bytes 1400840 | tf_op jit(solution)/shard_map/ppermute | solution.py:58
  18.0 9.8 %collective-permute-start.7 = (bf16[2,912,128]{2,1,0:T(8,128)(2,1)S(1)}, bf16[2,912,128]{2,1,0:T(8,128)(2,1)S(1)}, u32[]{:S(2)}, u32[]{:S(2)}) collective-permute-start(bf16[2,912,128]{2,1,0:T(8,128)(2,1)S(1)} %get-tuple-element.45), channel_id=1, source_target_pairs={{0,6},{1,97},{2,0},{3,99},{4,2},{5,101},{6,4},{7,103},{32,38},{33,... | collective-permute-start | bytes 1400840 | tf_op jit(solution)/shard_map/ppermute | solution.py:58
  22.0 1.3 %collective-permute-start.5 = (bf16[128,256]{1,0:T(8,128)(2,1)S(1)}, bf16[128,256]{1,0:T(8,128)(2,1)S(1)}, u32[]{:S(2)}, u32[]{:S(2)}) collective-permute-start(bf16[128,256]{1,0:T(8,128)(2,1)S(1)} %add_convert_fusion), channel_id=1, source_target_pairs={{0,1},{1,0},{2,3},{3,2},{4,5},{5,4},{6,7},{7,6},{8,9},{9,8},{10,11... | collective-permute-start | bytes 196616 | tf_op jit(solution)/shard_map/ppermute | solution.py:275
  23.3 7.7 %collective-permute-start.8 = (bf16[256,256]{1,0:T(8,128)(2,1)S(1)}, bf16[256,256]{1,0:T(8,128)(2,1)S(1)}, u32[]{:S(2)}, u32[]{:S(2)}) collective-permute-start(bf16[256,256]{1,0:T(8,128)(2,1)S(1)} %pad_maximum_fusion.rest_4_), channel_id=1, source_target_pairs={{0,2},{1,33},{2,4},{3,35},{4,6},{5,37},{6,0},{7,39},{32,34},{33,65... | collective-permute-start | bytes 393224 | tf_op jit(solution)/shard_map/ppermute | solution.py:58
  25.0 6.5 %collective-permute-start.9 = (bf16[256,256]{1,0:T(8,128)(2,1)S(1)}, bf16[256,256]{1,0:T(8,128)(2,1)S(1)}, u32[]{:S(2)}, u32[]{:S(2)}) collective-permute-start(bf16[256,256]{1,0:T(8,128)(2,1)S(1)} %pad_maximum_fusion.rest_4_), channel_id=1, source_target_pairs={{0,4},{1,65},{2,6},{3,67},{4,0},{5,69},{6,2},{7,71},{32,36},{33,97... | collective-permute-start | bytes 393224 | tf_op jit(solution)/shard_map/ppermute | solution.py:58
  26.7 5.2 %collective-permute-start.10 = (bf16[256,256]{1,0:T(8,128)(2,1)S(1)}, bf16[256,256]{1,0:T(8,128)(2,1)S(1)}, u32[]{:S(2)}, u32[]{:S(2)}) collective-permute-start(bf16[256,256]{1,0:T(8,128)(2,1)S(1)} %pad_maximum_fusion.rest_4_), channel_id=1, source_target_pairs={{0,6},{1,97},{2,0},{3,99},{4,2},{5,101},{6,4},{7,103},{32,38},{33,... | collective-permute-start | bytes 393224 | tf_op jit(solution)/shard_map/ppermute | solution.py:58
  27.8 10.9 %collective-permute-start.11 = (bf16[2,304,128]{2,1,0:T(8,128)(2,1)S(1)}, bf16[2,304,128]{2,1,0:T(8,128)(2,1)S(1)}, u32[]{:S(2)}, u32[]{:S(2)}) collective-permute-start(bf16[2,304,128]{2,1,0:T(8,128)(2,1)S(1)} %get-tuple-element.52), channel_id=1, source_target_pairs={{0,2},{1,33},{2,4},{3,35},{4,6},{5,37},{6,0},{7,39},{32,34},{33,65... | collective-permute-start | bytes 466952 | tf_op jit(solution)/shard_map/ppermute | solution.py:58
  28.7 10.0 %collective-permute-start.12 = (bf16[2,304,128]{2,1,0:T(8,128)(2,1)S(1)}, bf16[2,304,128]{2,1,0:T(8,128)(2,1)S(1)}, u32[]{:S(2)}, u32[]{:S(2)}) collective-permute-start(bf16[2,304,128]{2,1,0:T(8,128)(2,1)S(1)} %get-tuple-element.53), channel_id=1, source_target_pairs={{0,6},{1,97},{2,0},{3,99},{4,2},{5,101},{6,4},{7,103},{32,38},{33,... | collective-permute-start | bytes 466952 | tf_op jit(solution)/shard_map/ppermute | solution.py:58
  33.2 6.5 %copy-start.10 = (s32[1,231]{1,0:T(1,128)S(1)}, s32[1,231]{1,0:T(1,128)}, u32[]{:S(2)}) copy-start(s32[1,231]{1,0:T(1,128)} %param.21) | copy-start | bytes 2776
  33.2 6.7 %copy-start.8 = (f32[1,231,128]{2,0,1:T(1,128)S(1)}, f32[1,231,128]{2,0,1:T(1,128)}, u32[]{:S(2)}) copy-start(f32[1,231,128]{2,0,1:T(1,128)} %param.19) | copy-start | bytes 354820
  33.2 6.7 %copy-start.9 = (f32[1,231,128]{2,0,1:T(1,128)S(1)}, f32[1,231,128]{2,0,1:T(1,128)}, u32[]{:S(2)}) copy-start(f32[1,231,128]{2,0,1:T(1,128)} %param.18) | copy-start | bytes 354820
  33.2 8.6 %collective-permute-start.13 = (bf16[304,512]{1,0:T(8,128)(2,1)S(1)}, bf16[304,512]{1,0:T(8,128)(2,1)S(1)}, u32[]{:S(2)}, u32[]{:S(2)}) collective-permute-start(bf16[304,512]{1,0:T(8,128)(2,1)S(1)} %get-tuple-element.49), channel_id=1, source_target_pairs={{0,64},{1,5},{2,66},{3,7},{4,68},{5,1},{6,70},{7,3},{32,96},{33,37... | collective-permute-start | bytes 933896 | tf_op jit(solution)/shard_map/ppermute | solution.py:62
  35.4 9.6 %collective-permute-start.14 = (bf16[304,512]{1,0:T(8,128)(2,1)S(1)}, bf16[304,512]{1,0:T(8,128)(2,1)S(1)}, u32[]{:S(2)}, u32[]{:S(2)}) collective-permute-start(bf16[304,512]{1,0:T(8,128)(2,1)S(1)} %get-tuple-element.48), channel_id=1, source_target_pairs={{0,32},{1,3},{2,34},{3,5},{4,36},{5,7},{6,38},{7,1},{32,64},{33,35... | collective-permute-start | bytes 933896 | tf_op jit(solution)/shard_map/ppermute | solution.py:62
  36.3 8.7 %copy-start.6 = (f32[1,64,128]{2,1,0:T(8,128)S(1)}, f32[1,64,128]{2,1,0:T(8,128)}, u32[]{:S(2)}) copy-start(f32[1,64,128]{2,1,0:T(8,128)} %param.16) | copy-start | bytes 98308
  36.3 8.7 %copy-start.7 = (f32[1,64,128]{2,1,0:T(8,128)S(1)}, f32[1,64,128]{2,1,0:T(8,128)}, u32[]{:S(2)}) copy-start(f32[1,64,128]{2,1,0:T(8,128)} %param.17) | copy-start | bytes 98308
  36.3 8.7 %collective-permute-start.15 = (bf16[304,512]{1,0:T(8,128)(2,1)S(1)}, bf16[304,512]{1,0:T(8,128)(2,1)S(1)}, u32[]{:S(2)}, u32[]{:S(2)}) collective-permute-start(bf16[304,512]{1,0:T(8,128)(2,1)S(1)} %get-tuple-element.50), channel_id=1, source_target_pairs={{0,96},{1,7},{2,98},{3,1},{4,100},{5,3},{6,102},{7,5},{32,0},{33,3... | collective-permute-start | bytes 933896 | tf_op jit(solution)/shard_map/ppermute | solution.py:62
  45.0 26.2 %copy-start.4 = (bf16[16,128,64]{1,2,0:T(8,128)(2,1)S(1)}, bf16[16,128,64]{1,2,0:T(8,128)(2,1)}, u32[]{:S(2)}) copy-start(bf16[16,128,64]{1,2,0:T(8,128)(2,1)} %param.23) | copy-start | bytes 786436
  46.3 1.2 %collective-permute-start.16 = (f32[16,512]{1,0:T(8,128)S(1)}, f32[16,512]{1,0:T(8,128)S(1)}, u32[]{:S(2)}, u32[]{:S(2)}) collective-permute-start(f32[16,512]{1,0:T(8,128)S(1)} %shard_map.124), channel_id=1, source_target_pairs={{0,1},{1,0},{2,3},{3,2},{4,5},{5,4},{6,7},{7,6},{8,9},{9,8},{10,11... | collective-permute-start | bytes 98312 | tf_op jit(solution)/shard_map/ppermute | solution.py:315
  (5 other events, 18.0 us)

commit v14 on v13

--- a/solution.py
+++ b/solution.py
@@ -314,7 +314,7 @@
 
     summed = blocks + lax.ppermute(blocks, "co", [(0, 1), (1, 0)])
     summed = jnp.sum(spread(summed, False), axis=0)
-    arrived = spread(summed.astype(F32), True)
+    arrived = spread(summed.astype(BF), True)
     return pl.pallas_call(
         sketch_kernel,
         out_shape=jax.ShapeDtypeStruct((EXAMPLES, bank.shape[2]), F32),

time: 72.3 us -> 71.7 us (level)
  no operation moved by 1% of the time
where the time goes in v14:
time: 71.7 us; the launch traced here: 71.5 us
  starting transfers between devices  25.3 us (35%)
  blocking collectives  23.1 us (32%)
  waiting for transfers between devices  12.9 us (18%)
  Pallas kernels  6.38 us (9%)
  local copies, waits for them, and re-layouts  3.22 us (4%)
    all_to_all x2, blocking collectives, spread(): lax.all_to_all(copies, EVERY, split_axis=0, concat_axis=0, tiled=True, ax...  23.1 us
    ppermute x8, starting transfers between devices, send_same(): return lax.ppermute(value, PLANE, pairs(lambda p: along(p, shift)))  13.7 us
    ppermute x3, starting transfers between devices, on_device(): lax.ppermute(portion, ('t1', 't0'), [(i, (i + shift) % 4) for i in range(...  5.9 us
    ppermute x3, starting transfers between devices, send_across(): return lax.ppermute(value, PLANE, pairs(lambda p: across(p, shift)))  5.47 us
    ppermute x3, waiting for transfers between devices, send_across(): return lax.ppermute(value, PLANE, pairs(lambda p: across(p, shift)))  5.07 us
    unnamed x26, local copies, waits for them, and re-layouts  3.19 us
    ppermute x3, waiting for transfers between devices, on_device(): lax.ppermute(portion, ('t1', 't0'), [(i, (i + shift) % 4) for i in range(...  2.64 us
    pallas_call x2, Pallas kernels, partial_call(): pl.pallas_call(functools.partial(partial_kernel, count), out_shape=[jax.S...  2.16 us
  transfers between devices with their start and end apart: 17, of which 10 were waited for; matrix products, arithmetic and copies ran while one was open for 1% of the time, Pallas kernels for 4%

profile of v14, /device:TPU:0, one launch (start us, length us, event | category | flops | bytes accessed | tf_op | source)
XLA Modules:
  0.0 71.5 jit_solution(17198385889695380852)
XLA Ops:
  0.0 1.4 %copy.14 = bf16[128,2048]{0,1:T(8,128)(2,1)S(1)} copy(bf16[128,2048]{1,0:T(8,128)(2,1)} %tokens.1) | data formatting | bytes 1048576 | tf_op args[0]
  1.4 1.5 %copy-done = bf16[128,7392]{0,1:T(8,128)(2,1)S(1)} copy-done((bf16[128,7392]{0,1:T(8,128)(2,1)S(1)}, bf16[128,7392]{0,1:T(8,128)(2,1)}, u32[]{:S(2)}) %copy-start) | copy-done | bytes 1892376
  2.9 1.2 %shard_map.118 = (bf16[4,1216,128]{2,1,0:T(8,128)(2,1)S(1)}, bf16[1216,128]{1,0:T(8,128)(2,1)S(1)}, bf16[1216,128]{1,0:T(8,128)(2,1)S(1)}, bf16[1216,128]{1,0:T(8,128)(2,1)S(1)}, bf16[1216,128]{1,0:T(8,128)(2,1)S(1)}) custom-call(bf16[7392,128]{1,0:T(8,128)(2,1)S(1)} %bitcast.12, bf16[2048,128]{1,0:T(8,128)(2,1)S(1)} %bitcast.14), custom_call_target="tpu_custom_call" | custom-call | bytes 5242880 | tf_op jit(solution)/shard_map/pallas_call | solution.py:250
  5.3 1.9 %collective-permute-done.taken_ref = bf16[4,1216,128]{2,1,0:T(8,128)(2,1)S(1)} collective-permute-done((bf16[4,1216,128]{2,1,0:T(8,128)(2,1)S(1)}, bf16[4,1216,128]{2,1,0:T(8,128)(2,1)S(1)}, u32[]{:S(2)}, u32[]{:S(2)}) %collective-permute-start) | collective-permute-done | bytes 1245216 | tf_op jit(solution)/shard_map/ppermute | solution.py:266
  7.2 3.4 %collective-permute-start.6 = (bf16[2,1216,128]{2,1,0:T(8,128)(2,1)S(1)}, bf16[2,1216,128]{2,1,0:T(8,128)(2,1)S(1)}, u32[]{:S(2)}, u32[]{:S(2)}) collective-permute-start(bf16[2,1216,128]{2,1,0:T(8,128)(2,1)S(1)} %shard_map.121), channel_id=1, source_target_pairs={{0,4},{1,65},{2,6},{3,67},{4,0},{5,69},{6,2},{7,71},{32,36},{33,97... | collective-permute-start | bytes 1867784 | tf_op jit(solution)/shard_map/ppermute | solution.py:58
  10.6 1.9 %collective-permute-start.3 = (f32[128,256]{1,0:T(8,128)S(1)}, f32[128,256]{1,0:T(8,128)S(1)}, u32[]{:S(2)}, u32[]{:S(2)}) collective-permute-start(f32[128,256]{1,0:T(8,128)S(1)} %shard_map.119), channel_id=1, source_target_pairs={{0,8},{8,16},{16,24},{24,0},{1,9},{9,17},{17,25},{25,1},{2,10},{10... | collective-permute-start | bytes 393224 | tf_op jit(solution)/shard_map/ppermute | solution.py:271
  12.5 2.1 %collective-permute-start.4 = (f32[128,256]{1,0:T(8,128)S(1)}, f32[128,256]{1,0:T(8,128)S(1)}, u32[]{:S(2)}, u32[]{:S(2)}) collective-permute-start(f32[128,256]{1,0:T(8,128)S(1)} %shard_map.119), channel_id=1, source_target_pairs={{0,24},{8,0},{16,8},{24,16},{1,25},{9,1},{17,9},{25,17},{2,26},{10... | collective-permute-start | bytes 393224 | tf_op jit(solution)/shard_map/ppermute | solution.py:271
  14.6 1.9 %collective-permute-start.2 = (f32[128,256]{1,0:T(8,128)S(1)}, f32[128,256]{1,0:T(8,128)S(1)}, u32[]{:S(2)}, u32[]{:S(2)}) collective-permute-start(f32[128,256]{1,0:T(8,128)S(1)} %shard_map.119), channel_id=1, source_target_pairs={{0,16},{8,24},{16,0},{24,8},{1,17},{9,25},{17,1},{25,9},{2,18},{10... | collective-permute-start | bytes 393224 | tf_op jit(solution)/shard_map/ppermute | solution.py:271
  18.0 2.0 %collective-permute-start.7 = (bf16[2,912,128]{2,1,0:T(8,128)(2,1)S(1)}, bf16[2,912,128]{2,1,0:T(8,128)(2,1)S(1)}, u32[]{:S(2)}, u32[]{:S(2)}) collective-permute-start(bf16[2,912,128]{2,1,0:T(8,128)(2,1)S(1)} %get-tuple-element.45), channel_id=1, source_target_pairs={{0,6},{1,97},{2,0},{3,99},{4,2},{5,101},{6,4},{7,103},{32,38},{33,... | collective-permute-start | bytes 1400840 | tf_op jit(solution)/shard_map/ppermute | solution.py:58
  20.1 1.9 %collective-permute-done.2 = f32[128,256]{1,0:T(8,128)S(1)} collective-permute-done((f32[128,256]{1,0:T(8,128)S(1)}, f32[128,256]{1,0:T(8,128)S(1)}, u32[]{:S(2)}, u32[]{:S(2)}) %collective-permute-start.2) | collective-permute-done | bytes 131104 | tf_op jit(solution)/shard_map/ppermute | solution.py:271
  22.1 1.2 %collective-permute-done.5 = bf16[128,256]{1,0:T(8,128)(2,1)S(1)} collective-permute-done((bf16[128,256]{1,0:T(8,128)(2,1)S(1)}, bf16[128,256]{1,0:T(8,128)(2,1)S(1)}, u32[]{:S(2)}, u32[]{:S(2)}) %collective-permute-start.5) | collective-permute-done | bytes 65568 | tf_op jit(solution)/shard_map/ppermute | solution.py:275
  23.3 1.6 %collective-permute-start.8 = (bf16[256,256]{1,0:T(8,128)(2,1)S(1)}, bf16[256,256]{1,0:T(8,128)(2,1)S(1)}, u32[]{:S(2)}, u32[]{:S(2)}) collective-permute-start(bf16[256,256]{1,0:T(8,128)(2,1)S(1)} %pad_maximum_fusion.rest_4_), channel_id=1, source_target_pairs={{0,2},{1,33},{2,4},{3,35},{4,6},{5,37},{6,0},{7,39},{32,34},{33,65... | collective-permute-start | bytes 393224 | tf_op jit(solution)/shard_map/ppermute | solution.py:58
  25.0 1.7 %collective-permute-start.9 = (bf16[256,256]{1,0:T(8,128)(2,1)S(1)}, bf16[256,256]{1,0:T(8,128)(2,1)S(1)}, u32[]{:S(2)}, u32[]{:S(2)}) collective-permute-start(bf16[256,256]{1,0:T(8,128)(2,1)S(1)} %pad_maximum_fusion.rest_4_), channel_id=1, source_target_pairs={{0,4},{1,65},{2,6},{3,67},{4,0},{5,69},{6,2},{7,71},{32,36},{33,97... | collective-permute-start | bytes 393224 | tf_op jit(solution)/shard_map/ppermute | solution.py:58
  26.7 1.1 %collective-permute-start.10 = (bf16[256,256]{1,0:T(8,128)(2,1)S(1)}, bf16[256,256]{1,0:T(8,128)(2,1)S(1)}, u32[]{:S(2)}, u32[]{:S(2)}) collective-permute-start(bf16[256,256]{1,0:T(8,128)(2,1)S(1)} %pad_maximum_fusion.rest_4_), channel_id=1, source_target_pairs={{0,6},{1,97},{2,0},{3,99},{4,2},{5,101},{6,4},{7,103},{32,38},{33,... | collective-permute-start | bytes 393224 | tf_op jit(solution)/shard_map/ppermute | solution.py:58
  28.7 2.3 %collective-permute-start.12 = (bf16[2,304,128]{2,1,0:T(8,128)(2,1)S(1)}, bf16[2,304,128]{2,1,0:T(8,128)(2,1)S(1)}, u32[]{:S(2)}, u32[]{:S(2)}) collective-permute-start(bf16[2,304,128]{2,1,0:T(8,128)(2,1)S(1)} %get-tuple-element.53), channel_id=1, source_target_pairs={{0,6},{1,97},{2,0},{3,99},{4,2},{5,101},{6,4},{7,103},{32,38},{33,... | collective-permute-start | bytes 466952 | tf_op jit(solution)/shard_map/ppermute | solution.py:58
  31.9 1.3 %shard_map.122 = (bf16[304,512]{1,0:T(8,128)(2,1)S(1)}, bf16[304,512]{1,0:T(8,128)(2,1)S(1)}, bf16[304,512]{1,0:T(8,128)(2,1)S(1)}) custom-call(s32[32,128]{1,0:T(8,128)S(1)} %bitcast.16, bf16[2,1216,128]{2,1,0:T(8,128)(2,1)S(1)} %get-tuple-element.37.rest_0_, bf16[2,912,128]{2,1,0:T(8,128)(2,1)S(1)} %collective-permute-done.1.rest_1_, ...), custom_call_target="tpu_custom_call" | custom-call | flops 956301312 | bytes 6291456 | tf_op jit(solution)/shard_map/pallas_call | solution.py:156
  33.2 2.2 %collective-permute-start.13 = (bf16[304,512]{1,0:T(8,128)(2,1)S(1)}, bf16[304,512]{1,0:T(8,128)(2,1)S(1)}, u32[]{:S(2)}, u32[]{:S(2)}) collective-permute-start(bf16[304,512]{1,0:T(8,128)(2,1)S(1)} %get-tuple-element.49), channel_id=1, source_target_pairs={{0,64},{1,5},{2,66},{3,7},{4,68},{5,1},{6,70},{7,3},{32,96},{33,37... | collective-permute-start | bytes 933896 | tf_op jit(solution)/shard_map/ppermute | solution.py:62
  36.3 2.4 %collective-permute-start.15 = (bf16[304,512]{1,0:T(8,128)(2,1)S(1)}, bf16[304,512]{1,0:T(8,128)(2,1)S(1)}, u32[]{:S(2)}, u32[]{:S(2)}) collective-permute-start(bf16[304,512]{1,0:T(8,128)(2,1)S(1)} %get-tuple-element.50), channel_id=1, source_target_pairs={{0,96},{1,7},{2,98},{3,1},{4,100},{5,3},{6,102},{7,5},{32,0},{33,3... | collective-permute-start | bytes 933896 | tf_op jit(solution)/shard_map/ppermute | solution.py:62
  39.9 1.8 %collective-permute-done.13.a_ref = bf16[304,512]{1,0:T(8,128)(2,1)S(1)} collective-permute-done((bf16[304,512]{1,0:T(8,128)(2,1)S(1)}, bf16[304,512]{1,0:T(8,128)(2,1)S(1)}, u32[]{:S(2)}, u32[]{:S(2)}) %collective-permute-start.13) | collective-permute-done | bytes 311328 | tf_op jit(solution)/shard_map/ppermute | solution.py:62
  41.8 3.2 %collective-permute-done.14.b_ref = bf16[304,512]{1,0:T(8,128)(2,1)S(1)} collective-permute-done((bf16[304,512]{1,0:T(8,128)(2,1)S(1)}, bf16[304,512]{1,0:T(8,128)(2,1)S(1)}, u32[]{:S(2)}, u32[]{:S(2)}) %collective-permute-start.14) | collective-permute-done | bytes 311328 | tf_op jit(solution)/shard_map/ppermute | solution.py:62
  45.0 1.2 %shard_map.124 = f32[16,512]{1,0:T(8,128)S(1)} custom-call(f32[304,512]{1,0:T(8,128)S(1)} %convert_element_type.20.own_ref, bf16[304,512]{1,0:T(8,128)(2,1)S(1)} %collective-permute-done.13.a_ref, bf16[304,512]{1,0:T(8,128)(2,1)S(1)} %collective-permute-done.14.b_ref, bf16[304,512]{1,0:T(8,128)(2,1)S(1)} %collective-permute-done.15.c_ref, ...), custom_call_target="tpu_custom_call" | custom-call | bytes 3145728 | tf_op jit(solution)/shard_map/pallas_call | solution.py:302
  46.3 1.2 %collective-permute-done.16 = f32[16,512]{1,0:T(8,128)S(1)} collective-permute-done((f32[16,512]{1,0:T(8,128)S(1)}, f32[16,512]{1,0:T(8,128)S(1)}, u32[]{:S(2)}, u32[]{:S(2)}) %collective-permute-start.16) | collective-permute-done | bytes 32800 | tf_op jit(solution)/shard_map/ppermute | solution.py:315
  47.5 13.5 %all_to_all.10 = f32[8,16,512]{2,1,0:T(8,128)S(1)} all-to-all(f32[8,16,512]{2,1,0:T(8,128)S(1)} %broadcast_in_dim.4), channel_id=1, replica_groups={{0,24,2,26,4,28,6,30},{8,16,10,18,12,20,14,22},{1,25,3,27,5,29,7,31},{9..., dimensions={0} | all-to-all | bytes 524288 | tf_op jit(solution)/shard_map/all_to_all | solution.py:216
  61.0 9.6 %all_to_all.11.arrived_ref = bf16[8,16,512]{2,1,0:T(8,128)(2,1)S(1)} all-to-all(bf16[8,16,512]{2,1,0:T(8,128)(2,1)S(1)} %broadcast_in_dim.5), channel_id=1, replica_groups={{0,8,32,40,64,72,96,104},{16,24,48,56,80,88,112,120},{1,9,33,41,65,73,9..., dimensions={0} | all-to-all | bytes 262144 | tf_op jit(solution)/shard_map/all_to_all | solution.py:216
  (57 shorter events, 7.7 us)
Async XLA Ops:
  4.1 3.0 %collective-permute-start = (bf16[4,1216,128]{2,1,0:T(8,128)(2,1)S(1)}, bf16[4,1216,128]{2,1,0:T(8,128)(2,1)S(1)}, u32[]{:S(2)}, u32[]{:S(2)}) collective-permute-start(bf16[4,1216,128]{2,1,0:T(8,128)(2,1)S(1)} %get-tuple-element.32), channel_id=1, source_target_pairs={{0,1},{1,0},{2,3},{3,2},{4,5},{5,4},{6,7},{7,6},{8,9},{9,8},{10,11... | collective-permute-start | bytes 3735560 | tf_op jit(solution)/shard_map/ppermute | solution.py:266
  7.2 24.6 %copy-start.5 = (s32[4096]{0:T(1024)S(1)}, s32[4096]{0:T(1024)}, u32[]{:S(2)}) copy-start(s32[4096]{0:T(1024)} %param.22) | copy-start | bytes 49156
  7.2 19.5 %collective-permute-start.6 = (bf16[2,1216,128]{2,1,0:T(8,128)(2,1)S(1)}, bf16[2,1216,128]{2,1,0:T(8,128)(2,1)S(1)}, u32[]{:S(2)}, u32[]{:S(2)}) collective-permute-start(bf16[2,1216,128]{2,1,0:T(8,128)(2,1)S(1)} %shard_map.121), channel_id=1, source_target_pairs={{0,4},{1,65},{2,6},{3,67},{4,0},{5,69},{6,2},{7,71},{32,36},{33,97... | collective-permute-start | bytes 1867784 | tf_op jit(solution)/shard_map/ppermute | solution.py:58
  10.6 7.4 %collective-permute-start.3 = (f32[128,256]{1,0:T(8,128)S(1)}, f32[128,256]{1,0:T(8,128)S(1)}, u32[]{:S(2)}, u32[]{:S(2)}) collective-permute-start(f32[128,256]{1,0:T(8,128)S(1)} %shard_map.119), channel_id=1, source_target_pairs={{0,8},{8,16},{16,24},{24,0},{1,9},{9,17},{17,25},{25,1},{2,10},{10... | collective-permute-start | bytes 393224 | tf_op jit(solution)/shard_map/ppermute | solution.py:271
  12.5 7.6 %collective-permute-start.4 = (f32[128,256]{1,0:T(8,128)S(1)}, f32[128,256]{1,0:T(8,128)S(1)}, u32[]{:S(2)}, u32[]{:S(2)}) collective-permute-start(f32[128,256]{1,0:T(8,128)S(1)} %shard_map.119), channel_id=1, source_target_pairs={{0,24},{8,0},{16,8},{24,16},{1,25},{9,1},{17,9},{25,17},{2,26},{10... | collective-permute-start | bytes 393224 | tf_op jit(solution)/shard_map/ppermute | solution.py:271
  14.6 7.3 %collective-permute-start.2 = (f32[128,256]{1,0:T(8,128)S(1)}, f32[128,256]{1,0:T(8,128)S(1)}, u32[]{:S(2)}, u32[]{:S(2)}) collective-permute-start(f32[128,256]{1,0:T(8,128)S(1)} %shard_map.119), channel_id=1, source_target_pairs={{0,16},{8,24},{16,0},{24,8},{1,17},{9,25},{17,1},{25,9},{2,18},{10... | collective-permute-start | bytes 393224 | tf_op jit(solution)/shard_map/ppermute | solution.py:271
  16.6 11.2 %collective-permute-start.1 = (bf16[2,912,128]{2,1,0:T(8,128)(2,1)S(1)}, bf16[2,912,128]{2,1,0:T(8,128)(2,1)S(1)}, u32[]{:S(2)}, u32[]{:S(2)}) collective-permute-start(bf16[2,912,128]{2,1,0:T(8,128)(2,1)S(1)} %get-tuple-element.39), channel_id=1, source_target_pairs={{0,2},{1,33},{2,4},{3,35},{4,6},{5,37},{6,0},{7,39},{32,34},{33,65... | collective-permute-start | bytes 1400840 | tf_op jit(solution)/shard_map/ppermute | solution.py:58
  18.0 9.8 %collective-permute-start.7 = (bf16[2,912,128]{2,1,0:T(8,128)(2,1)S(1)}, bf16[2,912,128]{2,1,0:T(8,128)(2,1)S(1)}, u32[]{:S(2)}, u32[]{:S(2)}) collective-permute-start(bf16[2,912,128]{2,1,0:T(8,128)(2,1)S(1)} %get-tuple-element.45), channel_id=1, source_target_pairs={{0,6},{1,97},{2,0},{3,99},{4,2},{5,101},{6,4},{7,103},{32,38},{33,... | collective-permute-start | bytes 1400840 | tf_op jit(solution)/shard_map/ppermute | solution.py:58
  22.0 1.3 %collective-permute-start.5 = (bf16[128,256]{1,0:T(8,128)(2,1)S(1)}, bf16[128,256]{1,0:T(8,128)(2,1)S(1)}, u32[]{:S(2)}, u32[]{:S(2)}) collective-permute-start(bf16[128,256]{1,0:T(8,128)(2,1)S(1)} %add_convert_fusion), channel_id=1, source_target_pairs={{0,1},{1,0},{2,3},{3,2},{4,5},{5,4},{6,7},{7,6},{8,9},{9,8},{10,11... | collective-permute-start | bytes 196616 | tf_op jit(solution)/shard_map/ppermute | solution.py:275
  23.3 7.7 %collective-permute-start.8 = (bf16[256,256]{1,0:T(8,128)(2,1)S(1)}, bf16[256,256]{1,0:T(8,128)(2,1)S(1)}, u32[]{:S(2)}, u32[]{:S(2)}) collective-permute-start(bf16[256,256]{1,0:T(8,128)(2,1)S(1)} %pad_maximum_fusion.rest_4_), channel_id=1, source_target_pairs={{0,2},{1,33},{2,4},{3,35},{4,6},{5,37},{6,0},{7,39},{32,34},{33,65... | collective-permute-start | bytes 393224 | tf_op jit(solution)/shard_map/ppermute | solution.py:58
  25.0 6.5 %collective-permute-start.9 = (bf16[256,256]{1,0:T(8,128)(2,1)S(1)}, bf16[256,256]{1,0:T(8,128)(2,1)S(1)}, u32[]{:S(2)}, u32[]{:S(2)}) collective-permute-start(bf16[256,256]{1,0:T(8,128)(2,1)S(1)} %pad_maximum_fusion.rest_4_), channel_id=1, source_target_pairs={{0,4},{1,65},{2,6},{3,67},{4,0},{5,69},{6,2},{7,71},{32,36},{33,97... | collective-permute-start | bytes 393224 | tf_op jit(solution)/shard_map/ppermute | solution.py:58
  26.7 5.2 %collective-permute-start.10 = (bf16[256,256]{1,0:T(8,128)(2,1)S(1)}, bf16[256,256]{1,0:T(8,128)(2,1)S(1)}, u32[]{:S(2)}, u32[]{:S(2)}) collective-permute-start(bf16[256,256]{1,0:T(8,128)(2,1)S(1)} %pad_maximum_fusion.rest_4_), channel_id=1, source_target_pairs={{0,6},{1,97},{2,0},{3,99},{4,2},{5,101},{6,4},{7,103},{32,38},{33,... | collective-permute-start | bytes 393224 | tf_op jit(solution)/shard_map/ppermute | solution.py:58
  27.8 10.9 %collective-permute-start.11 = (bf16[2,304,128]{2,1,0:T(8,128)(2,1)S(1)}, bf16[2,304,128]{2,1,0:T(8,128)(2,1)S(1)}, u32[]{:S(2)}, u32[]{:S(2)}) collective-permute-start(bf16[2,304,128]{2,1,0:T(8,128)(2,1)S(1)} %get-tuple-element.52), channel_id=1, source_target_pairs={{0,2},{1,33},{2,4},{3,35},{4,6},{5,37},{6,0},{7,39},{32,34},{33,65... | collective-permute-start | bytes 466952 | tf_op jit(solution)/shard_map/ppermute | solution.py:58
  28.7 10.0 %collective-permute-start.12 = (bf16[2,304,128]{2,1,0:T(8,128)(2,1)S(1)}, bf16[2,304,128]{2,1,0:T(8,128)(2,1)S(1)}, u32[]{:S(2)}, u32[]{:S(2)}) collective-permute-start(bf16[2,304,128]{2,1,0:T(8,128)(2,1)S(1)} %get-tuple-element.53), channel_id=1, source_target_pairs={{0,6},{1,97},{2,0},{3,99},{4,2},{5,101},{6,4},{7,103},{32,38},{33,... | collective-permute-start | bytes 466952 | tf_op jit(solution)/shard_map/ppermute | solution.py:58
  33.2 6.5 %copy-start.10 = (s32[1,231]{1,0:T(1,128)S(1)}, s32[1,231]{1,0:T(1,128)}, u32[]{:S(2)}) copy-start(s32[1,231]{1,0:T(1,128)} %param.21) | copy-start | bytes 2776
  33.2 6.7 %copy-start.8 = (f32[1,231,128]{2,0,1:T(1,128)S(1)}, f32[1,231,128]{2,0,1:T(1,128)}, u32[]{:S(2)}) copy-start(f32[1,231,128]{2,0,1:T(1,128)} %param.19) | copy-start | bytes 354820
  33.2 6.7 %copy-start.9 = (f32[1,231,128]{2,0,1:T(1,128)S(1)}, f32[1,231,128]{2,0,1:T(1,128)}, u32[]{:S(2)}) copy-start(f32[1,231,128]{2,0,1:T(1,128)} %param.18) | copy-start | bytes 354820
  33.2 8.6 %collective-permute-start.13 = (bf16[304,512]{1,0:T(8,128)(2,1)S(1)}, bf16[304,512]{1,0:T(8,128)(2,1)S(1)}, u32[]{:S(2)}, u32[]{:S(2)}) collective-permute-start(bf16[304,512]{1,0:T(8,128)(2,1)S(1)} %get-tuple-element.49), channel_id=1, source_target_pairs={{0,64},{1,5},{2,66},{3,7},{4,68},{5,1},{6,70},{7,3},{32,96},{33,37... | collective-permute-start | bytes 933896 | tf_op jit(solution)/shard_map/ppermute | solution.py:62
  35.4 9.6 %collective-permute-start.14 = (bf16[304,512]{1,0:T(8,128)(2,1)S(1)}, bf16[304,512]{1,0:T(8,128)(2,1)S(1)}, u32[]{:S(2)}, u32[]{:S(2)}) collective-permute-start(bf16[304,512]{1,0:T(8,128)(2,1)S(1)} %get-tuple-element.48), channel_id=1, source_target_pairs={{0,32},{1,3},{2,34},{3,5},{4,36},{5,7},{6,38},{7,1},{32,64},{33,35... | collective-permute-start | bytes 933896 | tf_op jit(solution)/shard_map/ppermute | solution.py:62
  36.3 8.7 %copy-start.6 = (f32[1,64,128]{2,1,0:T(8,128)S(1)}, f32[1,64,128]{2,1,0:T(8,128)}, u32[]{:S(2)}) copy-start(f32[1,64,128]{2,1,0:T(8,128)} %param.16) | copy-start | bytes 98308
  36.3 8.7 %copy-start.7 = (f32[1,64,128]{2,1,0:T(8,128)S(1)}, f32[1,64,128]{2,1,0:T(8,128)}, u32[]{:S(2)}) copy-start(f32[1,64,128]{2,1,0:T(8,128)} %param.17) | copy-start | bytes 98308
  36.3 8.7 %collective-permute-start.15 = (bf16[304,512]{1,0:T(8,128)(2,1)S(1)}, bf16[304,512]{1,0:T(8,128)(2,1)S(1)}, u32[]{:S(2)}, u32[]{:S(2)}) collective-permute-start(bf16[304,512]{1,0:T(8,128)(2,1)S(1)} %get-tuple-element.50), channel_id=1, source_target_pairs={{0,96},{1,7},{2,98},{3,1},{4,100},{5,3},{6,102},{7,5},{32,0},{33,3... | collective-permute-start | bytes 933896 | tf_op jit(solution)/shard_map/ppermute | solution.py:62
  39.9 30.7 %copy-start.4 = (bf16[16,128,64]{1,2,0:T(8,128)(2,1)S(1)}, bf16[16,128,64]{1,2,0:T(8,128)(2,1)}, u32[]{:S(2)}) copy-start(bf16[16,128,64]{1,2,0:T(8,128)(2,1)} %param.23) | copy-start | bytes 786436
  46.3 1.2 %collective-permute-start.16 = (f32[16,512]{1,0:T(8,128)S(1)}, f32[16,512]{1,0:T(8,128)S(1)}, u32[]{:S(2)}, u32[]{:S(2)}) collective-permute-start(f32[16,512]{1,0:T(8,128)S(1)} %shard_map.124), channel_id=1, source_target_pairs={{0,1},{1,0},{2,3},{3,2},{4,5},{5,4},{6,7},{7,6},{8,9},{9,8},{10,11... | collective-permute-start | bytes 98312 | tf_op jit(solution)/shard_map/ppermute | solution.py:315
  (5 other events, 18.0 us)
